TPU v7x, 32 devices: a whole 2x2x4 slice. The times are simulated.
32 devices in a mesh: groups: 2 (over x), kx: 16 (over z, y, core).
Axes of the slice: x: 2, y: 2, z: 4, core: 2. Of those that a mesh axis runs over, the one named last changes fastest.
Arguments:
- latent: bfloat16 [2560, 16, 128], P(('groups', 'kx')), parts along dimension 0, may hold values from -6 to 6
- cond_lists: int32 [2560, 3], P(('groups', 'kx')), parts along dimension 0, may hold values from 0 to 1279, as said below
- cond_weights: bfloat16 [2560, 3, 128, 128], P(('groups', 'kx')), parts along dimension 0, may hold values from -0.3125 to 0.3125
- precision_factor: bfloat16 [2560, 128, 128], P(('groups', 'kx')), parts along dimension 0, may hold values from -0.5 to 0.5
Outputs:
- gradient: float32 [2560, 16, 128], P(('groups', 'kx')), parts along dimension 0
There are 2 independent parts, one for each index of `groups`. A program takes and returns all parts, laid end to end along the dimension named above; each array names one. Nothing has to cross between parts.
Inputs may be any that keep to these rules, and one draw needn't show every extreme that they name: `cond_lists`: leaf block l belongs to index l // 80 of kx. An entry of a leaf block of index d names a leaf block of index d, d - 1, d - 2, d - 4 or d - 8, never its own leaf block. For each o of 1, 2, 4, 8 with d - o not negative, exactly 30 of the 240 entries of index d name leaf blocks of index d - o; all others name leaf blocks of index d.
All inputs are finite; a program needn't handle non-finite values.
Results may differ from a plain program's by a relative error of at most 0.0037.
Values may be sent and summed in bfloat16 or wider, within the bound.
No kernel may reach another device: no remote copies, remote signals or barrier semaphores. Data moves between devices by JAX's collectives and lax.ppermute only.
A program may use at most 64 MiB of HBM per device.

v0:
```python
import jax
import jax.numpy as jnp
from jax import lax
from jax.sharding import PartitionSpec as P


def passed_along(block, axis, distance):
    devices = range(lax.axis_size(axis))
    route = [(i - distance, i) for i in devices if i - distance in devices]
    return lax.ppermute(block, axis, route)


def serve_rows(latent, wanted):
    valid = wanted >= 0
    picked = latent[jnp.maximum(wanted, 0)]
    return jnp.where(valid[:, None, None], picked, jnp.zeros_like(picked))


def per_device(latent, cond_lists, cond_weights, precision_factor):
    my_index = lax.axis_index("kx")
    leaf_dev, samples, width = latent.shape
    slots = 3 * leaf_dev
    capacity = slots // 8
    flat_lists = cond_lists.reshape(-1)
    owner_index = flat_lists // leaf_dev
    local_index = flat_lists % leaf_dev
    offset = my_index - owner_index
    slot_ids = jnp.arange(capacity, dtype=jnp.int32)
    leaf_ids = jnp.arange(leaf_dev, dtype=jnp.int32)
    near_rows = latent[local_index]
    records = []
    for step_offset in (1, 2, 4, 8):
        chosen = offset == step_offset
        slot_rank = jnp.cumsum(chosen.astype(jnp.int32)) - 1
        slot_place = jnp.where(chosen, slot_rank, capacity)
        matches = slot_place[:, None] == slot_ids[None, :]
        asked = jnp.sum(jnp.where(matches, local_index[:, None] + 1, 0), axis=0) - 1
        wanted = passed_along(asked, "kx", -step_offset)
        served = serve_rows(latent, wanted)
        arrived = passed_along(served, "kx", step_offset)
        taken = arrived[jnp.minimum(slot_place, capacity - 1)]
        near_rows = jnp.where(chosen[:, None, None], taken, near_rows)
        records.append((step_offset, chosen, slot_place, wanted))
    near_rows = near_rows.reshape(leaf_dev, 3, samples, width)
    mean_part = jnp.einsum(
        "gksb,gkba->gsa", near_rows, cond_weights, preferred_element_type=jnp.float32
    )
    residual_low = (latent.astype(jnp.float32) - mean_part).astype(jnp.bfloat16)
    innovation = jnp.einsum(
        "gsb,gba->gsa", residual_low, precision_factor, preferred_element_type=jnp.float32
    ).astype(jnp.bfloat16)
    back_full = jnp.einsum(
        "gsa,gba->gsb", innovation, precision_factor, preferred_element_type=jnp.float32
    )
    back_low = back_full.astype(jnp.bfloat16)
    term_all = jnp.einsum(
        "gsa,gkba->gksb", back_low, cond_weights, preferred_element_type=jnp.float32
    )
    term_flat = term_all.reshape(slots, samples * width)
    home_mask = (offset == 0)[None, :] & (local_index[None, :] == leaf_ids[:, None])
    gradient = jnp.dot(
        home_mask.astype(jnp.float32), term_flat, precision=lax.Precision.HIGHEST
    ) - back_full.reshape(leaf_dev, samples * width)
    for step_offset, chosen, slot_place, indices in records:
        outgoing = (
            jnp.zeros((capacity, samples * width), jnp.float32)
            .at[slot_place]
            .set(term_flat, mode="drop")
        )
        incoming = passed_along(outgoing, "kx", -step_offset)
        selector = (indices[None, :] == leaf_ids[:, None]).astype(jnp.float32)
        gradient = gradient + jnp.dot(selector, incoming, precision=lax.Precision.HIGHEST)
    return gradient.reshape(leaf_dev, samples, width)


def solution(mesh):
    return jax.shard_map(
        per_device,
        mesh=mesh,
        in_specs=(
            P(("groups", "kx"), None, None),
            P(("groups", "kx"), None),
            P(("groups", "kx"), None, None, None),
            P(("groups", "kx"), None, None),
        ),
        out_specs=P(("groups", "kx"), None, None),
        check_vma=False,
    )
```

profile of v0, /device:TPU:0, one launch (start us, length us, event | category | flops | bytes accessed | tf_op | source)
XLA Modules:
  0.0 116.4 jit_solution(15191581069142237278)
XLA Ops:
  0.0 0.8 broadcast_remainder_fusion
  0.9 0.7 broadcast_compare_fusion.2
  1.6 0.1 copy.17
  1.7 0.2 ne.98
  1.9 0.1 copy.18
  2.0 0.2 rem.54
  2.2 0.1 copy.19
  2.3 0.2 div.27
  2.5 0.3 reduce-window.48
  2.9 0.1 slice_reduce_fusion.1
  3.1 0.3 reduce-window.36
  3.5 0.1 slice_reduce_fusion.2
  3.7 0.3 reduce-window.34
  4.1 0.1 slice_reduce_fusion.3
  4.3 0.3 reduce-window.50
  4.7 0.1 slice_reduce_fusion
  5.0 0.2 select_reduce_fusion
  5.1 1.3 %collective-permute-start = (s32[30]{0:T(128)S(1)}, s32[30]{0:T(128)S(1)}, u32[]{:S(2)}, u32[]{:S(2)}) collective-permute-start(s32[30]{0:T(128)S(1)} %broadcast_add_fusion.4), channel_id=1, source_target_pairs={{8,0},{9,1},{10,2},{11,3},{12,4},{13,5},{14,6},{15,7},{24,16},{25,... | collective-permute-start | bytes 368 | tf_op jit(solution)/shard_map/ppermute | solution.py:10
  6.4 1.3 %collective-permute-start.4 = (s32[30]{0:T(128)S(1)}, s32[30]{0:T(128)S(1)}, u32[]{:S(2)}, u32[]{:S(2)}) collective-permute-start(s32[30]{0:T(128)S(1)} %broadcast_add_fusion.2), channel_id=1, source_target_pairs={{2,0},{3,1},{4,2},{5,3},{6,4},{7,5},{8,6},{9,7},{10,8},{11,9},{12,... | collective-permute-start | bytes 368 | tf_op jit(solution)/shard_map/ppermute | solution.py:10
  7.8 1.3 %collective-permute-start.2 = (s32[30]{0:T(128)S(1)}, s32[30]{0:T(128)S(1)}, u32[]{:S(2)}, u32[]{:S(2)}) collective-permute-start(s32[30]{0:T(128)S(1)} %broadcast_add_fusion.3), channel_id=1, source_target_pairs={{4,0},{5,1},{6,2},{7,3},{8,4},{9,5},{10,6},{11,7},{12,8},{13,9},{1... | collective-permute-start | bytes 368 | tf_op jit(solution)/shard_map/ppermute | solution.py:10
  9.1 1.3 %collective-permute-start.6 = (s32[30]{0:T(128)S(1)}, s32[30]{0:T(128)S(1)}, u32[]{:S(2)}, u32[]{:S(2)}) collective-permute-start(s32[30]{0:T(128)S(1)} %broadcast_add_fusion.1), channel_id=1, source_target_pairs={{1,0},{2,1},{3,2},{4,3},{5,4},{6,5},{7,6},{8,7},{9,8},{10,9},{11,1... | collective-permute-start | bytes 368 | tf_op jit(solution)/shard_map/ppermute | solution.py:10
  10.4 0.2 rem.56
  10.6 1.3 %collective-permute-done = s32[30]{0:T(128)S(1)} collective-permute-done((s32[30]{0:T(128)S(1)}, s32[30]{0:T(128)S(1)}, u32[]{:S(2)}, u32[]{:S(2)}) %collective-permute-start) | collective-permute-done | bytes 152 | tf_op jit(solution)/shard_map/ppermute | solution.py:10
  12.0 0.9 collective-permute-done.4
  12.8 3.4 %collective-permute-done.2 = s32[30]{0:T(128)S(1)} collective-permute-done((s32[30]{0:T(128)S(1)}, s32[30]{0:T(128)S(1)}, u32[]{:S(2)}, u32[]{:S(2)}) %collective-permute-start.2) | collective-permute-done | bytes 152 | tf_op jit(solution)/shard_map/ppermute | solution.py:10
  16.3 1.6 %gather_fusion.6 = bf16[30,16,128]{2,1,0:T(8,128)(2,1)S(1)} fusion(bf16[80,16,128]{2,1,0:T(8,128)(2,1)} %param.4, s32[1024]{0:T(1024)S(1)} %pad_clamp_fusion.2), kind=kCustom, calls=%fused_computation.6 | custom fusion | bytes 245880 | tf_op jit(solution)/shard_map/gather | solution.py:15
  17.8 1.6 %gather_fusion.2 = bf16[30,16,128]{2,1,0:T(8,128)(2,1)S(1)} fusion(bf16[80,16,128]{2,1,0:T(8,128)(2,1)} %param.4, s32[1024]{0:T(1024)S(1)} %pad_clamp_fusion.6), kind=kCustom, calls=%fused_computation.2 | custom fusion | bytes 245880 | tf_op jit(solution)/shard_map/gather | solution.py:15
  19.4 1.6 %gather_fusion.4 = bf16[30,16,128]{2,1,0:T(8,128)(2,1)S(1)} fusion(bf16[80,16,128]{2,1,0:T(8,128)(2,1)} %param.4, s32[1024]{0:T(1024)S(1)} %pad_clamp_fusion.4), kind=kCustom, calls=%fused_computation.4 | custom fusion | bytes 245880 | tf_op jit(solution)/shard_map/gather | solution.py:15
  21.0 1.6 %gather_fusion = bf16[30,16,128]{2,1,0:T(8,128)(2,1)S(1)} fusion(bf16[80,16,128]{2,1,0:T(8,128)(2,1)} %param.4, s32[1024]{0:T(1024)S(1)} %pad_clamp_fusion.8), kind=kCustom, calls=%fused_computation | custom fusion | bytes 245880 | tf_op jit(solution)/shard_map/gather | solution.py:15
  22.5 0.8 broadcast_select_fusion.3
  23.3 5.0 %collective-permute-start.1 = (bf16[30,16,128]{2,1,0:T(8,128)(2,1)}, bf16[30,16,128]{2,1,0:T(8,128)(2,1)S(1)}, u32[]{:S(2)}, u32[]{:S(2)}) collective-permute-start(bf16[30,16,128]{2,1,0:T(8,128)(2,1)} %broadcast_select_fusion.3), channel_id=1, source_target_pairs={{0,8},{1,9},{2,10},{3,11},{4,12},{5,13},{6,14},{7,15},{16,24},{17,... | collective-permute-start | bytes 368648 | tf_op jit(solution)/shard_map/ppermute | solution.py:10
  28.3 0.8 broadcast_select_fusion.1
  29.1 2.9 %collective-permute-start.5 = (bf16[30,16,128]{2,1,0:T(8,128)(2,1)}, bf16[30,16,128]{2,1,0:T(8,128)(2,1)S(1)}, u32[]{:S(2)}, u32[]{:S(2)}) collective-permute-start(bf16[30,16,128]{2,1,0:T(8,128)(2,1)} %broadcast_select_fusion.1), channel_id=1, source_target_pairs={{0,2},{1,3},{2,4},{3,5},{4,6},{5,7},{6,8},{7,9},{8,10},{9,11},{10,... | collective-permute-start | bytes 368648 | tf_op jit(solution)/shard_map/ppermute | solution.py:10
  32.0 0.8 broadcast_select_fusion.2
  32.8 3.6 %collective-permute-start.3 = (bf16[30,16,128]{2,1,0:T(8,128)(2,1)}, bf16[30,16,128]{2,1,0:T(8,128)(2,1)S(1)}, u32[]{:S(2)}, u32[]{:S(2)}) collective-permute-start(bf16[30,16,128]{2,1,0:T(8,128)(2,1)} %broadcast_select_fusion.2), channel_id=1, source_target_pairs={{0,4},{1,5},{2,6},{3,7},{4,8},{5,9},{6,10},{7,11},{8,12},{9,13},{1... | collective-permute-start | bytes 368648 | tf_op jit(solution)/shard_map/ppermute | solution.py:10
  36.3 0.8 broadcast_select_fusion
  37.1 1.4 %collective-permute-start.7 = (bf16[30,16,128]{2,1,0:T(8,128)(2,1)}, bf16[30,16,128]{2,1,0:T(8,128)(2,1)S(1)}, u32[]{:S(2)}, u32[]{:S(2)}) collective-permute-start(bf16[30,16,128]{2,1,0:T(8,128)(2,1)} %broadcast_select_fusion), channel_id=1, source_target_pairs={{0,1},{1,2},{2,3},{3,4},{4,5},{5,6},{6,7},{7,8},{8,9},{9,10},{10,1... | collective-permute-start | bytes 368648 | tf_op jit(solution)/shard_map/ppermute | solution.py:10
  38.5 0.1 copy.21
  38.6 0.1 copy.20
  38.8 0.1 copy.22
  38.9 0.1 copy.23
  39.0 1.7 %gather_fusion.8 = bf16[240,16,128]{2,1,0:T(8,128)(2,1)} fusion(bf16[80,16,128]{2,1,0:T(8,128)(2,1)S(1)} %copy-done.1, s32[1024]{0:T(1024)S(1)} %pad_clamp_fusion), kind=kCustom, calls=%fused_computation.8 | custom fusion | bytes 1967040 | tf_op jit(solution)/shard_map/gather | solution.py:30
  40.8 1.8 %gather_fusion.7 = bf16[240,16,128]{2,1,0:T(8,128)(2,1)} fusion(bf16[30,16,128]{2,1,0:T(8,128)(2,1)S(1)} %collective-permute-done.7, s32[1024]{0:T(1024)S(1)} %pad_clamp_fusion.1), kind=kCustom, calls=%fused_computation.7 | custom fusion | bytes 1967040 | tf_op jit(solution)/shard_map/gather | solution.py:41
  42.5 1.8 %gather_fusion.3 = bf16[240,16,128]{2,1,0:T(8,128)(2,1)} fusion(bf16[30,16,128]{2,1,0:T(8,128)(2,1)S(1)} %collective-permute-done.3, s32[1024]{0:T(1024)S(1)} %pad_clamp_fusion.5), kind=kCustom, calls=%fused_computation.3 | custom fusion | bytes 1967040 | tf_op jit(solution)/shard_map/gather | solution.py:41
  44.3 1.7 %gather_fusion.5 = bf16[240,16,128]{2,1,0:T(8,128)(2,1)} fusion(bf16[30,16,128]{2,1,0:T(8,128)(2,1)S(1)} %collective-permute-done.5, s32[1024]{0:T(1024)S(1)} %pad_clamp_fusion.3), kind=kCustom, calls=%fused_computation.5 | custom fusion | bytes 1967040 | tf_op jit(solution)/shard_map/gather | solution.py:41
  46.1 1.7 %gather_fusion.1 = bf16[240,16,128]{2,1,0:T(8,128)(2,1)} fusion(bf16[30,16,128]{2,1,0:T(8,128)(2,1)S(1)} %collective-permute-done.1, s32[1024]{0:T(1024)S(1)} %pad_clamp_fusion.7), kind=kCustom, calls=%fused_computation.1 | custom fusion | bytes 1967040 | tf_op jit(solution)/shard_map/gather | solution.py:41
  47.8 7.2 %fusion.19 = bf16[80,16,128]{2,1,0:T(8,128)(2,1)} fusion(bf16[80,3,128,128]{3,2,1,0:T(8,128)(2,1)} %param.6, bf16[80,3,16,128]{3,2,1,0:T(8,128)(2,1)} %bitcast.77, bf16[80,3,16,128]{3,2,1,0:T(8,128)(2,1)} %bitcast.75, bf16[80,3,16,128]{3,2,1,0:T(8,128)(2,1)} %bitcast.76, bf16[80,3,16,128]{3,2,1,0:T(8,128)(2,1)} %bitcast.74, ...), kind=kOutput, calls=%fused_computation.35 | convolution fusion | flops 128286720 | bytes 13435840 | tf_op jit(solution)/shard_map/gksb,gkba->gsa/dot_general | solution.py:45
  55.0 3.1 %fusion.20 = f32[80,16,128]{2,1,0:T(8,128)S(1)} fusion(bf16[80,128,128]{2,1,0:T(8,128)(2,1)S(1)} %copy-done, bf16[80,16,128]{2,1,0:T(8,128)(2,1)} %fusion.19), kind=kOutput, calls=%fused_computation.37 | convolution fusion | flops 84049920 | bytes 3604480 | tf_op jit(solution)/shard_map/gsa,gba->gsb/dot_general | solution.py:52
  58.1 7.4 %fusion.29 = f32[80,16,3,128]{3,1,2,0:T(8,128)} fusion(bf16[80,3,128,128]{3,2,1,0:T(8,128)(2,1)} %param.6, f32[80,16,128]{2,1,0:T(8,128)S(1)} %fusion.20), kind=kOutput, calls=%fused_computation.46 | convolution fusion | flops 125992960 | bytes 10485760 | tf_op jit(solution)/shard_map/gsa,gkba->gksb/dot_general | solution.py:56
  65.5 4.1 %scatter_custom_fusion.3 = f32[30,2048]{1,0:T(8,128)} fusion(s32[240]{0:T(256)S(1)} %compare_select_fusion.1, f32[30,8,16,128]{3,2,1,0:T(8,128)} %bitcast.67, f32[]{:T(128)} %constant.66.clone.1), kind=kCustom, calls=%fused_computation.18 | custom fusion | bytes 2211844 | tf_op jit(solution)/shard_map/scatter | solution.py:68
  69.5 4.1 %scatter_custom_fusion.2 = f32[30,2048]{1,0:T(8,128)} fusion(s32[240]{0:T(256)S(1)} %get-tuple-element.15, f32[30,8,16,128]{3,2,1,0:T(8,128)} %bitcast.68, f32[]{:T(128)} %constant.66.clone.1), kind=kCustom, calls=%fused_computation.20 | custom fusion | bytes 2211844 | tf_op jit(solution)/shard_map/scatter | solution.py:68
  73.6 4.1 %scatter_custom_fusion.1 = f32[30,2048]{1,0:T(8,128)} fusion(s32[240]{0:T(256)S(1)} %get-tuple-element.33, f32[30,8,16,128]{3,2,1,0:T(8,128)} %bitcast.69, f32[]{:T(128)} %constant.66.clone.1), kind=kCustom, calls=%fused_computation.22 | custom fusion | bytes 2211844 | tf_op jit(solution)/shard_map/scatter | solution.py:68
  77.7 3.5 %scatter_custom_fusion = f32[30,2048]{1,0:T(8,128)S(1)} fusion(s32[240]{0:T(256)S(1)} %get-tuple-element.9, f32[30,8,16,128]{3,2,1,0:T(8,128)} %bitcast.70, f32[]{:T(128)} %constant.66.clone.1), kind=kCustom, calls=%fused_computation.24 | custom fusion | bytes 2211844 | tf_op jit(solution)/shard_map/scatter | solution.py:68
  81.2 1.3 %collective-permute-start.8 = (f32[30,2048]{1,0:T(8,128)S(1)}, f32[30,2048]{1,0:T(8,128)S(1)}, u32[]{:S(2)}, u32[]{:S(2)}) collective-permute-start(f32[30,2048]{1,0:T(8,128)S(1)} %scatter_custom_fusion), channel_id=1, source_target_pairs={{1,0},{2,1},{3,2},{4,3},{5,4},{6,5},{7,6},{8,7},{9,8},{10,9},{11,1... | collective-permute-start | bytes 737288 | tf_op jit(solution)/shard_map/ppermute | solution.py:10
  82.5 1.3 %collective-permute-start.9 = (f32[30,2048]{1,0:T(8,128)}, f32[30,2048]{1,0:T(8,128)S(1)}, u32[]{:S(2)}, u32[]{:S(2)}) collective-permute-start(f32[30,2048]{1,0:T(8,128)} %scatter_custom_fusion.1), channel_id=1, source_target_pairs={{2,0},{3,1},{4,2},{5,3},{6,4},{7,5},{8,6},{9,7},{10,8},{11,9},{12,... | collective-permute-start | bytes 737288 | tf_op jit(solution)/shard_map/ppermute | solution.py:10
  83.8 1.3 %collective-permute-start.10 = (f32[30,2048]{1,0:T(8,128)}, f32[30,2048]{1,0:T(8,128)S(1)}, u32[]{:S(2)}, u32[]{:S(2)}) collective-permute-start(f32[30,2048]{1,0:T(8,128)} %scatter_custom_fusion.2), channel_id=1, source_target_pairs={{4,0},{5,1},{6,2},{7,3},{8,4},{9,5},{10,6},{11,7},{12,8},{13,9},{1... | collective-permute-start | bytes 737288 | tf_op jit(solution)/shard_map/ppermute | solution.py:10
  85.1 1.3 %collective-permute-start.11 = (f32[30,2048]{1,0:T(8,128)}, f32[30,2048]{1,0:T(8,128)S(1)}, u32[]{:S(2)}, u32[]{:S(2)}) collective-permute-start(f32[30,2048]{1,0:T(8,128)} %scatter_custom_fusion.3), channel_id=1, source_target_pairs={{8,0},{9,1},{10,2},{11,3},{12,4},{13,5},{14,6},{15,7},{24,16},{25,... | collective-permute-start | bytes 737288 | tf_op jit(solution)/shard_map/ppermute | solution.py:10
  86.4 3.0 %convolution_subtract_fusion = f32[80,2048]{1,0:T(8,128)S(1)} fusion(f32[30,8,16,128]{3,2,1,0:T(8,128)} %bitcast.71, f32[10,8,16,128]{3,2,1,0:T(8,128)S(1)} %bitcast.72, s32[240]{0:T(256)S(1)} %get-tuple-element.27, pred[240]{0:T(512)(128)(4,1)S(1)} %get-tuple-element.11), kind=kOutput, calls=%fused_computation.13 | convolution fusion | flops 472061440 | bytes 3278000 | tf_op jit(solution)/shard_map/dot_general | solution.py:61
  89.4 24.2 %collective-permute-done.11 = f32[30,2048]{1,0:T(8,128)S(1)} collective-permute-done((f32[30,2048]{1,0:T(8,128)}, f32[30,2048]{1,0:T(8,128)S(1)}, u32[]{:S(2)}, u32[]{:S(2)}) %collective-permute-start.11) | collective-permute-done | bytes 245792 | tf_op jit(solution)/shard_map/ppermute | solution.py:10
  113.6 0.4 fusion.41
  114.1 0.4 fusion.40
  114.5 0.4 fusion.39
  114.9 0.5 fusion.18
  115.4 1.0 copy.29
  (72 shorter events, 1.0 us)
Async XLA Ops:
  0.0 55.0 %copy-start = (bf16[80,128,128]{2,1,0:T(8,128)(2,1)S(1)}, bf16[80,128,128]{2,1,0:T(8,128)(2,1)}, u32[]{:S(2)}) copy-start(bf16[80,128,128]{2,1,0:T(8,128)(2,1)} %param.7) | copy-start | bytes 7864324
  0.0 39.0 %copy-start.1 = (bf16[80,16,128]{2,1,0:T(8,128)(2,1)S(1)}, bf16[80,16,128]{2,1,0:T(8,128)(2,1)}, u32[]{:S(2)}) copy-start(bf16[80,16,128]{2,1,0:T(8,128)(2,1)} %param.4) | copy-start | bytes 983044
  5.1 6.8 %collective-permute-start = (s32[30]{0:T(128)S(1)}, s32[30]{0:T(128)S(1)}, u32[]{:S(2)}, u32[]{:S(2)}) collective-permute-start(s32[30]{0:T(128)S(1)} %broadcast_add_fusion.4), channel_id=1, source_target_pairs={{8,0},{9,1},{10,2},{11,3},{12,4},{13,5},{14,6},{15,7},{24,16},{25,... | collective-permute-start | bytes 368 | tf_op jit(solution)/shard_map/ppermute | solution.py:10
  6.4 6.4 %collective-permute-start.4 = (s32[30]{0:T(128)S(1)}, s32[30]{0:T(128)S(1)}, u32[]{:S(2)}, u32[]{:S(2)}) collective-permute-start(s32[30]{0:T(128)S(1)} %broadcast_add_fusion.2), channel_id=1, source_target_pairs={{2,0},{3,1},{4,2},{5,3},{6,4},{7,5},{8,6},{9,7},{10,8},{11,9},{12,... | collective-permute-start | bytes 368 | tf_op jit(solution)/shard_map/ppermute | solution.py:10
  7.8 8.5 %collective-permute-start.2 = (s32[30]{0:T(128)S(1)}, s32[30]{0:T(128)S(1)}, u32[]{:S(2)}, u32[]{:S(2)}) collective-permute-start(s32[30]{0:T(128)S(1)} %broadcast_add_fusion.3), channel_id=1, source_target_pairs={{4,0},{5,1},{6,2},{7,3},{8,4},{9,5},{10,6},{11,7},{12,8},{13,9},{1... | collective-permute-start | bytes 368 | tf_op jit(solution)/shard_map/ppermute | solution.py:10
  9.1 7.2 %collective-permute-start.6 = (s32[30]{0:T(128)S(1)}, s32[30]{0:T(128)S(1)}, u32[]{:S(2)}, u32[]{:S(2)}) collective-permute-start(s32[30]{0:T(128)S(1)} %broadcast_add_fusion.1), channel_id=1, source_target_pairs={{1,0},{2,1},{3,2},{4,3},{5,4},{6,5},{7,6},{8,7},{9,8},{10,9},{11,1... | collective-permute-start | bytes 368 | tf_op jit(solution)/shard_map/ppermute | solution.py:10
  12.0 28.8 %copy-start.2 = (s32[30]{0:T(128)}, s32[30]{0:T(128)S(1)}, u32[]{:S(2)}) copy-start(s32[30]{0:T(128)S(1)} %collective-permute-done) | copy-start | bytes 364
  16.2 22.4 %copy-start.4 = (s32[30]{0:T(128)}, s32[30]{0:T(128)S(1)}, u32[]{:S(2)}) copy-start(s32[30]{0:T(128)S(1)} %collective-permute-done.2) | copy-start | bytes 364
  16.2 22.4 %copy-start.6 = (s32[30]{0:T(128)}, s32[30]{0:T(128)S(1)}, u32[]{:S(2)}) copy-start(s32[30]{0:T(128)S(1)} %collective-permute-done.6) | copy-start | bytes 364
  23.3 22.8 %collective-permute-start.1 = (bf16[30,16,128]{2,1,0:T(8,128)(2,1)}, bf16[30,16,128]{2,1,0:T(8,128)(2,1)S(1)}, u32[]{:S(2)}, u32[]{:S(2)}) collective-permute-start(bf16[30,16,128]{2,1,0:T(8,128)(2,1)} %broadcast_select_fusion.3), channel_id=1, source_target_pairs={{0,8},{1,9},{2,10},{3,11},{4,12},{5,13},{6,14},{7,15},{16,24},{17,... | collective-permute-start | bytes 368648 | tf_op jit(solution)/shard_map/ppermute | solution.py:10
  29.1 15.2 %collective-permute-start.5 = (bf16[30,16,128]{2,1,0:T(8,128)(2,1)}, bf16[30,16,128]{2,1,0:T(8,128)(2,1)S(1)}, u32[]{:S(2)}, u32[]{:S(2)}) collective-permute-start(bf16[30,16,128]{2,1,0:T(8,128)(2,1)} %broadcast_select_fusion.1), channel_id=1, source_target_pairs={{0,2},{1,3},{2,4},{3,5},{4,6},{5,7},{6,8},{7,9},{8,10},{9,11},{10,... | collective-permute-start | bytes 368648 | tf_op jit(solution)/shard_map/ppermute | solution.py:10
  32.8 9.8 %collective-permute-start.3 = (bf16[30,16,128]{2,1,0:T(8,128)(2,1)}, bf16[30,16,128]{2,1,0:T(8,128)(2,1)S(1)}, u32[]{:S(2)}, u32[]{:S(2)}) collective-permute-start(bf16[30,16,128]{2,1,0:T(8,128)(2,1)} %broadcast_select_fusion.2), channel_id=1, source_target_pairs={{0,4},{1,5},{2,6},{3,7},{4,8},{5,9},{6,10},{7,11},{8,12},{9,13},{1... | collective-permute-start | bytes 368648 | tf_op jit(solution)/shard_map/ppermute | solution.py:10
  37.1 3.7 %collective-permute-start.7 = (bf16[30,16,128]{2,1,0:T(8,128)(2,1)}, bf16[30,16,128]{2,1,0:T(8,128)(2,1)S(1)}, u32[]{:S(2)}, u32[]{:S(2)}) collective-permute-start(bf16[30,16,128]{2,1,0:T(8,128)(2,1)} %broadcast_select_fusion), channel_id=1, source_target_pairs={{0,1},{1,2},{2,3},{3,4},{4,5},{5,6},{6,7},{7,8},{8,9},{9,10},{10,1... | collective-permute-start | bytes 368648 | tf_op jit(solution)/shard_map/ppermute | solution.py:10
  81.1 32.5 %copy-start.3 = (s32[30]{0:T(128)S(1)}, s32[30]{0:T(128)}, u32[]{:S(2)}) copy-start(s32[30]{0:T(128)} %copy-done.2) | copy-start | bytes 364
  81.2 33.8 %collective-permute-start.8 = (f32[30,2048]{1,0:T(8,128)S(1)}, f32[30,2048]{1,0:T(8,128)S(1)}, u32[]{:S(2)}, u32[]{:S(2)}) collective-permute-start(f32[30,2048]{1,0:T(8,128)S(1)} %scatter_custom_fusion), channel_id=1, source_target_pairs={{1,0},{2,1},{3,2},{4,3},{5,4},{6,5},{7,6},{8,7},{9,8},{10,9},{11,1... | collective-permute-start | bytes 737288 | tf_op jit(solution)/shard_map/ppermute | solution.py:10
  82.5 32.0 %collective-permute-start.9 = (f32[30,2048]{1,0:T(8,128)}, f32[30,2048]{1,0:T(8,128)S(1)}, u32[]{:S(2)}, u32[]{:S(2)}) collective-permute-start(f32[30,2048]{1,0:T(8,128)} %scatter_custom_fusion.1), channel_id=1, source_target_pairs={{2,0},{3,1},{4,2},{5,3},{6,4},{7,5},{8,6},{9,7},{10,8},{11,9},{12,... | collective-permute-start | bytes 737288 | tf_op jit(solution)/shard_map/ppermute | solution.py:10
  83.8 30.3 %collective-permute-start.10 = (f32[30,2048]{1,0:T(8,128)}, f32[30,2048]{1,0:T(8,128)S(1)}, u32[]{:S(2)}, u32[]{:S(2)}) collective-permute-start(f32[30,2048]{1,0:T(8,128)} %scatter_custom_fusion.2), channel_id=1, source_target_pairs={{4,0},{5,1},{6,2},{7,3},{8,4},{9,5},{10,6},{11,7},{12,8},{13,9},{1... | collective-permute-start | bytes 737288 | tf_op jit(solution)/shard_map/ppermute | solution.py:10
  85.1 28.6 %collective-permute-start.11 = (f32[30,2048]{1,0:T(8,128)}, f32[30,2048]{1,0:T(8,128)S(1)}, u32[]{:S(2)}, u32[]{:S(2)}) collective-permute-start(f32[30,2048]{1,0:T(8,128)} %scatter_custom_fusion.3), channel_id=1, source_target_pairs={{8,0},{9,1},{10,2},{11,3},{12,4},{13,5},{14,6},{15,7},{24,16},{25,... | collective-permute-start | bytes 737288 | tf_op jit(solution)/shard_map/ppermute | solution.py:10
  86.4 27.7 %copy-start.5 = (s32[30]{0:T(128)S(1)}, s32[30]{0:T(128)}, u32[]{:S(2)}) copy-start(s32[30]{0:T(128)} %copy-done.4) | copy-start | bytes 364
  89.4 25.6 %copy-start.7 = (s32[30]{0:T(128)S(1)}, s32[30]{0:T(128)}, u32[]{:S(2)}) copy-start(s32[30]{0:T(128)} %copy-done.6) | copy-start | bytes 364
where the time goes:
time: 117 us; the launch traced here: 116 us
  local copies, waits for them, and re-layouts  33.8 us (29%)
  waiting for transfers between devices  29.8 us (25%)
  starting transfers between devices  23.2 us (20%)
  matrix products  22.4 us (19%)
  other arithmetic  6.65 us (6%)
    ppermute x12, waiting for transfers between devices, passed_along(): return lax.ppermute(block, axis, route)  29.8 us
    ppermute x12, starting transfers between devices, passed_along(): return lax.ppermute(block, axis, route)  23.2 us
    scatter x4, local copies, waits for them, and re-layouts, per_device(): outgoing = jnp.zeros((capacity, samples * width), jnp.float32).at[slot_pl...  15.7 us
    dot_general x1, matrix products, per_device(): jnp.einsum('gsa,gkba->gksb', back_low, cond_weights, preferred_element_ty...  7.38 us
    dot_general x1, matrix products, per_device(): jnp.einsum('gksb,gkba->gsa', near_rows, cond_weights, preferred_element_t...  7.19 us
    gather x4, local copies, waits for them, and re-layouts, per_device(): taken = arrived[jnp.minimum(slot_place, capacity - 1)]  7.01 us
    gather x4, local copies, waits for them, and re-layouts, serve_rows(): picked = latent[jnp.maximum(wanted, 0)]  6.25 us
    dot_general x1, matrix products, per_device(): jnp.einsum('gsa,gba->gsb', innovation, precision_factor, preferred_elemen...  3.1 us
  transfers between devices with their start and end apart: 12, of which 4 were waited for; matrix products, arithmetic and copies ran while one was open for 12% of the time, Pallas kernels for 0%

commit v1 on v0

v1 whole, which is shorter than its diff:
```python
import functools

import jax
import jax.numpy as jnp
from jax import lax
from jax.experimental import pallas as pl
from jax.experimental.pallas import tpu as pltpu
from jax.sharding import PartitionSpec as P

SLOTS = 32
CHUNK = 8
VMEM, SMEM, ANY = pltpu.VMEM, pltpu.SMEM, pl.ANY


def index_kernel(capacity, lists_ref, asked_ref, source_ref, target_ref):
    leaf_dev, fan = lists_ref.shape
    me = lax.axis_index("kx")
    behind = me * leaf_dev - lists_ref[...]
    kind = (
        (behind > 0).astype(jnp.int32)
        + (behind > leaf_dev).astype(jnp.int32)
        + (behind > 2 * leaf_dev).astype(jnp.int32)
        + (behind > 4 * leaf_dev).astype(jnp.int32)
    )
    reach = jnp.where(kind == 4, 8, jnp.where(kind == 3, 4, kind))
    row = reach * leaf_dev - behind
    eye = (
        lax.broadcasted_iota(jnp.int32, (leaf_dev, leaf_dev), 0)
        == lax.broadcasted_iota(jnp.int32, (leaf_dev, leaf_dev), 1)
    ).astype(jnp.bfloat16)
    before = (
        lax.broadcasted_iota(jnp.int32, (leaf_dev, leaf_dev), 0)
        < lax.broadcasted_iota(jnp.int32, (leaf_dev, leaf_dev), 1)
    ).astype(jnp.bfloat16)

    def turned(x):
        return lax.dot_general(
            x.astype(jnp.float32).astype(jnp.bfloat16), eye, (((0,), (0,)), ((), ())),
            preferred_element_type=jnp.float32,
        )

    kind_t = turned(kind)
    row_t = turned(row)
    source = row_t
    target = row_t
    slot = lax.broadcasted_iota(jnp.int32, (SLOTS, leaf_dev), 0).astype(jnp.float32)
    for o in range(1, 5):
        mask = kind_t == float(o)
        ones = mask.astype(jnp.float32)
        within = jnp.dot(ones.astype(jnp.bfloat16), before, preferred_element_type=jnp.float32)
        totals = jnp.sum(ones, axis=1, keepdims=True)
        base = jnp.zeros((1, 1), jnp.float32)
        asked = jnp.zeros((1, SLOTS), jnp.float32)
        for k in range(fan):
            rank = within[k : k + 1] + base
            base = base + totals[k : k + 1]
            hit = (jnp.where(mask[k : k + 1], rank, -1.0) == slot).astype(jnp.float32)
            asked = asked + lax.dot_general(
                row_t[k : k + 1].astype(jnp.bfloat16), hit.astype(jnp.bfloat16),
                (((1,), (1,)), ((), ())), preferred_element_type=jnp.float32,
            )
            place = leaf_dev + (o - 1) * capacity + rank
            near = row_t[k : k + 1] + leaf_dev if o == 3 else place + leaf_dev
            target_ref[k : k + 1] = jnp.where(
                mask[k : k + 1], place,
                target[k : k + 1] if o == 1 else target_ref[k : k + 1].astype(jnp.float32),
            ).astype(jnp.int32)
            source_ref[k : k + 1] = jnp.where(
                mask[k : k + 1], near,
                source[k : k + 1] if o == 1 else source_ref[k : k + 1].astype(jnp.float32),
            ).astype(jnp.int32)
        asked_ref[:, (o - 1) * SLOTS : o * SLOTS] = asked.astype(jnp.int32)


def serve_kernel(capacity, all_asked, latent, before, out8, out2, out1):
    me = lax.axis_index("kx")
    last = lax.axis_size("kx") - 1
    ahead = jnp.minimum(me + 4, last)
    across = lax.bitwise_xor(me, 2)
    low = lax.bitwise_and(me, 3)
    around = me - low + lax.bitwise_and(low + 1, 3)

    def pick(slots, rows, out, reader):
        def one(r, carry):
            out[r] = rows[all_asked[reader, slots * SLOTS + r]]
            return carry
        lax.fori_loop(0, capacity, one, 0, unroll=6)

    pick(3, before, out8, ahead)

    @pl.when(lax.bitwise_and(me, 2) == 0)
    def _():
        pick(1, latent, out2, across)

    @pl.when(lax.bitwise_and(me, 2) != 0)
    def _():
        pick(1, before, out2, across)

    @pl.when(low != 3)
    def _():
        pick(0, latent, out1, around)

    @pl.when(low == 3)
    def _():
        pick(0, before, out1, around)


def leaf_kernel(
    capacity, source, target, latent, from4, from8, from2, from1, weights, factor,
    grad, out1, out2, out4, out8, near, acc, w_v, f_v, row_sem, w_sem, f_sem,
):
    leaf_dev = latent.shape[0]
    fan, width = weights.shape[1], weights.shape[2]
    chunks = leaf_dev // CHUNK
    starts = (0, leaf_dev, 2 * leaf_dev, 2 * leaf_dev + capacity, 2 * leaf_dev + 3 * capacity)
    row_copies = [
        pltpu.make_async_copy(rows, near.at[pl.ds(at, rows.shape[0])], row_sem.at[n])
        for n, (rows, at) in enumerate(zip((latent, from4, from1, from2, from8), starts))
    ]

    def weight_copy(c):
        part = pl.ds(c * CHUNK, CHUNK)
        return pltpu.make_async_copy(weights.at[part], w_v.at[part], w_sem.at[c])

    def factor_copy(c):
        part = pl.ds(c * CHUNK, CHUNK)
        return pltpu.make_async_copy(factor.at[part], f_v.at[part], f_sem.at[c])

    for copy in row_copies:
        copy.start()
    for c in range(chunks):
        weight_copy(c).start()
        factor_copy(c).start()
    acc[...] = jnp.zeros_like(acc)
    for copy in row_copies:
        copy.wait()
    by_rows = (((1,), (1,)), ((), ()))

    def chunk(c, carry):
        weight_copy(c).wait()
        factor_copy(c).wait()
        leaves = [c * CHUNK + u for u in range(CHUNK)]
        resid, innov, back, term = [], [], [], []
        for i in leaves:
            rows = jnp.concatenate([near[source[k, i]] for k in range(fan)], axis=1)
            mean = jnp.dot(
                rows, w_v[i].reshape(fan * width, width), preferred_element_type=jnp.float32
            )
            resid.append((near[i].astype(jnp.float32) - mean).astype(jnp.bfloat16))
        for i, x in zip(leaves, resid):
            innov.append(
                jnp.dot(x, f_v[i], preferred_element_type=jnp.float32).astype(jnp.bfloat16)
            )
        for i, x in zip(leaves, innov):
            back.append(
                lax.dot_general(x, f_v[i], by_rows, preferred_element_type=jnp.float32)
            )
        for i, x in zip(leaves, back):
            term.append(lax.dot_general(
                x.astype(jnp.bfloat16), w_v[i].reshape(fan * width, width), by_rows,
                preferred_element_type=jnp.float32,
            ))
        for i, x in zip(leaves, back):
            acc[i] = acc[i] - x
        for i, x in zip(leaves, term):
            for k in range(fan):
                j = target[k, i]
                acc[j] = acc[j] + x[:, k * width : (k + 1) * width]
        return carry

    lax.fori_loop(0, chunks, chunk, 0)
    grad[...] = acc[pl.ds(0, leaf_dev)]
    for n, out in enumerate((out1, out2, out4, out8)):
        out[...] = acc[pl.ds(leaf_dev + n * capacity, capacity)].astype(out.dtype)


def add_kernel(capacity, all_asked, part, back1, back2, back4, back8, out):
    me = lax.axis_index("kx")
    last = lax.axis_size("kx") - 1
    out[...] = part[...]
    for n, (reach, rows) in enumerate(((1, back1), (2, back2), (4, back4), (8, back8))):
        asker = jnp.minimum(me + reach, last)

        def one(r, carry):
            j = all_asked[asker, n * SLOTS + r]
            out[j] = out[j] + rows[r].astype(jnp.float32)
            return carry

        lax.fori_loop(0, capacity, one, 0, unroll=6)


def per_device(latent, cond_lists, cond_weights, precision_factor):
    devices = lax.axis_size("kx")
    leaf_dev, samples, width = latent.shape
    fan = cond_lists.shape[1]
    capacity = fan * leaf_dev // 8
    spec = pl.BlockSpec
    some_rows = jax.ShapeDtypeStruct((capacity, samples, width), jnp.bfloat16)
    vmem, smem, anywhere = spec(memory_space=VMEM), spec(memory_space=SMEM), spec(memory_space=ANY)

    from4 = lax.ppermute(latent, "kx", [(i, i + 4) for i in range(devices - 4)])
    asked, source, target = pl.pallas_call(
        functools.partial(index_kernel, capacity),
        out_shape=(
            jax.ShapeDtypeStruct((1, 4 * SLOTS), jnp.int32),
            jax.ShapeDtypeStruct((fan, leaf_dev), jnp.int32),
            jax.ShapeDtypeStruct((fan, leaf_dev), jnp.int32),
        ),
        in_specs=[vmem],
        out_specs=(vmem, vmem, vmem),
        name="index",
    )(cond_lists)
    all_asked = lax.all_gather(asked, "kx", axis=0, tiled=True)
    serve8, serve2, serve1 = pl.pallas_call(
        functools.partial(serve_kernel, capacity),
        out_shape=(some_rows,) * 3,
        in_specs=[smem, vmem, vmem],
        out_specs=(vmem,) * 3,
        name="serve",
    )(all_asked, latent, from4)
    from8 = lax.ppermute(serve8, "kx", [(i, i + 4) for i in range(4, devices - 4)])
    from2 = lax.ppermute(serve2, "kx", [(i, i ^ 2) for i in range(devices)])
    from1 = lax.ppermute(serve1, "kx", [(i, i // 4 * 4 + (i + 1) % 4) for i in range(devices)])
    part, out1, out2, out4, out8 = pl.pallas_call(
        functools.partial(leaf_kernel, capacity),
        out_shape=(jax.ShapeDtypeStruct(latent.shape, jnp.float32),) + (some_rows,) * 4,
        in_specs=[smem, smem] + [anywhere] * 7,
        out_specs=(vmem,) * 5,
        scratch_shapes=[
            VMEM((2 * leaf_dev + 4 * capacity, samples, width), jnp.bfloat16),
            VMEM((leaf_dev + 4 * capacity, samples, width), jnp.float32),
            VMEM(cond_weights.shape, jnp.bfloat16),
            VMEM(precision_factor.shape, jnp.bfloat16),
            pltpu.SemaphoreType.DMA((5,)),
            pltpu.SemaphoreType.DMA((leaf_dev // CHUNK,)),
            pltpu.SemaphoreType.DMA((leaf_dev // CHUNK,)),
        ],
        compiler_params=pltpu.CompilerParams(vmem_limit_bytes=24 * 2**20),
        name="leaves",
    )(source, target, latent, from4, from8, from2, from1, cond_weights, precision_factor)
    returned = [
        lax.ppermute(x, "kx", [(i, i - reach) for i in range(reach, devices)])
        for reach, x in ((8, out8), (4, out4), (2, out2), (1, out1))
    ]
    return pl.pallas_call(
        functools.partial(add_kernel, capacity),
        out_shape=jax.ShapeDtypeStruct(latent.shape, jnp.float32),
        in_specs=[smem] + [vmem] * 5,
        out_specs=vmem,
        name="add",
    )(all_asked, part, *returned[::-1])


def solution(mesh):
    return jax.shard_map(
        per_device,
        mesh=mesh,
        in_specs=(
            P(("groups", "kx"), None, None),
            P(("groups", "kx"), None),
            P(("groups", "kx"), None, None, None),
            P(("groups", "kx"), None, None),
        ),
        out_specs=P(("groups", "kx"), None, None),
        check_vma=False,
    )
```

time: 117 us -> 79.8 us (0.68)
  matrix products: 22.4 us -> 0 us
  local copies, waits for them, and re-layouts: 33.8 us -> 11.9 us
  blocking collectives: 0 us -> 19.9 us
  Pallas kernels: 0 us -> 17.1 us
  starting transfers between devices: 23.2 us -> 11.2 us
  waiting for transfers between devices: 29.8 us -> 19.1 us
  other arithmetic: 6.65 us -> 0 us
    dot_general x8 -> x0, matrix products: 22.4 us -> none  [the longest x1 7.38 us: per_device(): jnp.einsum('gsa,gkba->gksb', back_low, cond_weights, preferred_element_ty...]
    all_gather x0 -> x1, blocking collectives: none -> 19.9 us  [per_device(): all_asked = lax.all_gather(asked, 'kx', axis=0, tiled=True)]
    pallas_call x0 -> x4, Pallas kernels: none -> 17.1 us  [the longest x1 10.3 us: per_device(): pl.pallas_call(functools.partial(leaf_kernel, capacity), out_shape=(jax.S...]
    scatter x4 -> x0, local copies, waits for them, and re-layouts: 15.7 us -> none  [per_device(): outgoing = jnp.zeros((capacity, samples * width), jnp.float32).at[slot_pl...]
    gather x9 -> x0, local copies, waits for them, and re-layouts: 15 us -> none  [the longest x4 7.01 us: per_device(): taken = arrived[jnp.minimum(slot_place, capacity - 1)]]
    ppermute x12 -> x8, starting transfers between devices: 23.2 us -> 11.2 us  [the longest x4 5.16 us: per_device(): lax.ppermute(x, 'kx', [(i, i - reach) for i in range(reach, devices)])]
    unnamed x17 -> x25, local copies, waits for them, and re-layouts: 0.99 us -> 11.9 us
    ppermute x12 -> x8, waiting for transfers between devices: 29.8 us -> 19.1 us  [the longest x4 12.4 us: per_device(): lax.ppermute(x, 'kx', [(i, i - reach) for i in range(reach, devices)])]
  transfers between devices with their start and end apart: 12 -> 8, of which waited for: 4 -> 5; matrix products, arithmetic and copies ran while one was open for 12% -> 2% of each run, Pallas kernels for 0% -> 3%
where the time goes in v1:
time: 79.8 us; the launch traced here: 79.3 us
  blocking collectives  19.9 us (25%)
  waiting for transfers between devices  19.1 us (24%)
  Pallas kernels  17.1 us (21%)
  local copies, waits for them, and re-layouts  11.9 us (15%)
  starting transfers between devices  11.2 us (14%)
    all_gather x1, blocking collectives, per_device(): all_asked = lax.all_gather(asked, 'kx', axis=0, tiled=True)  19.9 us
    ppermute x4, waiting for transfers between devices, per_device(): lax.ppermute(x, 'kx', [(i, i - reach) for i in range(reach, devices)])  12.4 us
    unnamed x25, local copies, waits for them, and re-layouts  11.9 us
    pallas_call x1, Pallas kernels, per_device(): pl.pallas_call(functools.partial(leaf_kernel, capacity), out_shape=(jax.S...  10.3 us
    ppermute x1, waiting for transfers between devices, per_device(): from2 = lax.ppermute(serve2, 'kx', [(i, i ^ 2) for i in range(devices)])  6.01 us
    ppermute x4, starting transfers between devices, per_device(): lax.ppermute(x, 'kx', [(i, i - reach) for i in range(reach, devices)])  5.16 us
    ppermute x1, starting transfers between devices, per_device(): from4 = lax.ppermute(latent, 'kx', [(i, i + 4) for i in range(devices - 4)])  4.94 us
    pallas_call x1, Pallas kernels, per_device(): pl.pallas_call(functools.partial(add_kernel, capacity), out_shape=jax.Sha...  2.68 us
  transfers between devices with their start and end apart: 8, of which 5 were waited for; matrix products, arithmetic and copies ran while one was open for 2% of the time, Pallas kernels for 3%

profile of v1, /device:TPU:0, one launch (start us, length us, event | category | flops | bytes accessed | tf_op | source)
XLA Modules:
  0.0 79.3 jit_solution(11838949928950368738)
XLA Ops:
  0.0 4.9 %collective-permute-start = (bf16[80,16,128]{2,1,0:T(8,128)(2,1)}, bf16[80,16,128]{2,1,0:T(8,128)(2,1)S(1)}, u32[]{:S(2)}, u32[]{:S(2)}) collective-permute-start(bf16[80,16,128]{2,1,0:T(8,128)(2,1)} %latent.3), channel_id=1, source_target_pairs={{0,4},{1,5},{2,6},{3,7},{4,8},{5,9},{6,10},{7,11},{8,12},{9,13},{1... | collective-permute-start | bytes 983048 | tf_op jit(solution)/shard_map/ppermute | solution.py:201
  4.9 1.4 %copy.7.lists_ref = s32[80,3]{1,0:T(8,128)} copy(s32[80,3]{0,1:T(4,128)} %param.5) | data formatting | bytes 1920 | tf_op args[1]
  6.3 2.0 %index.1 = (s32[1,128]{1,0:T(1,128)}, s32[3,80]{1,0:T(4,128)}, s32[3,80]{1,0:T(4,128)}) custom-call(s32[80,3]{1,0:T(8,128)} %copy.7.lists_ref), custom_call_target="tpu_custom_call" | custom-call | tf_op jit(solution)/shard_map/index/pallas_call | solution.py:202
  8.4 19.9 %all-gather = s32[16,1,128]{2,1,0:T(1,128)} all-gather(s32[1,1,128]{2,1,0:T(1,128)} %bitcast.4), channel_id=1, replica_groups=mesh['groups'=2,'kx'=16] {'kx'}, dimensions={0}, use_global_device_ids=true | all-gather | bytes 8704 | tf_op jit(solution)/shard_map/all_gather | solution.py:213
  28.3 0.0 collective-permute-done.before.from4
  28.3 0.0 copy-start.3
  28.3 0.7 copy-done.3
  29.0 2.1 %serve.1 = (bf16[30,16,128]{2,1,0:T(8,128)(2,1)}, bf16[30,16,128]{2,1,0:T(8,128)(2,1)}, bf16[30,16,128]{2,1,0:T(8,128)(2,1)}) custom-call(s32[16,128]{1,0:T(8,128)} %bitcast.2, bf16[80,16,128]{2,1,0:T(8,128)(2,1)} %latent.3, bf16[80,16,128]{2,1,0:T(8,128)(2,1)} %copy-done.3), custom_call_target="tpu_custom_call" | custom-call | tf_op jit(solution)/shard_map/serve/pallas_call | solution.py:214
  31.1 0.7 collective-permute-start.1
  31.8 0.1 collective-permute-start.2
  31.9 0.3 collective-permute-start.3
  32.2 0.0 collective-permute-done.1.from8
  32.2 6.0 %collective-permute-done.2.from2 = bf16[30,16,128]{2,1,0:T(8,128)(2,1)S(1)} collective-permute-done((bf16[30,16,128]{2,1,0:T(8,128)(2,1)}, bf16[30,16,128]{2,1,0:T(8,128)(2,1)S(1)}, u32[]{:S(2)}, u32[]{:S(2)}) %collective-permute-start.2) | collective-permute-done | bytes 122912 | tf_op jit(solution)/shard_map/ppermute | solution.py:222
  38.2 0.7 collective-permute-done.3.from1
  38.9 0.0 copy-start
  38.9 3.2 %copy-done = bf16[80,3,128,128]{3,2,1,0:T(8,128)(2,1)S(1)} copy-done((bf16[80,3,128,128]{3,2,1,0:T(8,128)(2,1)S(1)}, bf16[80,3,128,128]{3,2,1,0:T(8,128)(2,1)}, u32[]{:S(2)}) %copy-start) | copy-done | bytes 7864344
  42.1 0.0 copy-start.1
  42.1 1.7 %copy-done.1 = bf16[80,128,128]{2,1,0:T(8,128)(2,1)S(1)} copy-done((bf16[80,128,128]{2,1,0:T(8,128)(2,1)S(1)}, bf16[80,128,128]{2,1,0:T(8,128)(2,1)}, u32[]{:S(2)}) %copy-start.1) | copy-done | bytes 2621464
  43.9 0.0 copy-start.2
  43.9 1.0 %copy-done.2 = bf16[80,16,128]{2,1,0:T(8,128)(2,1)S(1)} copy-done((bf16[80,16,128]{2,1,0:T(8,128)(2,1)S(1)}, bf16[80,16,128]{2,1,0:T(8,128)(2,1)}, u32[]{:S(2)}) %copy-start.2) | copy-done | bytes 327704
  44.8 0.0 copy-start.4
  44.8 1.0 %copy-done.4 = bf16[80,16,128]{2,1,0:T(8,128)(2,1)S(1)} copy-done((bf16[80,16,128]{2,1,0:T(8,128)(2,1)S(1)}, bf16[80,16,128]{2,1,0:T(8,128)(2,1)}, u32[]{:S(2)}) %copy-start.4) | copy-done | bytes 327704
  45.8 0.0 copy-start.6
  45.8 0.7 copy-done.6
  46.5 0.0 copy-start.7
  46.5 0.7 copy-done.7
  47.2 10.3 %leaves.1 = (f32[80,16,128]{2,1,0:T(8,128)S(1)}, bf16[30,16,128]{2,1,0:T(8,128)(2,1)S(1)}, bf16[30,16,128]{2,1,0:T(8,128)(2,1)S(1)}, bf16[30,16,128]{2,1,0:T(8,128)(2,1)S(1)}, bf16[30,16,128]{2,1,0:T(8,128)(2,1)S(1)}) custom-call(s32[3,80]{1,0:T(4,128)S(1)} %copy-done.6, s32[3,80]{1,0:T(4,128)S(1)} %copy-done.7, bf16[80,16,128]{2,1,0:T(8,128)(2,1)S(1)} %copy-done.2, ...), custom_call_target="tpu_custom_call" | custom-call | tf_op jit(solution)/shard_map/leaves/pallas_call | solution.py:224
  57.5 0.0 copy-start.5
  57.5 0.9 %copy-done.5 = f32[80,16,128]{2,1,0:T(8,128)} copy-done((f32[80,16,128]{2,1,0:T(8,128)}, f32[80,16,128]{2,1,0:T(8,128)S(1)}, u32[]{:S(2)}) %copy-start.5) | copy-done | bytes 655384
  58.3 1.3 %collective-permute-start.4 = (bf16[30,16,128]{2,1,0:T(8,128)(2,1)S(1)}, bf16[30,16,128]{2,1,0:T(8,128)(2,1)S(1)}, u32[]{:S(2)}, u32[]{:S(2)}) collective-permute-start(bf16[30,16,128]{2,1,0:T(8,128)(2,1)S(1)} %get-tuple-element.23), channel_id=1, source_target_pairs={{1,0},{2,1},{3,2},{4,3},{5,4},{6,5},{7,6},{8,7},{9,8},{10,9},{11,1... | collective-permute-start | bytes 368648 | tf_op jit(solution)/shard_map/ppermute | solution.py:242
  59.6 1.3 %collective-permute-start.5 = (bf16[30,16,128]{2,1,0:T(8,128)(2,1)S(1)}, bf16[30,16,128]{2,1,0:T(8,128)(2,1)S(1)}, u32[]{:S(2)}, u32[]{:S(2)}) collective-permute-start(bf16[30,16,128]{2,1,0:T(8,128)(2,1)S(1)} %get-tuple-element.24), channel_id=1, source_target_pairs={{2,0},{3,1},{4,2},{5,3},{6,4},{7,5},{8,6},{9,7},{10,8},{11,9},{12,... | collective-permute-start | bytes 368648 | tf_op jit(solution)/shard_map/ppermute | solution.py:242
  60.9 1.3 %collective-permute-start.6 = (bf16[30,16,128]{2,1,0:T(8,128)(2,1)S(1)}, bf16[30,16,128]{2,1,0:T(8,128)(2,1)S(1)}, u32[]{:S(2)}, u32[]{:S(2)}) collective-permute-start(bf16[30,16,128]{2,1,0:T(8,128)(2,1)S(1)} %get-tuple-element.25), channel_id=1, source_target_pairs={{4,0},{5,1},{6,2},{7,3},{8,4},{9,5},{10,6},{11,7},{12,8},{13,9},{1... | collective-permute-start | bytes 368648 | tf_op jit(solution)/shard_map/ppermute | solution.py:242
  62.2 1.3 %collective-permute-start.7 = (bf16[30,16,128]{2,1,0:T(8,128)(2,1)S(1)}, bf16[30,16,128]{2,1,0:T(8,128)(2,1)S(1)}, u32[]{:S(2)}, u32[]{:S(2)}) collective-permute-start(bf16[30,16,128]{2,1,0:T(8,128)(2,1)S(1)} %get-tuple-element.26), channel_id=1, source_target_pairs={{8,0},{9,1},{10,2},{11,3},{12,4},{13,5},{14,6},{15,7},{24,16},{25,... | collective-permute-start | bytes 368648 | tf_op jit(solution)/shard_map/ppermute | solution.py:242
  63.5 0.0 collective-permute-done.4.back1
  63.5 0.0 copy-start.8
  63.6 4.0 %collective-permute-done.5.back2 = bf16[30,16,128]{2,1,0:T(8,128)(2,1)S(1)} collective-permute-done((bf16[30,16,128]{2,1,0:T(8,128)(2,1)S(1)}, bf16[30,16,128]{2,1,0:T(8,128)(2,1)S(1)}, u32[]{:S(2)}, u32[]{:S(2)}) %collective-permute-start.5) | collective-permute-done | bytes 122912 | tf_op jit(solution)/shard_map/ppermute | solution.py:242
  67.6 0.0 copy-start.9
  67.6 2.9 %collective-permute-done.6.back4 = bf16[30,16,128]{2,1,0:T(8,128)(2,1)S(1)} collective-permute-done((bf16[30,16,128]{2,1,0:T(8,128)(2,1)S(1)}, bf16[30,16,128]{2,1,0:T(8,128)(2,1)S(1)}, u32[]{:S(2)}, u32[]{:S(2)}) %collective-permute-start.6) | collective-permute-done | bytes 122912 | tf_op jit(solution)/shard_map/ppermute | solution.py:242
  70.5 0.0 copy-start.10
  70.5 5.5 %collective-permute-done.7.back8 = bf16[30,16,128]{2,1,0:T(8,128)(2,1)S(1)} collective-permute-done((bf16[30,16,128]{2,1,0:T(8,128)(2,1)S(1)}, bf16[30,16,128]{2,1,0:T(8,128)(2,1)S(1)}, u32[]{:S(2)}, u32[]{:S(2)}) %collective-permute-start.7) | collective-permute-done | bytes 122912 | tf_op jit(solution)/shard_map/ppermute | solution.py:242
  76.0 0.0 copy-start.11
  76.0 0.0 copy-done.8
  76.0 0.0 copy-done.9
  76.0 0.0 copy-done.10
  76.0 0.6 copy-done.11
  76.6 2.7 %add.1 = f32[80,16,128]{2,1,0:T(8,128)} custom-call(s32[16,128]{1,0:T(8,128)} %bitcast.3, f32[80,16,128]{2,1,0:T(8,128)} %copy-done.5, bf16[30,16,128]{2,1,0:T(8,128)(2,1)} %copy-done.8, bf16[30,16,128]{2,1,0:T(8,128)(2,1)} %copy-done.9, bf16[30,16,128]{2,1,0:T(8,128)(2,1)} %copy-done.10, bf16[30,16,128]{2,1,0:T(8,128)(2,1)} %copy-done.11), custom_call_target="tpu_custom_call" | custom-call | tf_op jit(solution)/shard_map/add/pallas_call | solution.py:245
Async XLA Ops:
  0.0 28.3 %collective-permute-start = (bf16[80,16,128]{2,1,0:T(8,128)(2,1)}, bf16[80,16,128]{2,1,0:T(8,128)(2,1)S(1)}, u32[]{:S(2)}, u32[]{:S(2)}) collective-permute-start(bf16[80,16,128]{2,1,0:T(8,128)(2,1)} %latent.3), channel_id=1, source_target_pairs={{0,4},{1,5},{2,6},{3,7},{4,8},{5,9},{6,10},{7,11},{8,12},{9,13},{1... | collective-permute-start | bytes 983048 | tf_op jit(solution)/shard_map/ppermute | solution.py:201
  28.3 0.7 copy-start.3
  31.1 1.1 %collective-permute-start.1 = (bf16[30,16,128]{2,1,0:T(8,128)(2,1)}, bf16[30,16,128]{2,1,0:T(8,128)(2,1)S(1)}, u32[]{:S(2)}, u32[]{:S(2)}) collective-permute-start(bf16[30,16,128]{2,1,0:T(8,128)(2,1)} %get-tuple-element.19), channel_id=1, source_target_pairs={{4,8},{5,9},{6,10},{7,11},{8,12},{9,13},{10,14},{11,15},{20,24},{2... | collective-permute-start | bytes 368648 | tf_op jit(solution)/shard_map/ppermute | solution.py:221
  31.8 6.4 %collective-permute-start.2 = (bf16[30,16,128]{2,1,0:T(8,128)(2,1)}, bf16[30,16,128]{2,1,0:T(8,128)(2,1)S(1)}, u32[]{:S(2)}, u32[]{:S(2)}) collective-permute-start(bf16[30,16,128]{2,1,0:T(8,128)(2,1)} %get-tuple-element.20), channel_id=1, source_target_pairs={{0,2},{1,3},{2,0},{3,1},{4,6},{5,7},{6,4},{7,5},{8,10},{9,11},{10,... | collective-permute-start | bytes 368648 | tf_op jit(solution)/shard_map/ppermute | solution.py:222
  31.9 7.0 %collective-permute-start.3 = (bf16[30,16,128]{2,1,0:T(8,128)(2,1)}, bf16[30,16,128]{2,1,0:T(8,128)(2,1)S(1)}, u32[]{:S(2)}, u32[]{:S(2)}) collective-permute-start(bf16[30,16,128]{2,1,0:T(8,128)(2,1)} %get-tuple-element.21), channel_id=1, source_target_pairs={{0,1},{1,2},{2,3},{3,0},{4,5},{5,6},{6,7},{7,4},{8,9},{9,10},{10,1... | collective-permute-start | bytes 368648 | tf_op jit(solution)/shard_map/ppermute | solution.py:223
  38.9 3.2 %copy-start = (bf16[80,3,128,128]{3,2,1,0:T(8,128)(2,1)S(1)}, bf16[80,3,128,128]{3,2,1,0:T(8,128)(2,1)}, u32[]{:S(2)}) copy-start(bf16[80,3,128,128]{3,2,1,0:T(8,128)(2,1)} %weights.1) | copy-start | bytes 23592964
  42.1 1.7 %copy-start.1 = (bf16[80,128,128]{2,1,0:T(8,128)(2,1)S(1)}, bf16[80,128,128]{2,1,0:T(8,128)(2,1)}, u32[]{:S(2)}) copy-start(bf16[80,128,128]{2,1,0:T(8,128)(2,1)} %factor.1) | copy-start | bytes 7864324
  43.9 1.0 %copy-start.2 = (bf16[80,16,128]{2,1,0:T(8,128)(2,1)S(1)}, bf16[80,16,128]{2,1,0:T(8,128)(2,1)}, u32[]{:S(2)}) copy-start(bf16[80,16,128]{2,1,0:T(8,128)(2,1)} %latent.3) | copy-start | bytes 983044
  44.8 1.0 %copy-start.4 = (bf16[80,16,128]{2,1,0:T(8,128)(2,1)S(1)}, bf16[80,16,128]{2,1,0:T(8,128)(2,1)}, u32[]{:S(2)}) copy-start(bf16[80,16,128]{2,1,0:T(8,128)(2,1)} %copy-done.3) | copy-start | bytes 983044
  45.8 0.7 copy-start.6
  46.5 0.7 copy-start.7
  57.5 0.9 %copy-start.5 = (f32[80,16,128]{2,1,0:T(8,128)}, f32[80,16,128]{2,1,0:T(8,128)S(1)}, u32[]{:S(2)}) copy-start(f32[80,16,128]{2,1,0:T(8,128)S(1)} %get-tuple-element.22.part) | copy-start | bytes 1966084
  58.3 5.2 %collective-permute-start.4 = (bf16[30,16,128]{2,1,0:T(8,128)(2,1)S(1)}, bf16[30,16,128]{2,1,0:T(8,128)(2,1)S(1)}, u32[]{:S(2)}, u32[]{:S(2)}) collective-permute-start(bf16[30,16,128]{2,1,0:T(8,128)(2,1)S(1)} %get-tuple-element.23), channel_id=1, source_target_pairs={{1,0},{2,1},{3,2},{4,3},{5,4},{6,5},{7,6},{8,7},{9,8},{10,9},{11,1... | collective-permute-start | bytes 368648 | tf_op jit(solution)/shard_map/ppermute | solution.py:242
  59.6 7.9 %collective-permute-start.5 = (bf16[30,16,128]{2,1,0:T(8,128)(2,1)S(1)}, bf16[30,16,128]{2,1,0:T(8,128)(2,1)S(1)}, u32[]{:S(2)}, u32[]{:S(2)}) collective-permute-start(bf16[30,16,128]{2,1,0:T(8,128)(2,1)S(1)} %get-tuple-element.24), channel_id=1, source_target_pairs={{2,0},{3,1},{4,2},{5,3},{6,4},{7,5},{8,6},{9,7},{10,8},{11,9},{12,... | collective-permute-start | bytes 368648 | tf_op jit(solution)/shard_map/ppermute | solution.py:242
  60.9 9.5 %collective-permute-start.6 = (bf16[30,16,128]{2,1,0:T(8,128)(2,1)S(1)}, bf16[30,16,128]{2,1,0:T(8,128)(2,1)S(1)}, u32[]{:S(2)}, u32[]{:S(2)}) collective-permute-start(bf16[30,16,128]{2,1,0:T(8,128)(2,1)S(1)} %get-tuple-element.25), channel_id=1, source_target_pairs={{4,0},{5,1},{6,2},{7,3},{8,4},{9,5},{10,6},{11,7},{12,8},{13,9},{1... | collective-permute-start | bytes 368648 | tf_op jit(solution)/shard_map/ppermute | solution.py:242
  62.2 13.7 %collective-permute-start.7 = (bf16[30,16,128]{2,1,0:T(8,128)(2,1)S(1)}, bf16[30,16,128]{2,1,0:T(8,128)(2,1)S(1)}, u32[]{:S(2)}, u32[]{:S(2)}) collective-permute-start(bf16[30,16,128]{2,1,0:T(8,128)(2,1)S(1)} %get-tuple-element.26), channel_id=1, source_target_pairs={{8,0},{9,1},{10,2},{11,3},{12,4},{13,5},{14,6},{15,7},{24,16},{25,... | collective-permute-start | bytes 368648 | tf_op jit(solution)/shard_map/ppermute | solution.py:242
  63.5 12.4 %copy-start.8 = (bf16[30,16,128]{2,1,0:T(8,128)(2,1)}, bf16[30,16,128]{2,1,0:T(8,128)(2,1)S(1)}, u32[]{:S(2)}) copy-start(bf16[30,16,128]{2,1,0:T(8,128)(2,1)S(1)} %collective-permute-done.4.back1) | copy-start | bytes 368644
  67.6 8.4 %copy-start.9 = (bf16[30,16,128]{2,1,0:T(8,128)(2,1)}, bf16[30,16,128]{2,1,0:T(8,128)(2,1)S(1)}, u32[]{:S(2)}) copy-start(bf16[30,16,128]{2,1,0:T(8,128)(2,1)S(1)} %collective-permute-done.5.back2) | copy-start | bytes 368644
  70.5 5.5 %copy-start.10 = (bf16[30,16,128]{2,1,0:T(8,128)(2,1)}, bf16[30,16,128]{2,1,0:T(8,128)(2,1)S(1)}, u32[]{:S(2)}) copy-start(bf16[30,16,128]{2,1,0:T(8,128)(2,1)S(1)} %collective-permute-done.6.back4) | copy-start | bytes 368644
  76.0 0.6 copy-start.11

commit v2 on v0

v2 whole, which is shorter than its diff:
```python
import functools

import jax
import jax.numpy as jnp
from jax import lax
from jax.experimental import pallas as pl
from jax.experimental.pallas import tpu as pltpu
from jax.sharding import PartitionSpec as P

SLOTS = 32
LEAVES = 16
ROWS = 15
MIB = 2**20
BY_ROWS = (((1,), (1,)), ((), ()))
VMEM, SMEM, HBM = pltpu.VMEM, pltpu.SMEM, pltpu.HBM


def index_kernel(lists, latent, asked, slots, home, held, sem):
    fan, leaf_dev = lists.shape
    fetch = pltpu.make_async_copy(latent, held, sem)
    fetch.start()
    me = lax.axis_index("kx")
    behind = me * leaf_dev - lists[...]
    kind = (
        (behind > 0).astype(jnp.int32)
        + (behind > leaf_dev).astype(jnp.int32)
        + (behind > 2 * leaf_dev).astype(jnp.int32)
        + (behind > 4 * leaf_dev).astype(jnp.int32)
    )
    reach = jnp.where(kind == 4, 8, jnp.where(kind == 3, 4, kind))
    row = reach * leaf_dev - behind
    home[...] = jnp.where(kind == 0, row, leaf_dev)

    def grid(shape, dim):
        return lax.broadcasted_iota(jnp.int32, shape, dim)

    def low(x):
        return x.astype(jnp.float32).astype(jnp.bfloat16)

    every = 4 * fan
    mask = jnp.concatenate([(kind == o).astype(jnp.float32) for o in range(1, 5)], axis=0)
    earlier = low(grid((leaf_dev, leaf_dev), 0) < grid((leaf_dev, leaf_dev), 1))
    a, b = grid((every, every), 0), grid((every, every), 1)
    above = (b < a)
    for o in range(1, 4):
        above = above & ((a < o * fan) | (b >= o * fan))
    within = jnp.dot(low(mask), earlier, preferred_element_type=jnp.float32)
    base = jnp.sum(
        jnp.dot(low(above), low(mask), preferred_element_type=jnp.float32), axis=1, keepdims=True
    )
    place = jnp.where(mask > 0.0, within + base, -1.0)
    slot = grid((SLOTS, leaf_dev), 0).astype(jnp.float32)
    leaf = grid((1, leaf_dev), 1).astype(jnp.float32)
    ones = jnp.ones((1, leaf_dev), jnp.float32)
    total = jnp.zeros((8, 4 * SLOTS), jnp.float32)
    for k in range(fan):
        hit = jnp.concatenate(
            [(place[o * fan + k : o * fan + k + 1] == slot).astype(jnp.float32) for o in range(4)],
            axis=0,
        )
        facts = jnp.concatenate(
            [row[k : k + 1].astype(jnp.float32), leaf, k * ones, ones]
            + [jnp.zeros((4, leaf_dev), jnp.float32)], axis=0,
        )
        total = total + lax.dot_general(
            low(facts), low(hit), BY_ROWS, preferred_element_type=jnp.float32
        )
    asked[...] = total[0:1].astype(jnp.int32)
    slots[0:1] = jnp.where(total[3:4] > 0.0, total[1:2], float(leaf_dev)).astype(jnp.int32)
    slots[1:2] = total[2:3].astype(jnp.int32)
    fetch.wait()


def local_kernel(home, latent, weights, factor, left, held_w, held_f, near, w_sem, f_sem):
    leaf_dev = latent.shape[0]
    fan, width = weights.shape[1], weights.shape[2]

    def fetch(c):
        part = pl.ds(c * LEAVES, LEAVES)
        return pltpu.make_async_copy(weights.at[part], held_w.at[part], w_sem.at[c])

    fetch_factor = pltpu.make_async_copy(factor, held_f, f_sem)
    for c in range(leaf_dev // LEAVES):
        fetch(c).start()
    fetch_factor.start()
    near[pl.ds(0, leaf_dev)] = latent[...]
    near[leaf_dev] = jnp.zeros(latent.shape[1:], latent.dtype)

    def some(c, carry):
        fetch(c).wait()
        for u in range(LEAVES):
            i = c * LEAVES + u
            rows = jnp.concatenate([near[home[k, i]] for k in range(fan)], axis=1)
            mean = jnp.dot(
                rows, held_w[i].reshape(fan * width, width), preferred_element_type=jnp.float32
            )
            left[i] = latent[i].astype(jnp.float32) - mean
        return carry

    lax.fori_loop(0, leaf_dev // LEAVES, some, 0)
    fetch_factor.wait()


def serve_kernel(capacity, ask8, ask2, ask1, latent, before, out8, out2, out1, heard):
    me = lax.axis_index("kx")
    for n, ask in enumerate((ask8, ask2, ask1)):
        for lane in range(4 * SLOTS):
            heard[n, lane] = ask[0, lane]

    def pick(o, ask, rows, out):
        for r in range(capacity):
            out[r] = rows[ask[0, o * SLOTS + r]]

    pick(3, ask8, before, out8)
    for o, ask, out, bits in ((1, ask2, out2, 2), (0, ask1, out1, 3)):
        relays = lax.bitwise_and(me, bits) == bits

        @pl.when(relays)
        def _():
            pick(o, ask, before, out)

        @pl.when(jnp.logical_not(relays))
        def _():
            pick(o, ask, latent, out)


def remote_kernel(
    capacity, asked, slots, left, before, from8, from2, from1, weights, factor,
    back, out8, out4, out2, out1, resid, low,
):
    leaf_dev = left.shape[0]
    resid[pl.ds(0, leaf_dev)] = left[...]
    resid[leaf_dev] = jnp.zeros(left.shape[1:], left.dtype)
    low[leaf_dev] = jnp.zeros(left.shape[1:], low.dtype)

    def asker(o, r):
        i = slots[0, o * SLOTS + r]
        return i, jnp.minimum(i, leaf_dev - 1), slots[1, o * SLOTS + r]

    for o, rows in ((2, before), (3, from8), (1, from2), (0, from1)):
        def some(c, carry):
            means = []
            for u in range(ROWS):
                r = c * ROWS + u
                i, held, k = asker(o, r)
                x = rows[asked[0, o * SLOTS + r]] if o == 2 else rows[r]
                means.append((i, jnp.dot(
                    x, weights[held, k], preferred_element_type=jnp.float32
                )))
            for i, mean in means:
                resid[i] = resid[i] - mean
            return carry

        lax.fori_loop(0, capacity // ROWS, some, 0)

    def leaves(c, carry):
        every = [c * LEAVES + u for u in range(LEAVES)]
        innov = [
            jnp.dot(
                resid[i].astype(jnp.bfloat16), factor[i], preferred_element_type=jnp.float32
            ).astype(jnp.bfloat16)
            for i in every
        ]
        for i, x in zip(every, innov):
            y = lax.dot_general(x, factor[i], BY_ROWS, preferred_element_type=jnp.float32)
            back[i] = y
            low[i] = y.astype(jnp.bfloat16)
        return carry

    lax.fori_loop(0, leaf_dev // LEAVES, leaves, 0)
    for o, out in ((3, out8), (2, out4), (1, out2), (0, out1)):
        def terms(c, carry):
            for u in range(ROWS):
                r = c * ROWS + u
                i, held, k = asker(o, r)
                out[r] = lax.dot_general(
                    low[i], weights[held, k], BY_ROWS, preferred_element_type=jnp.float32
                ).astype(out.dtype)
            return carry

        lax.fori_loop(0, capacity // ROWS, terms, 0)


def home_kernel(home, back, weights, part, acc):
    leaf_dev = back.shape[0]
    fan, width = weights.shape[1], weights.shape[2]
    acc[pl.ds(0, leaf_dev)] = -back[...]
    acc[leaf_dev] = jnp.zeros(back.shape[1:], back.dtype)

    def some(c, carry):
        every = [c * LEAVES + u for u in range(LEAVES)]
        terms = [
            lax.dot_general(
                back[i].astype(jnp.bfloat16), weights[i].reshape(fan * width, width), BY_ROWS,
                preferred_element_type=jnp.float32,
            )
            for i in every
        ]
        for i, x in zip(every, terms):
            for k in range(fan):
                j = home[k, i]
                acc[j] = acc[j] + x[:, k * width : (k + 1) * width]
        return carry

    lax.fori_loop(0, leaf_dev // LEAVES, some, 0)
    part[...] = acc[pl.ds(0, leaf_dev)]


def add_kernel(capacity, ask8, ask2, ask1, far, part, back8, back4, back2, back1, out):
    me = lax.axis_index("kx")
    out[...] = part[...]

    def add(o, lane, rows):
        for r in range(capacity):
            j = lane(o * SLOTS + r)
            out[j] = out[j] + rows[r].astype(jnp.float32)

    beyond2 = lax.bitwise_and(me, 2) == 2
    beyond1 = lax.bitwise_and(me, 3) == 3
    add(3, lambda at: far[0, at], back8)
    add(2, lambda at: ask8[0, at], back4)
    add(1, lambda at: jnp.where(beyond2, far[1, at], ask2[0, at]), back2)
    add(0, lambda at: jnp.where(beyond1, far[2, at], ask1[0, at]), back1)


def call(body, name, out_shape, ins, outs, limit, flops=0, moved=0, scratch=()):
    spec = lambda space: pl.BlockSpec(memory_space=space)
    return pl.pallas_call(
        body,
        out_shape=out_shape,
        in_specs=[spec(space) for space in ins],
        out_specs=tuple(spec(space) for space in outs),
        scratch_shapes=scratch,
        compiler_params=pltpu.CompilerParams(vmem_limit_bytes=limit * MIB),
        cost_estimate=pl.CostEstimate(flops=flops, bytes_accessed=moved, transcendentals=0),
        name=name,
    )


def in_hbm(x):
    return pltpu.with_memory_space_constraint(x, HBM)


def per_device(latent, cond_lists, cond_weights, precision_factor):
    devices = lax.axis_size("kx")
    leaf_dev, samples, width = latent.shape
    fan = cond_lists.shape[1]
    capacity = fan * leaf_dev // 8
    everyone = range(devices)
    shape = jax.ShapeDtypeStruct
    some_rows = shape((capacity, samples, width), jnp.bfloat16)
    all_rows = shape(latent.shape, jnp.float32)
    one_list = shape((1, 4 * SLOTS), jnp.int32)
    heavy = cond_weights.size * 2

    def passed(x, route):
        return lax.ppermute(x, "kx", route)

    before = passed(latent, [(i, i + 4) for i in everyone if i + 4 < devices])
    asked, slots, home, held_l = call(
        index_kernel, "index",
        (
            one_list, shape((2, 4 * SLOTS), jnp.int32), shape((fan, leaf_dev), jnp.int32),
            shape(latent.shape, latent.dtype),
        ),
        [VMEM, HBM], [VMEM] * 4, 4, moved=2 * MIB, scratch=[pltpu.SemaphoreType.DMA],
    )(in_hbm(cond_lists.T), in_hbm(latent))
    ask8 = passed(asked, [(i, i - 4) for i in everyone if i >= 4])
    ask2 = passed(asked, [(i, i ^ 2) for i in everyone])
    ask1 = passed(asked, [(i, i // 4 * 4 + (i + 3) % 4) for i in everyone])
    left, held_w, held_f = call(
        local_kernel, "local",
        (
            all_rows, shape(cond_weights.shape, jnp.bfloat16),
            shape(precision_factor.shape, jnp.bfloat16),
        ),
        [SMEM, VMEM, HBM, HBM], [VMEM] * 3, 16, moved=heavy,
        scratch=[
            VMEM((leaf_dev + 8, samples, width), jnp.bfloat16),
            pltpu.SemaphoreType.DMA((leaf_dev // LEAVES,)),
            pltpu.SemaphoreType.DMA,
        ],
    )(home, held_l, in_hbm(cond_weights), in_hbm(precision_factor))
    serve8, serve2, serve1, heard = call(
        functools.partial(serve_kernel, capacity), "serve",
        (some_rows,) * 3 + (shape((3, 4 * SLOTS), jnp.int32),),
        [SMEM] * 3 + [VMEM] * 2, [VMEM] * 3 + [SMEM], 4, moved=4 * MIB,
    )(ask8, ask2, ask1, held_l, before)
    from8 = passed(serve8, [(i, i + 4) for i in everyone if i >= 4 and i + 4 < devices])
    from2 = passed(serve2, [(i, i ^ 2) for i in everyone])
    from1 = passed(serve1, [(i, i // 4 * 4 + (i + 1) % 4) for i in everyone])
    far = passed(heard, [(i, i - 4) for i in everyone if i >= 4])
    back, out8, out4, out2, out1 = call(
        functools.partial(remote_kernel, capacity), "remote",
        (all_rows,) + (some_rows,) * 4, [SMEM] * 2 + [VMEM] * 7, [VMEM] * 5, 18,
        moved=2 * heavy,
        scratch=[
            VMEM((leaf_dev + 8, samples, width), jnp.float32),
            VMEM((leaf_dev + 8, samples, width), jnp.bfloat16),
        ],
    )(asked, slots, left, before, from8, from2, from1, held_w, held_f)
    returned = [
        passed(x, [(i, i - reach) for i in everyone if i >= reach])
        for reach, x in ((8, out8), (4, out4), (2, out2), (1, out1))
    ]
    (part,) = call(
        home_kernel, "home", (all_rows,), [SMEM, VMEM, VMEM], [VMEM], 16,
        moved=heavy, scratch=[VMEM((leaf_dev + 8, samples, width), jnp.float32)],
    )(home, back, held_w)
    (gradient,) = call(
        functools.partial(add_kernel, capacity), "add", (all_rows,),
        [SMEM] * 4 + [VMEM] * 5, [VMEM], 6, moved=4 * MIB,
    )(ask8, ask2, ask1, far, part, *returned)
    return gradient


def solution(mesh):
    return jax.shard_map(
        per_device,
        mesh=mesh,
        in_specs=(
            P(("groups", "kx"), None, None),
            P(("groups", "kx"), None),
            P(("groups", "kx"), None, None, None),
            P(("groups", "kx"), None, None),
        ),
        out_specs=P(("groups", "kx"), None, None),
        check_vma=False,
    )
```

time: 117 us -> 49.8 us (0.43)
  the two profiles are of different devices: /device:TPU:0 before, /device:TPU:15 now
where the time goes in v2:
time: 49.8 us; the launch traced here: 49.2 us
  starting transfers between devices  23.2 us (47%)
  Pallas kernels  22.1 us (44%)
  waiting for transfers between devices  3.75 us (8%)
    ppermute x12, starting transfers between devices, passed(): return lax.ppermute(x, 'kx', route)  23.2 us
    pallas_call x1, Pallas kernels, per_device(): call(functools.partial(remote_kernel, capacity), 'remote', (all_rows,) +...  8.4 us
    pallas_call x1, Pallas kernels, per_device(): call(local_kernel, 'local', (all_rows, shape(cond_weights.shape, jnp.bflo...  4.69 us
    pallas_call x1, Pallas kernels, per_device(): call(home_kernel, 'home', (all_rows,), [SMEM, VMEM, VMEM], [VMEM], 16, mo...  4.03 us
    ppermute x12, waiting for transfers between devices, passed(): return lax.ppermute(x, 'kx', route)  3.75 us
    pallas_call x1, Pallas kernels, per_device(): call(functools.partial(add_kernel, capacity), 'add', (all_rows,), [SMEM]...  1.84 us
    pallas_call x1, Pallas kernels, per_device(): call(index_kernel, 'index', (one_list, shape((2, 4 * SLOTS), jnp.int32),...  1.66 us
    pallas_call x1, Pallas kernels, per_device(): call(functools.partial(serve_kernel, capacity), 'serve', (some_rows,) * 3...  1.47 us
  transfers between devices with their start and end apart: 12, of which 4 were waited for; matrix products, arithmetic and copies ran while one was open for 0% of the time, Pallas kernels for 21%

profile of v2, /device:TPU:15, one launch (start us, length us, event | category | flops | bytes accessed | tf_op | source)
XLA Modules:
  0.0 49.2 jit_solution(928198256355070383)
XLA Ops:
  0.0 3.2 %collective-permute-start.3 = (bf16[80,16,128]{2,1,0:T(8,128)(2,1)}, bf16[80,16,128]{2,1,0:T(8,128)(2,1)S(1)}, u32[]{:S(2)}, u32[]{:S(2)}) collective-permute-start(bf16[80,16,128]{2,1,0:T(8,128)(2,1)} %latent.1), channel_id=1, source_target_pairs={{0,4},{1,5},{2,6},{3,7},{4,8},{5,9},{6,10},{7,11},{8,12},{9,13},{1... | collective-permute-start | bytes 983048 | tf_op jit(solution)/shard_map/ppermute | solution.py:257
  3.2 1.7 %index.1 = (s32[1,128]{1,0:T(1,128)S(1)}, s32[2,128]{1,0:T(2,128)S(1)}, s32[3,80]{1,0:T(4,128)S(1)}, bf16[80,16,128]{2,1,0:T(8,128)(2,1)S(1)}) custom-call(s32[3,80]{1,0:T(4,128)} %bitcast.1, bf16[80,16,128]{2,1,0:T(8,128)(2,1)} %latent.1), custom_call_target="tpu_custom_call" | custom-call | bytes 2097152 | tf_op jit(solution)/shard_map/index/pallas_call | solution.py:260
  4.9 1.0 %collective-permute-start.2 = (s32[1,128]{1,0:T(1,128)S(1)}, s32[1,128]{1,0:T(1,128)S(1)}, u32[]{:S(2)}, u32[]{:S(2)}) collective-permute-start(s32[1,128]{1,0:T(1,128)S(1)} %get-tuple-element.21.asked), channel_id=1, source_target_pairs={{0,3},{1,0},{2,1},{3,2},{4,7},{5,4},{6,5},{7,6},{8,11},{9,8},{10,9... | collective-permute-start | bytes 1544 | tf_op jit(solution)/shard_map/ppermute | solution.py:257
  5.9 0.2 collective-permute-start.1
  6.1 2.1 %collective-permute-start = (s32[1,128]{1,0:T(1,128)S(1)}, s32[1,128]{1,0:T(1,128)S(1)}, u32[]{:S(2)}, u32[]{:S(2)}) collective-permute-start(s32[1,128]{1,0:T(1,128)S(1)} %get-tuple-element.21.asked), channel_id=1, source_target_pairs={{4,0},{5,1},{6,2},{7,3},{8,4},{9,5},{10,6},{11,7},{12,8},{13,9},{1... | collective-permute-start | bytes 1544 | tf_op jit(solution)/shard_map/ppermute | solution.py:257
  8.2 0.0 collective-permute-done.2.ask1
  8.2 0.4 collective-permute-done.1.ask2
  8.6 2.1 %collective-permute-done.ask8 = s32[1,128]{1,0:T(1,128)S(1)} collective-permute-done((s32[1,128]{1,0:T(1,128)S(1)}, s32[1,128]{1,0:T(1,128)S(1)}, u32[]{:S(2)}, u32[]{:S(2)}) %collective-permute-start) | collective-permute-done | bytes 544 | tf_op jit(solution)/shard_map/ppermute | solution.py:257
  10.7 0.0 collective-permute-done.3.before
  10.7 1.5 %serve.1 = (bf16[30,16,128]{2,1,0:T(8,128)(2,1)S(1)}, bf16[30,16,128]{2,1,0:T(8,128)(2,1)S(1)}, bf16[30,16,128]{2,1,0:T(8,128)(2,1)S(1)}, s32[3,128]{1,0:T(4,128)S(1)}) custom-call(s32[1,128]{1,0:T(1,128)S(1)} %collective-permute-done.ask8, s32[1,128]{1,0:T(1,128)S(1)} %collective-permute-done.1.ask2, s32[1,128]{1,0:T(1,128)S(1)} %collective-permute-done.2.ask1, ...), custom_call_target="tpu_custom_call" | custom-call | bytes 4194304 | tf_op jit(solution)/shard_map/serve/pallas_call | solution.py:284
  12.2 3.2 %collective-permute-start.5 = (bf16[30,16,128]{2,1,0:T(8,128)(2,1)S(1)}, bf16[30,16,128]{2,1,0:T(8,128)(2,1)S(1)}, u32[]{:S(2)}, u32[]{:S(2)}) collective-permute-start(bf16[30,16,128]{2,1,0:T(8,128)(2,1)S(1)} %get-tuple-element.27), channel_id=1, source_target_pairs={{4,8},{5,9},{6,10},{7,11},{8,12},{9,13},{10,14},{11,15},{20,24},{2... | collective-permute-start | bytes 368648 | tf_op jit(solution)/shard_map/ppermute | solution.py:257
  15.4 1.3 %collective-permute-start.6 = (bf16[30,16,128]{2,1,0:T(8,128)(2,1)S(1)}, bf16[30,16,128]{2,1,0:T(8,128)(2,1)S(1)}, u32[]{:S(2)}, u32[]{:S(2)}) collective-permute-start(bf16[30,16,128]{2,1,0:T(8,128)(2,1)S(1)} %get-tuple-element.28), channel_id=1, source_target_pairs={{0,2},{1,3},{2,0},{3,1},{4,6},{5,7},{6,4},{7,5},{8,10},{9,11},{10,... | collective-permute-start | bytes 368648 | tf_op jit(solution)/shard_map/ppermute | solution.py:257
  16.7 2.5 %collective-permute-start.7 = (bf16[30,16,128]{2,1,0:T(8,128)(2,1)S(1)}, bf16[30,16,128]{2,1,0:T(8,128)(2,1)S(1)}, u32[]{:S(2)}, u32[]{:S(2)}) collective-permute-start(bf16[30,16,128]{2,1,0:T(8,128)(2,1)S(1)} %get-tuple-element.29), channel_id=1, source_target_pairs={{0,1},{1,2},{2,3},{3,0},{4,5},{5,6},{6,7},{7,4},{8,9},{9,10},{10,1... | collective-permute-start | bytes 368648 | tf_op jit(solution)/shard_map/ppermute | solution.py:257
  19.2 4.7 %local.1 = (f32[80,16,128]{2,1,0:T(8,128)S(1)}, bf16[80,3,128,128]{3,2,1,0:T(8,128)(2,1)S(1)}, bf16[80,128,128]{2,1,0:T(8,128)(2,1)S(1)}) custom-call(s32[3,80]{1,0:T(4,128)S(1)} %get-tuple-element.24.home, bf16[80,16,128]{2,1,0:T(8,128)(2,1)S(1)} %get-tuple-element.22.latent, bf16[80,3,128,128]{3,2,1,0:T(8,128)(2,1)} %weights.1, bf16[80,128,128]{2,1,0:T(8,128)(2,1)} %factor.1), custom_call_target="tpu_custom_call" | custom-call | bytes 7864320 | tf_op jit(solution)/shard_map/local/pallas_call | solution.py:271
  23.9 0.0 collective-permute-done.5.from8
  23.9 0.0 collective-permute-done.6.from2
  23.9 0.0 collective-permute-done.7.from1
  23.9 8.4 %remote.1 = (f32[80,16,128]{2,1,0:T(8,128)S(1)}, bf16[30,16,128]{2,1,0:T(8,128)(2,1)S(1)}, bf16[30,16,128]{2,1,0:T(8,128)(2,1)S(1)}, bf16[30,16,128]{2,1,0:T(8,128)(2,1)S(1)}, bf16[30,16,128]{2,1,0:T(8,128)(2,1)S(1)}) custom-call(s32[1,128]{1,0:T(1,128)S(1)} %get-tuple-element.21.asked, s32[2,128]{1,0:T(2,128)S(1)} %get-tuple-element.25.slots, ...), custom_call_target="tpu_custom_call" | custom-call | bytes 15728640 | tf_op jit(solution)/shard_map/remote/pallas_call | solution.py:293
  32.3 1.3 %collective-permute-start.8 = (bf16[30,16,128]{2,1,0:T(8,128)(2,1)S(1)}, bf16[30,16,128]{2,1,0:T(8,128)(2,1)S(1)}, u32[]{:S(2)}, u32[]{:S(2)}) collective-permute-start(bf16[30,16,128]{2,1,0:T(8,128)(2,1)S(1)} %get-tuple-element.33), channel_id=1, source_target_pairs={{8,0},{9,1},{10,2},{11,3},{12,4},{13,5},{14,6},{15,7},{24,16},{25,... | collective-permute-start | bytes 368648 | tf_op jit(solution)/shard_map/ppermute | solution.py:257
  33.6 1.9 %collective-permute-start.9 = (bf16[30,16,128]{2,1,0:T(8,128)(2,1)S(1)}, bf16[30,16,128]{2,1,0:T(8,128)(2,1)S(1)}, u32[]{:S(2)}, u32[]{:S(2)}) collective-permute-start(bf16[30,16,128]{2,1,0:T(8,128)(2,1)S(1)} %get-tuple-element.34), channel_id=1, source_target_pairs={{4,0},{5,1},{6,2},{7,3},{8,4},{9,5},{10,6},{11,7},{12,8},{13,9},{1... | collective-permute-start | bytes 368648 | tf_op jit(solution)/shard_map/ppermute | solution.py:257
  35.5 2.5 %collective-permute-start.10 = (bf16[30,16,128]{2,1,0:T(8,128)(2,1)S(1)}, bf16[30,16,128]{2,1,0:T(8,128)(2,1)S(1)}, u32[]{:S(2)}, u32[]{:S(2)}) collective-permute-start(bf16[30,16,128]{2,1,0:T(8,128)(2,1)S(1)} %get-tuple-element.35), channel_id=1, source_target_pairs={{2,0},{3,1},{4,2},{5,3},{6,4},{7,5},{8,6},{9,7},{10,8},{11,9},{12,... | collective-permute-start | bytes 368648 | tf_op jit(solution)/shard_map/ppermute | solution.py:257
  38.1 2.0 %collective-permute-start.11 = (bf16[30,16,128]{2,1,0:T(8,128)(2,1)S(1)}, bf16[30,16,128]{2,1,0:T(8,128)(2,1)S(1)}, u32[]{:S(2)}, u32[]{:S(2)}) collective-permute-start(bf16[30,16,128]{2,1,0:T(8,128)(2,1)S(1)} %get-tuple-element.36), channel_id=1, source_target_pairs={{1,0},{2,1},{3,2},{4,3},{5,4},{6,5},{7,6},{8,7},{9,8},{10,9},{11,1... | collective-permute-start | bytes 368648 | tf_op jit(solution)/shard_map/ppermute | solution.py:257
  40.1 1.9 %collective-permute-start.4 = (s32[3,128]{1,0:T(4,128)S(1)}, s32[3,128]{1,0:T(4,128)S(1)}, u32[]{:S(2)}, u32[]{:S(2)}) collective-permute-start(s32[3,128]{1,0:T(4,128)S(1)} %get-tuple-element.23), channel_id=1, source_target_pairs={{4,0},{5,1},{6,2},{7,3},{8,4},{9,5},{10,6},{11,7},{12,8},{13,9},{1... | collective-permute-start | bytes 4616 | tf_op jit(solution)/shard_map/ppermute | solution.py:257
  42.0 4.0 %home.1.part = f32[80,16,128]{2,1,0:T(8,128)S(1)} custom-call(s32[3,80]{1,0:T(4,128)S(1)} %get-tuple-element.24.home, f32[80,16,128]{2,1,0:T(8,128)S(1)} %get-tuple-element.32.back, bf16[80,3,128,128]{3,2,1,0:T(8,128)(2,1)S(1)} %get-tuple-element.30.weights), custom_call_target="tpu_custom_call" | custom-call | bytes 7864320 | tf_op jit(solution)/shard_map/home/pallas_call | solution.py:306
  46.1 0.0 collective-permute-done.4.far
  46.1 0.0 collective-permute-done.8.back8
  46.1 0.0 collective-permute-done.9.back4
  46.1 0.1 collective-permute-done.10.back2
  46.3 1.1 %collective-permute-done.11.back1 = bf16[30,16,128]{2,1,0:T(8,128)(2,1)S(1)} collective-permute-done((bf16[30,16,128]{2,1,0:T(8,128)(2,1)S(1)}, bf16[30,16,128]{2,1,0:T(8,128)(2,1)S(1)}, u32[]{:S(2)}, u32[]{:S(2)}) %collective-permute-start.11) | collective-permute-done | bytes 122912 | tf_op jit(solution)/shard_map/ppermute | solution.py:257
  47.4 1.8 %add.1 = f32[80,16,128]{2,1,0:T(8,128)} custom-call(s32[1,128]{1,0:T(1,128)S(1)} %collective-permute-done.ask8, s32[1,128]{1,0:T(1,128)S(1)} %collective-permute-done.1.ask2, s32[1,128]{1,0:T(1,128)S(1)} %collective-permute-done.2.ask1, s32[3,128]{1,0:T(4,128)S(1)} %collective-permute-done.4.far, f32[80,16,128]{2,1,0:T(8,128)S(1)} %home.1.part, ...), custom_call_target="tpu_custom_call" | custom-call | bytes 4194304 | tf_op jit(solution)/shard_map/add/pallas_call | solution.py:310
Async XLA Ops:
  0.0 10.7 %collective-permute-start.3 = (bf16[80,16,128]{2,1,0:T(8,128)(2,1)}, bf16[80,16,128]{2,1,0:T(8,128)(2,1)S(1)}, u32[]{:S(2)}, u32[]{:S(2)}) collective-permute-start(bf16[80,16,128]{2,1,0:T(8,128)(2,1)} %latent.1), channel_id=1, source_target_pairs={{0,4},{1,5},{2,6},{3,7},{4,8},{5,9},{6,10},{7,11},{8,12},{9,13},{1... | collective-permute-start | bytes 983048 | tf_op jit(solution)/shard_map/ppermute | solution.py:257
  4.9 3.3 %collective-permute-start.2 = (s32[1,128]{1,0:T(1,128)S(1)}, s32[1,128]{1,0:T(1,128)S(1)}, u32[]{:S(2)}, u32[]{:S(2)}) collective-permute-start(s32[1,128]{1,0:T(1,128)S(1)} %get-tuple-element.21.asked), channel_id=1, source_target_pairs={{0,3},{1,0},{2,1},{3,2},{4,7},{5,4},{6,5},{7,6},{8,11},{9,8},{10,9... | collective-permute-start | bytes 1544 | tf_op jit(solution)/shard_map/ppermute | solution.py:257
  5.9 2.7 %collective-permute-start.1 = (s32[1,128]{1,0:T(1,128)S(1)}, s32[1,128]{1,0:T(1,128)S(1)}, u32[]{:S(2)}, u32[]{:S(2)}) collective-permute-start(s32[1,128]{1,0:T(1,128)S(1)} %get-tuple-element.21.asked), channel_id=1, source_target_pairs={{0,2},{1,3},{2,0},{3,1},{4,6},{5,7},{6,4},{7,5},{8,10},{9,11},{10,... | collective-permute-start | bytes 1544 | tf_op jit(solution)/shard_map/ppermute | solution.py:257
  6.1 4.6 %collective-permute-start = (s32[1,128]{1,0:T(1,128)S(1)}, s32[1,128]{1,0:T(1,128)S(1)}, u32[]{:S(2)}, u32[]{:S(2)}) collective-permute-start(s32[1,128]{1,0:T(1,128)S(1)} %get-tuple-element.21.asked), channel_id=1, source_target_pairs={{4,0},{5,1},{6,2},{7,3},{8,4},{9,5},{10,6},{11,7},{12,8},{13,9},{1... | collective-permute-start | bytes 1544 | tf_op jit(solution)/shard_map/ppermute | solution.py:257
  12.2 11.7 %collective-permute-start.5 = (bf16[30,16,128]{2,1,0:T(8,128)(2,1)S(1)}, bf16[30,16,128]{2,1,0:T(8,128)(2,1)S(1)}, u32[]{:S(2)}, u32[]{:S(2)}) collective-permute-start(bf16[30,16,128]{2,1,0:T(8,128)(2,1)S(1)} %get-tuple-element.27), channel_id=1, source_target_pairs={{4,8},{5,9},{6,10},{7,11},{8,12},{9,13},{10,14},{11,15},{20,24},{2... | collective-permute-start | bytes 368648 | tf_op jit(solution)/shard_map/ppermute | solution.py:257
  15.4 8.5 %collective-permute-start.6 = (bf16[30,16,128]{2,1,0:T(8,128)(2,1)S(1)}, bf16[30,16,128]{2,1,0:T(8,128)(2,1)S(1)}, u32[]{:S(2)}, u32[]{:S(2)}) collective-permute-start(bf16[30,16,128]{2,1,0:T(8,128)(2,1)S(1)} %get-tuple-element.28), channel_id=1, source_target_pairs={{0,2},{1,3},{2,0},{3,1},{4,6},{5,7},{6,4},{7,5},{8,10},{9,11},{10,... | collective-permute-start | bytes 368648 | tf_op jit(solution)/shard_map/ppermute | solution.py:257
  16.7 7.2 %collective-permute-start.7 = (bf16[30,16,128]{2,1,0:T(8,128)(2,1)S(1)}, bf16[30,16,128]{2,1,0:T(8,128)(2,1)S(1)}, u32[]{:S(2)}, u32[]{:S(2)}) collective-permute-start(bf16[30,16,128]{2,1,0:T(8,128)(2,1)S(1)} %get-tuple-element.29), channel_id=1, source_target_pairs={{0,1},{1,2},{2,3},{3,0},{4,5},{5,6},{6,7},{7,4},{8,9},{9,10},{10,1... | collective-permute-start | bytes 368648 | tf_op jit(solution)/shard_map/ppermute | solution.py:257
  32.3 13.8 %collective-permute-start.8 = (bf16[30,16,128]{2,1,0:T(8,128)(2,1)S(1)}, bf16[30,16,128]{2,1,0:T(8,128)(2,1)S(1)}, u32[]{:S(2)}, u32[]{:S(2)}) collective-permute-start(bf16[30,16,128]{2,1,0:T(8,128)(2,1)S(1)} %get-tuple-element.33), channel_id=1, source_target_pairs={{8,0},{9,1},{10,2},{11,3},{12,4},{13,5},{14,6},{15,7},{24,16},{25,... | collective-permute-start | bytes 368648 | tf_op jit(solution)/shard_map/ppermute | solution.py:257
  33.6 12.5 %collective-permute-start.9 = (bf16[30,16,128]{2,1,0:T(8,128)(2,1)S(1)}, bf16[30,16,128]{2,1,0:T(8,128)(2,1)S(1)}, u32[]{:S(2)}, u32[]{:S(2)}) collective-permute-start(bf16[30,16,128]{2,1,0:T(8,128)(2,1)S(1)} %get-tuple-element.34), channel_id=1, source_target_pairs={{4,0},{5,1},{6,2},{7,3},{8,4},{9,5},{10,6},{11,7},{12,8},{13,9},{1... | collective-permute-start | bytes 368648 | tf_op jit(solution)/shard_map/ppermute | solution.py:257
  35.5 10.7 %collective-permute-start.10 = (bf16[30,16,128]{2,1,0:T(8,128)(2,1)S(1)}, bf16[30,16,128]{2,1,0:T(8,128)(2,1)S(1)}, u32[]{:S(2)}, u32[]{:S(2)}) collective-permute-start(bf16[30,16,128]{2,1,0:T(8,128)(2,1)S(1)} %get-tuple-element.35), channel_id=1, source_target_pairs={{2,0},{3,1},{4,2},{5,3},{6,4},{7,5},{8,6},{9,7},{10,8},{11,9},{12,... | collective-permute-start | bytes 368648 | tf_op jit(solution)/shard_map/ppermute | solution.py:257
  38.1 9.3 %collective-permute-start.11 = (bf16[30,16,128]{2,1,0:T(8,128)(2,1)S(1)}, bf16[30,16,128]{2,1,0:T(8,128)(2,1)S(1)}, u32[]{:S(2)}, u32[]{:S(2)}) collective-permute-start(bf16[30,16,128]{2,1,0:T(8,128)(2,1)S(1)} %get-tuple-element.36), channel_id=1, source_target_pairs={{1,0},{2,1},{3,2},{4,3},{5,4},{6,5},{7,6},{8,7},{9,8},{10,9},{11,1... | collective-permute-start | bytes 368648 | tf_op jit(solution)/shard_map/ppermute | solution.py:257
  40.1 6.0 %collective-permute-start.4 = (s32[3,128]{1,0:T(4,128)S(1)}, s32[3,128]{1,0:T(4,128)S(1)}, u32[]{:S(2)}, u32[]{:S(2)}) collective-permute-start(s32[3,128]{1,0:T(4,128)S(1)} %get-tuple-element.23), channel_id=1, source_target_pairs={{4,0},{5,1},{6,2},{7,3},{8,4},{9,5},{10,6},{11,7},{12,8},{13,9},{1... | collective-permute-start | bytes 4616 | tf_op jit(solution)/shard_map/ppermute | solution.py:257

commit v3 on v2

v3 whole, which is shorter than its diff:
```python
import functools

import jax
import jax.numpy as jnp
from jax import lax
from jax.experimental import pallas as pl
from jax.experimental.pallas import tpu as pltpu
from jax.sharding import PartitionSpec as P

SLOTS = 32
LEAVES = 16
MIB = 2**20
BY_ROWS = (((1,), (1,)), ((), ()))
VMEM, SMEM, HBM = pltpu.VMEM, pltpu.SMEM, pltpu.HBM


def index_kernel(lists, asked, slots, close, home):
    fan, leaf_dev = lists.shape
    me = lax.axis_index("kx")
    behind = me * leaf_dev - lists[...]
    kind = (
        (behind > 0).astype(jnp.int32)
        + (behind > leaf_dev).astype(jnp.int32)
        + (behind > 2 * leaf_dev).astype(jnp.int32)
        + (behind > 4 * leaf_dev).astype(jnp.int32)
    )
    reach = jnp.where(kind == 4, 8, jnp.where(kind == 3, 4, kind))
    row = reach * leaf_dev - behind
    home[...] = jnp.where(kind == 0, row, leaf_dev)
    close[...] = jnp.where(kind == 0, row, jnp.where(kind == 3, row + leaf_dev, 2 * leaf_dev))

    def grid(shape, dim):
        return lax.broadcasted_iota(jnp.int32, shape, dim)

    def low(x):
        return x.astype(jnp.float32).astype(jnp.bfloat16)

    every = 4 * fan
    mask = jnp.concatenate([(kind == o).astype(jnp.float32) for o in range(1, 5)], axis=0)
    earlier = low(grid((leaf_dev, leaf_dev), 0) < grid((leaf_dev, leaf_dev), 1))
    a, b = grid((every, every), 0), grid((every, every), 1)
    above = (b < a)
    for o in range(1, 4):
        above = above & ((a < o * fan) | (b >= o * fan))
    within = jnp.dot(low(mask), earlier, preferred_element_type=jnp.float32)
    base = jnp.sum(
        jnp.dot(low(above), low(mask), preferred_element_type=jnp.float32), axis=1, keepdims=True
    )
    place = jnp.where(mask > 0.0, within + base, -1.0)
    slot = grid((SLOTS, leaf_dev), 0).astype(jnp.float32)
    leaf = grid((1, leaf_dev), 1).astype(jnp.float32)
    ones = jnp.ones((1, leaf_dev), jnp.float32)
    total = jnp.zeros((8, 4 * SLOTS), jnp.float32)
    for k in range(fan):
        hit = jnp.concatenate(
            [(place[o * fan + k : o * fan + k + 1] == slot).astype(jnp.float32) for o in range(4)],
            axis=0,
        )
        facts = jnp.concatenate(
            [row[k : k + 1].astype(jnp.float32), leaf, k * ones, ones]
            + [jnp.zeros((4, leaf_dev), jnp.float32)], axis=0,
        )
        total = total + lax.dot_general(
            low(facts), low(hit), BY_ROWS, preferred_element_type=jnp.float32
        )
    asked[...] = total[0:1].astype(jnp.int32)
    slots[0:1] = jnp.where(total[3:4] > 0.0, total[1:2], float(leaf_dev)).astype(jnp.int32)
    slots[1:2] = total[2:3].astype(jnp.int32)


def beside(xs):
    return jnp.concatenate(xs, axis=1)


def below(xs):
    return jnp.concatenate(xs, axis=0)


def paired(x, y, left, right, by_rows=False):
    samples = x.shape[0]
    if by_rows:
        wide = left.shape[0]
        both = lax.dot_general(
            below([x, y]), below([left, right]), BY_ROWS, preferred_element_type=jnp.float32
        )
    else:
        wide = left.shape[1]
        both = jnp.dot(below([x, y]), beside([left, right]), preferred_element_type=jnp.float32)
    return both[:samples, :wide], both[samples:, wide:]


def near_kernel(
    close, latent, before, weights, factor, left, held_w, held_f, rows, row_sem, w_sem, f_sem
):
    leaf_dev = latent.shape[0]
    fan, width = weights.shape[1], weights.shape[2]

    def fetch(c):
        part = pl.ds(c * LEAVES, LEAVES)
        return pltpu.make_async_copy(weights.at[part], held_w.at[part], w_sem.at[c])

    fetch_rows = pltpu.make_async_copy(latent, rows.at[pl.ds(0, leaf_dev)], row_sem)
    fetch_factor = pltpu.make_async_copy(factor, held_f, f_sem)
    fetch_rows.start()
    for c in range(leaf_dev // LEAVES):
        fetch(c).start()
    fetch_factor.start()
    rows[pl.ds(leaf_dev, leaf_dev)] = before[...]
    rows[2 * leaf_dev] = jnp.zeros(latent.shape[1:], latent.dtype)
    fetch_rows.wait()

    def some(c, carry):
        fetch(c).wait()
        for u in range(0, LEAVES, 2):
            i = c * LEAVES + u
            means = paired(
                beside([rows[close[k, i]] for k in range(fan)]),
                beside([rows[close[k, i + 1]] for k in range(fan)]),
                held_w[i].reshape(fan * width, width),
                held_w[i + 1].reshape(fan * width, width),
            )
            for j, mean in zip((i, i + 1), means):
                left[j] = rows[j].astype(jnp.float32) - mean
        return carry

    lax.fori_loop(0, leaf_dev // LEAVES, some, 0)
    fetch_factor.wait()


def remote_kernel(
    capacity, asked, slots, asked_row, left, from8, low2, high2, odd1, high1, low1,
    weights, factor, back, out8, out4, out2, out1, resid, low,
):
    leaf_dev = left.shape[0]
    resid[pl.ds(0, leaf_dev)] = left[...]
    resid[leaf_dev] = jnp.zeros(left.shape[1:], left.dtype)
    low[leaf_dev] = jnp.zeros(left.shape[1:], low.dtype)

    def asker(o, r):
        i = slots[0, o * SLOTS + r]
        return i, weights[jnp.minimum(i, leaf_dev - 1), slots[1, o * SLOTS + r]]

    for o, sources in ((3, (from8,)), (1, (low2, high2)), (0, (odd1, high1, low1))):
        def row(r):
            return functools.reduce(lax.add, [x[asked[0, o * SLOTS + r]] for x in sources])

        found = []
        for r in range(0, capacity, 2):
            (i, w), (j, v) = asker(o, r), asker(o, r + 1)
            found += zip((i, j), paired(row(r), row(r + 1), w, v))
        for i, mean in found:
            resid[i] = resid[i] - mean

    def leaves(c, carry):
        pairs = [c * LEAVES + u for u in range(0, LEAVES, 2)]
        innov = [
            paired(
                resid[i].astype(jnp.bfloat16), resid[i + 1].astype(jnp.bfloat16),
                factor[i], factor[i + 1],
            )
            for i in pairs
        ]
        for i, (x, y) in zip(pairs, innov):
            both = paired(
                x.astype(jnp.bfloat16), y.astype(jnp.bfloat16), factor[i], factor[i + 1], True
            )
            for j, z in zip((i, i + 1), both):
                back[j] = z
                low[j] = z.astype(jnp.bfloat16)
        return carry

    lax.fori_loop(0, leaf_dev // LEAVES, leaves, 0)
    listed = jnp.broadcast_to(asked_row[...].astype(jnp.float32), left.shape[1:])
    for o, out in ((3, out8), (2, out4), (1, out2), (0, out1)):
        for r in range(0, capacity, 2):
            (i, w), (j, v) = asker(o, r), asker(o, r + 1)
            for at, x in zip((r, r + 1), paired(low[i], low[j], w, v, True)):
                out[at] = x.astype(out.dtype)
        out[capacity] = listed.astype(out.dtype)


def home_kernel(home, back, weights, part, acc):
    leaf_dev = back.shape[0]
    fan, width = weights.shape[1], weights.shape[2]
    acc[pl.ds(0, leaf_dev)] = -back[...]
    acc[leaf_dev] = jnp.zeros(back.shape[1:], back.dtype)

    def some(c, carry):
        found = []
        for u in range(0, LEAVES, 2):
            i = c * LEAVES + u
            found += zip((i, i + 1), paired(
                back[i].astype(jnp.bfloat16), back[i + 1].astype(jnp.bfloat16),
                weights[i].reshape(fan * width, width),
                weights[i + 1].reshape(fan * width, width), True,
            ))
        for i, x in found:
            for k in range(fan):
                j = home[k, i]
                acc[j] = acc[j] + x[:, k * width : (k + 1) * width]
        return carry

    lax.fori_loop(0, leaf_dev // LEAVES, some, 0)
    part[...] = acc[pl.ds(0, leaf_dev)]


def add_kernel(capacity, part, back8, back4, back2, back1, out, listed, wanted, sem):
    returned = ((3, back8), (2, back4), (1, back2), (0, back1))
    for o, rows in returned:
        listed[o : o + 1] = rows[capacity].astype(jnp.float32)[0:1].astype(jnp.int32)
    fetch = pltpu.make_async_copy(listed, wanted, sem)
    fetch.start()
    out[...] = part[...]
    fetch.wait()
    for o, rows in returned:
        for r in range(capacity):
            j = wanted[o, o * SLOTS + r]
            out[j] = out[j] + rows[r].astype(jnp.float32)


def call(body, name, out_shape, ins, outs, limit, flops=0, moved=0, scratch=()):
    spec = lambda space: pl.BlockSpec(memory_space=space)
    return pl.pallas_call(
        body,
        out_shape=out_shape,
        in_specs=[spec(space) for space in ins],
        out_specs=tuple(spec(space) for space in outs),
        scratch_shapes=scratch,
        compiler_params=pltpu.CompilerParams(vmem_limit_bytes=limit * MIB),
        cost_estimate=pl.CostEstimate(flops=flops, bytes_accessed=moved, transcendentals=0),
        name=name,
    )


def in_hbm(x):
    return pltpu.with_memory_space_constraint(x, HBM)


def per_device(latent, cond_lists, cond_weights, precision_factor):
    devices = lax.axis_size("kx")
    leaf_dev, samples, width = latent.shape
    fan = cond_lists.shape[1]
    capacity = fan * leaf_dev // 8
    everyone = range(devices)
    shape = jax.ShapeDtypeStruct
    sent = shape((capacity + 1, samples, width), jnp.bfloat16)
    all_rows = shape(latent.shape, jnp.float32)
    one_list = shape((1, 4 * SLOTS), jnp.int32)
    indices = shape((fan, leaf_dev), jnp.int32)
    heavy = cond_weights.size * 2

    def passed(x, step, chosen=lambda i: True):
        return lax.ppermute(
            x, "kx", [(i, i + step) for i in everyone if 0 <= i + step < devices and chosen(i)]
        )

    before = passed(latent, 4)
    low2 = passed(latent, 2, lambda i: i % 4 < 2)
    odd1 = passed(latent, 1, lambda i: i % 2 == 0)
    high1 = passed(low2, -1, lambda i: i % 4 == 3)
    asked, slots, close, home = call(
        index_kernel, "index", (one_list, shape((2, 4 * SLOTS), jnp.int32), indices, indices),
        [VMEM], [VMEM] * 4, 4, moved=2 * MIB,
    )(in_hbm(cond_lists.T))
    high2 = passed(before, -2, lambda i: i % 4 >= 2)
    from8 = passed(before, 4, lambda i: i >= 4)
    low1 = passed(high2, -1, lambda i: i % 4 == 1)
    left, held_w, held_f = call(
        near_kernel, "near",
        (
            all_rows, shape(cond_weights.shape, jnp.bfloat16),
            shape(precision_factor.shape, jnp.bfloat16),
        ),
        [SMEM, HBM, VMEM, HBM, HBM], [VMEM] * 3, 16, moved=heavy,
        scratch=[
            VMEM((2 * leaf_dev + 8, samples, width), jnp.bfloat16),
            pltpu.SemaphoreType.DMA,
            pltpu.SemaphoreType.DMA((leaf_dev // LEAVES,)),
            pltpu.SemaphoreType.DMA,
        ],
    )(close, in_hbm(latent), before, in_hbm(cond_weights), in_hbm(precision_factor))
    back, out8, out4, out2, out1 = call(
        functools.partial(remote_kernel, capacity), "remote",
        (all_rows,) + (sent,) * 4, [SMEM] * 2 + [VMEM] * 10, [VMEM] * 5, 18,
        moved=heavy,
        scratch=[
            VMEM((leaf_dev + 8, samples, width), jnp.float32),
            VMEM((leaf_dev + 8, samples, width), jnp.bfloat16),
        ],
    )(asked, slots, asked, left, from8, low2, high2, odd1, high1, low1, held_w, held_f)
    returned = [passed(x, -reach) for reach, x in ((8, out8), (4, out4), (2, out2), (1, out1))]
    (part,) = call(
        home_kernel, "home", (all_rows,), [SMEM, VMEM, VMEM], [VMEM], 16,
        moved=heavy, scratch=[VMEM((leaf_dev + 8, samples, width), jnp.float32)],
    )(home, back, held_w)
    (gradient,) = call(
        functools.partial(add_kernel, capacity), "add", (all_rows,), [VMEM] * 5, [VMEM], 6,
        moved=4 * MIB,
        scratch=[
            VMEM((4, 4 * SLOTS), jnp.int32), SMEM((4, 4 * SLOTS), jnp.int32),
            pltpu.SemaphoreType.DMA,
        ],
    )(part, *returned)
    return gradient


def solution(mesh):
    return jax.shard_map(
        per_device,
        mesh=mesh,
        in_specs=(
            P(("groups", "kx"), None, None),
            P(("groups", "kx"), None),
            P(("groups", "kx"), None, None, None),
            P(("groups", "kx"), None, None),
        ),
        out_specs=P(("groups", "kx"), None, None),
        check_vma=False,
    )
```

time: 49.8 us -> 53 us (1.064)
  waiting for transfers between devices: 3.75 us -> 10.5 us
  Pallas kernels: 22.1 us -> 16.4 us
  starting transfers between devices: 23.2 us -> 25.6 us
    ppermute x12 -> x11, waiting for transfers between devices: 3.75 us -> 10.5 us  [passed(): lax.ppermute(x, 'kx', [(i, i + step) for i in everyone if 0 <= i + step <...]
    pallas_call x1, Pallas kernels: 8.4 us -> 4.72 us  [per_device(): call(functools.partial(remote_kernel, capacity), 'remote', (all_rows,) +...]
    ppermute x12 -> x11, starting transfers between devices: 23.2 us -> 25.6 us  [passed(): lax.ppermute(x, 'kx', [(i, i + step) for i in everyone if 0 <= i + step <...]
    pallas_call x3 -> x2, Pallas kernels: 8 us -> 6.82 us  [the longest x1 4.98 us: per_device(): call(near_kernel, 'near', (all_rows, shape(cond_weights.shape, jnp.bfloat...]
    pallas_call x1, Pallas kernels: 1.66 us -> 1.01 us  [per_device(): call(index_kernel, 'index', (one_list, shape((2, 4 * SLOTS), jnp.int32),...]
  transfers between devices with their start and end apart: 12 -> 11, of which waited for: 4 -> 3; matrix products, arithmetic and copies ran while one was open for 0% -> 0% of each run, Pallas kernels for 21% -> 19%
where the time goes in v3:
time: 53 us; the launch traced here: 52.7 us
  starting transfers between devices  25.6 us (48%)
  Pallas kernels  16.4 us (31%)
  waiting for transfers between devices  10.5 us (20%)
    ppermute x11, starting transfers between devices, passed(): lax.ppermute(x, 'kx', [(i, i + step) for i in everyone if 0 <= i + step <...  25.6 us
    ppermute x11, waiting for transfers between devices, passed(): lax.ppermute(x, 'kx', [(i, i + step) for i in everyone if 0 <= i + step <...  10.5 us
    pallas_call x1, Pallas kernels, per_device(): call(near_kernel, 'near', (all_rows, shape(cond_weights.shape, jnp.bfloat...  4.98 us
    pallas_call x1, Pallas kernels, per_device(): call(functools.partial(remote_kernel, capacity), 'remote', (all_rows,) +...  4.72 us
    pallas_call x1, Pallas kernels, per_device(): call(home_kernel, 'home', (all_rows,), [SMEM, VMEM, VMEM], [VMEM], 16, mo...  3.86 us
    pallas_call x1, Pallas kernels, per_device(): call(functools.partial(add_kernel, capacity), 'add', (all_rows,), [VMEM]...  1.84 us
  transfers between devices with their start and end apart: 11, of which 3 were waited for; matrix products, arithmetic and copies ran while one was open for 0% of the time, Pallas kernels for 19%

profile of v3, /device:TPU:15, one launch (start us, length us, event | category | flops | bytes accessed | tf_op | source)
XLA Modules:
  0.0 52.7 jit_solution(4180971059449827568)
XLA Ops:
  0.0 3.2 %collective-permute-start = (bf16[80,16,128]{2,1,0:T(8,128)(2,1)}, bf16[80,16,128]{2,1,0:T(8,128)(2,1)S(1)}, u32[]{:S(2)}, u32[]{:S(2)}) collective-permute-start(bf16[80,16,128]{2,1,0:T(8,128)(2,1)} %latent.1), channel_id=1, source_target_pairs={{0,4},{1,5},{2,6},{3,7},{4,8},{5,9},{6,10},{7,11},{8,12},{9,13},{1... | collective-permute-start | bytes 983048 | tf_op jit(solution)/shard_map/ppermute | solution.py:253
  3.2 1.3 %collective-permute-start.2 = (bf16[80,16,128]{2,1,0:T(8,128)(2,1)}, bf16[80,16,128]{2,1,0:T(8,128)(2,1)S(1)}, u32[]{:S(2)}, u32[]{:S(2)}) collective-permute-start(bf16[80,16,128]{2,1,0:T(8,128)(2,1)} %latent.1), channel_id=1, source_target_pairs={{0,2},{1,3},{4,6},{5,7},{8,10},{9,11},{12,14},{13,15},{16,18},{17,... | collective-permute-start | bytes 983048 | tf_op jit(solution)/shard_map/ppermute | solution.py:253
  4.5 6.2 %collective-permute-done.before = bf16[80,16,128]{2,1,0:T(8,128)(2,1)S(1)} collective-permute-done((bf16[80,16,128]{2,1,0:T(8,128)(2,1)}, bf16[80,16,128]{2,1,0:T(8,128)(2,1)S(1)}, u32[]{:S(2)}, u32[]{:S(2)}) %collective-permute-start) | collective-permute-done | bytes 327712 | tf_op jit(solution)/shard_map/ppermute | solution.py:253
  10.7 2.1 %collective-permute-start.3 = (bf16[80,16,128]{2,1,0:T(8,128)(2,1)S(1)}, bf16[80,16,128]{2,1,0:T(8,128)(2,1)S(1)}, u32[]{:S(2)}, u32[]{:S(2)}) collective-permute-start(bf16[80,16,128]{2,1,0:T(8,128)(2,1)S(1)} %collective-permute-done.before), channel_id=1, source_target_pairs={{2,0},{3,1},{6,4},{7,5},{10,8},{11,9},{14,12},{15,13},{18,16},{19,... | collective-permute-start | bytes 983048 | tf_op jit(solution)/shard_map/ppermute | solution.py:253
  12.8 1.3 %collective-permute-start.4 = (bf16[80,16,128]{2,1,0:T(8,128)(2,1)}, bf16[80,16,128]{2,1,0:T(8,128)(2,1)S(1)}, u32[]{:S(2)}, u32[]{:S(2)}) collective-permute-start(bf16[80,16,128]{2,1,0:T(8,128)(2,1)} %latent.1), channel_id=1, source_target_pairs={{0,1},{2,3},{4,5},{6,7},{8,9},{10,11},{12,13},{14,15},{16,17},{18,... | collective-permute-start | bytes 983048 | tf_op jit(solution)/shard_map/ppermute | solution.py:253
  14.1 3.2 %collective-permute-start.1 = (bf16[80,16,128]{2,1,0:T(8,128)(2,1)S(1)}, bf16[80,16,128]{2,1,0:T(8,128)(2,1)S(1)}, u32[]{:S(2)}, u32[]{:S(2)}) collective-permute-start(bf16[80,16,128]{2,1,0:T(8,128)(2,1)S(1)} %collective-permute-done.before), channel_id=1, source_target_pairs={{4,8},{5,9},{6,10},{7,11},{8,12},{9,13},{10,14},{11,15},{20,24},{2... | collective-permute-start | bytes 983048 | tf_op jit(solution)/shard_map/ppermute | solution.py:253
  17.3 0.0 collective-permute-done.2.low2
  17.4 4.1 %collective-permute-start.5 = (bf16[80,16,128]{2,1,0:T(8,128)(2,1)S(1)}, bf16[80,16,128]{2,1,0:T(8,128)(2,1)S(1)}, u32[]{:S(2)}, u32[]{:S(2)}) collective-permute-start(bf16[80,16,128]{2,1,0:T(8,128)(2,1)S(1)} %collective-permute-done.2.low2), channel_id=1, source_target_pairs={{3,2},{7,6},{11,10},{15,14},{19,18},{23,22},{27,26},{31,30}} | collective-permute-start | bytes 983048 | tf_op jit(solution)/shard_map/ppermute | solution.py:253
  21.4 0.0 collective-permute-done.3.high2
  21.4 0.7 %collective-permute-start.6 = (bf16[80,16,128]{2,1,0:T(8,128)(2,1)S(1)}, bf16[80,16,128]{2,1,0:T(8,128)(2,1)S(1)}, u32[]{:S(2)}, u32[]{:S(2)}) collective-permute-start(bf16[80,16,128]{2,1,0:T(8,128)(2,1)S(1)} %collective-permute-done.3.high2), channel_id=1, source_target_pairs={{1,0},{5,4},{9,8},{13,12},{17,16},{21,20},{25,24},{29,28}} | collective-permute-start | bytes 983048 | tf_op jit(solution)/shard_map/ppermute | solution.py:253
  22.1 1.0 %index.1 = (s32[1,128]{1,0:T(1,128)S(1)}, s32[2,128]{1,0:T(2,128)S(1)}, s32[3,80]{1,0:T(4,128)S(1)}, s32[3,80]{1,0:T(4,128)S(1)}) custom-call(s32[3,80]{1,0:T(4,128)} %bitcast.1), custom_call_target="tpu_custom_call" | custom-call | bytes 2097152 | tf_op jit(solution)/shard_map/index/pallas_call | solution.py:261
  23.1 5.0 %near.1 = (f32[80,16,128]{2,1,0:T(8,128)S(1)}, bf16[80,3,128,128]{3,2,1,0:T(8,128)(2,1)S(1)}, bf16[80,128,128]{2,1,0:T(8,128)(2,1)S(1)}) custom-call(s32[3,80]{1,0:T(4,128)S(1)} %get-tuple-element.20.close, bf16[80,16,128]{2,1,0:T(8,128)(2,1)} %latent.1, bf16[80,16,128]{2,1,0:T(8,128)(2,1)S(1)} %collective-permute-done.before, ...), custom_call_target="tpu_custom_call" | custom-call | bytes 7864320 | tf_op jit(solution)/shard_map/near/pallas_call | solution.py:268
  28.1 0.0 collective-permute-done.4.odd1
  28.1 0.0 collective-permute-done.1.from8
  28.1 0.0 collective-permute-done.5.high1
  28.2 0.0 collective-permute-done.6.low1
  28.2 4.7 %remote.1 = (f32[80,16,128]{2,1,0:T(8,128)S(1)}, bf16[31,16,128]{2,1,0:T(8,128)(2,1)S(1)}, bf16[31,16,128]{2,1,0:T(8,128)(2,1)S(1)}, bf16[31,16,128]{2,1,0:T(8,128)(2,1)S(1)}, bf16[31,16,128]{2,1,0:T(8,128)(2,1)S(1)}) custom-call(s32[1,128]{1,0:T(1,128)S(1)} %get-tuple-element.18.asked.asked_row, s32[2,128]{1,0:T(2,128)S(1)} %get-tuple-element.19.slots, ...), custom_call_target="tpu_custom_call" | custom-call | bytes 7864320 | tf_op jit(solution)/shard_map/remote/pallas_call | solution.py:282
  32.9 1.3 %collective-permute-start.7 = (bf16[31,16,128]{2,1,0:T(8,128)(2,1)S(1)}, bf16[31,16,128]{2,1,0:T(8,128)(2,1)S(1)}, u32[]{:S(2)}, u32[]{:S(2)}) collective-permute-start(bf16[31,16,128]{2,1,0:T(8,128)(2,1)S(1)} %get-tuple-element.25), channel_id=1, source_target_pairs={{8,0},{9,1},{10,2},{11,3},{12,4},{13,5},{14,6},{15,7},{24,16},{25,... | collective-permute-start | bytes 380936 | tf_op jit(solution)/shard_map/ppermute | solution.py:253
  34.2 1.9 %collective-permute-start.8 = (bf16[31,16,128]{2,1,0:T(8,128)(2,1)S(1)}, bf16[31,16,128]{2,1,0:T(8,128)(2,1)S(1)}, u32[]{:S(2)}, u32[]{:S(2)}) collective-permute-start(bf16[31,16,128]{2,1,0:T(8,128)(2,1)S(1)} %get-tuple-element.26), channel_id=1, source_target_pairs={{4,0},{5,1},{6,2},{7,3},{8,4},{9,5},{10,6},{11,7},{12,8},{13,9},{1... | collective-permute-start | bytes 380936 | tf_op jit(solution)/shard_map/ppermute | solution.py:253
  36.1 4.6 %collective-permute-start.9 = (bf16[31,16,128]{2,1,0:T(8,128)(2,1)S(1)}, bf16[31,16,128]{2,1,0:T(8,128)(2,1)S(1)}, u32[]{:S(2)}, u32[]{:S(2)}) collective-permute-start(bf16[31,16,128]{2,1,0:T(8,128)(2,1)S(1)} %get-tuple-element.27), channel_id=1, source_target_pairs={{2,0},{3,1},{4,2},{5,3},{6,4},{7,5},{8,6},{9,7},{10,8},{11,9},{12,... | collective-permute-start | bytes 380936 | tf_op jit(solution)/shard_map/ppermute | solution.py:253
  40.7 1.9 %collective-permute-start.10 = (bf16[31,16,128]{2,1,0:T(8,128)(2,1)S(1)}, bf16[31,16,128]{2,1,0:T(8,128)(2,1)S(1)}, u32[]{:S(2)}, u32[]{:S(2)}) collective-permute-start(bf16[31,16,128]{2,1,0:T(8,128)(2,1)S(1)} %get-tuple-element.28), channel_id=1, source_target_pairs={{1,0},{2,1},{3,2},{4,3},{5,4},{6,5},{7,6},{8,7},{9,8},{10,9},{11,1... | collective-permute-start | bytes 380936 | tf_op jit(solution)/shard_map/ppermute | solution.py:253
  42.7 3.9 %home.1.part = f32[80,16,128]{2,1,0:T(8,128)S(1)} custom-call(s32[3,80]{1,0:T(4,128)S(1)} %get-tuple-element.17.home, f32[80,16,128]{2,1,0:T(8,128)S(1)} %get-tuple-element.24.back, bf16[80,3,128,128]{3,2,1,0:T(8,128)(2,1)S(1)} %get-tuple-element.22.weights), custom_call_target="tpu_custom_call" | custom-call | bytes 7864320 | tf_op jit(solution)/shard_map/home/pallas_call | solution.py:292
  46.5 0.0 collective-permute-done.7.back8
  46.6 0.0 collective-permute-done.8.back4
  46.6 3.1 %collective-permute-done.9.back2 = bf16[31,16,128]{2,1,0:T(8,128)(2,1)S(1)} collective-permute-done((bf16[31,16,128]{2,1,0:T(8,128)(2,1)S(1)}, bf16[31,16,128]{2,1,0:T(8,128)(2,1)S(1)}, u32[]{:S(2)}, u32[]{:S(2)}) %collective-permute-start.9) | collective-permute-done | bytes 127008 | tf_op jit(solution)/shard_map/ppermute | solution.py:253
  49.7 1.2 %collective-permute-done.10.back1 = bf16[31,16,128]{2,1,0:T(8,128)(2,1)S(1)} collective-permute-done((bf16[31,16,128]{2,1,0:T(8,128)(2,1)S(1)}, bf16[31,16,128]{2,1,0:T(8,128)(2,1)S(1)}, u32[]{:S(2)}, u32[]{:S(2)}) %collective-permute-start.10) | collective-permute-done | bytes 127008 | tf_op jit(solution)/shard_map/ppermute | solution.py:253
  50.9 1.8 %add.1 = f32[80,16,128]{2,1,0:T(8,128)} custom-call(f32[80,16,128]{2,1,0:T(8,128)S(1)} %home.1.part, bf16[31,16,128]{2,1,0:T(8,128)(2,1)S(1)} %collective-permute-done.7.back8, bf16[31,16,128]{2,1,0:T(8,128)(2,1)S(1)} %collective-permute-done.8.back4, bf16[31,16,128]{2,1,0:T(8,128)(2,1)S(1)} %collective-permute-done.9.back2, ...), custom_call_target="tpu_custom_call" | custom-call | bytes 4194304 | tf_op jit(solution)/shard_map/add/pallas_call | solution.py:296
Async XLA Ops:
  0.0 10.7 %collective-permute-start = (bf16[80,16,128]{2,1,0:T(8,128)(2,1)}, bf16[80,16,128]{2,1,0:T(8,128)(2,1)S(1)}, u32[]{:S(2)}, u32[]{:S(2)}) collective-permute-start(bf16[80,16,128]{2,1,0:T(8,128)(2,1)} %latent.1), channel_id=1, source_target_pairs={{0,4},{1,5},{2,6},{3,7},{4,8},{5,9},{6,10},{7,11},{8,12},{9,13},{1... | collective-permute-start | bytes 983048 | tf_op jit(solution)/shard_map/ppermute | solution.py:253
  3.2 14.1 %collective-permute-start.2 = (bf16[80,16,128]{2,1,0:T(8,128)(2,1)}, bf16[80,16,128]{2,1,0:T(8,128)(2,1)S(1)}, u32[]{:S(2)}, u32[]{:S(2)}) collective-permute-start(bf16[80,16,128]{2,1,0:T(8,128)(2,1)} %latent.1), channel_id=1, source_target_pairs={{0,2},{1,3},{4,6},{5,7},{8,10},{9,11},{12,14},{13,15},{16,18},{17,... | collective-permute-start | bytes 983048 | tf_op jit(solution)/shard_map/ppermute | solution.py:253
  10.7 10.7 %collective-permute-start.3 = (bf16[80,16,128]{2,1,0:T(8,128)(2,1)S(1)}, bf16[80,16,128]{2,1,0:T(8,128)(2,1)S(1)}, u32[]{:S(2)}, u32[]{:S(2)}) collective-permute-start(bf16[80,16,128]{2,1,0:T(8,128)(2,1)S(1)} %collective-permute-done.before), channel_id=1, source_target_pairs={{2,0},{3,1},{6,4},{7,5},{10,8},{11,9},{14,12},{15,13},{18,16},{19,... | collective-permute-start | bytes 983048 | tf_op jit(solution)/shard_map/ppermute | solution.py:253
  12.8 15.3 %collective-permute-start.4 = (bf16[80,16,128]{2,1,0:T(8,128)(2,1)}, bf16[80,16,128]{2,1,0:T(8,128)(2,1)S(1)}, u32[]{:S(2)}, u32[]{:S(2)}) collective-permute-start(bf16[80,16,128]{2,1,0:T(8,128)(2,1)} %latent.1), channel_id=1, source_target_pairs={{0,1},{2,3},{4,5},{6,7},{8,9},{10,11},{12,13},{14,15},{16,17},{18,... | collective-permute-start | bytes 983048 | tf_op jit(solution)/shard_map/ppermute | solution.py:253
  14.1 14.0 %collective-permute-start.1 = (bf16[80,16,128]{2,1,0:T(8,128)(2,1)S(1)}, bf16[80,16,128]{2,1,0:T(8,128)(2,1)S(1)}, u32[]{:S(2)}, u32[]{:S(2)}) collective-permute-start(bf16[80,16,128]{2,1,0:T(8,128)(2,1)S(1)} %collective-permute-done.before), channel_id=1, source_target_pairs={{4,8},{5,9},{6,10},{7,11},{8,12},{9,13},{10,14},{11,15},{20,24},{2... | collective-permute-start | bytes 983048 | tf_op jit(solution)/shard_map/ppermute | solution.py:253
  17.4 10.8 %collective-permute-start.5 = (bf16[80,16,128]{2,1,0:T(8,128)(2,1)S(1)}, bf16[80,16,128]{2,1,0:T(8,128)(2,1)S(1)}, u32[]{:S(2)}, u32[]{:S(2)}) collective-permute-start(bf16[80,16,128]{2,1,0:T(8,128)(2,1)S(1)} %collective-permute-done.2.low2), channel_id=1, source_target_pairs={{3,2},{7,6},{11,10},{15,14},{19,18},{23,22},{27,26},{31,30}} | collective-permute-start | bytes 983048 | tf_op jit(solution)/shard_map/ppermute | solution.py:253
  21.4 6.7 %collective-permute-start.6 = (bf16[80,16,128]{2,1,0:T(8,128)(2,1)S(1)}, bf16[80,16,128]{2,1,0:T(8,128)(2,1)S(1)}, u32[]{:S(2)}, u32[]{:S(2)}) collective-permute-start(bf16[80,16,128]{2,1,0:T(8,128)(2,1)S(1)} %collective-permute-done.3.high2), channel_id=1, source_target_pairs={{1,0},{5,4},{9,8},{13,12},{17,16},{21,20},{25,24},{29,28}} | collective-permute-start | bytes 983048 | tf_op jit(solution)/shard_map/ppermute | solution.py:253
  32.9 13.7 %collective-permute-start.7 = (bf16[31,16,128]{2,1,0:T(8,128)(2,1)S(1)}, bf16[31,16,128]{2,1,0:T(8,128)(2,1)S(1)}, u32[]{:S(2)}, u32[]{:S(2)}) collective-permute-start(bf16[31,16,128]{2,1,0:T(8,128)(2,1)S(1)} %get-tuple-element.25), channel_id=1, source_target_pairs={{8,0},{9,1},{10,2},{11,3},{12,4},{13,5},{14,6},{15,7},{24,16},{25,... | collective-permute-start | bytes 380936 | tf_op jit(solution)/shard_map/ppermute | solution.py:253
  34.2 12.4 %collective-permute-start.8 = (bf16[31,16,128]{2,1,0:T(8,128)(2,1)S(1)}, bf16[31,16,128]{2,1,0:T(8,128)(2,1)S(1)}, u32[]{:S(2)}, u32[]{:S(2)}) collective-permute-start(bf16[31,16,128]{2,1,0:T(8,128)(2,1)S(1)} %get-tuple-element.26), channel_id=1, source_target_pairs={{4,0},{5,1},{6,2},{7,3},{8,4},{9,5},{10,6},{11,7},{12,8},{13,9},{1... | collective-permute-start | bytes 380936 | tf_op jit(solution)/shard_map/ppermute | solution.py:253
  36.1 13.6 %collective-permute-start.9 = (bf16[31,16,128]{2,1,0:T(8,128)(2,1)S(1)}, bf16[31,16,128]{2,1,0:T(8,128)(2,1)S(1)}, u32[]{:S(2)}, u32[]{:S(2)}) collective-permute-start(bf16[31,16,128]{2,1,0:T(8,128)(2,1)S(1)} %get-tuple-element.27), channel_id=1, source_target_pairs={{2,0},{3,1},{4,2},{5,3},{6,4},{7,5},{8,6},{9,7},{10,8},{11,9},{12,... | collective-permute-start | bytes 380936 | tf_op jit(solution)/shard_map/ppermute | solution.py:253
  40.7 10.1 %collective-permute-start.10 = (bf16[31,16,128]{2,1,0:T(8,128)(2,1)S(1)}, bf16[31,16,128]{2,1,0:T(8,128)(2,1)S(1)}, u32[]{:S(2)}, u32[]{:S(2)}) collective-permute-start(bf16[31,16,128]{2,1,0:T(8,128)(2,1)S(1)} %get-tuple-element.28), channel_id=1, source_target_pairs={{1,0},{2,1},{3,2},{4,3},{5,4},{6,5},{7,6},{8,7},{9,8},{10,9},{11,1... | collective-permute-start | bytes 380936 | tf_op jit(solution)/shard_map/ppermute | solution.py:253

commit v4 on v3

--- a/solution.py
+++ b/solution.py
@@ -11,10 +11,10 @@
 LEAVES = 16
 MIB = 2**20
 BY_ROWS = (((1,), (1,)), ((), ()))
-VMEM, SMEM, HBM = pltpu.VMEM, pltpu.SMEM, pltpu.HBM
-
-
-def index_kernel(lists, asked, slots, close, home):
+VMEM, SMEM, HBM, ANY = pltpu.VMEM, pltpu.SMEM, pltpu.HBM, pl.ANY
+
+
+def index_kernel(lists, asked, slots, home):
     fan, leaf_dev = lists.shape
     me = lax.axis_index("kx")
     behind = me * leaf_dev - lists[...]
@@ -27,7 +27,6 @@
     reach = jnp.where(kind == 4, 8, jnp.where(kind == 3, 4, kind))
     row = reach * leaf_dev - behind
     home[...] = jnp.where(kind == 0, row, leaf_dev)
-    close[...] = jnp.where(kind == 0, row, jnp.where(kind == 3, row + leaf_dev, 2 * leaf_dev))
 
     def grid(shape, dim):
         return lax.broadcasted_iota(jnp.int32, shape, dim)
@@ -89,9 +88,7 @@
     return both[:samples, :wide], both[samples:, wide:]
 
 
-def near_kernel(
-    close, latent, before, weights, factor, left, held_w, held_f, rows, row_sem, w_sem, f_sem
-):
+def local_kernel(home, latent, weights, left, held_w, held_l, rows, row_sem, w_sem):
     leaf_dev = latent.shape[0]
     fan, width = weights.shape[1], weights.shape[2]
 
@@ -99,23 +96,21 @@
         part = pl.ds(c * LEAVES, LEAVES)
         return pltpu.make_async_copy(weights.at[part], held_w.at[part], w_sem.at[c])
 
-    fetch_rows = pltpu.make_async_copy(latent, rows.at[pl.ds(0, leaf_dev)], row_sem)
-    fetch_factor = pltpu.make_async_copy(factor, held_f, f_sem)
+    fetch_rows = pltpu.make_async_copy(latent, held_l, row_sem)
     fetch_rows.start()
     for c in range(leaf_dev // LEAVES):
         fetch(c).start()
-    fetch_factor.start()
-    rows[pl.ds(leaf_dev, leaf_dev)] = before[...]
-    rows[2 * leaf_dev] = jnp.zeros(latent.shape[1:], latent.dtype)
     fetch_rows.wait()
+    rows[pl.ds(0, leaf_dev)] = held_l[...]
+    rows[leaf_dev] = jnp.zeros(latent.shape[1:], latent.dtype)
 
     def some(c, carry):
         fetch(c).wait()
         for u in range(0, LEAVES, 2):
             i = c * LEAVES + u
             means = paired(
-                beside([rows[close[k, i]] for k in range(fan)]),
-                beside([rows[close[k, i + 1]] for k in range(fan)]),
+                beside([rows[home[k, i]] for k in range(fan)]),
+                beside([rows[home[k, i + 1]] for k in range(fan)]),
                 held_w[i].reshape(fan * width, width),
                 held_w[i + 1].reshape(fan * width, width),
             )
@@ -124,14 +119,34 @@
         return carry
 
     lax.fori_loop(0, leaf_dev // LEAVES, some, 0)
-    fetch_factor.wait()
+
+
+def serve_kernel(capacity, ask8, ask2, ask1, latent, before, left, out8, out2, out1):
+    me = lax.axis_index("kx")
+    def pick(o, ask, rows, out):
+        for r in range(capacity):
+            out[r] = rows[ask[0, o * SLOTS + r]]
+
+    pick(3, ask8, before, out8)
+    for o, ask, out, bits in ((1, ask2, out2, 2), (0, ask1, out1, 3)):
+        relays = lax.bitwise_and(me, bits) == bits
+
+        @pl.when(relays)
+        def _():
+            pick(o, ask, before, out)
+
+        @pl.when(jnp.logical_not(relays))
+        def _():
+            pick(o, ask, latent, out)
 
 
 def remote_kernel(
-    capacity, asked, slots, asked_row, left, from8, low2, high2, odd1, high1, low1,
-    weights, factor, back, out8, out4, out2, out1, resid, low,
+    capacity, asked, slots, asked_row, left, before, from8, from2, from1,
+    weights, factor, back, out8, out4, out2, out1, resid, low, held_f, f_sem,
 ):
     leaf_dev = left.shape[0]
+    fetch = pltpu.make_async_copy(factor, held_f, f_sem)
+    fetch.start()
     resid[pl.ds(0, leaf_dev)] = left[...]
     resid[leaf_dev] = jnp.zeros(left.shape[1:], left.dtype)
     low[leaf_dev] = jnp.zeros(left.shape[1:], low.dtype)
@@ -140,29 +155,29 @@
         i = slots[0, o * SLOTS + r]
         return i, weights[jnp.minimum(i, leaf_dev - 1), slots[1, o * SLOTS + r]]
 
-    for o, sources in ((3, (from8,)), (1, (low2, high2)), (0, (odd1, high1, low1))):
-        def row(r):
-            return functools.reduce(lax.add, [x[asked[0, o * SLOTS + r]] for x in sources])
-
+    for o, rows in ((2, before), (3, from8), (1, from2), (0, from1)):
         found = []
         for r in range(0, capacity, 2):
             (i, w), (j, v) = asker(o, r), asker(o, r + 1)
-            found += zip((i, j), paired(row(r), row(r + 1), w, v))
+            at = (asked[0, o * SLOTS + r], asked[0, o * SLOTS + r + 1]) if o == 2 else (r, r + 1)
+            found += zip((i, j), paired(rows[at[0]], rows[at[1]], w, v))
         for i, mean in found:
             resid[i] = resid[i] - mean
+
+    fetch.wait()
 
     def leaves(c, carry):
         pairs = [c * LEAVES + u for u in range(0, LEAVES, 2)]
         innov = [
             paired(
                 resid[i].astype(jnp.bfloat16), resid[i + 1].astype(jnp.bfloat16),
-                factor[i], factor[i + 1],
+                held_f[i], held_f[i + 1],
             )
             for i in pairs
         ]
         for i, (x, y) in zip(pairs, innov):
             both = paired(
-                x.astype(jnp.bfloat16), y.astype(jnp.bfloat16), factor[i], factor[i + 1], True
+                x.astype(jnp.bfloat16), y.astype(jnp.bfloat16), held_f[i], held_f[i + 1], True
             )
             for j, z in zip((i, i + 1), both):
                 back[j] = z
@@ -232,8 +247,8 @@
     )
 
 
-def in_hbm(x):
-    return pltpu.with_memory_space_constraint(x, HBM)
+def placed(x, space):
+    return pltpu.with_memory_space_constraint(x, space)
 
 
 def per_device(latent, cond_lists, cond_weights, precision_factor):
@@ -243,55 +258,57 @@
     capacity = fan * leaf_dev // 8
     everyone = range(devices)
     shape = jax.ShapeDtypeStruct
+    some_rows = shape((capacity, samples, width), jnp.bfloat16)
     sent = shape((capacity + 1, samples, width), jnp.bfloat16)
     all_rows = shape(latent.shape, jnp.float32)
     one_list = shape((1, 4 * SLOTS), jnp.int32)
-    indices = shape((fan, leaf_dev), jnp.int32)
     heavy = cond_weights.size * 2
 
-    def passed(x, step, chosen=lambda i: True):
-        return lax.ppermute(
-            x, "kx", [(i, i + step) for i in everyone if 0 <= i + step < devices and chosen(i)]
-        )
-
-    before = passed(latent, 4)
-    low2 = passed(latent, 2, lambda i: i % 4 < 2)
-    odd1 = passed(latent, 1, lambda i: i % 2 == 0)
-    high1 = passed(low2, -1, lambda i: i % 4 == 3)
-    asked, slots, close, home = call(
-        index_kernel, "index", (one_list, shape((2, 4 * SLOTS), jnp.int32), indices, indices),
-        [VMEM], [VMEM] * 4, 4, moved=2 * MIB,
-    )(in_hbm(cond_lists.T))
-    high2 = passed(before, -2, lambda i: i % 4 >= 2)
-    from8 = passed(before, 4, lambda i: i >= 4)
-    low1 = passed(high2, -1, lambda i: i % 4 == 1)
-    left, held_w, held_f = call(
-        near_kernel, "near",
-        (
-            all_rows, shape(cond_weights.shape, jnp.bfloat16),
-            shape(precision_factor.shape, jnp.bfloat16),
-        ),
-        [SMEM, HBM, VMEM, HBM, HBM], [VMEM] * 3, 16, moved=heavy,
+    def passed(x, route):
+        return lax.ppermute(x, "kx", route)
+
+    before = passed(latent, [(i, i + 4) for i in everyone if i + 4 < devices])
+    asked, slots, home = call(
+        index_kernel, "index",
+        (one_list, shape((2, 4 * SLOTS), jnp.int32), shape((fan, leaf_dev), jnp.int32)),
+        [VMEM], [VMEM] * 3, 4, moved=2 * MIB,
+    )(placed(cond_lists.T, HBM))
+    ask8 = passed(asked, [(i, i - 4) for i in everyone if i >= 4])
+    ask2 = passed(asked, [(i, i ^ 2) for i in everyone])
+    ask1 = passed(asked, [(i, i // 4 * 4 + (i + 3) % 4) for i in everyone])
+    left, held_w, held_l = call(
+        local_kernel, "local",
+        (all_rows, shape(cond_weights.shape, jnp.bfloat16), shape(latent.shape, jnp.bfloat16)),
+        [SMEM, HBM, HBM], [VMEM] * 3, 14, moved=heavy,
         scratch=[
-            VMEM((2 * leaf_dev + 8, samples, width), jnp.bfloat16),
-            pltpu.SemaphoreType.DMA,
-            pltpu.SemaphoreType.DMA((leaf_dev // LEAVES,)),
-            pltpu.SemaphoreType.DMA,
+            VMEM((leaf_dev + 8, samples, width), jnp.bfloat16),
+            pltpu.SemaphoreType.DMA, pltpu.SemaphoreType.DMA((leaf_dev // LEAVES,)),
         ],
-    )(close, in_hbm(latent), before, in_hbm(cond_weights), in_hbm(precision_factor))
+    )(home, placed(latent, HBM), placed(cond_weights, HBM))
+    serve8, serve2, serve1 = call(
+        functools.partial(serve_kernel, capacity), "serve", (some_rows,) * 3,
+        [SMEM] * 3 + [VMEM] * 2 + [ANY], [VMEM] * 3, 4, moved=4 * MIB,
+    )(ask8, ask2, ask1, held_l, before, left)
+    from8 = passed(serve8, [(i, i + 4) for i in everyone if i >= 4 and i + 4 < devices])
+    from2 = passed(serve2, [(i, i ^ 2) for i in everyone])
+    from1 = passed(serve1, [(i, i // 4 * 4 + (i + 1) % 4) for i in everyone])
     back, out8, out4, out2, out1 = call(
         functools.partial(remote_kernel, capacity), "remote",
-        (all_rows,) + (sent,) * 4, [SMEM] * 2 + [VMEM] * 10, [VMEM] * 5, 18,
-        moved=heavy,
+        (all_rows,) + (sent,) * 4, [SMEM] * 2 + [VMEM] * 7 + [HBM], [VMEM] * 5, 12, moved=heavy,
         scratch=[
             VMEM((leaf_dev + 8, samples, width), jnp.float32),
             VMEM((leaf_dev + 8, samples, width), jnp.bfloat16),
+            VMEM(precision_factor.shape, jnp.bfloat16),
+            pltpu.SemaphoreType.DMA,
         ],
-    )(asked, slots, asked, left, from8, low2, high2, odd1, high1, low1, held_w, held_f)
-    returned = [passed(x, -reach) for reach, x in ((8, out8), (4, out4), (2, out2), (1, out1))]
+    )(asked, slots, asked, left, before, from8, from2, from1, held_w, placed(precision_factor, HBM))
+    returned = [
+        passed(x, [(i, i - reach) for i in everyone if i >= reach])
+        for reach, x in ((8, out8), (4, out4), (2, out2), (1, out1))
+    ]
     (part,) = call(
-        home_kernel, "home", (all_rows,), [SMEM, VMEM, VMEM], [VMEM], 16,
-        moved=heavy, scratch=[VMEM((leaf_dev + 8, samples, width), jnp.float32)],
+        home_kernel, "home", (all_rows,), [SMEM, VMEM, VMEM], [VMEM], 6, moved=heavy,
+        scratch=[VMEM((leaf_dev + 8, samples, width), jnp.float32)],
     )(home, back, held_w)
     (gradient,) = call(
         functools.partial(add_kernel, capacity), "add", (all_rows,), [VMEM] * 5, [VMEM], 6,

time: 53 us -> 47.9 us (0.904)
  waiting for transfers between devices: 10.5 us -> 5.42 us
  Pallas kernels: 16.4 us -> 19.2 us
  starting transfers between devices: 25.6 us -> 22.8 us
    ppermute x11, waiting for transfers between devices: 10.5 us -> 5.42 us  [passed(): return lax.ppermute(x, 'kx', route)]
    ppermute x11, starting transfers between devices: 25.6 us -> 22.8 us  [passed(): return lax.ppermute(x, 'kx', route)]
    pallas_call x1, Pallas kernels: 4.72 us -> 6.48 us  [per_device(): call(functools.partial(remote_kernel, capacity), 'remote', (all_rows,) +...]
    pallas_call x2 -> x3, Pallas kernels: 8.84 us -> 9.9 us  [the longest x1 5.38 us: per_device(): call(local_kernel, 'local', (all_rows, shape(cond_weights.shape, jnp.bflo...]
  transfers between devices with their start and end apart: 11 -> 11, of which waited for: 3 -> 4; matrix products, arithmetic and copies ran while one was open for 0% -> 0% of each run, Pallas kernels for 19% -> 22%
where the time goes in v4:
time: 47.9 us; the launch traced here: 47.6 us
  starting transfers between devices  22.8 us (48%)
  Pallas kernels  19.2 us (40%)
  waiting for transfers between devices  5.42 us (11%)
    ppermute x11, starting transfers between devices, passed(): return lax.ppermute(x, 'kx', route)  22.8 us
    pallas_call x1, Pallas kernels, per_device(): call(functools.partial(remote_kernel, capacity), 'remote', (all_rows,) +...  6.48 us
    ppermute x11, waiting for transfers between devices, passed(): return lax.ppermute(x, 'kx', route)  5.42 us
    pallas_call x1, Pallas kernels, per_device(): call(local_kernel, 'local', (all_rows, shape(cond_weights.shape, jnp.bflo...  5.38 us
    pallas_call x1, Pallas kernels, per_device(): call(home_kernel, 'home', (all_rows,), [SMEM, VMEM, VMEM], [VMEM], 6, mov...  3.87 us
    pallas_call x1, Pallas kernels, per_device(): call(functools.partial(add_kernel, capacity), 'add', (all_rows,), [VMEM]...  1.83 us
    pallas_call x1, Pallas kernels, per_device(): call(index_kernel, 'index', (one_list, shape((2, 4 * SLOTS), jnp.int32),...  1.01 us
  transfers between devices with their start and end apart: 11, of which 4 were waited for; matrix products, arithmetic and copies ran while one was open for 0% of the time, Pallas kernels for 22%

profile of v4, /device:TPU:15, one launch (start us, length us, event | category | flops | bytes accessed | tf_op | source)
XLA Modules:
  0.0 47.6 jit_solution(10693316335382856065)
XLA Ops:
  0.0 3.2 %collective-permute-start = (bf16[80,16,128]{2,1,0:T(8,128)(2,1)}, bf16[80,16,128]{2,1,0:T(8,128)(2,1)S(1)}, u32[]{:S(2)}, u32[]{:S(2)}) collective-permute-start(bf16[80,16,128]{2,1,0:T(8,128)(2,1)} %latent.1), channel_id=1, source_target_pairs={{0,4},{1,5},{2,6},{3,7},{4,8},{5,9},{6,10},{7,11},{8,12},{9,13},{1... | collective-permute-start | bytes 983048 | tf_op jit(solution)/shard_map/ppermute | solution.py:268
  3.2 1.0 %index.1 = (s32[1,128]{1,0:T(1,128)S(1)}, s32[2,128]{1,0:T(2,128)S(1)}, s32[3,80]{1,0:T(4,128)S(1)}) custom-call(s32[3,80]{1,0:T(4,128)} %bitcast.1), custom_call_target="tpu_custom_call" | custom-call | bytes 2097152 | tf_op jit(solution)/shard_map/index/pallas_call | solution.py:271
  4.2 1.0 %collective-permute-start.3 = (s32[1,128]{1,0:T(1,128)S(1)}, s32[1,128]{1,0:T(1,128)S(1)}, u32[]{:S(2)}, u32[]{:S(2)}) collective-permute-start(s32[1,128]{1,0:T(1,128)S(1)} %get-tuple-element.20.asked.asked_row), channel_id=1, source_target_pairs={{0,3},{1,0},{2,1},{3,2},{4,7},{5,4},{6,5},{7,6},{8,11},{9,8},{10,9... | collective-permute-start | bytes 1544 | tf_op jit(solution)/shard_map/ppermute | solution.py:268
  5.2 0.2 collective-permute-start.2
  5.5 2.1 %collective-permute-start.1 = (s32[1,128]{1,0:T(1,128)S(1)}, s32[1,128]{1,0:T(1,128)S(1)}, u32[]{:S(2)}, u32[]{:S(2)}) collective-permute-start(s32[1,128]{1,0:T(1,128)S(1)} %get-tuple-element.20.asked.asked_row), channel_id=1, source_target_pairs={{4,0},{5,1},{6,2},{7,3},{8,4},{9,5},{10,6},{11,7},{12,8},{13,9},{1... | collective-permute-start | bytes 1544 | tf_op jit(solution)/shard_map/ppermute | solution.py:268
  7.6 5.4 %local.1 = (f32[80,16,128]{2,1,0:T(8,128)S(1)}, bf16[80,3,128,128]{3,2,1,0:T(8,128)(2,1)S(1)}, bf16[80,16,128]{2,1,0:T(8,128)(2,1)S(1)}) custom-call(s32[3,80]{1,0:T(4,128)S(1)} %get-tuple-element.19.home, bf16[80,16,128]{2,1,0:T(8,128)(2,1)} %latent.1, bf16[80,3,128,128]{3,2,1,0:T(8,128)(2,1)} %weights.1), custom_call_target="tpu_custom_call" | custom-call | bytes 7864320 | tf_op jit(solution)/shard_map/local/pallas_call | solution.py:279
  12.9 0.0 collective-permute-done.3.ask1
  13.0 0.0 collective-permute-done.2.ask2
  13.0 0.0 collective-permute-done.1.ask8
  13.0 0.0 collective-permute-done.before
  13.0 0.6 %serve.1 = (bf16[30,16,128]{2,1,0:T(8,128)(2,1)S(1)}, bf16[30,16,128]{2,1,0:T(8,128)(2,1)S(1)}, bf16[30,16,128]{2,1,0:T(8,128)(2,1)S(1)}) custom-call(s32[1,128]{1,0:T(1,128)S(1)} %collective-permute-done.1.ask8, s32[1,128]{1,0:T(1,128)S(1)} %collective-permute-done.2.ask2, s32[1,128]{1,0:T(1,128)S(1)} %collective-permute-done.3.ask1, ...), custom_call_target="tpu_custom_call" | custom-call | bytes 4194304 | tf_op jit(solution)/shard_map/serve/pallas_call | solution.py:288
  13.6 3.2 %collective-permute-start.4 = (bf16[30,16,128]{2,1,0:T(8,128)(2,1)S(1)}, bf16[30,16,128]{2,1,0:T(8,128)(2,1)S(1)}, u32[]{:S(2)}, u32[]{:S(2)}) collective-permute-start(bf16[30,16,128]{2,1,0:T(8,128)(2,1)S(1)} %get-tuple-element.24), channel_id=1, source_target_pairs={{4,8},{5,9},{6,10},{7,11},{8,12},{9,13},{10,14},{11,15},{20,24},{2... | collective-permute-start | bytes 368648 | tf_op jit(solution)/shard_map/ppermute | solution.py:268
  16.8 1.3 %collective-permute-start.5 = (bf16[30,16,128]{2,1,0:T(8,128)(2,1)S(1)}, bf16[30,16,128]{2,1,0:T(8,128)(2,1)S(1)}, u32[]{:S(2)}, u32[]{:S(2)}) collective-permute-start(bf16[30,16,128]{2,1,0:T(8,128)(2,1)S(1)} %get-tuple-element.25), channel_id=1, source_target_pairs={{0,2},{1,3},{2,0},{3,1},{4,6},{5,7},{6,4},{7,5},{8,10},{9,11},{10,... | collective-permute-start | bytes 368648 | tf_op jit(solution)/shard_map/ppermute | solution.py:268
  18.1 1.9 %collective-permute-start.6 = (bf16[30,16,128]{2,1,0:T(8,128)(2,1)S(1)}, bf16[30,16,128]{2,1,0:T(8,128)(2,1)S(1)}, u32[]{:S(2)}, u32[]{:S(2)}) collective-permute-start(bf16[30,16,128]{2,1,0:T(8,128)(2,1)S(1)} %get-tuple-element.26), channel_id=1, source_target_pairs={{0,1},{1,2},{2,3},{3,0},{4,5},{5,6},{6,7},{7,4},{8,9},{9,10},{10,1... | collective-permute-start | bytes 368648 | tf_op jit(solution)/shard_map/ppermute | solution.py:268
  20.1 0.0 collective-permute-done.4.from8
  20.1 0.6 %collective-permute-done.5.from2 = bf16[30,16,128]{2,1,0:T(8,128)(2,1)S(1)} collective-permute-done((bf16[30,16,128]{2,1,0:T(8,128)(2,1)S(1)}, bf16[30,16,128]{2,1,0:T(8,128)(2,1)S(1)}, u32[]{:S(2)}, u32[]{:S(2)}) %collective-permute-start.5) | collective-permute-done | bytes 122912 | tf_op jit(solution)/shard_map/ppermute | solution.py:268
  20.6 2.0 %collective-permute-done.6.from1 = bf16[30,16,128]{2,1,0:T(8,128)(2,1)S(1)} collective-permute-done((bf16[30,16,128]{2,1,0:T(8,128)(2,1)S(1)}, bf16[30,16,128]{2,1,0:T(8,128)(2,1)S(1)}, u32[]{:S(2)}, u32[]{:S(2)}) %collective-permute-start.6) | collective-permute-done | bytes 122912 | tf_op jit(solution)/shard_map/ppermute | solution.py:268
  22.6 6.5 %remote.1 = (f32[80,16,128]{2,1,0:T(8,128)S(1)}, bf16[31,16,128]{2,1,0:T(8,128)(2,1)S(1)}, bf16[31,16,128]{2,1,0:T(8,128)(2,1)S(1)}, bf16[31,16,128]{2,1,0:T(8,128)(2,1)S(1)}, bf16[31,16,128]{2,1,0:T(8,128)(2,1)S(1)}) custom-call(s32[1,128]{1,0:T(1,128)S(1)} %get-tuple-element.20.asked.asked_row, s32[2,128]{1,0:T(2,128)S(1)} %get-tuple-element.21.slots, ...), custom_call_target="tpu_custom_call" | custom-call | bytes 7864320 | tf_op jit(solution)/shard_map/remote/pallas_call | solution.py:295
  29.1 1.3 %collective-permute-start.7 = (bf16[31,16,128]{2,1,0:T(8,128)(2,1)S(1)}, bf16[31,16,128]{2,1,0:T(8,128)(2,1)S(1)}, u32[]{:S(2)}, u32[]{:S(2)}) collective-permute-start(bf16[31,16,128]{2,1,0:T(8,128)(2,1)S(1)} %get-tuple-element.29), channel_id=1, source_target_pairs={{8,0},{9,1},{10,2},{11,3},{12,4},{13,5},{14,6},{15,7},{24,16},{25,... | collective-permute-start | bytes 380936 | tf_op jit(solution)/shard_map/ppermute | solution.py:268
  30.4 1.9 %collective-permute-start.8 = (bf16[31,16,128]{2,1,0:T(8,128)(2,1)S(1)}, bf16[31,16,128]{2,1,0:T(8,128)(2,1)S(1)}, u32[]{:S(2)}, u32[]{:S(2)}) collective-permute-start(bf16[31,16,128]{2,1,0:T(8,128)(2,1)S(1)} %get-tuple-element.30), channel_id=1, source_target_pairs={{4,0},{5,1},{6,2},{7,3},{8,4},{9,5},{10,6},{11,7},{12,8},{13,9},{1... | collective-permute-start | bytes 380936 | tf_op jit(solution)/shard_map/ppermute | solution.py:268
  32.3 2.8 %collective-permute-start.9 = (bf16[31,16,128]{2,1,0:T(8,128)(2,1)S(1)}, bf16[31,16,128]{2,1,0:T(8,128)(2,1)S(1)}, u32[]{:S(2)}, u32[]{:S(2)}) collective-permute-start(bf16[31,16,128]{2,1,0:T(8,128)(2,1)S(1)} %get-tuple-element.31), channel_id=1, source_target_pairs={{2,0},{3,1},{4,2},{5,3},{6,4},{7,5},{8,6},{9,7},{10,8},{11,9},{12,... | collective-permute-start | bytes 380936 | tf_op jit(solution)/shard_map/ppermute | solution.py:268
  35.1 3.9 %collective-permute-start.10 = (bf16[31,16,128]{2,1,0:T(8,128)(2,1)S(1)}, bf16[31,16,128]{2,1,0:T(8,128)(2,1)S(1)}, u32[]{:S(2)}, u32[]{:S(2)}) collective-permute-start(bf16[31,16,128]{2,1,0:T(8,128)(2,1)S(1)} %get-tuple-element.32), channel_id=1, source_target_pairs={{1,0},{2,1},{3,2},{4,3},{5,4},{6,5},{7,6},{8,7},{9,8},{10,9},{11,1... | collective-permute-start | bytes 380936 | tf_op jit(solution)/shard_map/ppermute | solution.py:268
  39.0 3.9 %home.1.part = f32[80,16,128]{2,1,0:T(8,128)S(1)} custom-call(s32[3,80]{1,0:T(4,128)S(1)} %get-tuple-element.19.home, f32[80,16,128]{2,1,0:T(8,128)S(1)} %get-tuple-element.28.back, bf16[80,3,128,128]{3,2,1,0:T(8,128)(2,1)S(1)} %get-tuple-element.27.weights), custom_call_target="tpu_custom_call" | custom-call | bytes 7864320 | tf_op jit(solution)/shard_map/home/pallas_call | solution.py:309
  42.9 0.0 collective-permute-done.7.back8
  42.9 0.0 collective-permute-done.8.back4
  42.9 0.4 collective-permute-done.9.back2
  43.3 2.4 %collective-permute-done.10.back1 = bf16[31,16,128]{2,1,0:T(8,128)(2,1)S(1)} collective-permute-done((bf16[31,16,128]{2,1,0:T(8,128)(2,1)S(1)}, bf16[31,16,128]{2,1,0:T(8,128)(2,1)S(1)}, u32[]{:S(2)}, u32[]{:S(2)}) %collective-permute-start.10) | collective-permute-done | bytes 127008 | tf_op jit(solution)/shard_map/ppermute | solution.py:268
  45.8 1.8 %add.1 = f32[80,16,128]{2,1,0:T(8,128)} custom-call(f32[80,16,128]{2,1,0:T(8,128)S(1)} %home.1.part, bf16[31,16,128]{2,1,0:T(8,128)(2,1)S(1)} %collective-permute-done.7.back8, bf16[31,16,128]{2,1,0:T(8,128)(2,1)S(1)} %collective-permute-done.8.back4, bf16[31,16,128]{2,1,0:T(8,128)(2,1)S(1)} %collective-permute-done.9.back2, ...), custom_call_target="tpu_custom_call" | custom-call | bytes 4194304 | tf_op jit(solution)/shard_map/add/pallas_call | solution.py:313
Async XLA Ops:
  0.0 13.0 %collective-permute-start = (bf16[80,16,128]{2,1,0:T(8,128)(2,1)}, bf16[80,16,128]{2,1,0:T(8,128)(2,1)S(1)}, u32[]{:S(2)}, u32[]{:S(2)}) collective-permute-start(bf16[80,16,128]{2,1,0:T(8,128)(2,1)} %latent.1), channel_id=1, source_target_pairs={{0,4},{1,5},{2,6},{3,7},{4,8},{5,9},{6,10},{7,11},{8,12},{9,13},{1... | collective-permute-start | bytes 983048 | tf_op jit(solution)/shard_map/ppermute | solution.py:268
  4.2 8.7 %collective-permute-start.3 = (s32[1,128]{1,0:T(1,128)S(1)}, s32[1,128]{1,0:T(1,128)S(1)}, u32[]{:S(2)}, u32[]{:S(2)}) collective-permute-start(s32[1,128]{1,0:T(1,128)S(1)} %get-tuple-element.20.asked.asked_row), channel_id=1, source_target_pairs={{0,3},{1,0},{2,1},{3,2},{4,7},{5,4},{6,5},{7,6},{8,11},{9,8},{10,9... | collective-permute-start | bytes 1544 | tf_op jit(solution)/shard_map/ppermute | solution.py:268
  5.2 7.7 %collective-permute-start.2 = (s32[1,128]{1,0:T(1,128)S(1)}, s32[1,128]{1,0:T(1,128)S(1)}, u32[]{:S(2)}, u32[]{:S(2)}) collective-permute-start(s32[1,128]{1,0:T(1,128)S(1)} %get-tuple-element.20.asked.asked_row), channel_id=1, source_target_pairs={{0,2},{1,3},{2,0},{3,1},{4,6},{5,7},{6,4},{7,5},{8,10},{9,11},{10,... | collective-permute-start | bytes 1544 | tf_op jit(solution)/shard_map/ppermute | solution.py:268
  5.5 7.5 %collective-permute-start.1 = (s32[1,128]{1,0:T(1,128)S(1)}, s32[1,128]{1,0:T(1,128)S(1)}, u32[]{:S(2)}, u32[]{:S(2)}) collective-permute-start(s32[1,128]{1,0:T(1,128)S(1)} %get-tuple-element.20.asked.asked_row), channel_id=1, source_target_pairs={{4,0},{5,1},{6,2},{7,3},{8,4},{9,5},{10,6},{11,7},{12,8},{13,9},{1... | collective-permute-start | bytes 1544 | tf_op jit(solution)/shard_map/ppermute | solution.py:268
  13.6 6.4 %collective-permute-start.4 = (bf16[30,16,128]{2,1,0:T(8,128)(2,1)S(1)}, bf16[30,16,128]{2,1,0:T(8,128)(2,1)S(1)}, u32[]{:S(2)}, u32[]{:S(2)}) collective-permute-start(bf16[30,16,128]{2,1,0:T(8,128)(2,1)S(1)} %get-tuple-element.24), channel_id=1, source_target_pairs={{4,8},{5,9},{6,10},{7,11},{8,12},{9,13},{10,14},{11,15},{20,24},{2... | collective-permute-start | bytes 368648 | tf_op jit(solution)/shard_map/ppermute | solution.py:268
  16.8 3.8 %collective-permute-start.5 = (bf16[30,16,128]{2,1,0:T(8,128)(2,1)S(1)}, bf16[30,16,128]{2,1,0:T(8,128)(2,1)S(1)}, u32[]{:S(2)}, u32[]{:S(2)}) collective-permute-start(bf16[30,16,128]{2,1,0:T(8,128)(2,1)S(1)} %get-tuple-element.25), channel_id=1, source_target_pairs={{0,2},{1,3},{2,0},{3,1},{4,6},{5,7},{6,4},{7,5},{8,10},{9,11},{10,... | collective-permute-start | bytes 368648 | tf_op jit(solution)/shard_map/ppermute | solution.py:268
  18.1 4.5 %collective-permute-start.6 = (bf16[30,16,128]{2,1,0:T(8,128)(2,1)S(1)}, bf16[30,16,128]{2,1,0:T(8,128)(2,1)S(1)}, u32[]{:S(2)}, u32[]{:S(2)}) collective-permute-start(bf16[30,16,128]{2,1,0:T(8,128)(2,1)S(1)} %get-tuple-element.26), channel_id=1, source_target_pairs={{0,1},{1,2},{2,3},{3,0},{4,5},{5,6},{6,7},{7,4},{8,9},{9,10},{10,1... | collective-permute-start | bytes 368648 | tf_op jit(solution)/shard_map/ppermute | solution.py:268
  29.1 13.8 %collective-permute-start.7 = (bf16[31,16,128]{2,1,0:T(8,128)(2,1)S(1)}, bf16[31,16,128]{2,1,0:T(8,128)(2,1)S(1)}, u32[]{:S(2)}, u32[]{:S(2)}) collective-permute-start(bf16[31,16,128]{2,1,0:T(8,128)(2,1)S(1)} %get-tuple-element.29), channel_id=1, source_target_pairs={{8,0},{9,1},{10,2},{11,3},{12,4},{13,5},{14,6},{15,7},{24,16},{25,... | collective-permute-start | bytes 380936 | tf_op jit(solution)/shard_map/ppermute | solution.py:268
  30.4 12.5 %collective-permute-start.8 = (bf16[31,16,128]{2,1,0:T(8,128)(2,1)S(1)}, bf16[31,16,128]{2,1,0:T(8,128)(2,1)S(1)}, u32[]{:S(2)}, u32[]{:S(2)}) collective-permute-start(bf16[31,16,128]{2,1,0:T(8,128)(2,1)S(1)} %get-tuple-element.30), channel_id=1, source_target_pairs={{4,0},{5,1},{6,2},{7,3},{8,4},{9,5},{10,6},{11,7},{12,8},{13,9},{1... | collective-permute-start | bytes 380936 | tf_op jit(solution)/shard_map/ppermute | solution.py:268
  32.3 11.0 %collective-permute-start.9 = (bf16[31,16,128]{2,1,0:T(8,128)(2,1)S(1)}, bf16[31,16,128]{2,1,0:T(8,128)(2,1)S(1)}, u32[]{:S(2)}, u32[]{:S(2)}) collective-permute-start(bf16[31,16,128]{2,1,0:T(8,128)(2,1)S(1)} %get-tuple-element.31), channel_id=1, source_target_pairs={{2,0},{3,1},{4,2},{5,3},{6,4},{7,5},{8,6},{9,7},{10,8},{11,9},{12,... | collective-permute-start | bytes 380936 | tf_op jit(solution)/shard_map/ppermute | solution.py:268
  35.1 10.7 %collective-permute-start.10 = (bf16[31,16,128]{2,1,0:T(8,128)(2,1)S(1)}, bf16[31,16,128]{2,1,0:T(8,128)(2,1)S(1)}, u32[]{:S(2)}, u32[]{:S(2)}) collective-permute-start(bf16[31,16,128]{2,1,0:T(8,128)(2,1)S(1)} %get-tuple-element.32), channel_id=1, source_target_pairs={{1,0},{2,1},{3,2},{4,3},{5,4},{6,5},{7,6},{8,7},{9,8},{10,9},{11,1... | collective-permute-start | bytes 380936 | tf_op jit(solution)/shard_map/ppermute | solution.py:268

commit v5 on v4

--- a/solution.py
+++ b/solution.py
@@ -8,6 +8,7 @@
 from jax.sharding import PartitionSpec as P
 
 SLOTS = 32
+CHUNK = 8
 LEAVES = 16
 MIB = 2**20
 BY_ROWS = (((1,), (1,)), ((), ()))
@@ -88,37 +89,48 @@
     return both[:samples, :wide], both[samples:, wide:]
 
 
-def local_kernel(home, latent, weights, left, held_w, held_l, rows, row_sem, w_sem):
+def local_means(leaves, home, rows, weights, left, first):
+    fan, width = weights.shape[1], weights.shape[2]
+    for i in leaves:
+        means = paired(
+            beside([rows[home[k, i]] for k in range(fan)]),
+            beside([rows[home[k, i + 1]] for k in range(fan)]),
+            weights[i].reshape(fan * width, width),
+            weights[i + 1].reshape(fan * width, width),
+        )
+        for j, mean in zip((i, i + 1), means):
+            left[j - first] = rows[j].astype(jnp.float32) - mean
+
+
+def early_kernel(home, latent, weights, left, held_w, rows, row_sem, w_sem):
     leaf_dev = latent.shape[0]
-    fan, width = weights.shape[1], weights.shape[2]
+    chunks, ahead = leaf_dev // CHUNK, 3
 
     def fetch(c):
-        part = pl.ds(c * LEAVES, LEAVES)
+        part = pl.ds(c * CHUNK, CHUNK)
         return pltpu.make_async_copy(weights.at[part], held_w.at[part], w_sem.at[c])
 
-    fetch_rows = pltpu.make_async_copy(latent, held_l, row_sem)
+    fetch_rows = pltpu.make_async_copy(latent, rows.at[pl.ds(0, leaf_dev)], row_sem)
     fetch_rows.start()
-    for c in range(leaf_dev // LEAVES):
+    for c in range(ahead):
         fetch(c).start()
+    rows[leaf_dev] = jnp.zeros(latent.shape[1:], latent.dtype)
     fetch_rows.wait()
-    rows[pl.ds(0, leaf_dev)] = held_l[...]
-    rows[leaf_dev] = jnp.zeros(latent.shape[1:], latent.dtype)
-
-    def some(c, carry):
+    for c in range(chunks):
         fetch(c).wait()
-        for u in range(0, LEAVES, 2):
-            i = c * LEAVES + u
-            means = paired(
-                beside([rows[home[k, i]] for k in range(fan)]),
-                beside([rows[home[k, i + 1]] for k in range(fan)]),
-                held_w[i].reshape(fan * width, width),
-                held_w[i + 1].reshape(fan * width, width),
-            )
-            for j, mean in zip((i, i + 1), means):
-                left[j] = rows[j].astype(jnp.float32) - mean
-        return carry
-
-    lax.fori_loop(0, leaf_dev // LEAVES, some, 0)
+        if c + ahead < chunks:
+            fetch(c + ahead).start()
+        if (c + 1) * CHUNK <= left.shape[0]:
+            local_means(range(c * CHUNK, (c + 1) * CHUNK, 2), home, rows, held_w, left, 0)
+
+
+def late_kernel(home, rows, before, weights, factor, left, held_f, f_sem):
+    leaf_dev = weights.shape[0]
+    fetch = pltpu.make_async_copy(factor, held_f, f_sem)
+    fetch.start()
+    first = leaf_dev - left.shape[0]
+    local_means(range(first, leaf_dev, 2), home, rows, weights, left, first)
+    fetch.wait()
 
 
 def serve_kernel(capacity, ask8, ask2, ask1, latent, before, left, out8, out2, out1):
@@ -140,44 +152,52 @@
             pick(o, ask, latent, out)
 
 
+def asker(slots, weights, o, r):
+    i = slots[0, o * SLOTS + r]
+    return i, weights[jnp.minimum(i, weights.shape[0] - 1), slots[1, o * SLOTS + r]]
+
+
+def remote_terms(capacity, slots, asked_row, low, weights, outs):
+    listed = jnp.broadcast_to(asked_row[...].astype(jnp.float32), low.shape[1:])
+    for o, out in outs:
+        for r in range(0, capacity, 2):
+            (i, w), (j, v) = asker(slots, weights, o, r), asker(slots, weights, o, r + 1)
+            for at, x in zip((r, r + 1), paired(low[i], low[j], w, v, True)):
+                out[at] = x.astype(out.dtype)
+        out[capacity] = listed.astype(out.dtype)
+
+
 def remote_kernel(
-    capacity, asked, slots, asked_row, left, before, from8, from2, from1,
-    weights, factor, back, out8, out4, out2, out1, resid, low, held_f, f_sem,
+    capacity, asked, slots, asked_row, left, later, before, from8, from2, from1,
+    weights, factor, back, low, out8, out4, out2, out1, resid,
 ):
-    leaf_dev = left.shape[0]
-    fetch = pltpu.make_async_copy(factor, held_f, f_sem)
-    fetch.start()
-    resid[pl.ds(0, leaf_dev)] = left[...]
+    leaf_dev, half = back.shape[0], left.shape[0]
+    resid[pl.ds(0, half)] = left[...]
+    resid[pl.ds(half, leaf_dev - half)] = later[...]
     resid[leaf_dev] = jnp.zeros(left.shape[1:], left.dtype)
     low[leaf_dev] = jnp.zeros(left.shape[1:], low.dtype)
-
-    def asker(o, r):
-        i = slots[0, o * SLOTS + r]
-        return i, weights[jnp.minimum(i, leaf_dev - 1), slots[1, o * SLOTS + r]]
 
     for o, rows in ((2, before), (3, from8), (1, from2), (0, from1)):
         found = []
         for r in range(0, capacity, 2):
-            (i, w), (j, v) = asker(o, r), asker(o, r + 1)
+            (i, w), (j, v) = asker(slots, weights, o, r), asker(slots, weights, o, r + 1)
             at = (asked[0, o * SLOTS + r], asked[0, o * SLOTS + r + 1]) if o == 2 else (r, r + 1)
             found += zip((i, j), paired(rows[at[0]], rows[at[1]], w, v))
         for i, mean in found:
             resid[i] = resid[i] - mean
-
-    fetch.wait()
 
     def leaves(c, carry):
         pairs = [c * LEAVES + u for u in range(0, LEAVES, 2)]
         innov = [
             paired(
                 resid[i].astype(jnp.bfloat16), resid[i + 1].astype(jnp.bfloat16),
-                held_f[i], held_f[i + 1],
+                factor[i], factor[i + 1],
             )
             for i in pairs
         ]
         for i, (x, y) in zip(pairs, innov):
             both = paired(
-                x.astype(jnp.bfloat16), y.astype(jnp.bfloat16), held_f[i], held_f[i + 1], True
+                x.astype(jnp.bfloat16), y.astype(jnp.bfloat16), factor[i], factor[i + 1], True
             )
             for j, z in zip((i, i + 1), both):
                 back[j] = z
@@ -185,16 +205,12 @@
         return carry
 
     lax.fori_loop(0, leaf_dev // LEAVES, leaves, 0)
-    listed = jnp.broadcast_to(asked_row[...].astype(jnp.float32), left.shape[1:])
-    for o, out in ((3, out8), (2, out4), (1, out2), (0, out1)):
-        for r in range(0, capacity, 2):
-            (i, w), (j, v) = asker(o, r), asker(o, r + 1)
-            for at, x in zip((r, r + 1), paired(low[i], low[j], w, v, True)):
-                out[at] = x.astype(out.dtype)
-        out[capacity] = listed.astype(out.dtype)
-
-
-def home_kernel(home, back, weights, part, acc):
+    remote_terms(
+        capacity, slots, asked_row, low, weights, ((3, out8), (2, out4), (1, out2), (0, out1))
+    )
+
+
+def home_kernel(home, back, low, weights, part, acc):
     leaf_dev = back.shape[0]
     fan, width = weights.shape[1], weights.shape[2]
     acc[pl.ds(0, leaf_dev)] = -back[...]
@@ -205,7 +221,7 @@
         for u in range(0, LEAVES, 2):
             i = c * LEAVES + u
             found += zip((i, i + 1), paired(
-                back[i].astype(jnp.bfloat16), back[i + 1].astype(jnp.bfloat16),
+                low[i], low[i + 1],
                 weights[i].reshape(fan * width, width),
                 weights[i + 1].reshape(fan * width, width), True,
             ))
@@ -219,17 +235,17 @@
     part[...] = acc[pl.ds(0, leaf_dev)]
 
 
-def add_kernel(capacity, part, back8, back4, back2, back1, out, listed, wanted, sem):
-    returned = ((3, back8), (2, back4), (1, back2), (0, back1))
-    for o, rows in returned:
-        listed[o : o + 1] = rows[capacity].astype(jnp.float32)[0:1].astype(jnp.int32)
+def add_kernel(capacity, offsets, part, *refs):
+    returned, (out, listed, wanted, sem) = refs[: len(offsets)], refs[len(offsets) :]
+    for n, (o, rows) in enumerate(zip(offsets, returned)):
+        listed[n : n + 1] = rows[capacity].astype(jnp.float32)[0:1].astype(jnp.int32)
     fetch = pltpu.make_async_copy(listed, wanted, sem)
     fetch.start()
     out[...] = part[...]
     fetch.wait()
-    for o, rows in returned:
+    for n, (o, rows) in enumerate(zip(offsets, returned)):
         for r in range(capacity):
-            j = wanted[o, o * SLOTS + r]
+            j = wanted[n, o * SLOTS + r]
             out[j] = out[j] + rows[r].astype(jnp.float32)
 
 
@@ -276,47 +292,51 @@
     ask8 = passed(asked, [(i, i - 4) for i in everyone if i >= 4])
     ask2 = passed(asked, [(i, i ^ 2) for i in everyone])
     ask1 = passed(asked, [(i, i // 4 * 4 + (i + 3) % 4) for i in everyone])
-    left, held_w, held_l = call(
-        local_kernel, "local",
-        (all_rows, shape(cond_weights.shape, jnp.bfloat16), shape(latent.shape, jnp.bfloat16)),
-        [SMEM, HBM, HBM], [VMEM] * 3, 14, moved=heavy,
-        scratch=[
-            VMEM((leaf_dev + 8, samples, width), jnp.bfloat16),
-            pltpu.SemaphoreType.DMA, pltpu.SemaphoreType.DMA((leaf_dev // LEAVES,)),
-        ],
+    half = leaf_dev // 2
+    left, held_w, rows = call(
+        early_kernel, "early",
+        (
+            shape((half, samples, width), jnp.float32), shape(cond_weights.shape, jnp.bfloat16),
+            shape((leaf_dev + 8, samples, width), jnp.bfloat16),
+        ),
+        [SMEM, HBM, HBM], [VMEM] * 3, 14, moved=heavy // 2,
+        scratch=[pltpu.SemaphoreType.DMA, pltpu.SemaphoreType.DMA((leaf_dev // CHUNK,))],
     )(home, placed(latent, HBM), placed(cond_weights, HBM))
     serve8, serve2, serve1 = call(
         functools.partial(serve_kernel, capacity), "serve", (some_rows,) * 3,
         [SMEM] * 3 + [VMEM] * 2 + [ANY], [VMEM] * 3, 4, moved=4 * MIB,
-    )(ask8, ask2, ask1, held_l, before, left)
+    )(ask8, ask2, ask1, rows, before, left)
     from8 = passed(serve8, [(i, i + 4) for i in everyone if i >= 4 and i + 4 < devices])
     from2 = passed(serve2, [(i, i ^ 2) for i in everyone])
     from1 = passed(serve1, [(i, i // 4 * 4 + (i + 1) % 4) for i in everyone])
-    back, out8, out4, out2, out1 = call(
+    later, held_f = call(
+        late_kernel, "late",
+        (
+            shape((leaf_dev - half, samples, width), jnp.float32),
+            shape(precision_factor.shape, jnp.bfloat16),
+        ),
+        [SMEM, VMEM, ANY, VMEM, HBM], [VMEM] * 2, 8, moved=heavy // 2,
+        scratch=[pltpu.SemaphoreType.DMA],
+    )(home, rows, before, held_w, placed(precision_factor, HBM))
+    back, low, out8, out4, out2, out1 = call(
         functools.partial(remote_kernel, capacity), "remote",
-        (all_rows,) + (sent,) * 4, [SMEM] * 2 + [VMEM] * 7 + [HBM], [VMEM] * 5, 12, moved=heavy,
-        scratch=[
-            VMEM((leaf_dev + 8, samples, width), jnp.float32),
-            VMEM((leaf_dev + 8, samples, width), jnp.bfloat16),
-            VMEM(precision_factor.shape, jnp.bfloat16),
-            pltpu.SemaphoreType.DMA,
-        ],
-    )(asked, slots, asked, left, before, from8, from2, from1, held_w, placed(precision_factor, HBM))
+        (all_rows, shape((leaf_dev + 8, samples, width), jnp.bfloat16)) + (sent,) * 4,
+        [SMEM] * 2 + [VMEM] * 9, [VMEM] * 6, 8, moved=heavy,
+        scratch=[VMEM((leaf_dev + 8, samples, width), jnp.float32)],
+    )(asked, slots, asked, left, later, before, from8, from2, from1, held_w, held_f)
     returned = [
         passed(x, [(i, i - reach) for i in everyone if i >= reach])
         for reach, x in ((8, out8), (4, out4), (2, out2), (1, out1))
     ]
     (part,) = call(
-        home_kernel, "home", (all_rows,), [SMEM, VMEM, VMEM], [VMEM], 6, moved=heavy,
+        home_kernel, "home", (all_rows,), [SMEM] + [VMEM] * 3, [VMEM], 6, moved=heavy,
         scratch=[VMEM((leaf_dev + 8, samples, width), jnp.float32)],
-    )(home, back, held_w)
+    )(home, back, low, held_w)
+    lists = (4, 4 * SLOTS)
     (gradient,) = call(
-        functools.partial(add_kernel, capacity), "add", (all_rows,), [VMEM] * 5, [VMEM], 6,
-        moved=4 * MIB,
-        scratch=[
-            VMEM((4, 4 * SLOTS), jnp.int32), SMEM((4, 4 * SLOTS), jnp.int32),
-            pltpu.SemaphoreType.DMA,
-        ],
+        functools.partial(add_kernel, capacity, (3, 2, 1, 0)), "add", (all_rows,), [VMEM] * 5,
+        [VMEM], 6, moved=4 * MIB,
+        scratch=[VMEM(lists, jnp.int32), SMEM(lists, jnp.int32), pltpu.SemaphoreType.DMA],
     )(part, *returned)
     return gradient
 

time: 47.9 us -> 46.7 us (0.975)
  waiting for transfers between devices: 5.42 us -> 2.95 us
  Pallas kernels: 19.2 us -> 20.7 us
    ppermute x11, waiting for transfers between devices: 5.42 us -> 2.95 us  [passed(): return lax.ppermute(x, 'kx', route)]
    pallas_call x4 -> x5, Pallas kernels: 17.6 us -> 19.1 us  [the longest x1 5.62 us: per_device(): call(early_kernel, 'early', (shape((half, samples, width), jnp.float32),...]
  transfers between devices with their start and end apart: 11 -> 11, of which waited for: 4 -> 2; matrix products, arithmetic and copies ran while one was open for 0% -> 0% of each run, Pallas kernels for 22% -> 29%
where the time goes in v5:
time: 46.7 us; the launch traced here: 46.3 us
  starting transfers between devices  22.5 us (48%)
  Pallas kernels  20.7 us (44%)
  waiting for transfers between devices  2.95 us (6%)
    ppermute x11, starting transfers between devices, passed(): return lax.ppermute(x, 'kx', route)  22.5 us
    pallas_call x1, Pallas kernels, per_device(): call(early_kernel, 'early', (shape((half, samples, width), jnp.float32),...  5.62 us
    pallas_call x1, Pallas kernels, per_device(): call(functools.partial(remote_kernel, capacity), 'remote', (all_rows, sha...  4.85 us
    pallas_call x1, Pallas kernels, per_device(): call(home_kernel, 'home', (all_rows,), [SMEM] + [VMEM] * 3, [VMEM], 6, mo...  3.88 us
    ppermute x11, waiting for transfers between devices, passed(): return lax.ppermute(x, 'kx', route)  2.95 us
    pallas_call x1, Pallas kernels, per_device(): call(late_kernel, 'late', (shape((leaf_dev - half, samples, width), jnp.f...  2.88 us
    pallas_call x1, Pallas kernels, per_device(): call(functools.partial(add_kernel, capacity, (3, 2, 1, 0)), 'add', (all_r...  1.83 us
    pallas_call x1, Pallas kernels, per_device(): call(index_kernel, 'index', (one_list, shape((2, 4 * SLOTS), jnp.int32),...  1.01 us
  transfers between devices with their start and end apart: 11, of which 2 were waited for; matrix products, arithmetic and copies ran while one was open for 0% of the time, Pallas kernels for 29%

profile of v5, /device:TPU:15, one launch (start us, length us, event | category | flops | bytes accessed | tf_op | source)
XLA Modules:
  0.0 46.3 jit_solution(10648196262217980423)
XLA Ops:
  0.0 3.2 %collective-permute-start = (bf16[80,16,128]{2,1,0:T(8,128)(2,1)}, bf16[80,16,128]{2,1,0:T(8,128)(2,1)S(1)}, u32[]{:S(2)}, u32[]{:S(2)}) collective-permute-start(bf16[80,16,128]{2,1,0:T(8,128)(2,1)} %latent.1), channel_id=1, source_target_pairs={{0,4},{1,5},{2,6},{3,7},{4,8},{5,9},{6,10},{7,11},{8,12},{9,13},{1... | collective-permute-start | bytes 983048 | tf_op jit(solution)/shard_map/ppermute | solution.py:284
  3.2 1.0 %index.1 = (s32[1,128]{1,0:T(1,128)S(1)}, s32[2,128]{1,0:T(2,128)S(1)}, s32[3,80]{1,0:T(4,128)S(1)}) custom-call(s32[3,80]{1,0:T(4,128)} %bitcast.1), custom_call_target="tpu_custom_call" | custom-call | bytes 2097152 | tf_op jit(solution)/shard_map/index/pallas_call | solution.py:287
  4.2 1.0 %collective-permute-start.3 = (s32[1,128]{1,0:T(1,128)S(1)}, s32[1,128]{1,0:T(1,128)S(1)}, u32[]{:S(2)}, u32[]{:S(2)}) collective-permute-start(s32[1,128]{1,0:T(1,128)S(1)} %get-tuple-element.23.asked.asked_row), channel_id=1, source_target_pairs={{0,3},{1,0},{2,1},{3,2},{4,7},{5,4},{6,5},{7,6},{8,11},{9,8},{10,9... | collective-permute-start | bytes 1544 | tf_op jit(solution)/shard_map/ppermute | solution.py:284
  5.2 0.2 collective-permute-start.2
  5.5 2.1 %collective-permute-start.1 = (s32[1,128]{1,0:T(1,128)S(1)}, s32[1,128]{1,0:T(1,128)S(1)}, u32[]{:S(2)}, u32[]{:S(2)}) collective-permute-start(s32[1,128]{1,0:T(1,128)S(1)} %get-tuple-element.23.asked.asked_row), channel_id=1, source_target_pairs={{4,0},{5,1},{6,2},{7,3},{8,4},{9,5},{10,6},{11,7},{12,8},{13,9},{1... | collective-permute-start | bytes 1544 | tf_op jit(solution)/shard_map/ppermute | solution.py:284
  7.6 5.6 %early.1 = (f32[40,16,128]{2,1,0:T(8,128)S(1)}, bf16[80,3,128,128]{3,2,1,0:T(8,128)(2,1)S(1)}, bf16[88,16,128]{2,1,0:T(8,128)(2,1)S(1)}) custom-call(s32[3,80]{1,0:T(4,128)S(1)} %get-tuple-element.22.home, bf16[80,16,128]{2,1,0:T(8,128)(2,1)} %latent.1, bf16[80,3,128,128]{3,2,1,0:T(8,128)(2,1)} %weights.1), custom_call_target="tpu_custom_call" | custom-call | bytes 3932160 | tf_op jit(solution)/shard_map/early/pallas_call | solution.py:296
  13.2 0.0 collective-permute-done.3.ask1
  13.2 0.0 collective-permute-done.2.ask2
  13.2 0.0 collective-permute-done.1.ask8
  13.2 0.0 collective-permute-done.before
  13.2 0.6 %serve.1 = (bf16[30,16,128]{2,1,0:T(8,128)(2,1)S(1)}, bf16[30,16,128]{2,1,0:T(8,128)(2,1)S(1)}, bf16[30,16,128]{2,1,0:T(8,128)(2,1)S(1)}) custom-call(s32[1,128]{1,0:T(1,128)S(1)} %collective-permute-done.1.ask8, s32[1,128]{1,0:T(1,128)S(1)} %collective-permute-done.2.ask2, s32[1,128]{1,0:T(1,128)S(1)} %collective-permute-done.3.ask1, ...), custom_call_target="tpu_custom_call" | custom-call | bytes 4194304 | tf_op jit(solution)/shard_map/serve/pallas_call | solution.py:305
  13.9 3.2 %collective-permute-start.4 = (bf16[30,16,128]{2,1,0:T(8,128)(2,1)S(1)}, bf16[30,16,128]{2,1,0:T(8,128)(2,1)S(1)}, u32[]{:S(2)}, u32[]{:S(2)}) collective-permute-start(bf16[30,16,128]{2,1,0:T(8,128)(2,1)S(1)} %get-tuple-element.29), channel_id=1, source_target_pairs={{4,8},{5,9},{6,10},{7,11},{8,12},{9,13},{10,14},{11,15},{20,24},{2... | collective-permute-start | bytes 368648 | tf_op jit(solution)/shard_map/ppermute | solution.py:284
  17.1 1.3 %collective-permute-start.5 = (bf16[30,16,128]{2,1,0:T(8,128)(2,1)S(1)}, bf16[30,16,128]{2,1,0:T(8,128)(2,1)S(1)}, u32[]{:S(2)}, u32[]{:S(2)}) collective-permute-start(bf16[30,16,128]{2,1,0:T(8,128)(2,1)S(1)} %get-tuple-element.30), channel_id=1, source_target_pairs={{0,2},{1,3},{2,0},{3,1},{4,6},{5,7},{6,4},{7,5},{8,10},{9,11},{10,... | collective-permute-start | bytes 368648 | tf_op jit(solution)/shard_map/ppermute | solution.py:284
  18.4 1.9 %collective-permute-start.6 = (bf16[30,16,128]{2,1,0:T(8,128)(2,1)S(1)}, bf16[30,16,128]{2,1,0:T(8,128)(2,1)S(1)}, u32[]{:S(2)}, u32[]{:S(2)}) collective-permute-start(bf16[30,16,128]{2,1,0:T(8,128)(2,1)S(1)} %get-tuple-element.31), channel_id=1, source_target_pairs={{0,1},{1,2},{2,3},{3,0},{4,5},{5,6},{6,7},{7,4},{8,9},{9,10},{10,1... | collective-permute-start | bytes 368648 | tf_op jit(solution)/shard_map/ppermute | solution.py:284
  20.3 2.9 %late.1 = (f32[40,16,128]{2,1,0:T(8,128)S(1)}, bf16[80,128,128]{2,1,0:T(8,128)(2,1)S(1)}) custom-call(s32[3,80]{1,0:T(4,128)S(1)} %get-tuple-element.22.home, bf16[88,16,128]{2,1,0:T(8,128)(2,1)S(1)} %get-tuple-element.26.rows.latent, bf16[80,16,128]{2,1,0:T(8,128)(2,1)S(1)} %collective-permute-done.before, ...), custom_call_target="tpu_custom_call" | custom-call | bytes 3932160 | tf_op jit(solution)/shard_map/late/pallas_call | solution.py:312
  23.2 0.0 collective-permute-done.4.from8
  23.2 0.0 collective-permute-done.5.from2
  23.2 0.0 collective-permute-done.6.from1
  23.2 4.8 %remote.1 = (f32[80,16,128]{2,1,0:T(8,128)S(1)}, bf16[88,16,128]{2,1,0:T(8,128)(2,1)S(1)}, bf16[31,16,128]{2,1,0:T(8,128)(2,1)S(1)}, bf16[31,16,128]{2,1,0:T(8,1...) custom-call(s32[1,128]{1,0:T(1,128)S(1)} %get-tuple-element.23.asked.asked_row, ...), custom_call_target="tpu_custom_call" | custom-call | bytes 7864320 | tf_op jit(solution)/shard_map/remote/pallas_call | solution.py:321
  28.1 1.3 %collective-permute-start.7 = (bf16[31,16,128]{2,1,0:T(8,128)(2,1)S(1)}, bf16[31,16,128]{2,1,0:T(8,128)(2,1)S(1)}, u32[]{:S(2)}, u32[]{:S(2)}) collective-permute-start(bf16[31,16,128]{2,1,0:T(8,128)(2,1)S(1)} %get-tuple-element.35), channel_id=1, source_target_pairs={{8,0},{9,1},{10,2},{11,3},{12,4},{13,5},{14,6},{15,7},{24,16},{25,... | collective-permute-start | bytes 380936 | tf_op jit(solution)/shard_map/ppermute | solution.py:284
  29.4 1.9 %collective-permute-start.8 = (bf16[31,16,128]{2,1,0:T(8,128)(2,1)S(1)}, bf16[31,16,128]{2,1,0:T(8,128)(2,1)S(1)}, u32[]{:S(2)}, u32[]{:S(2)}) collective-permute-start(bf16[31,16,128]{2,1,0:T(8,128)(2,1)S(1)} %get-tuple-element.36), channel_id=1, source_target_pairs={{4,0},{5,1},{6,2},{7,3},{8,4},{9,5},{10,6},{11,7},{12,8},{13,9},{1... | collective-permute-start | bytes 380936 | tf_op jit(solution)/shard_map/ppermute | solution.py:284
  31.3 2.5 %collective-permute-start.9 = (bf16[31,16,128]{2,1,0:T(8,128)(2,1)S(1)}, bf16[31,16,128]{2,1,0:T(8,128)(2,1)S(1)}, u32[]{:S(2)}, u32[]{:S(2)}) collective-permute-start(bf16[31,16,128]{2,1,0:T(8,128)(2,1)S(1)} %get-tuple-element.37), channel_id=1, source_target_pairs={{2,0},{3,1},{4,2},{5,3},{6,4},{7,5},{8,6},{9,7},{10,8},{11,9},{12,... | collective-permute-start | bytes 380936 | tf_op jit(solution)/shard_map/ppermute | solution.py:284
  33.8 3.8 %collective-permute-start.10 = (bf16[31,16,128]{2,1,0:T(8,128)(2,1)S(1)}, bf16[31,16,128]{2,1,0:T(8,128)(2,1)S(1)}, u32[]{:S(2)}, u32[]{:S(2)}) collective-permute-start(bf16[31,16,128]{2,1,0:T(8,128)(2,1)S(1)} %get-tuple-element.38), channel_id=1, source_target_pairs={{1,0},{2,1},{3,2},{4,3},{5,4},{6,5},{7,6},{8,7},{9,8},{10,9},{11,1... | collective-permute-start | bytes 380936 | tf_op jit(solution)/shard_map/ppermute | solution.py:284
  37.6 3.9 %home.1.part = f32[80,16,128]{2,1,0:T(8,128)S(1)} custom-call(s32[3,80]{1,0:T(4,128)S(1)} %get-tuple-element.22.home, f32[80,16,128]{2,1,0:T(8,128)S(1)} %get-tuple-element.33.back, bf16[88,16,128]{2,1,0:T(8,128)(2,1)S(1)} %get-tuple-element.34.low, bf16[80,3,128,128]{3,2,1,0:T(8,128)(2,1)S(1)} %get-tuple-element.27.weights), custom_call_target="tpu_custom_call" | custom-call | bytes 7864320 | tf_op jit(solution)/shard_map/home/pallas_call | solution.py:331
  41.5 0.0 collective-permute-done.7.refs_0_
  41.6 0.0 collective-permute-done.8.refs_1_
  41.6 0.5 %collective-permute-done.9.refs_2_ = bf16[31,16,128]{2,1,0:T(8,128)(2,1)S(1)} collective-permute-done((bf16[31,16,128]{2,1,0:T(8,128)(2,1)S(1)}, bf16[31,16,128]{2,1,0:T(8,128)(2,1)S(1)}, u32[]{:S(2)}, u32[]{:S(2)}) %collective-permute-start.9) | collective-permute-done | bytes 127008 | tf_op jit(solution)/shard_map/ppermute | solution.py:284
  42.1 2.4 %collective-permute-done.10.refs_3_ = bf16[31,16,128]{2,1,0:T(8,128)(2,1)S(1)} collective-permute-done((bf16[31,16,128]{2,1,0:T(8,128)(2,1)S(1)}, bf16[31,16,128]{2,1,0:T(8,128)(2,1)S(1)}, u32[]{:S(2)}, u32[]{:S(2)}) %collective-permute-start.10) | collective-permute-done | bytes 127008 | tf_op jit(solution)/shard_map/ppermute | solution.py:284
  44.5 1.8 %add.1 = f32[80,16,128]{2,1,0:T(8,128)} custom-call(f32[80,16,128]{2,1,0:T(8,128)S(1)} %home.1.part, bf16[31,16,128]{2,1,0:T(8,128)(2,1)S(1)} %collective-permute-done.7.refs_0_, bf16[31,16,128]{2,1,0:T(8,128)(2,1)S(1)} %collective-permute-done.8.refs_1_, bf16[31,16,128]{2,1,0:T(8,128)(2,1)S(1)} %collective-permute-done.9.refs_2_, ...), custom_call_target="tpu_custom_call" | custom-call | bytes 4194304 | tf_op jit(solution)/shard_map/add/pallas_call | solution.py:336
Async XLA Ops:
  0.0 13.2 %collective-permute-start = (bf16[80,16,128]{2,1,0:T(8,128)(2,1)}, bf16[80,16,128]{2,1,0:T(8,128)(2,1)S(1)}, u32[]{:S(2)}, u32[]{:S(2)}) collective-permute-start(bf16[80,16,128]{2,1,0:T(8,128)(2,1)} %latent.1), channel_id=1, source_target_pairs={{0,4},{1,5},{2,6},{3,7},{4,8},{5,9},{6,10},{7,11},{8,12},{9,13},{1... | collective-permute-start | bytes 983048 | tf_op jit(solution)/shard_map/ppermute | solution.py:284
  4.2 9.0 %collective-permute-start.3 = (s32[1,128]{1,0:T(1,128)S(1)}, s32[1,128]{1,0:T(1,128)S(1)}, u32[]{:S(2)}, u32[]{:S(2)}) collective-permute-start(s32[1,128]{1,0:T(1,128)S(1)} %get-tuple-element.23.asked.asked_row), channel_id=1, source_target_pairs={{0,3},{1,0},{2,1},{3,2},{4,7},{5,4},{6,5},{7,6},{8,11},{9,8},{10,9... | collective-permute-start | bytes 1544 | tf_op jit(solution)/shard_map/ppermute | solution.py:284
  5.2 8.0 %collective-permute-start.2 = (s32[1,128]{1,0:T(1,128)S(1)}, s32[1,128]{1,0:T(1,128)S(1)}, u32[]{:S(2)}, u32[]{:S(2)}) collective-permute-start(s32[1,128]{1,0:T(1,128)S(1)} %get-tuple-element.23.asked.asked_row), channel_id=1, source_target_pairs={{0,2},{1,3},{2,0},{3,1},{4,6},{5,7},{6,4},{7,5},{8,10},{9,11},{10,... | collective-permute-start | bytes 1544 | tf_op jit(solution)/shard_map/ppermute | solution.py:284
  5.5 7.7 %collective-permute-start.1 = (s32[1,128]{1,0:T(1,128)S(1)}, s32[1,128]{1,0:T(1,128)S(1)}, u32[]{:S(2)}, u32[]{:S(2)}) collective-permute-start(s32[1,128]{1,0:T(1,128)S(1)} %get-tuple-element.23.asked.asked_row), channel_id=1, source_target_pairs={{4,0},{5,1},{6,2},{7,3},{8,4},{9,5},{10,6},{11,7},{12,8},{13,9},{1... | collective-permute-start | bytes 1544 | tf_op jit(solution)/shard_map/ppermute | solution.py:284
  13.9 9.3 %collective-permute-start.4 = (bf16[30,16,128]{2,1,0:T(8,128)(2,1)S(1)}, bf16[30,16,128]{2,1,0:T(8,128)(2,1)S(1)}, u32[]{:S(2)}, u32[]{:S(2)}) collective-permute-start(bf16[30,16,128]{2,1,0:T(8,128)(2,1)S(1)} %get-tuple-element.29), channel_id=1, source_target_pairs={{4,8},{5,9},{6,10},{7,11},{8,12},{9,13},{10,14},{11,15},{20,24},{2... | collective-permute-start | bytes 368648 | tf_op jit(solution)/shard_map/ppermute | solution.py:284
  17.1 6.1 %collective-permute-start.5 = (bf16[30,16,128]{2,1,0:T(8,128)(2,1)S(1)}, bf16[30,16,128]{2,1,0:T(8,128)(2,1)S(1)}, u32[]{:S(2)}, u32[]{:S(2)}) collective-permute-start(bf16[30,16,128]{2,1,0:T(8,128)(2,1)S(1)} %get-tuple-element.30), channel_id=1, source_target_pairs={{0,2},{1,3},{2,0},{3,1},{4,6},{5,7},{6,4},{7,5},{8,10},{9,11},{10,... | collective-permute-start | bytes 368648 | tf_op jit(solution)/shard_map/ppermute | solution.py:284
  18.4 4.8 %collective-permute-start.6 = (bf16[30,16,128]{2,1,0:T(8,128)(2,1)S(1)}, bf16[30,16,128]{2,1,0:T(8,128)(2,1)S(1)}, u32[]{:S(2)}, u32[]{:S(2)}) collective-permute-start(bf16[30,16,128]{2,1,0:T(8,128)(2,1)S(1)} %get-tuple-element.31), channel_id=1, source_target_pairs={{0,1},{1,2},{2,3},{3,0},{4,5},{5,6},{6,7},{7,4},{8,9},{9,10},{10,1... | collective-permute-start | bytes 368648 | tf_op jit(solution)/shard_map/ppermute | solution.py:284
  28.1 13.5 %collective-permute-start.7 = (bf16[31,16,128]{2,1,0:T(8,128)(2,1)S(1)}, bf16[31,16,128]{2,1,0:T(8,128)(2,1)S(1)}, u32[]{:S(2)}, u32[]{:S(2)}) collective-permute-start(bf16[31,16,128]{2,1,0:T(8,128)(2,1)S(1)} %get-tuple-element.35), channel_id=1, source_target_pairs={{8,0},{9,1},{10,2},{11,3},{12,4},{13,5},{14,6},{15,7},{24,16},{25,... | collective-permute-start | bytes 380936 | tf_op jit(solution)/shard_map/ppermute | solution.py:284
  29.4 12.2 %collective-permute-start.8 = (bf16[31,16,128]{2,1,0:T(8,128)(2,1)S(1)}, bf16[31,16,128]{2,1,0:T(8,128)(2,1)S(1)}, u32[]{:S(2)}, u32[]{:S(2)}) collective-permute-start(bf16[31,16,128]{2,1,0:T(8,128)(2,1)S(1)} %get-tuple-element.36), channel_id=1, source_target_pairs={{4,0},{5,1},{6,2},{7,3},{8,4},{9,5},{10,6},{11,7},{12,8},{13,9},{1... | collective-permute-start | bytes 380936 | tf_op jit(solution)/shard_map/ppermute | solution.py:284
  31.3 10.8 %collective-permute-start.9 = (bf16[31,16,128]{2,1,0:T(8,128)(2,1)S(1)}, bf16[31,16,128]{2,1,0:T(8,128)(2,1)S(1)}, u32[]{:S(2)}, u32[]{:S(2)}) collective-permute-start(bf16[31,16,128]{2,1,0:T(8,128)(2,1)S(1)} %get-tuple-element.37), channel_id=1, source_target_pairs={{2,0},{3,1},{4,2},{5,3},{6,4},{7,5},{8,6},{9,7},{10,8},{11,9},{12,... | collective-permute-start | bytes 380936 | tf_op jit(solution)/shard_map/ppermute | solution.py:284
  33.8 10.7 %collective-permute-start.10 = (bf16[31,16,128]{2,1,0:T(8,128)(2,1)S(1)}, bf16[31,16,128]{2,1,0:T(8,128)(2,1)S(1)}, u32[]{:S(2)}, u32[]{:S(2)}) collective-permute-start(bf16[31,16,128]{2,1,0:T(8,128)(2,1)S(1)} %get-tuple-element.38), channel_id=1, source_target_pairs={{1,0},{2,1},{3,2},{4,3},{5,4},{6,5},{7,6},{8,7},{9,8},{10,9},{11,1... | collective-permute-start | bytes 380936 | tf_op jit(solution)/shard_map/ppermute | solution.py:284

commit v6 on v5

--- a/solution.py
+++ b/solution.py
@@ -102,35 +102,42 @@
             left[j - first] = rows[j].astype(jnp.float32) - mean
 
 
+def fetches(weights, held, sem, first, leaves):
+    parts = [(at, pl.ds(at, CHUNK)) for at in range(first, first + leaves, CHUNK)]
+    return [
+        (range(at, at + CHUNK, 2), pltpu.make_async_copy(weights.at[p], held.at[p], sem.at[n]))
+        for n, (at, p) in enumerate(parts)
+    ]
+
+
 def early_kernel(home, latent, weights, left, held_w, rows, row_sem, w_sem):
-    leaf_dev = latent.shape[0]
-    chunks, ahead = leaf_dev // CHUNK, 3
-
-    def fetch(c):
-        part = pl.ds(c * CHUNK, CHUNK)
-        return pltpu.make_async_copy(weights.at[part], held_w.at[part], w_sem.at[c])
-
+    leaf_dev, half = latent.shape[0], left.shape[0]
     fetch_rows = pltpu.make_async_copy(latent, rows.at[pl.ds(0, leaf_dev)], row_sem)
     fetch_rows.start()
-    for c in range(ahead):
-        fetch(c).start()
+    parts = fetches(weights, held_w, w_sem, 0, half)
+    for _, fetch in parts:
+        fetch.start()
     rows[leaf_dev] = jnp.zeros(latent.shape[1:], latent.dtype)
     fetch_rows.wait()
-    for c in range(chunks):
-        fetch(c).wait()
-        if c + ahead < chunks:
-            fetch(c + ahead).start()
-        if (c + 1) * CHUNK <= left.shape[0]:
-            local_means(range(c * CHUNK, (c + 1) * CHUNK, 2), home, rows, held_w, left, 0)
-
-
-def late_kernel(home, rows, before, weights, factor, left, held_f, f_sem):
-    leaf_dev = weights.shape[0]
-    fetch = pltpu.make_async_copy(factor, held_f, f_sem)
-    fetch.start()
-    first = leaf_dev - left.shape[0]
-    local_means(range(first, leaf_dev, 2), home, rows, weights, left, first)
-    fetch.wait()
+    for leaves, fetch in parts:
+        fetch.wait()
+        local_means(leaves, home, rows, held_w, left, 0)
+
+
+def late_kernel(
+    home, rows, before, partly_held, weights, factor, left, held_w, held_f, w_sem, f_sem
+):
+    leaf_dev, half = weights.shape[0], left.shape[0]
+    first = leaf_dev - half
+    parts = fetches(weights, held_w, w_sem, first, half)
+    for _, fetch in parts:
+        fetch.start()
+    fetch_factor = pltpu.make_async_copy(factor, held_f, f_sem)
+    fetch_factor.start()
+    for leaves, fetch in parts:
+        fetch.wait()
+        local_means(leaves, home, rows, held_w, left, first)
+    fetch_factor.wait()
 
 
 def serve_kernel(capacity, ask8, ask2, ask1, latent, before, left, out8, out2, out1):
@@ -249,7 +256,7 @@
             out[j] = out[j] + rows[r].astype(jnp.float32)
 
 
-def call(body, name, out_shape, ins, outs, limit, flops=0, moved=0, scratch=()):
+def call(body, name, out_shape, ins, outs, limit, flops=0, moved=0, scratch=(), aliases={}):
     spec = lambda space: pl.BlockSpec(memory_space=space)
     return pl.pallas_call(
         body,
@@ -257,6 +264,7 @@
         in_specs=[spec(space) for space in ins],
         out_specs=tuple(spec(space) for space in outs),
         scratch_shapes=scratch,
+        input_output_aliases=aliases,
         compiler_params=pltpu.CompilerParams(vmem_limit_bytes=limit * MIB),
         cost_estimate=pl.CostEstimate(flops=flops, bytes_accessed=moved, transcendentals=0),
         name=name,
@@ -300,7 +308,7 @@
             shape((leaf_dev + 8, samples, width), jnp.bfloat16),
         ),
         [SMEM, HBM, HBM], [VMEM] * 3, 14, moved=heavy // 2,
-        scratch=[pltpu.SemaphoreType.DMA, pltpu.SemaphoreType.DMA((leaf_dev // CHUNK,))],
+        scratch=[pltpu.SemaphoreType.DMA, pltpu.SemaphoreType.DMA((half // CHUNK,))],
     )(home, placed(latent, HBM), placed(cond_weights, HBM))
     serve8, serve2, serve1 = call(
         functools.partial(serve_kernel, capacity), "serve", (some_rows,) * 3,
@@ -309,15 +317,18 @@
     from8 = passed(serve8, [(i, i + 4) for i in everyone if i >= 4 and i + 4 < devices])
     from2 = passed(serve2, [(i, i ^ 2) for i in everyone])
     from1 = passed(serve1, [(i, i // 4 * 4 + (i + 1) % 4) for i in everyone])
-    later, held_f = call(
+    later, held_w, held_f = call(
         late_kernel, "late",
         (
             shape((leaf_dev - half, samples, width), jnp.float32),
-            shape(precision_factor.shape, jnp.bfloat16),
+            shape(cond_weights.shape, jnp.bfloat16), shape(precision_factor.shape, jnp.bfloat16),
         ),
-        [SMEM, VMEM, ANY, VMEM, HBM], [VMEM] * 2, 8, moved=heavy // 2,
-        scratch=[pltpu.SemaphoreType.DMA],
-    )(home, rows, before, held_w, placed(precision_factor, HBM))
+        [SMEM, VMEM, ANY, VMEM, HBM, HBM], [VMEM] * 3, 14, moved=heavy // 2,
+        scratch=[
+            pltpu.SemaphoreType.DMA(((leaf_dev - half) // CHUNK,)), pltpu.SemaphoreType.DMA
+        ],
+        aliases={3: 1},
+    )(home, rows, before, held_w, placed(cond_weights, HBM), placed(precision_factor, HBM))
     back, low, out8, out4, out2, out1 = call(
         functools.partial(remote_kernel, capacity), "remote",
         (all_rows, shape((leaf_dev + 8, samples, width), jnp.bfloat16)) + (sent,) * 4,

time: 46.7 us -> 45.2 us (0.968)
  Pallas kernels: 20.7 us -> 19.4 us
    pallas_call x1, Pallas kernels: 5.62 us -> 3.55 us  [per_device(): call(early_kernel, 'early', (shape((half, samples, width), jnp.float32),...]
    pallas_call x1, Pallas kernels: 2.88 us -> 3.56 us  [per_device(): call(late_kernel, 'late', (shape((leaf_dev - half, samples, width), jnp.f...]
  transfers between devices with their start and end apart: 11 -> 11, of which waited for: 2 -> 2; matrix products, arithmetic and copies ran while one was open for 0% -> 0% of each run, Pallas kernels for 29% -> 27%
where the time goes in v6:
time: 45.2 us; the launch traced here: 44.9 us
  starting transfers between devices  22.4 us (50%)
  Pallas kernels  19.4 us (43%)
  waiting for transfers between devices  3.02 us (7%)
    ppermute x11, starting transfers between devices, passed(): return lax.ppermute(x, 'kx', route)  22.4 us
    pallas_call x1, Pallas kernels, per_device(): call(functools.partial(remote_kernel, capacity), 'remote', (all_rows, sha...  4.86 us
    pallas_call x1, Pallas kernels, per_device(): call(home_kernel, 'home', (all_rows,), [SMEM] + [VMEM] * 3, [VMEM], 6, mo...  3.89 us
    pallas_call x1, Pallas kernels, per_device(): call(late_kernel, 'late', (shape((leaf_dev - half, samples, width), jnp.f...  3.56 us
    pallas_call x1, Pallas kernels, per_device(): call(early_kernel, 'early', (shape((half, samples, width), jnp.float32),...  3.55 us
    ppermute x11, waiting for transfers between devices, passed(): return lax.ppermute(x, 'kx', route)  3.02 us
    pallas_call x1, Pallas kernels, per_device(): call(functools.partial(add_kernel, capacity, (3, 2, 1, 0)), 'add', (all_r...  1.84 us
    pallas_call x1, Pallas kernels, per_device(): call(index_kernel, 'index', (one_list, shape((2, 4 * SLOTS), jnp.int32),...  1.01 us
  transfers between devices with their start and end apart: 11, of which 2 were waited for; matrix products, arithmetic and copies ran while one was open for 0% of the time, Pallas kernels for 27%

profile of v6, /device:TPU:15, one launch (start us, length us, event | category | flops | bytes accessed | tf_op | source)
XLA Modules:
  0.0 44.9 jit_solution(2072601939409225183)
XLA Ops:
  0.0 3.2 %collective-permute-start = (bf16[80,16,128]{2,1,0:T(8,128)(2,1)}, bf16[80,16,128]{2,1,0:T(8,128)(2,1)S(1)}, u32[]{:S(2)}, u32[]{:S(2)}) collective-permute-start(bf16[80,16,128]{2,1,0:T(8,128)(2,1)} %latent.1), channel_id=1, source_target_pairs={{0,4},{1,5},{2,6},{3,7},{4,8},{5,9},{6,10},{7,11},{8,12},{9,13},{1... | collective-permute-start | bytes 983048 | tf_op jit(solution)/shard_map/ppermute | solution.py:292
  3.2 1.0 %index.1 = (s32[1,128]{1,0:T(1,128)S(1)}, s32[2,128]{1,0:T(2,128)S(1)}, s32[3,80]{1,0:T(4,128)S(1)}) custom-call(s32[3,80]{1,0:T(4,128)} %bitcast.1), custom_call_target="tpu_custom_call" | custom-call | bytes 2097152 | tf_op jit(solution)/shard_map/index/pallas_call | solution.py:295
  4.2 2.1 %collective-permute-start.1 = (s32[1,128]{1,0:T(1,128)S(1)}, s32[1,128]{1,0:T(1,128)S(1)}, u32[]{:S(2)}, u32[]{:S(2)}) collective-permute-start(s32[1,128]{1,0:T(1,128)S(1)} %get-tuple-element.24.asked.asked_row), channel_id=1, source_target_pairs={{4,0},{5,1},{6,2},{7,3},{8,4},{9,5},{10,6},{11,7},{12,8},{13,9},{1... | collective-permute-start | bytes 1544 | tf_op jit(solution)/shard_map/ppermute | solution.py:292
  6.4 0.3 collective-permute-start.2
  6.7 1.5 %collective-permute-start.3 = (s32[1,128]{1,0:T(1,128)S(1)}, s32[1,128]{1,0:T(1,128)S(1)}, u32[]{:S(2)}, u32[]{:S(2)}) collective-permute-start(s32[1,128]{1,0:T(1,128)S(1)} %get-tuple-element.24.asked.asked_row), channel_id=1, source_target_pairs={{0,3},{1,0},{2,1},{3,2},{4,7},{5,4},{6,5},{7,6},{8,11},{9,8},{10,9... | collective-permute-start | bytes 1544 | tf_op jit(solution)/shard_map/ppermute | solution.py:292
  8.2 3.6 %early.1 = (f32[40,16,128]{2,1,0:T(8,128)S(1)}, bf16[80,3,128,128]{3,2,1,0:T(8,128)(2,1)S(1)}, bf16[88,16,128]{2,1,0:T(8,128)(2,1)S(1)}) custom-call(s32[3,80]{1,0:T(4,128)S(1)} %get-tuple-element.23.home, bf16[80,16,128]{2,1,0:T(8,128)(2,1)} %latent.1, bf16[80,3,128,128]{3,2,1,0:T(8,128)(2,1)} %weights.3), custom_call_target="tpu_custom_call" | custom-call | bytes 3932160 | tf_op jit(solution)/shard_map/early/pallas_call | solution.py:304
  11.7 0.0 collective-permute-done.1.ask8
  11.8 0.0 collective-permute-done.2.ask2
  11.8 0.0 collective-permute-done.3.ask1
  11.8 0.0 collective-permute-done.before
  11.8 0.6 %serve.1 = (bf16[30,16,128]{2,1,0:T(8,128)(2,1)S(1)}, bf16[30,16,128]{2,1,0:T(8,128)(2,1)S(1)}, bf16[30,16,128]{2,1,0:T(8,128)(2,1)S(1)}) custom-call(s32[1,128]{1,0:T(1,128)S(1)} %collective-permute-done.1.ask8, s32[1,128]{1,0:T(1,128)S(1)} %collective-permute-done.2.ask2, s32[1,128]{1,0:T(1,128)S(1)} %collective-permute-done.3.ask1, ...), custom_call_target="tpu_custom_call" | custom-call | bytes 4194304 | tf_op jit(solution)/shard_map/serve/pallas_call | solution.py:313
  12.4 3.2 %collective-permute-start.4 = (bf16[30,16,128]{2,1,0:T(8,128)(2,1)S(1)}, bf16[30,16,128]{2,1,0:T(8,128)(2,1)S(1)}, u32[]{:S(2)}, u32[]{:S(2)}) collective-permute-start(bf16[30,16,128]{2,1,0:T(8,128)(2,1)S(1)} %get-tuple-element.30), channel_id=1, source_target_pairs={{4,8},{5,9},{6,10},{7,11},{8,12},{9,13},{10,14},{11,15},{20,24},{2... | collective-permute-start | bytes 368648 | tf_op jit(solution)/shard_map/ppermute | solution.py:292
  15.6 1.3 %collective-permute-start.5 = (bf16[30,16,128]{2,1,0:T(8,128)(2,1)S(1)}, bf16[30,16,128]{2,1,0:T(8,128)(2,1)S(1)}, u32[]{:S(2)}, u32[]{:S(2)}) collective-permute-start(bf16[30,16,128]{2,1,0:T(8,128)(2,1)S(1)} %get-tuple-element.31), channel_id=1, source_target_pairs={{0,2},{1,3},{2,0},{3,1},{4,6},{5,7},{6,4},{7,5},{8,10},{9,11},{10,... | collective-permute-start | bytes 368648 | tf_op jit(solution)/shard_map/ppermute | solution.py:292
  16.9 1.1 %collective-permute-start.6 = (bf16[30,16,128]{2,1,0:T(8,128)(2,1)S(1)}, bf16[30,16,128]{2,1,0:T(8,128)(2,1)S(1)}, u32[]{:S(2)}, u32[]{:S(2)}) collective-permute-start(bf16[30,16,128]{2,1,0:T(8,128)(2,1)S(1)} %get-tuple-element.32), channel_id=1, source_target_pairs={{0,1},{1,2},{2,3},{3,0},{4,5},{5,6},{6,7},{7,4},{8,9},{9,10},{10,1... | collective-permute-start | bytes 368648 | tf_op jit(solution)/shard_map/ppermute | solution.py:292
  18.1 3.6 %late.1 = (f32[40,16,128]{2,1,0:T(8,128)S(1)}, bf16[80,3,128,128]{3,2,1,0:T(8,128)(2,1)S(1)}, bf16[80,128,128]{2,1,0:T(8,128)(2,1)S(1)}) custom-call(s32[3,80]{1,0:T(4,128)S(1)} %get-tuple-element.23.home, bf16[88,16,128]{2,1,0:T(8,128)(2,1)S(1)} %get-tuple-element.27.rows.latent, ...), custom_call_target="tpu_custom_call", output_to_operand_aliasing={{1}: (3, {})} | custom-call | bytes 3932160 | tf_op jit(solution)/shard_map/late/pallas_call | solution.py:320
  21.6 0.0 collective-permute-done.4.from8
  21.6 0.0 collective-permute-done.5.from2
  21.7 0.0 collective-permute-done.6.from1
  21.7 4.9 %remote.1 = (f32[80,16,128]{2,1,0:T(8,128)S(1)}, bf16[88,16,128]{2,1,0:T(8,128)(2,1)S(1)}, bf16[31,16,128]{2,1,0:T(8,128)(2,1)S(1)}, bf16[31,16,128]{2,1,0:T(8,1...) custom-call(s32[1,128]{1,0:T(1,128)S(1)} %get-tuple-element.24.asked.asked_row, ...), custom_call_target="tpu_custom_call" | custom-call | bytes 7864320 | tf_op jit(solution)/shard_map/remote/pallas_call | solution.py:332
  26.5 1.3 %collective-permute-start.7 = (bf16[31,16,128]{2,1,0:T(8,128)(2,1)S(1)}, bf16[31,16,128]{2,1,0:T(8,128)(2,1)S(1)}, u32[]{:S(2)}, u32[]{:S(2)}) collective-permute-start(bf16[31,16,128]{2,1,0:T(8,128)(2,1)S(1)} %get-tuple-element.37), channel_id=1, source_target_pairs={{8,0},{9,1},{10,2},{11,3},{12,4},{13,5},{14,6},{15,7},{24,16},{25,... | collective-permute-start | bytes 380936 | tf_op jit(solution)/shard_map/ppermute | solution.py:292
  27.8 1.9 %collective-permute-start.8 = (bf16[31,16,128]{2,1,0:T(8,128)(2,1)S(1)}, bf16[31,16,128]{2,1,0:T(8,128)(2,1)S(1)}, u32[]{:S(2)}, u32[]{:S(2)}) collective-permute-start(bf16[31,16,128]{2,1,0:T(8,128)(2,1)S(1)} %get-tuple-element.38), channel_id=1, source_target_pairs={{4,0},{5,1},{6,2},{7,3},{8,4},{9,5},{10,6},{11,7},{12,8},{13,9},{1... | collective-permute-start | bytes 380936 | tf_op jit(solution)/shard_map/ppermute | solution.py:292
  29.8 2.7 %collective-permute-start.9 = (bf16[31,16,128]{2,1,0:T(8,128)(2,1)S(1)}, bf16[31,16,128]{2,1,0:T(8,128)(2,1)S(1)}, u32[]{:S(2)}, u32[]{:S(2)}) collective-permute-start(bf16[31,16,128]{2,1,0:T(8,128)(2,1)S(1)} %get-tuple-element.39), channel_id=1, source_target_pairs={{2,0},{3,1},{4,2},{5,3},{6,4},{7,5},{8,6},{9,7},{10,8},{11,9},{12,... | collective-permute-start | bytes 380936 | tf_op jit(solution)/shard_map/ppermute | solution.py:292
  32.5 3.7 %collective-permute-start.10 = (bf16[31,16,128]{2,1,0:T(8,128)(2,1)S(1)}, bf16[31,16,128]{2,1,0:T(8,128)(2,1)S(1)}, u32[]{:S(2)}, u32[]{:S(2)}) collective-permute-start(bf16[31,16,128]{2,1,0:T(8,128)(2,1)S(1)} %get-tuple-element.40), channel_id=1, source_target_pairs={{1,0},{2,1},{3,2},{4,3},{5,4},{6,5},{7,6},{8,7},{9,8},{10,9},{11,1... | collective-permute-start | bytes 380936 | tf_op jit(solution)/shard_map/ppermute | solution.py:292
  36.2 3.9 %home.1.part = f32[80,16,128]{2,1,0:T(8,128)S(1)} custom-call(s32[3,80]{1,0:T(4,128)S(1)} %get-tuple-element.23.home, f32[80,16,128]{2,1,0:T(8,128)S(1)} %get-tuple-element.35.back, bf16[88,16,128]{2,1,0:T(8,128)(2,1)S(1)} %get-tuple-element.36.low, bf16[80,3,128,128]{3,2,1,0:T(8,128)(2,1)S(1)} %get-tuple-element.33.weights), custom_call_target="tpu_custom_call" | custom-call | bytes 7864320 | tf_op jit(solution)/shard_map/home/pallas_call | solution.py:342
  40.1 0.0 collective-permute-done.7.refs_0_
  40.1 0.0 collective-permute-done.8.refs_1_
  40.1 0.7 %collective-permute-done.9.refs_2_ = bf16[31,16,128]{2,1,0:T(8,128)(2,1)S(1)} collective-permute-done((bf16[31,16,128]{2,1,0:T(8,128)(2,1)S(1)}, bf16[31,16,128]{2,1,0:T(8,128)(2,1)S(1)}, u32[]{:S(2)}, u32[]{:S(2)}) %collective-permute-start.9) | collective-permute-done | bytes 127008 | tf_op jit(solution)/shard_map/ppermute | solution.py:292
  40.8 2.3 %collective-permute-done.10.refs_3_ = bf16[31,16,128]{2,1,0:T(8,128)(2,1)S(1)} collective-permute-done((bf16[31,16,128]{2,1,0:T(8,128)(2,1)S(1)}, bf16[31,16,128]{2,1,0:T(8,128)(2,1)S(1)}, u32[]{:S(2)}, u32[]{:S(2)}) %collective-permute-start.10) | collective-permute-done | bytes 127008 | tf_op jit(solution)/shard_map/ppermute | solution.py:292
  43.1 1.8 %add.1 = f32[80,16,128]{2,1,0:T(8,128)} custom-call(f32[80,16,128]{2,1,0:T(8,128)S(1)} %home.1.part, bf16[31,16,128]{2,1,0:T(8,128)(2,1)S(1)} %collective-permute-done.7.refs_0_, bf16[31,16,128]{2,1,0:T(8,128)(2,1)S(1)} %collective-permute-done.8.refs_1_, bf16[31,16,128]{2,1,0:T(8,128)(2,1)S(1)} %collective-permute-done.9.refs_2_, ...), custom_call_target="tpu_custom_call" | custom-call | bytes 4194304 | tf_op jit(solution)/shard_map/add/pallas_call | solution.py:347
Async XLA Ops:
  0.0 11.8 %collective-permute-start = (bf16[80,16,128]{2,1,0:T(8,128)(2,1)}, bf16[80,16,128]{2,1,0:T(8,128)(2,1)S(1)}, u32[]{:S(2)}, u32[]{:S(2)}) collective-permute-start(bf16[80,16,128]{2,1,0:T(8,128)(2,1)} %latent.1), channel_id=1, source_target_pairs={{0,4},{1,5},{2,6},{3,7},{4,8},{5,9},{6,10},{7,11},{8,12},{9,13},{1... | collective-permute-start | bytes 983048 | tf_op jit(solution)/shard_map/ppermute | solution.py:292
  4.2 7.5 %collective-permute-start.1 = (s32[1,128]{1,0:T(1,128)S(1)}, s32[1,128]{1,0:T(1,128)S(1)}, u32[]{:S(2)}, u32[]{:S(2)}) collective-permute-start(s32[1,128]{1,0:T(1,128)S(1)} %get-tuple-element.24.asked.asked_row), channel_id=1, source_target_pairs={{4,0},{5,1},{6,2},{7,3},{8,4},{9,5},{10,6},{11,7},{12,8},{13,9},{1... | collective-permute-start | bytes 1544 | tf_op jit(solution)/shard_map/ppermute | solution.py:292
  6.4 5.4 %collective-permute-start.2 = (s32[1,128]{1,0:T(1,128)S(1)}, s32[1,128]{1,0:T(1,128)S(1)}, u32[]{:S(2)}, u32[]{:S(2)}) collective-permute-start(s32[1,128]{1,0:T(1,128)S(1)} %get-tuple-element.24.asked.asked_row), channel_id=1, source_target_pairs={{0,2},{1,3},{2,0},{3,1},{4,6},{5,7},{6,4},{7,5},{8,10},{9,11},{10,... | collective-permute-start | bytes 1544 | tf_op jit(solution)/shard_map/ppermute | solution.py:292
  6.7 5.1 %collective-permute-start.3 = (s32[1,128]{1,0:T(1,128)S(1)}, s32[1,128]{1,0:T(1,128)S(1)}, u32[]{:S(2)}, u32[]{:S(2)}) collective-permute-start(s32[1,128]{1,0:T(1,128)S(1)} %get-tuple-element.24.asked.asked_row), channel_id=1, source_target_pairs={{0,3},{1,0},{2,1},{3,2},{4,7},{5,4},{6,5},{7,6},{8,11},{9,8},{10,9... | collective-permute-start | bytes 1544 | tf_op jit(solution)/shard_map/ppermute | solution.py:292
  12.4 9.2 %collective-permute-start.4 = (bf16[30,16,128]{2,1,0:T(8,128)(2,1)S(1)}, bf16[30,16,128]{2,1,0:T(8,128)(2,1)S(1)}, u32[]{:S(2)}, u32[]{:S(2)}) collective-permute-start(bf16[30,16,128]{2,1,0:T(8,128)(2,1)S(1)} %get-tuple-element.30), channel_id=1, source_target_pairs={{4,8},{5,9},{6,10},{7,11},{8,12},{9,13},{10,14},{11,15},{20,24},{2... | collective-permute-start | bytes 368648 | tf_op jit(solution)/shard_map/ppermute | solution.py:292
  15.6 6.0 %collective-permute-start.5 = (bf16[30,16,128]{2,1,0:T(8,128)(2,1)S(1)}, bf16[30,16,128]{2,1,0:T(8,128)(2,1)S(1)}, u32[]{:S(2)}, u32[]{:S(2)}) collective-permute-start(bf16[30,16,128]{2,1,0:T(8,128)(2,1)S(1)} %get-tuple-element.31), channel_id=1, source_target_pairs={{0,2},{1,3},{2,0},{3,1},{4,6},{5,7},{6,4},{7,5},{8,10},{9,11},{10,... | collective-permute-start | bytes 368648 | tf_op jit(solution)/shard_map/ppermute | solution.py:292
  16.9 4.7 %collective-permute-start.6 = (bf16[30,16,128]{2,1,0:T(8,128)(2,1)S(1)}, bf16[30,16,128]{2,1,0:T(8,128)(2,1)S(1)}, u32[]{:S(2)}, u32[]{:S(2)}) collective-permute-start(bf16[30,16,128]{2,1,0:T(8,128)(2,1)S(1)} %get-tuple-element.32), channel_id=1, source_target_pairs={{0,1},{1,2},{2,3},{3,0},{4,5},{5,6},{6,7},{7,4},{8,9},{9,10},{10,1... | collective-permute-start | bytes 368648 | tf_op jit(solution)/shard_map/ppermute | solution.py:292
  26.5 13.5 %collective-permute-start.7 = (bf16[31,16,128]{2,1,0:T(8,128)(2,1)S(1)}, bf16[31,16,128]{2,1,0:T(8,128)(2,1)S(1)}, u32[]{:S(2)}, u32[]{:S(2)}) collective-permute-start(bf16[31,16,128]{2,1,0:T(8,128)(2,1)S(1)} %get-tuple-element.37), channel_id=1, source_target_pairs={{8,0},{9,1},{10,2},{11,3},{12,4},{13,5},{14,6},{15,7},{24,16},{25,... | collective-permute-start | bytes 380936 | tf_op jit(solution)/shard_map/ppermute | solution.py:292
  27.8 12.2 %collective-permute-start.8 = (bf16[31,16,128]{2,1,0:T(8,128)(2,1)S(1)}, bf16[31,16,128]{2,1,0:T(8,128)(2,1)S(1)}, u32[]{:S(2)}, u32[]{:S(2)}) collective-permute-start(bf16[31,16,128]{2,1,0:T(8,128)(2,1)S(1)} %get-tuple-element.38), channel_id=1, source_target_pairs={{4,0},{5,1},{6,2},{7,3},{8,4},{9,5},{10,6},{11,7},{12,8},{13,9},{1... | collective-permute-start | bytes 380936 | tf_op jit(solution)/shard_map/ppermute | solution.py:292
  29.8 11.0 %collective-permute-start.9 = (bf16[31,16,128]{2,1,0:T(8,128)(2,1)S(1)}, bf16[31,16,128]{2,1,0:T(8,128)(2,1)S(1)}, u32[]{:S(2)}, u32[]{:S(2)}) collective-permute-start(bf16[31,16,128]{2,1,0:T(8,128)(2,1)S(1)} %get-tuple-element.39), channel_id=1, source_target_pairs={{2,0},{3,1},{4,2},{5,3},{6,4},{7,5},{8,6},{9,7},{10,8},{11,9},{12,... | collective-permute-start | bytes 380936 | tf_op jit(solution)/shard_map/ppermute | solution.py:292
  32.5 10.6 %collective-permute-start.10 = (bf16[31,16,128]{2,1,0:T(8,128)(2,1)S(1)}, bf16[31,16,128]{2,1,0:T(8,128)(2,1)S(1)}, u32[]{:S(2)}, u32[]{:S(2)}) collective-permute-start(bf16[31,16,128]{2,1,0:T(8,128)(2,1)S(1)} %get-tuple-element.40), channel_id=1, source_target_pairs={{1,0},{2,1},{3,2},{4,3},{5,4},{6,5},{7,6},{8,7},{9,8},{10,9},{11,1... | collective-permute-start | bytes 380936 | tf_op jit(solution)/shard_map/ppermute | solution.py:292

commit v7 on v6

--- a/solution.py
+++ b/solution.py
@@ -77,16 +77,11 @@
 
 
 def paired(x, y, left, right, by_rows=False):
-    samples = x.shape[0]
-    if by_rows:
-        wide = left.shape[0]
-        both = lax.dot_general(
-            below([x, y]), below([left, right]), BY_ROWS, preferred_element_type=jnp.float32
-        )
-    else:
-        wide = left.shape[1]
-        both = jnp.dot(below([x, y]), beside([left, right]), preferred_element_type=jnp.float32)
-    return both[:samples, :wide], both[samples:, wide:]
+    dims = BY_ROWS if by_rows else (((1,), (0,)), ((), ()))
+    return tuple(
+        lax.dot_general(rows, weights, dims, preferred_element_type=jnp.float32)
+        for rows, weights in ((x, left), (y, right))
+    )
 
 
 def local_means(leaves, home, rows, weights, left, first):
@@ -140,7 +135,7 @@
     fetch_factor.wait()
 
 
-def serve_kernel(capacity, ask8, ask2, ask1, latent, before, left, out8, out2, out1):
+def serve_kernel(capacity, ask1, ask2, ask8, latent, before, left, out8, out2, out1):
     me = lax.axis_index("kx")
     def pick(o, ask, rows, out):
         for r in range(capacity):
@@ -175,7 +170,7 @@
 
 
 def remote_kernel(
-    capacity, asked, slots, asked_row, left, later, before, from8, from2, from1,
+    capacity, asked, slots, asked_row, left, later, before, from2, from1, from8,
     weights, factor, back, low, out8, out4, out2, out1, resid,
 ):
     leaf_dev, half = back.shape[0], left.shape[0]
@@ -313,7 +308,7 @@
     serve8, serve2, serve1 = call(
         functools.partial(serve_kernel, capacity), "serve", (some_rows,) * 3,
         [SMEM] * 3 + [VMEM] * 2 + [ANY], [VMEM] * 3, 4, moved=4 * MIB,
-    )(ask8, ask2, ask1, rows, before, left)
+    )(ask1, ask2, ask8, rows, before, left)
     from8 = passed(serve8, [(i, i + 4) for i in everyone if i >= 4 and i + 4 < devices])
     from2 = passed(serve2, [(i, i ^ 2) for i in everyone])
     from1 = passed(serve1, [(i, i // 4 * 4 + (i + 1) % 4) for i in everyone])
@@ -334,7 +329,7 @@
         (all_rows, shape((leaf_dev + 8, samples, width), jnp.bfloat16)) + (sent,) * 4,
         [SMEM] * 2 + [VMEM] * 9, [VMEM] * 6, 8, moved=heavy,
         scratch=[VMEM((leaf_dev + 8, samples, width), jnp.float32)],
-    )(asked, slots, asked, left, later, before, from8, from2, from1, held_w, held_f)
+    )(asked, slots, asked, left, later, before, from2, from1, from8, held_w, held_f)
     returned = [
         passed(x, [(i, i - reach) for i in everyone if i >= reach])
         for reach, x in ((8, out8), (4, out4), (2, out2), (1, out1))

time: 45.2 us -> 46.7 us (1.033)
  starting transfers between devices: 22.4 us -> 20.4 us
  Pallas kernels: 19.4 us -> 21.3 us
  waiting for transfers between devices: 3.02 us -> 4.58 us
    ppermute x11, starting transfers between devices: 22.4 us -> 20.4 us  [passed(): return lax.ppermute(x, 'kx', route)]
    pallas_call x1, Pallas kernels: 4.86 us -> 6.57 us  [per_device(): call(functools.partial(remote_kernel, capacity), 'remote', (all_rows, sha...]
    ppermute x11, waiting for transfers between devices: 3.02 us -> 4.58 us  [passed(): return lax.ppermute(x, 'kx', route)]
  transfers between devices with their start and end apart: 11 -> 11, of which waited for: 2 -> 2; matrix products, arithmetic and copies ran while one was open for 0% -> 0% of each run, Pallas kernels for 27% -> 26%
where the time goes in v7:
time: 46.7 us; the launch traced here: 46.4 us
  Pallas kernels  21.3 us (46%)
  starting transfers between devices  20.4 us (44%)
  waiting for transfers between devices  4.58 us (10%)
    ppermute x11, starting transfers between devices, passed(): return lax.ppermute(x, 'kx', route)  20.4 us
    pallas_call x1, Pallas kernels, per_device(): call(functools.partial(remote_kernel, capacity), 'remote', (all_rows, sha...  6.57 us
    ppermute x11, waiting for transfers between devices, passed(): return lax.ppermute(x, 'kx', route)  4.58 us
    pallas_call x1, Pallas kernels, per_device(): call(home_kernel, 'home', (all_rows,), [SMEM] + [VMEM] * 3, [VMEM], 6, mo...  4.03 us
    pallas_call x1, Pallas kernels, per_device(): call(early_kernel, 'early', (shape((half, samples, width), jnp.float32),...  3.59 us
    pallas_call x1, Pallas kernels, per_device(): call(late_kernel, 'late', (shape((leaf_dev - half, samples, width), jnp.f...  3.57 us
    pallas_call x1, Pallas kernels, per_device(): call(functools.partial(add_kernel, capacity, (3, 2, 1, 0)), 'add', (all_r...  1.85 us
    pallas_call x1, Pallas kernels, per_device(): call(index_kernel, 'index', (one_list, shape((2, 4 * SLOTS), jnp.int32),...  1.01 us
  transfers between devices with their start and end apart: 11, of which 2 were waited for; matrix products, arithmetic and copies ran while one was open for 0% of the time, Pallas kernels for 26%

profile of v7, /device:TPU:15, one launch (start us, length us, event | category | flops | bytes accessed | tf_op | source)
XLA Modules:
  0.0 46.4 jit_solution(15263367765152390767)
XLA Ops:
  0.0 3.2 %collective-permute-start = (bf16[80,16,128]{2,1,0:T(8,128)(2,1)}, bf16[80,16,128]{2,1,0:T(8,128)(2,1)S(1)}, u32[]{:S(2)}, u32[]{:S(2)}) collective-permute-start(bf16[80,16,128]{2,1,0:T(8,128)(2,1)} %latent.1), channel_id=1, source_target_pairs={{0,4},{1,5},{2,6},{3,7},{4,8},{5,9},{6,10},{7,11},{8,12},{9,13},{1... | collective-permute-start | bytes 983048 | tf_op jit(solution)/shard_map/ppermute | solution.py:287
  3.2 1.0 %index.1 = (s32[1,128]{1,0:T(1,128)S(1)}, s32[2,128]{1,0:T(2,128)S(1)}, s32[3,80]{1,0:T(4,128)S(1)}) custom-call(s32[3,80]{1,0:T(4,128)} %bitcast.1), custom_call_target="tpu_custom_call" | custom-call | bytes 2097152 | tf_op jit(solution)/shard_map/index/pallas_call | solution.py:290
  4.2 1.0 %collective-permute-start.1 = (s32[1,128]{1,0:T(1,128)S(1)}, s32[1,128]{1,0:T(1,128)S(1)}, u32[]{:S(2)}, u32[]{:S(2)}) collective-permute-start(s32[1,128]{1,0:T(1,128)S(1)} %get-tuple-element.24.asked.asked_row), channel_id=1, source_target_pairs={{0,3},{1,0},{2,1},{3,2},{4,7},{5,4},{6,5},{7,6},{8,11},{9,8},{10,9... | collective-permute-start | bytes 1544 | tf_op jit(solution)/shard_map/ppermute | solution.py:287
  5.2 0.2 collective-permute-start.2
  5.5 2.1 %collective-permute-start.3 = (s32[1,128]{1,0:T(1,128)S(1)}, s32[1,128]{1,0:T(1,128)S(1)}, u32[]{:S(2)}, u32[]{:S(2)}) collective-permute-start(s32[1,128]{1,0:T(1,128)S(1)} %get-tuple-element.24.asked.asked_row), channel_id=1, source_target_pairs={{4,0},{5,1},{6,2},{7,3},{8,4},{9,5},{10,6},{11,7},{12,8},{13,9},{1... | collective-permute-start | bytes 1544 | tf_op jit(solution)/shard_map/ppermute | solution.py:287
  7.6 3.6 %early.1 = (f32[40,16,128]{2,1,0:T(8,128)S(1)}, bf16[80,3,128,128]{3,2,1,0:T(8,128)(2,1)S(1)}, bf16[88,16,128]{2,1,0:T(8,128)(2,1)S(1)}) custom-call(s32[3,80]{1,0:T(4,128)S(1)} %get-tuple-element.23.home, bf16[80,16,128]{2,1,0:T(8,128)(2,1)} %latent.1, bf16[80,3,128,128]{3,2,1,0:T(8,128)(2,1)} %weights.3), custom_call_target="tpu_custom_call" | custom-call | bytes 3932160 | tf_op jit(solution)/shard_map/early/pallas_call | solution.py:299
  11.2 0.0 collective-permute-done.1.ask1
  11.2 0.0 collective-permute-done.2.ask2
  11.2 0.0 collective-permute-done.3.ask8
  11.2 0.0 collective-permute-done.before
  11.2 0.6 %serve.1 = (bf16[30,16,128]{2,1,0:T(8,128)(2,1)S(1)}, bf16[30,16,128]{2,1,0:T(8,128)(2,1)S(1)}, bf16[30,16,128]{2,1,0:T(8,128)(2,1)S(1)}) custom-call(s32[1,128]{1,0:T(1,128)S(1)} %collective-permute-done.1.ask1, s32[1,128]{1,0:T(1,128)S(1)} %collective-permute-done.2.ask2, s32[1,128]{1,0:T(1,128)S(1)} %collective-permute-done.3.ask8, ...), custom_call_target="tpu_custom_call" | custom-call | bytes 4194304 | tf_op jit(solution)/shard_map/serve/pallas_call | solution.py:308
  11.9 1.3 %collective-permute-start.4 = (bf16[30,16,128]{2,1,0:T(8,128)(2,1)S(1)}, bf16[30,16,128]{2,1,0:T(8,128)(2,1)S(1)}, u32[]{:S(2)}, u32[]{:S(2)}) collective-permute-start(bf16[30,16,128]{2,1,0:T(8,128)(2,1)S(1)} %get-tuple-element.30), channel_id=1, source_target_pairs={{0,2},{1,3},{2,0},{3,1},{4,6},{5,7},{6,4},{7,5},{8,10},{9,11},{10,... | collective-permute-start | bytes 368648 | tf_op jit(solution)/shard_map/ppermute | solution.py:287
  13.2 1.6 %collective-permute-start.5 = (bf16[30,16,128]{2,1,0:T(8,128)(2,1)S(1)}, bf16[30,16,128]{2,1,0:T(8,128)(2,1)S(1)}, u32[]{:S(2)}, u32[]{:S(2)}) collective-permute-start(bf16[30,16,128]{2,1,0:T(8,128)(2,1)S(1)} %get-tuple-element.31), channel_id=1, source_target_pairs={{0,1},{1,2},{2,3},{3,0},{4,5},{5,6},{6,7},{7,4},{8,9},{9,10},{10,1... | collective-permute-start | bytes 368648 | tf_op jit(solution)/shard_map/ppermute | solution.py:287
  14.8 3.2 %collective-permute-start.6 = (bf16[30,16,128]{2,1,0:T(8,128)(2,1)S(1)}, bf16[30,16,128]{2,1,0:T(8,128)(2,1)S(1)}, u32[]{:S(2)}, u32[]{:S(2)}) collective-permute-start(bf16[30,16,128]{2,1,0:T(8,128)(2,1)S(1)} %get-tuple-element.32), channel_id=1, source_target_pairs={{4,8},{5,9},{6,10},{7,11},{8,12},{9,13},{10,14},{11,15},{20,24},{2... | collective-permute-start | bytes 368648 | tf_op jit(solution)/shard_map/ppermute | solution.py:287
  18.0 3.6 %late.1 = (f32[40,16,128]{2,1,0:T(8,128)S(1)}, bf16[80,3,128,128]{3,2,1,0:T(8,128)(2,1)S(1)}, bf16[80,128,128]{2,1,0:T(8,128)(2,1)S(1)}) custom-call(s32[3,80]{1,0:T(4,128)S(1)} %get-tuple-element.23.home, bf16[88,16,128]{2,1,0:T(8,128)(2,1)S(1)} %get-tuple-element.27.rows.latent, ...), custom_call_target="tpu_custom_call", output_to_operand_aliasing={{1}: (3, {})} | custom-call | bytes 3932160 | tf_op jit(solution)/shard_map/late/pallas_call | solution.py:315
  21.6 0.0 collective-permute-done.4.from2
  21.6 0.0 collective-permute-done.5.from1
  21.6 0.0 collective-permute-done.6.from8
  21.6 6.6 %remote.1 = (f32[80,16,128]{2,1,0:T(8,128)S(1)}, bf16[88,16,128]{2,1,0:T(8,128)(2,1)S(1)}, bf16[31,16,128]{2,1,0:T(8,128)(2,1)S(1)}, bf16[31,16,128]{2,1,0:T(8,1...) custom-call(s32[1,128]{1,0:T(1,128)S(1)} %get-tuple-element.24.asked.asked_row, ...), custom_call_target="tpu_custom_call" | custom-call | bytes 7864320 | tf_op jit(solution)/shard_map/remote/pallas_call | solution.py:327
  28.2 1.3 %collective-permute-start.7 = (bf16[31,16,128]{2,1,0:T(8,128)(2,1)S(1)}, bf16[31,16,128]{2,1,0:T(8,128)(2,1)S(1)}, u32[]{:S(2)}, u32[]{:S(2)}) collective-permute-start(bf16[31,16,128]{2,1,0:T(8,128)(2,1)S(1)} %get-tuple-element.37), channel_id=1, source_target_pairs={{8,0},{9,1},{10,2},{11,3},{12,4},{13,5},{14,6},{15,7},{24,16},{25,... | collective-permute-start | bytes 380936 | tf_op jit(solution)/shard_map/ppermute | solution.py:287
  29.5 1.9 %collective-permute-start.8 = (bf16[31,16,128]{2,1,0:T(8,128)(2,1)S(1)}, bf16[31,16,128]{2,1,0:T(8,128)(2,1)S(1)}, u32[]{:S(2)}, u32[]{:S(2)}) collective-permute-start(bf16[31,16,128]{2,1,0:T(8,128)(2,1)S(1)} %get-tuple-element.38), channel_id=1, source_target_pairs={{4,0},{5,1},{6,2},{7,3},{8,4},{9,5},{10,6},{11,7},{12,8},{13,9},{1... | collective-permute-start | bytes 380936 | tf_op jit(solution)/shard_map/ppermute | solution.py:287
  31.4 2.5 %collective-permute-start.9 = (bf16[31,16,128]{2,1,0:T(8,128)(2,1)S(1)}, bf16[31,16,128]{2,1,0:T(8,128)(2,1)S(1)}, u32[]{:S(2)}, u32[]{:S(2)}) collective-permute-start(bf16[31,16,128]{2,1,0:T(8,128)(2,1)S(1)} %get-tuple-element.39), channel_id=1, source_target_pairs={{2,0},{3,1},{4,2},{5,3},{6,4},{7,5},{8,6},{9,7},{10,8},{11,9},{12,... | collective-permute-start | bytes 380936 | tf_op jit(solution)/shard_map/ppermute | solution.py:287
  33.9 2.0 %collective-permute-start.10 = (bf16[31,16,128]{2,1,0:T(8,128)(2,1)S(1)}, bf16[31,16,128]{2,1,0:T(8,128)(2,1)S(1)}, u32[]{:S(2)}, u32[]{:S(2)}) collective-permute-start(bf16[31,16,128]{2,1,0:T(8,128)(2,1)S(1)} %get-tuple-element.40), channel_id=1, source_target_pairs={{1,0},{2,1},{3,2},{4,3},{5,4},{6,5},{7,6},{8,7},{9,8},{10,9},{11,1... | collective-permute-start | bytes 380936 | tf_op jit(solution)/shard_map/ppermute | solution.py:287
  35.9 4.0 %home.1.part = f32[80,16,128]{2,1,0:T(8,128)S(1)} custom-call(s32[3,80]{1,0:T(4,128)S(1)} %get-tuple-element.23.home, f32[80,16,128]{2,1,0:T(8,128)S(1)} %get-tuple-element.35.back, bf16[88,16,128]{2,1,0:T(8,128)(2,1)S(1)} %get-tuple-element.36.low, bf16[80,3,128,128]{3,2,1,0:T(8,128)(2,1)S(1)} %get-tuple-element.33.weights), custom_call_target="tpu_custom_call" | custom-call | bytes 7864320 | tf_op jit(solution)/shard_map/home/pallas_call | solution.py:337
  40.0 0.0 collective-permute-done.7.refs_0_
  40.0 0.0 collective-permute-done.8.refs_1_
  40.0 3.0 %collective-permute-done.9.refs_2_ = bf16[31,16,128]{2,1,0:T(8,128)(2,1)S(1)} collective-permute-done((bf16[31,16,128]{2,1,0:T(8,128)(2,1)S(1)}, bf16[31,16,128]{2,1,0:T(8,128)(2,1)S(1)}, u32[]{:S(2)}, u32[]{:S(2)}) %collective-permute-start.9) | collective-permute-done | bytes 127008 | tf_op jit(solution)/shard_map/ppermute | solution.py:287
  43.0 1.6 %collective-permute-done.10.refs_3_ = bf16[31,16,128]{2,1,0:T(8,128)(2,1)S(1)} collective-permute-done((bf16[31,16,128]{2,1,0:T(8,128)(2,1)S(1)}, bf16[31,16,128]{2,1,0:T(8,128)(2,1)S(1)}, u32[]{:S(2)}, u32[]{:S(2)}) %collective-permute-start.10) | collective-permute-done | bytes 127008 | tf_op jit(solution)/shard_map/ppermute | solution.py:287
  44.6 1.8 %add.1 = f32[80,16,128]{2,1,0:T(8,128)} custom-call(f32[80,16,128]{2,1,0:T(8,128)S(1)} %home.1.part, bf16[31,16,128]{2,1,0:T(8,128)(2,1)S(1)} %collective-permute-done.7.refs_0_, bf16[31,16,128]{2,1,0:T(8,128)(2,1)S(1)} %collective-permute-done.8.refs_1_, bf16[31,16,128]{2,1,0:T(8,128)(2,1)S(1)} %collective-permute-done.9.refs_2_, ...), custom_call_target="tpu_custom_call" | custom-call | bytes 4194304 | tf_op jit(solution)/shard_map/add/pallas_call | solution.py:342
Async XLA Ops:
  0.0 11.2 %collective-permute-start = (bf16[80,16,128]{2,1,0:T(8,128)(2,1)}, bf16[80,16,128]{2,1,0:T(8,128)(2,1)S(1)}, u32[]{:S(2)}, u32[]{:S(2)}) collective-permute-start(bf16[80,16,128]{2,1,0:T(8,128)(2,1)} %latent.1), channel_id=1, source_target_pairs={{0,4},{1,5},{2,6},{3,7},{4,8},{5,9},{6,10},{7,11},{8,12},{9,13},{1... | collective-permute-start | bytes 983048 | tf_op jit(solution)/shard_map/ppermute | solution.py:287
  4.2 6.9 %collective-permute-start.1 = (s32[1,128]{1,0:T(1,128)S(1)}, s32[1,128]{1,0:T(1,128)S(1)}, u32[]{:S(2)}, u32[]{:S(2)}) collective-permute-start(s32[1,128]{1,0:T(1,128)S(1)} %get-tuple-element.24.asked.asked_row), channel_id=1, source_target_pairs={{0,3},{1,0},{2,1},{3,2},{4,7},{5,4},{6,5},{7,6},{8,11},{9,8},{10,9... | collective-permute-start | bytes 1544 | tf_op jit(solution)/shard_map/ppermute | solution.py:287
  5.2 5.9 %collective-permute-start.2 = (s32[1,128]{1,0:T(1,128)S(1)}, s32[1,128]{1,0:T(1,128)S(1)}, u32[]{:S(2)}, u32[]{:S(2)}) collective-permute-start(s32[1,128]{1,0:T(1,128)S(1)} %get-tuple-element.24.asked.asked_row), channel_id=1, source_target_pairs={{0,2},{1,3},{2,0},{3,1},{4,6},{5,7},{6,4},{7,5},{8,10},{9,11},{10,... | collective-permute-start | bytes 1544 | tf_op jit(solution)/shard_map/ppermute | solution.py:287
  5.5 5.7 %collective-permute-start.3 = (s32[1,128]{1,0:T(1,128)S(1)}, s32[1,128]{1,0:T(1,128)S(1)}, u32[]{:S(2)}, u32[]{:S(2)}) collective-permute-start(s32[1,128]{1,0:T(1,128)S(1)} %get-tuple-element.24.asked.asked_row), channel_id=1, source_target_pairs={{4,0},{5,1},{6,2},{7,3},{8,4},{9,5},{10,6},{11,7},{12,8},{13,9},{1... | collective-permute-start | bytes 1544 | tf_op jit(solution)/shard_map/ppermute | solution.py:287
  11.9 9.7 %collective-permute-start.4 = (bf16[30,16,128]{2,1,0:T(8,128)(2,1)S(1)}, bf16[30,16,128]{2,1,0:T(8,128)(2,1)S(1)}, u32[]{:S(2)}, u32[]{:S(2)}) collective-permute-start(bf16[30,16,128]{2,1,0:T(8,128)(2,1)S(1)} %get-tuple-element.30), channel_id=1, source_target_pairs={{0,2},{1,3},{2,0},{3,1},{4,6},{5,7},{6,4},{7,5},{8,10},{9,11},{10,... | collective-permute-start | bytes 368648 | tf_op jit(solution)/shard_map/ppermute | solution.py:287
  13.2 8.4 %collective-permute-start.5 = (bf16[30,16,128]{2,1,0:T(8,128)(2,1)S(1)}, bf16[30,16,128]{2,1,0:T(8,128)(2,1)S(1)}, u32[]{:S(2)}, u32[]{:S(2)}) collective-permute-start(bf16[30,16,128]{2,1,0:T(8,128)(2,1)S(1)} %get-tuple-element.31), channel_id=1, source_target_pairs={{0,1},{1,2},{2,3},{3,0},{4,5},{5,6},{6,7},{7,4},{8,9},{9,10},{10,1... | collective-permute-start | bytes 368648 | tf_op jit(solution)/shard_map/ppermute | solution.py:287
  14.8 6.8 %collective-permute-start.6 = (bf16[30,16,128]{2,1,0:T(8,128)(2,1)S(1)}, bf16[30,16,128]{2,1,0:T(8,128)(2,1)S(1)}, u32[]{:S(2)}, u32[]{:S(2)}) collective-permute-start(bf16[30,16,128]{2,1,0:T(8,128)(2,1)S(1)} %get-tuple-element.32), channel_id=1, source_target_pairs={{4,8},{5,9},{6,10},{7,11},{8,12},{9,13},{10,14},{11,15},{20,24},{2... | collective-permute-start | bytes 368648 | tf_op jit(solution)/shard_map/ppermute | solution.py:287
  28.2 11.8 %collective-permute-start.7 = (bf16[31,16,128]{2,1,0:T(8,128)(2,1)S(1)}, bf16[31,16,128]{2,1,0:T(8,128)(2,1)S(1)}, u32[]{:S(2)}, u32[]{:S(2)}) collective-permute-start(bf16[31,16,128]{2,1,0:T(8,128)(2,1)S(1)} %get-tuple-element.37), channel_id=1, source_target_pairs={{8,0},{9,1},{10,2},{11,3},{12,4},{13,5},{14,6},{15,7},{24,16},{25,... | collective-permute-start | bytes 380936 | tf_op jit(solution)/shard_map/ppermute | solution.py:287
  29.5 10.5 %collective-permute-start.8 = (bf16[31,16,128]{2,1,0:T(8,128)(2,1)S(1)}, bf16[31,16,128]{2,1,0:T(8,128)(2,1)S(1)}, u32[]{:S(2)}, u32[]{:S(2)}) collective-permute-start(bf16[31,16,128]{2,1,0:T(8,128)(2,1)S(1)} %get-tuple-element.38), channel_id=1, source_target_pairs={{4,0},{5,1},{6,2},{7,3},{8,4},{9,5},{10,6},{11,7},{12,8},{13,9},{1... | collective-permute-start | bytes 380936 | tf_op jit(solution)/shard_map/ppermute | solution.py:287
  31.4 11.6 %collective-permute-start.9 = (bf16[31,16,128]{2,1,0:T(8,128)(2,1)S(1)}, bf16[31,16,128]{2,1,0:T(8,128)(2,1)S(1)}, u32[]{:S(2)}, u32[]{:S(2)}) collective-permute-start(bf16[31,16,128]{2,1,0:T(8,128)(2,1)S(1)} %get-tuple-element.39), channel_id=1, source_target_pairs={{2,0},{3,1},{4,2},{5,3},{6,4},{7,5},{8,6},{9,7},{10,8},{11,9},{12,... | collective-permute-start | bytes 380936 | tf_op jit(solution)/shard_map/ppermute | solution.py:287
  33.9 10.6 %collective-permute-start.10 = (bf16[31,16,128]{2,1,0:T(8,128)(2,1)S(1)}, bf16[31,16,128]{2,1,0:T(8,128)(2,1)S(1)}, u32[]{:S(2)}, u32[]{:S(2)}) collective-permute-start(bf16[31,16,128]{2,1,0:T(8,128)(2,1)S(1)} %get-tuple-element.40), channel_id=1, source_target_pairs={{1,0},{2,1},{3,2},{4,3},{5,4},{6,5},{7,6},{8,7},{9,8},{10,9},{11,1... | collective-permute-start | bytes 380936 | tf_op jit(solution)/shard_map/ppermute | solution.py:287

commit v8 on v6

--- a/solution.py
+++ b/solution.py
@@ -89,58 +89,54 @@
     return both[:samples, :wide], both[samples:, wide:]
 
 
-def local_means(leaves, home, rows, weights, left, first):
+def local_means(home, rows, latent_rows, weights, held, left, sem, first):
     fan, width = weights.shape[1], weights.shape[2]
-    for i in leaves:
-        means = paired(
-            beside([rows[home[k, i]] for k in range(fan)]),
-            beside([rows[home[k, i + 1]] for k in range(fan)]),
-            weights[i].reshape(fan * width, width),
-            weights[i + 1].reshape(fan * width, width),
-        )
-        for j, mean in zip((i, i + 1), means):
-            left[j - first] = rows[j].astype(jnp.float32) - mean
-
-
-def fetches(weights, held, sem, first, leaves):
-    parts = [(at, pl.ds(at, CHUNK)) for at in range(first, first + leaves, CHUNK)]
-    return [
-        (range(at, at + CHUNK, 2), pltpu.make_async_copy(weights.at[p], held.at[p], sem.at[n]))
-        for n, (at, p) in enumerate(parts)
-    ]
+    leaves = left.shape[0]
+
+    def fetch(c):
+        part = pl.ds(first + c * CHUNK, CHUNK)
+        return pltpu.make_async_copy(weights.at[part], held.at[part], sem.at[c])
+
+    for c in range(leaves // CHUNK):
+        fetch(c).start()
+    latent_rows()
+
+    def some(c, carry):
+        fetch(c).wait()
+        for u in range(CHUNK):
+            i = first + c * CHUNK + u
+            mean = jnp.dot(
+                beside([rows[home[k, i]] for k in range(fan)]),
+                held[i].reshape(fan * width, width), preferred_element_type=jnp.float32,
+            )
+            left[c * CHUNK + u] = rows[i].astype(jnp.float32) - mean
+        return carry
+
+    lax.fori_loop(0, leaves // CHUNK, some, 0)
 
 
 def early_kernel(home, latent, weights, left, held_w, rows, row_sem, w_sem):
-    leaf_dev, half = latent.shape[0], left.shape[0]
+    leaf_dev = latent.shape[0]
     fetch_rows = pltpu.make_async_copy(latent, rows.at[pl.ds(0, leaf_dev)], row_sem)
     fetch_rows.start()
-    parts = fetches(weights, held_w, w_sem, 0, half)
-    for _, fetch in parts:
-        fetch.start()
-    rows[leaf_dev] = jnp.zeros(latent.shape[1:], latent.dtype)
-    fetch_rows.wait()
-    for leaves, fetch in parts:
-        fetch.wait()
-        local_means(leaves, home, rows, held_w, left, 0)
+
+    def latent_rows():
+        rows[leaf_dev] = jnp.zeros(latent.shape[1:], latent.dtype)
+        fetch_rows.wait()
+
+    local_means(home, rows, latent_rows, weights, held_w, left, w_sem, 0)
 
 
 def late_kernel(
     home, rows, before, partly_held, weights, factor, left, held_w, held_f, w_sem, f_sem
 ):
-    leaf_dev, half = weights.shape[0], left.shape[0]
-    first = leaf_dev - half
-    parts = fetches(weights, held_w, w_sem, first, half)
-    for _, fetch in parts:
-        fetch.start()
     fetch_factor = pltpu.make_async_copy(factor, held_f, f_sem)
-    fetch_factor.start()
-    for leaves, fetch in parts:
-        fetch.wait()
-        local_means(leaves, home, rows, held_w, left, first)
+    first = weights.shape[0] - left.shape[0]
+    local_means(home, rows, fetch_factor.start, weights, held_w, left, w_sem, first)
     fetch_factor.wait()
 
 
-def serve_kernel(capacity, ask8, ask2, ask1, latent, before, left, out8, out2, out1):
+def serve_kernel(capacity, ask1, ask2, ask8, latent, before, left, out8, out2, out1):
     me = lax.axis_index("kx")
     def pick(o, ask, rows, out):
         for r in range(capacity):
@@ -175,7 +171,7 @@
 
 
 def remote_kernel(
-    capacity, asked, slots, asked_row, left, later, before, from8, from2, from1,
+    capacity, asked, slots, asked_row, left, later, before, from2, from8, from1,
     weights, factor, back, low, out8, out4, out2, out1, resid,
 ):
     leaf_dev, half = back.shape[0], left.shape[0]
@@ -225,13 +221,12 @@
 
     def some(c, carry):
         found = []
-        for u in range(0, LEAVES, 2):
+        for u in range(LEAVES):
             i = c * LEAVES + u
-            found += zip((i, i + 1), paired(
-                low[i], low[i + 1],
-                weights[i].reshape(fan * width, width),
-                weights[i + 1].reshape(fan * width, width), True,
-            ))
+            found.append((i, lax.dot_general(
+                low[i], weights[i].reshape(fan * width, width), BY_ROWS,
+                preferred_element_type=jnp.float32,
+            )))
         for i, x in found:
             for k in range(fan):
                 j = home[k, i]
@@ -313,7 +308,7 @@
     serve8, serve2, serve1 = call(
         functools.partial(serve_kernel, capacity), "serve", (some_rows,) * 3,
         [SMEM] * 3 + [VMEM] * 2 + [ANY], [VMEM] * 3, 4, moved=4 * MIB,
-    )(ask8, ask2, ask1, rows, before, left)
+    )(ask1, ask2, ask8, rows, before, left)
     from8 = passed(serve8, [(i, i + 4) for i in everyone if i >= 4 and i + 4 < devices])
     from2 = passed(serve2, [(i, i ^ 2) for i in everyone])
     from1 = passed(serve1, [(i, i // 4 * 4 + (i + 1) % 4) for i in everyone])
@@ -334,7 +329,7 @@
         (all_rows, shape((leaf_dev + 8, samples, width), jnp.bfloat16)) + (sent,) * 4,
         [SMEM] * 2 + [VMEM] * 9, [VMEM] * 6, 8, moved=heavy,
         scratch=[VMEM((leaf_dev + 8, samples, width), jnp.float32)],
-    )(asked, slots, asked, left, later, before, from8, from2, from1, held_w, held_f)
+    )(asked, slots, asked, left, later, before, from2, from8, from1, held_w, held_f)
     returned = [
         passed(x, [(i, i - reach) for i in everyone if i >= reach])
         for reach, x in ((8, out8), (4, out4), (2, out2), (1, out1))

time: 45.2 us -> 44.9 us (level)
  starting transfers between devices: 22.4 us -> 21.1 us
  waiting for transfers between devices: 3.02 us -> 3.87 us
    ppermute x11, starting transfers between devices: 22.4 us -> 21.1 us  [passed(): return lax.ppermute(x, 'kx', route)]
    ppermute x11, waiting for transfers between devices: 3.02 us -> 3.87 us  [passed(): return lax.ppermute(x, 'kx', route)]
where the time goes in v8:
time: 44.9 us; the launch traced here: 44.7 us
  starting transfers between devices  21.1 us (47%)
  Pallas kernels  19.5 us (43%)
  waiting for transfers between devices  3.87 us (9%)
    ppermute x11, starting transfers between devices, passed(): return lax.ppermute(x, 'kx', route)  21.1 us
    pallas_call x1, Pallas kernels, per_device(): call(functools.partial(remote_kernel, capacity), 'remote', (all_rows, sha...  4.85 us
    pallas_call x1, Pallas kernels, per_device(): call(home_kernel, 'home', (all_rows,), [SMEM] + [VMEM] * 3, [VMEM], 6, mo...  4.03 us
    ppermute x11, waiting for transfers between devices, passed(): return lax.ppermute(x, 'kx', route)  3.87 us
    pallas_call x1, Pallas kernels, per_device(): call(early_kernel, 'early', (shape((half, samples, width), jnp.float32),...  3.6 us
    pallas_call x1, Pallas kernels, per_device(): call(late_kernel, 'late', (shape((leaf_dev - half, samples, width), jnp.f...  3.56 us
    pallas_call x1, Pallas kernels, per_device(): call(functools.partial(add_kernel, capacity, (3, 2, 1, 0)), 'add', (all_r...  1.84 us
    pallas_call x1, Pallas kernels, per_device(): call(index_kernel, 'index', (one_list, shape((2, 4 * SLOTS), jnp.int32),...  1.01 us
  transfers between devices with their start and end apart: 11, of which 2 were waited for; matrix products, arithmetic and copies ran while one was open for 0% of the time, Pallas kernels for 27%

profile of v8, /device:TPU:15, one launch (start us, length us, event | category | flops | bytes accessed | tf_op | source)
XLA Modules:
  0.0 44.7 jit_solution(14173603296028585997)
XLA Ops:
  0.0 3.2 %collective-permute-start = (bf16[80,16,128]{2,1,0:T(8,128)(2,1)}, bf16[80,16,128]{2,1,0:T(8,128)(2,1)S(1)}, u32[]{:S(2)}, u32[]{:S(2)}) collective-permute-start(bf16[80,16,128]{2,1,0:T(8,128)(2,1)} %latent.1), channel_id=1, source_target_pairs={{0,4},{1,5},{2,6},{3,7},{4,8},{5,9},{6,10},{7,11},{8,12},{9,13},{1... | collective-permute-start | bytes 983048 | tf_op jit(solution)/shard_map/ppermute | solution.py:287
  3.2 1.0 %index.1 = (s32[1,128]{1,0:T(1,128)S(1)}, s32[2,128]{1,0:T(2,128)S(1)}, s32[3,80]{1,0:T(4,128)S(1)}) custom-call(s32[3,80]{1,0:T(4,128)} %bitcast.1), custom_call_target="tpu_custom_call" | custom-call | bytes 2097152 | tf_op jit(solution)/shard_map/index/pallas_call | solution.py:290
  4.2 1.0 %collective-permute-start.1 = (s32[1,128]{1,0:T(1,128)S(1)}, s32[1,128]{1,0:T(1,128)S(1)}, u32[]{:S(2)}, u32[]{:S(2)}) collective-permute-start(s32[1,128]{1,0:T(1,128)S(1)} %get-tuple-element.24.asked.asked_row), channel_id=1, source_target_pairs={{0,3},{1,0},{2,1},{3,2},{4,7},{5,4},{6,5},{7,6},{8,11},{9,8},{10,9... | collective-permute-start | bytes 1544 | tf_op jit(solution)/shard_map/ppermute | solution.py:287
  5.2 0.2 collective-permute-start.2
  5.5 2.1 %collective-permute-start.3 = (s32[1,128]{1,0:T(1,128)S(1)}, s32[1,128]{1,0:T(1,128)S(1)}, u32[]{:S(2)}, u32[]{:S(2)}) collective-permute-start(s32[1,128]{1,0:T(1,128)S(1)} %get-tuple-element.24.asked.asked_row), channel_id=1, source_target_pairs={{4,0},{5,1},{6,2},{7,3},{8,4},{9,5},{10,6},{11,7},{12,8},{13,9},{1... | collective-permute-start | bytes 1544 | tf_op jit(solution)/shard_map/ppermute | solution.py:287
  7.6 3.6 %early.1 = (f32[40,16,128]{2,1,0:T(8,128)S(1)}, bf16[80,3,128,128]{3,2,1,0:T(8,128)(2,1)S(1)}, bf16[88,16,128]{2,1,0:T(8,128)(2,1)S(1)}) custom-call(s32[3,80]{1,0:T(4,128)S(1)} %get-tuple-element.23.home, bf16[80,16,128]{2,1,0:T(8,128)(2,1)} %latent.1, bf16[80,3,128,128]{3,2,1,0:T(8,128)(2,1)} %weights.3), custom_call_target="tpu_custom_call" | custom-call | bytes 3932160 | tf_op jit(solution)/shard_map/early/pallas_call | solution.py:299
  11.2 0.0 collective-permute-done.1.ask1
  11.2 0.0 collective-permute-done.2.ask2
  11.2 0.0 collective-permute-done.3.ask8
  11.2 0.0 collective-permute-done.before
  11.2 0.6 %serve.1 = (bf16[30,16,128]{2,1,0:T(8,128)(2,1)S(1)}, bf16[30,16,128]{2,1,0:T(8,128)(2,1)S(1)}, bf16[30,16,128]{2,1,0:T(8,128)(2,1)S(1)}) custom-call(s32[1,128]{1,0:T(1,128)S(1)} %collective-permute-done.1.ask1, s32[1,128]{1,0:T(1,128)S(1)} %collective-permute-done.2.ask2, s32[1,128]{1,0:T(1,128)S(1)} %collective-permute-done.3.ask8, ...), custom_call_target="tpu_custom_call" | custom-call | bytes 4194304 | tf_op jit(solution)/shard_map/serve/pallas_call | solution.py:308
  11.9 1.3 %collective-permute-start.4 = (bf16[30,16,128]{2,1,0:T(8,128)(2,1)S(1)}, bf16[30,16,128]{2,1,0:T(8,128)(2,1)S(1)}, u32[]{:S(2)}, u32[]{:S(2)}) collective-permute-start(bf16[30,16,128]{2,1,0:T(8,128)(2,1)S(1)} %get-tuple-element.30), channel_id=1, source_target_pairs={{0,2},{1,3},{2,0},{3,1},{4,6},{5,7},{6,4},{7,5},{8,10},{9,11},{10,... | collective-permute-start | bytes 368648 | tf_op jit(solution)/shard_map/ppermute | solution.py:287
  13.2 3.2 %collective-permute-start.5 = (bf16[30,16,128]{2,1,0:T(8,128)(2,1)S(1)}, bf16[30,16,128]{2,1,0:T(8,128)(2,1)S(1)}, u32[]{:S(2)}, u32[]{:S(2)}) collective-permute-start(bf16[30,16,128]{2,1,0:T(8,128)(2,1)S(1)} %get-tuple-element.31), channel_id=1, source_target_pairs={{4,8},{5,9},{6,10},{7,11},{8,12},{9,13},{10,14},{11,15},{20,24},{2... | collective-permute-start | bytes 368648 | tf_op jit(solution)/shard_map/ppermute | solution.py:287
  16.4 2.0 %collective-permute-start.6 = (bf16[30,16,128]{2,1,0:T(8,128)(2,1)S(1)}, bf16[30,16,128]{2,1,0:T(8,128)(2,1)S(1)}, u32[]{:S(2)}, u32[]{:S(2)}) collective-permute-start(bf16[30,16,128]{2,1,0:T(8,128)(2,1)S(1)} %get-tuple-element.32), channel_id=1, source_target_pairs={{0,1},{1,2},{2,3},{3,0},{4,5},{5,6},{6,7},{7,4},{8,9},{9,10},{10,1... | collective-permute-start | bytes 368648 | tf_op jit(solution)/shard_map/ppermute | solution.py:287
  18.3 3.6 %late.1 = (f32[40,16,128]{2,1,0:T(8,128)S(1)}, bf16[80,3,128,128]{3,2,1,0:T(8,128)(2,1)S(1)}, bf16[80,128,128]{2,1,0:T(8,128)(2,1)S(1)}) custom-call(s32[3,80]{1,0:T(4,128)S(1)} %get-tuple-element.23.home, bf16[88,16,128]{2,1,0:T(8,128)(2,1)S(1)} %get-tuple-element.27.rows.latent, ...), custom_call_target="tpu_custom_call", output_to_operand_aliasing={{1}: (3, {})} | custom-call | bytes 3932160 | tf_op jit(solution)/shard_map/late/pallas_call | solution.py:315
  21.9 0.0 collective-permute-done.4.from2
  21.9 0.0 collective-permute-done.5.from8
  21.9 0.0 collective-permute-done.6.from1
  21.9 4.9 %remote.1 = (f32[80,16,128]{2,1,0:T(8,128)S(1)}, bf16[88,16,128]{2,1,0:T(8,128)(2,1)S(1)}, bf16[31,16,128]{2,1,0:T(8,128)(2,1)S(1)}, bf16[31,16,128]{2,1,0:T(8,1...) custom-call(s32[1,128]{1,0:T(1,128)S(1)} %get-tuple-element.24.asked.asked_row, ...), custom_call_target="tpu_custom_call" | custom-call | bytes 7864320 | tf_op jit(solution)/shard_map/remote/pallas_call | solution.py:327
  26.8 1.3 %collective-permute-start.7 = (bf16[31,16,128]{2,1,0:T(8,128)(2,1)S(1)}, bf16[31,16,128]{2,1,0:T(8,128)(2,1)S(1)}, u32[]{:S(2)}, u32[]{:S(2)}) collective-permute-start(bf16[31,16,128]{2,1,0:T(8,128)(2,1)S(1)} %get-tuple-element.37), channel_id=1, source_target_pairs={{8,0},{9,1},{10,2},{11,3},{12,4},{13,5},{14,6},{15,7},{24,16},{25,... | collective-permute-start | bytes 380936 | tf_op jit(solution)/shard_map/ppermute | solution.py:287
  28.1 1.9 %collective-permute-start.8 = (bf16[31,16,128]{2,1,0:T(8,128)(2,1)S(1)}, bf16[31,16,128]{2,1,0:T(8,128)(2,1)S(1)}, u32[]{:S(2)}, u32[]{:S(2)}) collective-permute-start(bf16[31,16,128]{2,1,0:T(8,128)(2,1)S(1)} %get-tuple-element.38), channel_id=1, source_target_pairs={{4,0},{5,1},{6,2},{7,3},{8,4},{9,5},{10,6},{11,7},{12,8},{13,9},{1... | collective-permute-start | bytes 380936 | tf_op jit(solution)/shard_map/ppermute | solution.py:287
  30.0 2.5 %collective-permute-start.9 = (bf16[31,16,128]{2,1,0:T(8,128)(2,1)S(1)}, bf16[31,16,128]{2,1,0:T(8,128)(2,1)S(1)}, u32[]{:S(2)}, u32[]{:S(2)}) collective-permute-start(bf16[31,16,128]{2,1,0:T(8,128)(2,1)S(1)} %get-tuple-element.39), channel_id=1, source_target_pairs={{2,0},{3,1},{4,2},{5,3},{6,4},{7,5},{8,6},{9,7},{10,8},{11,9},{12,... | collective-permute-start | bytes 380936 | tf_op jit(solution)/shard_map/ppermute | solution.py:287
  32.5 2.4 %collective-permute-start.10 = (bf16[31,16,128]{2,1,0:T(8,128)(2,1)S(1)}, bf16[31,16,128]{2,1,0:T(8,128)(2,1)S(1)}, u32[]{:S(2)}, u32[]{:S(2)}) collective-permute-start(bf16[31,16,128]{2,1,0:T(8,128)(2,1)S(1)} %get-tuple-element.40), channel_id=1, source_target_pairs={{1,0},{2,1},{3,2},{4,3},{5,4},{6,5},{7,6},{8,7},{9,8},{10,9},{11,1... | collective-permute-start | bytes 380936 | tf_op jit(solution)/shard_map/ppermute | solution.py:287
  34.9 4.0 %home.1.part = f32[80,16,128]{2,1,0:T(8,128)S(1)} custom-call(s32[3,80]{1,0:T(4,128)S(1)} %get-tuple-element.23.home, f32[80,16,128]{2,1,0:T(8,128)S(1)} %get-tuple-element.35.back, bf16[88,16,128]{2,1,0:T(8,128)(2,1)S(1)} %get-tuple-element.36.low, bf16[80,3,128,128]{3,2,1,0:T(8,128)(2,1)S(1)} %get-tuple-element.33.weights), custom_call_target="tpu_custom_call" | custom-call | bytes 7864320 | tf_op jit(solution)/shard_map/home/pallas_call | solution.py:337
  39.0 0.0 collective-permute-done.7.refs_0_
  39.0 0.0 collective-permute-done.8.refs_1_
  39.0 2.5 %collective-permute-done.9.refs_2_ = bf16[31,16,128]{2,1,0:T(8,128)(2,1)S(1)} collective-permute-done((bf16[31,16,128]{2,1,0:T(8,128)(2,1)S(1)}, bf16[31,16,128]{2,1,0:T(8,128)(2,1)S(1)}, u32[]{:S(2)}, u32[]{:S(2)}) %collective-permute-start.9) | collective-permute-done | bytes 127008 | tf_op jit(solution)/shard_map/ppermute | solution.py:287
  41.5 1.4 %collective-permute-done.10.refs_3_ = bf16[31,16,128]{2,1,0:T(8,128)(2,1)S(1)} collective-permute-done((bf16[31,16,128]{2,1,0:T(8,128)(2,1)S(1)}, bf16[31,16,128]{2,1,0:T(8,128)(2,1)S(1)}, u32[]{:S(2)}, u32[]{:S(2)}) %collective-permute-start.10) | collective-permute-done | bytes 127008 | tf_op jit(solution)/shard_map/ppermute | solution.py:287
  42.8 1.8 %add.1 = f32[80,16,128]{2,1,0:T(8,128)} custom-call(f32[80,16,128]{2,1,0:T(8,128)S(1)} %home.1.part, bf16[31,16,128]{2,1,0:T(8,128)(2,1)S(1)} %collective-permute-done.7.refs_0_, bf16[31,16,128]{2,1,0:T(8,128)(2,1)S(1)} %collective-permute-done.8.refs_1_, bf16[31,16,128]{2,1,0:T(8,128)(2,1)S(1)} %collective-permute-done.9.refs_2_, ...), custom_call_target="tpu_custom_call" | custom-call | bytes 4194304 | tf_op jit(solution)/shard_map/add/pallas_call | solution.py:342
Async XLA Ops:
  0.0 11.2 %collective-permute-start = (bf16[80,16,128]{2,1,0:T(8,128)(2,1)}, bf16[80,16,128]{2,1,0:T(8,128)(2,1)S(1)}, u32[]{:S(2)}, u32[]{:S(2)}) collective-permute-start(bf16[80,16,128]{2,1,0:T(8,128)(2,1)} %latent.1), channel_id=1, source_target_pairs={{0,4},{1,5},{2,6},{3,7},{4,8},{5,9},{6,10},{7,11},{8,12},{9,13},{1... | collective-permute-start | bytes 983048 | tf_op jit(solution)/shard_map/ppermute | solution.py:287
  4.2 6.9 %collective-permute-start.1 = (s32[1,128]{1,0:T(1,128)S(1)}, s32[1,128]{1,0:T(1,128)S(1)}, u32[]{:S(2)}, u32[]{:S(2)}) collective-permute-start(s32[1,128]{1,0:T(1,128)S(1)} %get-tuple-element.24.asked.asked_row), channel_id=1, source_target_pairs={{0,3},{1,0},{2,1},{3,2},{4,7},{5,4},{6,5},{7,6},{8,11},{9,8},{10,9... | collective-permute-start | bytes 1544 | tf_op jit(solution)/shard_map/ppermute | solution.py:287
  5.2 5.9 %collective-permute-start.2 = (s32[1,128]{1,0:T(1,128)S(1)}, s32[1,128]{1,0:T(1,128)S(1)}, u32[]{:S(2)}, u32[]{:S(2)}) collective-permute-start(s32[1,128]{1,0:T(1,128)S(1)} %get-tuple-element.24.asked.asked_row), channel_id=1, source_target_pairs={{0,2},{1,3},{2,0},{3,1},{4,6},{5,7},{6,4},{7,5},{8,10},{9,11},{10,... | collective-permute-start | bytes 1544 | tf_op jit(solution)/shard_map/ppermute | solution.py:287
  5.5 5.7 %collective-permute-start.3 = (s32[1,128]{1,0:T(1,128)S(1)}, s32[1,128]{1,0:T(1,128)S(1)}, u32[]{:S(2)}, u32[]{:S(2)}) collective-permute-start(s32[1,128]{1,0:T(1,128)S(1)} %get-tuple-element.24.asked.asked_row), channel_id=1, source_target_pairs={{4,0},{5,1},{6,2},{7,3},{8,4},{9,5},{10,6},{11,7},{12,8},{13,9},{1... | collective-permute-start | bytes 1544 | tf_op jit(solution)/shard_map/ppermute | solution.py:287
  11.9 10.0 %collective-permute-start.4 = (bf16[30,16,128]{2,1,0:T(8,128)(2,1)S(1)}, bf16[30,16,128]{2,1,0:T(8,128)(2,1)S(1)}, u32[]{:S(2)}, u32[]{:S(2)}) collective-permute-start(bf16[30,16,128]{2,1,0:T(8,128)(2,1)S(1)} %get-tuple-element.30), channel_id=1, source_target_pairs={{0,2},{1,3},{2,0},{3,1},{4,6},{5,7},{6,4},{7,5},{8,10},{9,11},{10,... | collective-permute-start | bytes 368648 | tf_op jit(solution)/shard_map/ppermute | solution.py:287
  13.2 8.7 %collective-permute-start.5 = (bf16[30,16,128]{2,1,0:T(8,128)(2,1)S(1)}, bf16[30,16,128]{2,1,0:T(8,128)(2,1)S(1)}, u32[]{:S(2)}, u32[]{:S(2)}) collective-permute-start(bf16[30,16,128]{2,1,0:T(8,128)(2,1)S(1)} %get-tuple-element.31), channel_id=1, source_target_pairs={{4,8},{5,9},{6,10},{7,11},{8,12},{9,13},{10,14},{11,15},{20,24},{2... | collective-permute-start | bytes 368648 | tf_op jit(solution)/shard_map/ppermute | solution.py:287
  16.4 5.6 %collective-permute-start.6 = (bf16[30,16,128]{2,1,0:T(8,128)(2,1)S(1)}, bf16[30,16,128]{2,1,0:T(8,128)(2,1)S(1)}, u32[]{:S(2)}, u32[]{:S(2)}) collective-permute-start(bf16[30,16,128]{2,1,0:T(8,128)(2,1)S(1)} %get-tuple-element.32), channel_id=1, source_target_pairs={{0,1},{1,2},{2,3},{3,0},{4,5},{5,6},{6,7},{7,4},{8,9},{9,10},{10,1... | collective-permute-start | bytes 368648 | tf_op jit(solution)/shard_map/ppermute | solution.py:287
  26.8 12.2 %collective-permute-start.7 = (bf16[31,16,128]{2,1,0:T(8,128)(2,1)S(1)}, bf16[31,16,128]{2,1,0:T(8,128)(2,1)S(1)}, u32[]{:S(2)}, u32[]{:S(2)}) collective-permute-start(bf16[31,16,128]{2,1,0:T(8,128)(2,1)S(1)} %get-tuple-element.37), channel_id=1, source_target_pairs={{8,0},{9,1},{10,2},{11,3},{12,4},{13,5},{14,6},{15,7},{24,16},{25,... | collective-permute-start | bytes 380936 | tf_op jit(solution)/shard_map/ppermute | solution.py:287
  28.1 10.9 %collective-permute-start.8 = (bf16[31,16,128]{2,1,0:T(8,128)(2,1)S(1)}, bf16[31,16,128]{2,1,0:T(8,128)(2,1)S(1)}, u32[]{:S(2)}, u32[]{:S(2)}) collective-permute-start(bf16[31,16,128]{2,1,0:T(8,128)(2,1)S(1)} %get-tuple-element.38), channel_id=1, source_target_pairs={{4,0},{5,1},{6,2},{7,3},{8,4},{9,5},{10,6},{11,7},{12,8},{13,9},{1... | collective-permute-start | bytes 380936 | tf_op jit(solution)/shard_map/ppermute | solution.py:287
  30.0 11.5 %collective-permute-start.9 = (bf16[31,16,128]{2,1,0:T(8,128)(2,1)S(1)}, bf16[31,16,128]{2,1,0:T(8,128)(2,1)S(1)}, u32[]{:S(2)}, u32[]{:S(2)}) collective-permute-start(bf16[31,16,128]{2,1,0:T(8,128)(2,1)S(1)} %get-tuple-element.39), channel_id=1, source_target_pairs={{2,0},{3,1},{4,2},{5,3},{6,4},{7,5},{8,6},{9,7},{10,8},{11,9},{12,... | collective-permute-start | bytes 380936 | tf_op jit(solution)/shard_map/ppermute | solution.py:287
  32.5 10.3 %collective-permute-start.10 = (bf16[31,16,128]{2,1,0:T(8,128)(2,1)S(1)}, bf16[31,16,128]{2,1,0:T(8,128)(2,1)S(1)}, u32[]{:S(2)}, u32[]{:S(2)}) collective-permute-start(bf16[31,16,128]{2,1,0:T(8,128)(2,1)S(1)} %get-tuple-element.40), channel_id=1, source_target_pairs={{1,0},{2,1},{3,2},{4,3},{5,4},{6,5},{7,6},{8,7},{9,8},{10,9},{11,1... | collective-permute-start | bytes 380936 | tf_op jit(solution)/shard_map/ppermute | solution.py:287

commit v9 on v8

--- a/solution.py
+++ b/solution.py
@@ -8,15 +8,29 @@
 from jax.sharding import PartitionSpec as P
 
 SLOTS = 32
-CHUNK = 8
-LEAVES = 16
+PART = 16
+LEAVES = 40
 MIB = 2**20
 BY_ROWS = (((1,), (1,)), ((), ()))
 VMEM, SMEM, HBM, ANY = pltpu.VMEM, pltpu.SMEM, pltpu.HBM, pl.ANY
 
 
-def index_kernel(lists, asked, slots, home):
+def fetched(weights, held, sem, n):
+    part = pl.ds(n * PART, PART)
+    return pltpu.make_async_copy(weights.at[part], held.at[part], sem)
+
+
+def index_kernel(
+    lists, latent, weights, asked, slots, home, rows, held_w, row_sem, w_sem
+):
     fan, leaf_dev = lists.shape
+    fetches = (
+        pltpu.make_async_copy(latent, rows.at[pl.ds(0, leaf_dev)], row_sem),
+        fetched(weights, held_w, w_sem, 0),
+    )
+    for fetch in fetches:
+        fetch.start()
+    rows[leaf_dev] = jnp.zeros(latent.shape[1:], latent.dtype)
     me = lax.axis_index("kx")
     behind = me * leaf_dev - lists[...]
     kind = (
@@ -66,6 +80,8 @@
     asked[...] = total[0:1].astype(jnp.int32)
     slots[0:1] = jnp.where(total[3:4] > 0.0, total[1:2], float(leaf_dev)).astype(jnp.int32)
     slots[1:2] = total[2:3].astype(jnp.int32)
+    for fetch in fetches:
+        fetch.wait()
 
 
 def beside(xs):
@@ -89,50 +105,42 @@
     return both[:samples, :wide], both[samples:, wide:]
 
 
-def local_means(home, rows, latent_rows, weights, held, left, sem, first):
-    fan, width = weights.shape[1], weights.shape[2]
-    leaves = left.shape[0]
-
-    def fetch(c):
-        part = pl.ds(first + c * CHUNK, CHUNK)
-        return pltpu.make_async_copy(weights.at[part], held.at[part], sem.at[c])
-
-    for c in range(leaves // CHUNK):
-        fetch(c).start()
-    latent_rows()
-
-    def some(c, carry):
-        fetch(c).wait()
-        for u in range(CHUNK):
-            i = first + c * CHUNK + u
-            mean = jnp.dot(
-                beside([rows[home[k, i]] for k in range(fan)]),
-                held[i].reshape(fan * width, width), preferred_element_type=jnp.float32,
-            )
-            left[c * CHUNK + u] = rows[i].astype(jnp.float32) - mean
-        return carry
-
-    lax.fori_loop(0, leaves // CHUNK, some, 0)
-
-
-def early_kernel(home, latent, weights, left, held_w, rows, row_sem, w_sem):
-    leaf_dev = latent.shape[0]
-    fetch_rows = pltpu.make_async_copy(latent, rows.at[pl.ds(0, leaf_dev)], row_sem)
-    fetch_rows.start()
-
-    def latent_rows():
-        rows[leaf_dev] = jnp.zeros(latent.shape[1:], latent.dtype)
-        fetch_rows.wait()
-
-    local_means(home, rows, latent_rows, weights, held_w, left, w_sem, 0)
-
-
-def late_kernel(
-    home, rows, before, partly_held, weights, factor, left, held_w, held_f, w_sem, f_sem
-):
+def local_means(home, rows, held, left, first, leaves):
+    fan, width = held.shape[1], held.shape[2]
+    for i in leaves:
+        mean = jnp.dot(
+            beside([rows[home[k, i]] for k in range(fan)]),
+            held[i].reshape(fan * width, width), preferred_element_type=jnp.float32,
+        )
+        left[i - first] = rows[i].astype(jnp.float32) - mean
+
+
+def early_kernel(home, rows, held_part, weights, left, held_w, w_sem):
+    parts = left.shape[0] // PART
+    fetches = [fetched(weights, held_w, w_sem.at[n], n + 1) for n in range(parts)]
+    for fetch in fetches:
+        fetch.start()
+    for n in range(parts):
+        if n > 0:
+            fetches[n - 1].wait()
+        held = held_w if n > 0 else held_part
+        local_means(home, rows, held, left, 0, range(n * PART, (n + 1) * PART))
+    fetches[-1].wait()
+
+
+def late_kernel(home, rows, before, held_part, weights, factor, left, held_w, held_f, w_sem, f_sem):
+    parts, first = left.shape[0] // PART, weights.shape[0] - left.shape[0]
+    fetches = [fetched(weights, held_w, w_sem.at[n - 1], first // PART + n) for n in range(1, parts)]
     fetch_factor = pltpu.make_async_copy(factor, held_f, f_sem)
-    first = weights.shape[0] - left.shape[0]
-    local_means(home, rows, fetch_factor.start, weights, held_w, left, w_sem, first)
+    for fetch in fetches:
+        fetch.start()
+    fetch_factor.start()
+    for n in range(parts):
+        if n > 0:
+            fetches[n - 1].wait()
+        at = first + n * PART
+        held = held_w if n > 0 else held_part
+        local_means(home, rows, held, left, first, range(at, at + PART))
     fetch_factor.wait()
 
 
@@ -237,18 +245,24 @@
     part[...] = acc[pl.ds(0, leaf_dev)]
 
 
-def add_kernel(capacity, offsets, part, *refs):
-    returned, (out, listed, wanted, sem) = refs[: len(offsets)], refs[len(offsets) :]
-    for n, (o, rows) in enumerate(zip(offsets, returned)):
-        listed[n : n + 1] = rows[capacity].astype(jnp.float32)[0:1].astype(jnp.int32)
+def add_kernel(capacity, part, back8, ring, back4, back2, relayed, out, listed, wanted, sem):
+    last = lax.bitwise_and(lax.axis_index("kx"), 3) == 3
+
+    def back1(r):
+        return jnp.where(last, relayed[r].astype(jnp.float32), ring[r].astype(jnp.float32))
+
+    returned = [(3, back8), (2, back4), (1, back2)]
+    returned = [(o, lambda r, x=x: x[r].astype(jnp.float32)) for o, x in returned] + [(0, back1)]
+    for o, row in returned:
+        listed[o : o + 1] = row(capacity)[0:1].astype(jnp.int32)
     fetch = pltpu.make_async_copy(listed, wanted, sem)
     fetch.start()
     out[...] = part[...]
     fetch.wait()
-    for n, (o, rows) in enumerate(zip(offsets, returned)):
+    for o, row in returned:
         for r in range(capacity):
-            j = wanted[n, o * SLOTS + r]
-            out[j] = out[j] + rows[r].astype(jnp.float32)
+            j = wanted[o, o * SLOTS + r]
+            out[j] = out[j] + row(r)
 
 
 def call(body, name, out_shape, ins, outs, limit, flops=0, moved=0, scratch=(), aliases={}):
@@ -287,24 +301,26 @@
         return lax.ppermute(x, "kx", route)
 
     before = passed(latent, [(i, i + 4) for i in everyone if i + 4 < devices])
-    asked, slots, home = call(
+    held = shape(cond_weights.shape, jnp.bfloat16)
+    weights = placed(cond_weights, HBM)
+    dma = pltpu.SemaphoreType.DMA
+    asked, slots, home, rows, held_w = call(
         index_kernel, "index",
-        (one_list, shape((2, 4 * SLOTS), jnp.int32), shape((fan, leaf_dev), jnp.int32)),
-        [VMEM], [VMEM] * 3, 4, moved=2 * MIB,
-    )(placed(cond_lists.T, HBM))
+        (
+            one_list, shape((2, 4 * SLOTS), jnp.int32), shape((fan, leaf_dev), jnp.int32),
+            shape((leaf_dev + 8, samples, width), jnp.bfloat16), held,
+        ),
+        [VMEM, HBM, HBM], [VMEM] * 5, 14, moved=2 * MIB, scratch=[dma, dma],
+    )(placed(cond_lists.T, HBM), placed(latent, HBM), weights)
     ask8 = passed(asked, [(i, i - 4) for i in everyone if i >= 4])
     ask2 = passed(asked, [(i, i ^ 2) for i in everyone])
     ask1 = passed(asked, [(i, i // 4 * 4 + (i + 3) % 4) for i in everyone])
-    half = leaf_dev // 2
-    left, held_w, rows = call(
-        early_kernel, "early",
-        (
-            shape((half, samples, width), jnp.float32), shape(cond_weights.shape, jnp.bfloat16),
-            shape((leaf_dev + 8, samples, width), jnp.bfloat16),
-        ),
-        [SMEM, HBM, HBM], [VMEM] * 3, 14, moved=heavy // 2,
-        scratch=[pltpu.SemaphoreType.DMA, pltpu.SemaphoreType.DMA((half // CHUNK,))],
-    )(home, placed(latent, HBM), placed(cond_weights, HBM))
+    most = -(-leaf_dev // (2 * PART)) * PART
+    left, held_w = call(
+        early_kernel, "early", (shape((most, samples, width), jnp.float32), held),
+        [SMEM, VMEM, VMEM, HBM], [VMEM] * 2, 14, moved=heavy // 2,
+        scratch=[dma((most // PART,))], aliases={2: 1},
+    )(home, rows, held_w, weights)
     serve8, serve2, serve1 = call(
         functools.partial(serve_kernel, capacity), "serve", (some_rows,) * 3,
         [SMEM] * 3 + [VMEM] * 2 + [ANY], [VMEM] * 3, 4, moved=4 * MIB,
@@ -315,35 +331,33 @@
     later, held_w, held_f = call(
         late_kernel, "late",
         (
-            shape((leaf_dev - half, samples, width), jnp.float32),
-            shape(cond_weights.shape, jnp.bfloat16), shape(precision_factor.shape, jnp.bfloat16),
+            shape((leaf_dev - most, samples, width), jnp.float32), held,
+            shape(precision_factor.shape, jnp.bfloat16),
         ),
         [SMEM, VMEM, ANY, VMEM, HBM, HBM], [VMEM] * 3, 14, moved=heavy // 2,
-        scratch=[
-            pltpu.SemaphoreType.DMA(((leaf_dev - half) // CHUNK,)), pltpu.SemaphoreType.DMA
-        ],
-        aliases={3: 1},
-    )(home, rows, before, held_w, placed(cond_weights, HBM), placed(precision_factor, HBM))
+        scratch=[dma(((leaf_dev - most) // PART - 1,)), dma], aliases={3: 1},
+    )(home, rows, before, held_w, weights, placed(precision_factor, HBM))
     back, low, out8, out4, out2, out1 = call(
         functools.partial(remote_kernel, capacity), "remote",
         (all_rows, shape((leaf_dev + 8, samples, width), jnp.bfloat16)) + (sent,) * 4,
         [SMEM] * 2 + [VMEM] * 9, [VMEM] * 6, 8, moved=heavy,
         scratch=[VMEM((leaf_dev + 8, samples, width), jnp.float32)],
     )(asked, slots, asked, left, later, before, from2, from8, from1, held_w, held_f)
-    returned = [
-        passed(x, [(i, i - reach) for i in everyone if i >= reach])
-        for reach, x in ((8, out8), (4, out4), (2, out2), (1, out1))
-    ]
+    def back_by(x, reach):
+        return passed(x, [(i, i - reach) for i in everyone if i >= reach])
+
+    ring = passed(out1, [(i, i // 4 * 4 + (i + 3) % 4) for i in everyone])
+    back8, back4, back2 = back_by(out8, 8), back_by(out4, 4), back_by(out2, 2)
+    relayed = passed(ring, [(i, i - 4) for i in everyone if i >= 4 and i % 4 == 3])
     (part,) = call(
         home_kernel, "home", (all_rows,), [SMEM] + [VMEM] * 3, [VMEM], 6, moved=heavy,
         scratch=[VMEM((leaf_dev + 8, samples, width), jnp.float32)],
     )(home, back, low, held_w)
     lists = (4, 4 * SLOTS)
     (gradient,) = call(
-        functools.partial(add_kernel, capacity, (3, 2, 1, 0)), "add", (all_rows,), [VMEM] * 5,
-        [VMEM], 6, moved=4 * MIB,
-        scratch=[VMEM(lists, jnp.int32), SMEM(lists, jnp.int32), pltpu.SemaphoreType.DMA],
-    )(part, *returned)
+        functools.partial(add_kernel, capacity), "add", (all_rows,), [VMEM] * 6,
+        [VMEM], 6, moved=4 * MIB, scratch=[VMEM(lists, jnp.int32), SMEM(lists, jnp.int32), dma],
+    )(part, back8, ring, back4, back2, relayed)
     return gradient
 
 

time: 44.9 us -> 43.9 us (0.978)
  Pallas kernels: 19.5 us -> 18.5 us
  waiting for transfers between devices: 3.87 us -> 3.09 us
  starting transfers between devices: 21.1 us -> 21.6 us
    pallas_call x3, Pallas kernels: 9 us -> 7.61 us  [the longest x1 2.95 us: per_device(): call(early_kernel, 'early', (shape((most, samples, width), jnp.float32),...]
    pallas_call x1, Pallas kernels: 1.01 us -> 2.22 us  [per_device(): call(index_kernel, 'index', (one_list, shape((2, 4 * SLOTS), jnp.int32),...]
    ppermute x11 -> x12, waiting for transfers between devices: 3.87 us -> 3.09 us  [passed(): return lax.ppermute(x, 'kx', route)]
    ppermute x11 -> x12, starting transfers between devices: 21.1 us -> 21.6 us  [passed(): return lax.ppermute(x, 'kx', route)]
    pallas_call x1, Pallas kernels: 4.85 us -> 4.39 us  [per_device(): call(functools.partial(remote_kernel, capacity), 'remote', (all_rows, sha...]
  transfers between devices with their start and end apart: 11 -> 12, of which waited for: 2 -> 1; matrix products, arithmetic and copies ran while one was open for 0% -> 0% of each run, Pallas kernels for 27% -> 27%
where the time goes in v9:
time: 43.9 us; the launch traced here: 43.4 us
  starting transfers between devices  21.6 us (49%)
  Pallas kernels  18.5 us (42%)
  waiting for transfers between devices  3.09 us (7%)
    ppermute x12, starting transfers between devices, passed(): return lax.ppermute(x, 'kx', route)  21.6 us
    pallas_call x1, Pallas kernels, per_device(): call(functools.partial(remote_kernel, capacity), 'remote', (all_rows, sha...  4.39 us
    pallas_call x1, Pallas kernels, per_device(): call(home_kernel, 'home', (all_rows,), [SMEM] + [VMEM] * 3, [VMEM], 6, mo...  3.67 us
    ppermute x12, waiting for transfers between devices, passed(): return lax.ppermute(x, 'kx', route)  3.09 us
    pallas_call x1, Pallas kernels, per_device(): call(early_kernel, 'early', (shape((most, samples, width), jnp.float32),...  2.95 us
    pallas_call x1, Pallas kernels, per_device(): call(late_kernel, 'late', (shape((leaf_dev - most, samples, width), jnp.f...  2.86 us
    pallas_call x1, Pallas kernels, per_device(): call(index_kernel, 'index', (one_list, shape((2, 4 * SLOTS), jnp.int32),...  2.22 us
    pallas_call x1, Pallas kernels, per_device(): call(functools.partial(add_kernel, capacity), 'add', (all_rows,), [VMEM]...  1.8 us
  transfers between devices with their start and end apart: 12, of which 1 were waited for; matrix products, arithmetic and copies ran while one was open for 0% of the time, Pallas kernels for 27%

profile of v9, /device:TPU:15, one launch (start us, length us, event | category | flops | bytes accessed | tf_op | source)
XLA Modules:
  0.0 43.4 jit_solution(16523000639195425433)
XLA Ops:
  0.0 3.2 %collective-permute-start = (bf16[80,16,128]{2,1,0:T(8,128)(2,1)}, bf16[80,16,128]{2,1,0:T(8,128)(2,1)S(1)}, u32[]{:S(2)}, u32[]{:S(2)}) collective-permute-start(bf16[80,16,128]{2,1,0:T(8,128)(2,1)} %latent.1), channel_id=1, source_target_pairs={{0,4},{1,5},{2,6},{3,7},{4,8},{5,9},{6,10},{7,11},{8,12},{9,13},{1... | collective-permute-start | bytes 983048 | tf_op jit(solution)/shard_map/ppermute | solution.py:301
  3.2 2.2 %index.1 = (s32[1,128]{1,0:T(1,128)S(1)}, s32[2,128]{1,0:T(2,128)S(1)}, s32[3,80]{1,0:T(4,128)S(1)}, bf16[88,16,128]{2,1,0:T(8,128)(2,1)S(1)}, bf16[80,3,128,128]{3,2,1,0:T(8,128)(2,1)S(1)}) custom-call(s32[3,80]{1,0:T(4,128)} %bitcast.1, bf16[80,16,128]{2,1,0:T(8,128)(2,1)} %latent.1, bf16[80,3,128,128]{3,2,1,0:T(8,128)(2,1)} %weights.5), custom_call_target="tpu_custom_call" | custom-call | bytes 2097152 | tf_op jit(solution)/shard_map/index/pallas_call | solution.py:307
  5.4 1.0 %collective-permute-start.1 = (s32[1,128]{1,0:T(1,128)S(1)}, s32[1,128]{1,0:T(1,128)S(1)}, u32[]{:S(2)}, u32[]{:S(2)}) collective-permute-start(s32[1,128]{1,0:T(1,128)S(1)} %get-tuple-element.25.asked.asked_row), channel_id=1, source_target_pairs={{0,3},{1,0},{2,1},{3,2},{4,7},{5,4},{6,5},{7,6},{8,11},{9,8},{10,9... | collective-permute-start | bytes 1544 | tf_op jit(solution)/shard_map/ppermute | solution.py:301
  6.4 0.2 collective-permute-start.2
  6.7 2.1 %collective-permute-start.3 = (s32[1,128]{1,0:T(1,128)S(1)}, s32[1,128]{1,0:T(1,128)S(1)}, u32[]{:S(2)}, u32[]{:S(2)}) collective-permute-start(s32[1,128]{1,0:T(1,128)S(1)} %get-tuple-element.25.asked.asked_row), channel_id=1, source_target_pairs={{4,0},{5,1},{6,2},{7,3},{8,4},{9,5},{10,6},{11,7},{12,8},{13,9},{1... | collective-permute-start | bytes 1544 | tf_op jit(solution)/shard_map/ppermute | solution.py:301
  8.8 2.9 %early.1 = (f32[48,16,128]{2,1,0:T(8,128)S(1)}, bf16[80,3,128,128]{3,2,1,0:T(8,128)(2,1)S(1)}) custom-call(s32[3,80]{1,0:T(4,128)S(1)} %get-tuple-element.24.home, bf16[88,16,128]{2,1,0:T(8,128)(2,1)S(1)} %get-tuple-element.27.rows.latent, bf16[80,3,128,128]{3,2,1,0:T(8,128)(2,1)S(1)} %get-tuple-element.28.held_part, ...), custom_call_target="tpu_custom_call", output_to_operand_aliasing={{1}: (2, {})} | custom-call | bytes 3932160 | tf_op jit(solution)/shard_map/early/pallas_call | solution.py:319
  11.7 0.0 collective-permute-done.1.ask1
  11.7 0.0 collective-permute-done.2.ask2
  11.7 0.0 collective-permute-done.3.ask8
  11.7 0.0 collective-permute-done.before
  11.8 0.6 %serve.1 = (bf16[30,16,128]{2,1,0:T(8,128)(2,1)S(1)}, bf16[30,16,128]{2,1,0:T(8,128)(2,1)S(1)}, bf16[30,16,128]{2,1,0:T(8,128)(2,1)S(1)}) custom-call(s32[1,128]{1,0:T(1,128)S(1)} %collective-permute-done.1.ask1, s32[1,128]{1,0:T(1,128)S(1)} %collective-permute-done.2.ask2, s32[1,128]{1,0:T(1,128)S(1)} %collective-permute-done.3.ask8, ...), custom_call_target="tpu_custom_call" | custom-call | bytes 4194304 | tf_op jit(solution)/shard_map/serve/pallas_call | solution.py:324
  12.4 1.3 %collective-permute-start.4 = (bf16[30,16,128]{2,1,0:T(8,128)(2,1)S(1)}, bf16[30,16,128]{2,1,0:T(8,128)(2,1)S(1)}, u32[]{:S(2)}, u32[]{:S(2)}) collective-permute-start(bf16[30,16,128]{2,1,0:T(8,128)(2,1)S(1)} %get-tuple-element.32), channel_id=1, source_target_pairs={{0,2},{1,3},{2,0},{3,1},{4,6},{5,7},{6,4},{7,5},{8,10},{9,11},{10,... | collective-permute-start | bytes 368648 | tf_op jit(solution)/shard_map/ppermute | solution.py:301
  13.7 3.2 %collective-permute-start.5 = (bf16[30,16,128]{2,1,0:T(8,128)(2,1)S(1)}, bf16[30,16,128]{2,1,0:T(8,128)(2,1)S(1)}, u32[]{:S(2)}, u32[]{:S(2)}) collective-permute-start(bf16[30,16,128]{2,1,0:T(8,128)(2,1)S(1)} %get-tuple-element.33), channel_id=1, source_target_pairs={{4,8},{5,9},{6,10},{7,11},{8,12},{9,13},{10,14},{11,15},{20,24},{2... | collective-permute-start | bytes 368648 | tf_op jit(solution)/shard_map/ppermute | solution.py:301
  16.9 2.0 %collective-permute-start.6 = (bf16[30,16,128]{2,1,0:T(8,128)(2,1)S(1)}, bf16[30,16,128]{2,1,0:T(8,128)(2,1)S(1)}, u32[]{:S(2)}, u32[]{:S(2)}) collective-permute-start(bf16[30,16,128]{2,1,0:T(8,128)(2,1)S(1)} %get-tuple-element.34), channel_id=1, source_target_pairs={{0,1},{1,2},{2,3},{3,0},{4,5},{5,6},{6,7},{7,4},{8,9},{9,10},{10,1... | collective-permute-start | bytes 368648 | tf_op jit(solution)/shard_map/ppermute | solution.py:301
  18.9 2.9 %late.1 = (f32[32,16,128]{2,1,0:T(8,128)S(1)}, bf16[80,3,128,128]{3,2,1,0:T(8,128)(2,1)S(1)}, bf16[80,128,128]{2,1,0:T(8,128)(2,1)S(1)}) custom-call(s32[3,80]{1,0:T(4,128)S(1)} %get-tuple-element.24.home, bf16[88,16,128]{2,1,0:T(8,128)(2,1)S(1)} %get-tuple-element.27.rows.latent, ...), custom_call_target="tpu_custom_call", output_to_operand_aliasing={{1}: (3, {})} | custom-call | bytes 3932160 | tf_op jit(solution)/shard_map/late/pallas_call | solution.py:331
  21.8 0.0 collective-permute-done.4.from2
  21.8 0.0 collective-permute-done.5.from8
  21.8 0.0 collective-permute-done.6.from1
  21.8 4.4 %remote.1 = (f32[80,16,128]{2,1,0:T(8,128)S(1)}, bf16[88,16,128]{2,1,0:T(8,128)(2,1)S(1)}, bf16[31,16,128]{2,1,0:T(8,128)(2,1)S(1)}, bf16[31,16,128]{2,1,0:T(8,1...) custom-call(s32[1,128]{1,0:T(1,128)S(1)} %get-tuple-element.25.asked.asked_row, ...), custom_call_target="tpu_custom_call" | custom-call | bytes 7864320 | tf_op jit(solution)/shard_map/remote/pallas_call | solution.py:340
  26.2 0.7 %collective-permute-start.8 = (bf16[31,16,128]{2,1,0:T(8,128)(2,1)S(1)}, bf16[31,16,128]{2,1,0:T(8,128)(2,1)S(1)}, u32[]{:S(2)}, u32[]{:S(2)}) collective-permute-start(bf16[31,16,128]{2,1,0:T(8,128)(2,1)S(1)} %get-tuple-element.40), channel_id=1, source_target_pairs={{0,3},{1,0},{2,1},{3,2},{4,7},{5,4},{6,5},{7,6},{8,11},{9,8},{10,9... | collective-permute-start | bytes 380936 | tf_op jit(solution)/shard_map/ppermute | solution.py:301
  27.0 1.3 %collective-permute-start.7 = (bf16[31,16,128]{2,1,0:T(8,128)(2,1)S(1)}, bf16[31,16,128]{2,1,0:T(8,128)(2,1)S(1)}, u32[]{:S(2)}, u32[]{:S(2)}) collective-permute-start(bf16[31,16,128]{2,1,0:T(8,128)(2,1)S(1)} %get-tuple-element.39), channel_id=1, source_target_pairs={{8,0},{9,1},{10,2},{11,3},{12,4},{13,5},{14,6},{15,7},{24,16},{25,... | collective-permute-start | bytes 380936 | tf_op jit(solution)/shard_map/ppermute | solution.py:301
  28.2 1.9 %collective-permute-start.9 = (bf16[31,16,128]{2,1,0:T(8,128)(2,1)S(1)}, bf16[31,16,128]{2,1,0:T(8,128)(2,1)S(1)}, u32[]{:S(2)}, u32[]{:S(2)}) collective-permute-start(bf16[31,16,128]{2,1,0:T(8,128)(2,1)S(1)} %get-tuple-element.41), channel_id=1, source_target_pairs={{4,0},{5,1},{6,2},{7,3},{8,4},{9,5},{10,6},{11,7},{12,8},{13,9},{1... | collective-permute-start | bytes 380936 | tf_op jit(solution)/shard_map/ppermute | solution.py:301
  30.2 2.7 %collective-permute-start.10 = (bf16[31,16,128]{2,1,0:T(8,128)(2,1)S(1)}, bf16[31,16,128]{2,1,0:T(8,128)(2,1)S(1)}, u32[]{:S(2)}, u32[]{:S(2)}) collective-permute-start(bf16[31,16,128]{2,1,0:T(8,128)(2,1)S(1)} %get-tuple-element.42), channel_id=1, source_target_pairs={{2,0},{3,1},{4,2},{5,3},{6,4},{7,5},{8,6},{9,7},{10,8},{11,9},{12,... | collective-permute-start | bytes 380936 | tf_op jit(solution)/shard_map/ppermute | solution.py:301
  32.9 0.0 collective-permute-done.8.ring
  32.9 1.9 %collective-permute-start.11 = (bf16[31,16,128]{2,1,0:T(8,128)(2,1)S(1)}, bf16[31,16,128]{2,1,0:T(8,128)(2,1)S(1)}, u32[]{:S(2)}, u32[]{:S(2)}) collective-permute-start(bf16[31,16,128]{2,1,0:T(8,128)(2,1)S(1)} %collective-permute-done.8.ring), channel_id=1, source_target_pairs={{7,3},{11,7},{15,11},{23,19},{27,23},{31,27}} | collective-permute-start | bytes 380936 | tf_op jit(solution)/shard_map/ppermute | solution.py:301
  34.9 3.7 %home.1.part = f32[80,16,128]{2,1,0:T(8,128)S(1)} custom-call(s32[3,80]{1,0:T(4,128)S(1)} %get-tuple-element.24.home, f32[80,16,128]{2,1,0:T(8,128)S(1)} %get-tuple-element.37.back, bf16[88,16,128]{2,1,0:T(8,128)(2,1)S(1)} %get-tuple-element.38.low, bf16[80,3,128,128]{3,2,1,0:T(8,128)(2,1)S(1)} %get-tuple-element.35.weights), custom_call_target="tpu_custom_call" | custom-call | bytes 7864320 | tf_op jit(solution)/shard_map/home/pallas_call | solution.py:352
  38.5 0.0 collective-permute-done.7.back8
  38.5 0.0 collective-permute-done.9.back4
  38.6 3.1 %collective-permute-done.10.back2 = bf16[31,16,128]{2,1,0:T(8,128)(2,1)S(1)} collective-permute-done((bf16[31,16,128]{2,1,0:T(8,128)(2,1)S(1)}, bf16[31,16,128]{2,1,0:T(8,128)(2,1)S(1)}, u32[]{:S(2)}, u32[]{:S(2)}) %collective-permute-start.10) | collective-permute-done | bytes 127008 | tf_op jit(solution)/shard_map/ppermute | solution.py:301
  41.6 0.0 collective-permute-done.11.relayed
  41.6 1.8 %add.1 = f32[80,16,128]{2,1,0:T(8,128)} custom-call(f32[80,16,128]{2,1,0:T(8,128)S(1)} %home.1.part, bf16[31,16,128]{2,1,0:T(8,128)(2,1)S(1)} %collective-permute-done.7.back8, bf16[31,16,128]{2,1,0:T(8,128)(2,1)S(1)} %collective-permute-done.8.ring, bf16[31,16,128]{2,1,0:T(8,128)(2,1)S(1)} %collective-permute-done.9.back4, ...), custom_call_target="tpu_custom_call" | custom-call | bytes 4194304 | tf_op jit(solution)/shard_map/add/pallas_call | solution.py:357
Async XLA Ops:
  0.0 11.7 %collective-permute-start = (bf16[80,16,128]{2,1,0:T(8,128)(2,1)}, bf16[80,16,128]{2,1,0:T(8,128)(2,1)S(1)}, u32[]{:S(2)}, u32[]{:S(2)}) collective-permute-start(bf16[80,16,128]{2,1,0:T(8,128)(2,1)} %latent.1), channel_id=1, source_target_pairs={{0,4},{1,5},{2,6},{3,7},{4,8},{5,9},{6,10},{7,11},{8,12},{9,13},{1... | collective-permute-start | bytes 983048 | tf_op jit(solution)/shard_map/ppermute | solution.py:301
  5.4 6.3 %collective-permute-start.1 = (s32[1,128]{1,0:T(1,128)S(1)}, s32[1,128]{1,0:T(1,128)S(1)}, u32[]{:S(2)}, u32[]{:S(2)}) collective-permute-start(s32[1,128]{1,0:T(1,128)S(1)} %get-tuple-element.25.asked.asked_row), channel_id=1, source_target_pairs={{0,3},{1,0},{2,1},{3,2},{4,7},{5,4},{6,5},{7,6},{8,11},{9,8},{10,9... | collective-permute-start | bytes 1544 | tf_op jit(solution)/shard_map/ppermute | solution.py:301
  6.4 5.3 %collective-permute-start.2 = (s32[1,128]{1,0:T(1,128)S(1)}, s32[1,128]{1,0:T(1,128)S(1)}, u32[]{:S(2)}, u32[]{:S(2)}) collective-permute-start(s32[1,128]{1,0:T(1,128)S(1)} %get-tuple-element.25.asked.asked_row), channel_id=1, source_target_pairs={{0,2},{1,3},{2,0},{3,1},{4,6},{5,7},{6,4},{7,5},{8,10},{9,11},{10,... | collective-permute-start | bytes 1544 | tf_op jit(solution)/shard_map/ppermute | solution.py:301
  6.7 5.1 %collective-permute-start.3 = (s32[1,128]{1,0:T(1,128)S(1)}, s32[1,128]{1,0:T(1,128)S(1)}, u32[]{:S(2)}, u32[]{:S(2)}) collective-permute-start(s32[1,128]{1,0:T(1,128)S(1)} %get-tuple-element.25.asked.asked_row), channel_id=1, source_target_pairs={{4,0},{5,1},{6,2},{7,3},{8,4},{9,5},{10,6},{11,7},{12,8},{13,9},{1... | collective-permute-start | bytes 1544 | tf_op jit(solution)/shard_map/ppermute | solution.py:301
  12.4 9.4 %collective-permute-start.4 = (bf16[30,16,128]{2,1,0:T(8,128)(2,1)S(1)}, bf16[30,16,128]{2,1,0:T(8,128)(2,1)S(1)}, u32[]{:S(2)}, u32[]{:S(2)}) collective-permute-start(bf16[30,16,128]{2,1,0:T(8,128)(2,1)S(1)} %get-tuple-element.32), channel_id=1, source_target_pairs={{0,2},{1,3},{2,0},{3,1},{4,6},{5,7},{6,4},{7,5},{8,10},{9,11},{10,... | collective-permute-start | bytes 368648 | tf_op jit(solution)/shard_map/ppermute | solution.py:301
  13.7 8.1 %collective-permute-start.5 = (bf16[30,16,128]{2,1,0:T(8,128)(2,1)S(1)}, bf16[30,16,128]{2,1,0:T(8,128)(2,1)S(1)}, u32[]{:S(2)}, u32[]{:S(2)}) collective-permute-start(bf16[30,16,128]{2,1,0:T(8,128)(2,1)S(1)} %get-tuple-element.33), channel_id=1, source_target_pairs={{4,8},{5,9},{6,10},{7,11},{8,12},{9,13},{10,14},{11,15},{20,24},{2... | collective-permute-start | bytes 368648 | tf_op jit(solution)/shard_map/ppermute | solution.py:301
  16.9 4.9 %collective-permute-start.6 = (bf16[30,16,128]{2,1,0:T(8,128)(2,1)S(1)}, bf16[30,16,128]{2,1,0:T(8,128)(2,1)S(1)}, u32[]{:S(2)}, u32[]{:S(2)}) collective-permute-start(bf16[30,16,128]{2,1,0:T(8,128)(2,1)S(1)} %get-tuple-element.34), channel_id=1, source_target_pairs={{0,1},{1,2},{2,3},{3,0},{4,5},{5,6},{6,7},{7,4},{8,9},{9,10},{10,1... | collective-permute-start | bytes 368648 | tf_op jit(solution)/shard_map/ppermute | solution.py:301
  26.2 6.7 %collective-permute-start.8 = (bf16[31,16,128]{2,1,0:T(8,128)(2,1)S(1)}, bf16[31,16,128]{2,1,0:T(8,128)(2,1)S(1)}, u32[]{:S(2)}, u32[]{:S(2)}) collective-permute-start(bf16[31,16,128]{2,1,0:T(8,128)(2,1)S(1)} %get-tuple-element.40), channel_id=1, source_target_pairs={{0,3},{1,0},{2,1},{3,2},{4,7},{5,4},{6,5},{7,6},{8,11},{9,8},{10,9... | collective-permute-start | bytes 380936 | tf_op jit(solution)/shard_map/ppermute | solution.py:301
  27.0 11.6 %collective-permute-start.7 = (bf16[31,16,128]{2,1,0:T(8,128)(2,1)S(1)}, bf16[31,16,128]{2,1,0:T(8,128)(2,1)S(1)}, u32[]{:S(2)}, u32[]{:S(2)}) collective-permute-start(bf16[31,16,128]{2,1,0:T(8,128)(2,1)S(1)} %get-tuple-element.39), channel_id=1, source_target_pairs={{8,0},{9,1},{10,2},{11,3},{12,4},{13,5},{14,6},{15,7},{24,16},{25,... | collective-permute-start | bytes 380936 | tf_op jit(solution)/shard_map/ppermute | solution.py:301
  28.2 10.3 %collective-permute-start.9 = (bf16[31,16,128]{2,1,0:T(8,128)(2,1)S(1)}, bf16[31,16,128]{2,1,0:T(8,128)(2,1)S(1)}, u32[]{:S(2)}, u32[]{:S(2)}) collective-permute-start(bf16[31,16,128]{2,1,0:T(8,128)(2,1)S(1)} %get-tuple-element.41), channel_id=1, source_target_pairs={{4,0},{5,1},{6,2},{7,3},{8,4},{9,5},{10,6},{11,7},{12,8},{13,9},{1... | collective-permute-start | bytes 380936 | tf_op jit(solution)/shard_map/ppermute | solution.py:301
  30.2 11.4 %collective-permute-start.10 = (bf16[31,16,128]{2,1,0:T(8,128)(2,1)S(1)}, bf16[31,16,128]{2,1,0:T(8,128)(2,1)S(1)}, u32[]{:S(2)}, u32[]{:S(2)}) collective-permute-start(bf16[31,16,128]{2,1,0:T(8,128)(2,1)S(1)} %get-tuple-element.42), channel_id=1, source_target_pairs={{2,0},{3,1},{4,2},{5,3},{6,4},{7,5},{8,6},{9,7},{10,8},{11,9},{12,... | collective-permute-start | bytes 380936 | tf_op jit(solution)/shard_map/ppermute | solution.py:301
  32.9 8.7 %collective-permute-start.11 = (bf16[31,16,128]{2,1,0:T(8,128)(2,1)S(1)}, bf16[31,16,128]{2,1,0:T(8,128)(2,1)S(1)}, u32[]{:S(2)}, u32[]{:S(2)}) collective-permute-start(bf16[31,16,128]{2,1,0:T(8,128)(2,1)S(1)} %collective-permute-done.8.ring), channel_id=1, source_target_pairs={{7,3},{11,7},{15,11},{23,19},{27,23},{31,27}} | collective-permute-start | bytes 380936 | tf_op jit(solution)/shard_map/ppermute | solution.py:301

commit v10 on v9

--- a/solution.py
+++ b/solution.py
@@ -15,21 +15,12 @@
 VMEM, SMEM, HBM, ANY = pltpu.VMEM, pltpu.SMEM, pltpu.HBM, pl.ANY
 
 
-def fetched(weights, held, sem, n):
-    part = pl.ds(n * PART, PART)
-    return pltpu.make_async_copy(weights.at[part], held.at[part], sem)
-
-
 def index_kernel(
-    lists, latent, weights, asked, slots, home, rows, held_w, row_sem, w_sem
+    lists, latent, asked, slots, home, rows, row_sem
 ):
     fan, leaf_dev = lists.shape
-    fetches = (
-        pltpu.make_async_copy(latent, rows.at[pl.ds(0, leaf_dev)], row_sem),
-        fetched(weights, held_w, w_sem, 0),
-    )
-    for fetch in fetches:
-        fetch.start()
+    fetch = pltpu.make_async_copy(latent, rows.at[pl.ds(0, leaf_dev)], row_sem)
+    fetch.start()
     rows[leaf_dev] = jnp.zeros(latent.shape[1:], latent.dtype)
     me = lax.axis_index("kx")
     behind = me * leaf_dev - lists[...]
@@ -80,8 +71,7 @@
     asked[...] = total[0:1].astype(jnp.int32)
     slots[0:1] = jnp.where(total[3:4] > 0.0, total[1:2], float(leaf_dev)).astype(jnp.int32)
     slots[1:2] = total[2:3].astype(jnp.int32)
-    for fetch in fetches:
-        fetch.wait()
+    fetch.wait()
 
 
 def beside(xs):
@@ -115,33 +105,22 @@
         left[i - first] = rows[i].astype(jnp.float32) - mean
 
 
-def early_kernel(home, rows, held_part, weights, left, held_w, w_sem):
-    parts = left.shape[0] // PART
-    fetches = [fetched(weights, held_w, w_sem.at[n], n + 1) for n in range(parts)]
+def early_kernel(home, rows, weights, left, held, sem):
+    parts = [pl.ds(at, PART) for at in range(0, left.shape[0], PART)]
+    fetches = [
+        pltpu.make_async_copy(weights.at[p], held.at[p], sem.at[n]) for n, p in enumerate(parts)
+    ]
     for fetch in fetches:
         fetch.start()
-    for n in range(parts):
-        if n > 0:
-            fetches[n - 1].wait()
-        held = held_w if n > 0 else held_part
+    for n, fetch in enumerate(fetches):
+        fetch.wait()
         local_means(home, rows, held, left, 0, range(n * PART, (n + 1) * PART))
-    fetches[-1].wait()
-
-
-def late_kernel(home, rows, before, held_part, weights, factor, left, held_w, held_f, w_sem, f_sem):
-    parts, first = left.shape[0] // PART, weights.shape[0] - left.shape[0]
-    fetches = [fetched(weights, held_w, w_sem.at[n - 1], first // PART + n) for n in range(1, parts)]
-    fetch_factor = pltpu.make_async_copy(factor, held_f, f_sem)
-    for fetch in fetches:
-        fetch.start()
-    fetch_factor.start()
-    for n in range(parts):
-        if n > 0:
-            fetches[n - 1].wait()
-        at = first + n * PART
-        held = held_w if n > 0 else held_part
-        local_means(home, rows, held, left, first, range(at, at + PART))
-    fetch_factor.wait()
+
+
+def late_kernel(home, rows, before, weights, left):
+    leaf_dev = weights.shape[0]
+    first = leaf_dev - left.shape[0]
+    local_means(home, rows, weights, left, first, range(first, leaf_dev))
 
 
 def serve_kernel(capacity, ask1, ask2, ask8, latent, before, left, out8, out2, out1):
@@ -301,26 +280,25 @@
         return lax.ppermute(x, "kx", route)
 
     before = passed(latent, [(i, i + 4) for i in everyone if i + 4 < devices])
-    held = shape(cond_weights.shape, jnp.bfloat16)
-    weights = placed(cond_weights, HBM)
+    weights, factor = placed(cond_weights, VMEM), placed(precision_factor, VMEM)
     dma = pltpu.SemaphoreType.DMA
-    asked, slots, home, rows, held_w = call(
+    asked, slots, home, rows = call(
         index_kernel, "index",
         (
             one_list, shape((2, 4 * SLOTS), jnp.int32), shape((fan, leaf_dev), jnp.int32),
-            shape((leaf_dev + 8, samples, width), jnp.bfloat16), held,
+            shape((leaf_dev + 8, samples, width), jnp.bfloat16),
         ),
-        [VMEM, HBM, HBM], [VMEM] * 5, 14, moved=2 * MIB, scratch=[dma, dma],
-    )(placed(cond_lists.T, HBM), placed(latent, HBM), weights)
+        [VMEM, HBM], [VMEM] * 4, 4, moved=2 * MIB, scratch=[dma],
+    )(placed(cond_lists.T, HBM), placed(latent, HBM))
     ask8 = passed(asked, [(i, i - 4) for i in everyone if i >= 4])
     ask2 = passed(asked, [(i, i ^ 2) for i in everyone])
     ask1 = passed(asked, [(i, i // 4 * 4 + (i + 3) % 4) for i in everyone])
-    most = -(-leaf_dev // (2 * PART)) * PART
-    left, held_w = call(
-        early_kernel, "early", (shape((most, samples, width), jnp.float32), held),
-        [SMEM, VMEM, VMEM, HBM], [VMEM] * 2, 14, moved=heavy // 2,
-        scratch=[dma((most // PART,))], aliases={2: 1},
-    )(home, rows, held_w, weights)
+    most = 2 * leaf_dev // 5 // PART * PART
+    (left,) = call(
+        early_kernel, "early", (shape((most, samples, width), jnp.float32),),
+        [SMEM, VMEM, HBM], [VMEM], 6, moved=heavy // 2,
+        scratch=[VMEM((most,) + cond_weights.shape[1:], jnp.bfloat16), dma((most // PART,))],
+    )(home, rows, placed(cond_weights, HBM))
     serve8, serve2, serve1 = call(
         functools.partial(serve_kernel, capacity), "serve", (some_rows,) * 3,
         [SMEM] * 3 + [VMEM] * 2 + [ANY], [VMEM] * 3, 4, moved=4 * MIB,
@@ -328,21 +306,16 @@
     from8 = passed(serve8, [(i, i + 4) for i in everyone if i >= 4 and i + 4 < devices])
     from2 = passed(serve2, [(i, i ^ 2) for i in everyone])
     from1 = passed(serve1, [(i, i // 4 * 4 + (i + 1) % 4) for i in everyone])
-    later, held_w, held_f = call(
-        late_kernel, "late",
-        (
-            shape((leaf_dev - most, samples, width), jnp.float32), held,
-            shape(precision_factor.shape, jnp.bfloat16),
-        ),
-        [SMEM, VMEM, ANY, VMEM, HBM, HBM], [VMEM] * 3, 14, moved=heavy // 2,
-        scratch=[dma(((leaf_dev - most) // PART - 1,)), dma], aliases={3: 1},
-    )(home, rows, before, held_w, weights, placed(precision_factor, HBM))
+    (later,) = call(
+        late_kernel, "late", (shape((leaf_dev - most, samples, width), jnp.float32),),
+        [SMEM, VMEM, ANY, VMEM], [VMEM], 4, moved=heavy // 2,
+    )(home, rows, before, weights)
     back, low, out8, out4, out2, out1 = call(
         functools.partial(remote_kernel, capacity), "remote",
         (all_rows, shape((leaf_dev + 8, samples, width), jnp.bfloat16)) + (sent,) * 4,
         [SMEM] * 2 + [VMEM] * 9, [VMEM] * 6, 8, moved=heavy,
         scratch=[VMEM((leaf_dev + 8, samples, width), jnp.float32)],
-    )(asked, slots, asked, left, later, before, from2, from8, from1, held_w, held_f)
+    )(asked, slots, asked, left, later, before, from2, from8, from1, weights, factor)
     def back_by(x, reach):
         return passed(x, [(i, i - reach) for i in everyone if i >= reach])
 
@@ -352,7 +325,7 @@
     (part,) = call(
         home_kernel, "home", (all_rows,), [SMEM] + [VMEM] * 3, [VMEM], 6, moved=heavy,
         scratch=[VMEM((leaf_dev + 8, samples, width), jnp.float32)],
-    )(home, back, low, held_w)
+    )(home, back, low, weights)
     lists = (4, 4 * SLOTS)
     (gradient,) = call(
         functools.partial(add_kernel, capacity), "add", (all_rows,), [VMEM] * 6,

time: 43.9 us -> 43.5 us (level)
  Pallas kernels: 18.5 us -> 16.7 us
  starting transfers between devices: 21.6 us -> 22.5 us
  waiting for transfers between devices: 3.09 us -> 3.75 us
    pallas_call x1, Pallas kernels: 2.86 us -> 1.51 us  [per_device(): call(late_kernel, 'late', (shape((leaf_dev - most, samples, width), jnp.f...]
    ppermute x12, starting transfers between devices: 21.6 us -> 22.5 us  [passed(): return lax.ppermute(x, 'kx', route)]
    ppermute x12, waiting for transfers between devices: 3.09 us -> 3.75 us  [passed(): return lax.ppermute(x, 'kx', route)]
    pallas_call x1, Pallas kernels: 2.22 us -> 1.66 us  [per_device(): call(index_kernel, 'index', (one_list, shape((2, 4 * SLOTS), jnp.int32),...]
  transfers between devices with their start and end apart: 12 -> 12, of which waited for: 1 -> 3; matrix products, arithmetic and copies ran while one was open for 0% -> 0% of each run, Pallas kernels for 27% -> 23%
where the time goes in v10:
time: 43.5 us; the launch traced here: 43.2 us
  starting transfers between devices  22.5 us (52%)
  Pallas kernels  16.7 us (38%)
  waiting for transfers between devices  3.75 us (9%)
    ppermute x12, starting transfers between devices, passed(): return lax.ppermute(x, 'kx', route)  22.5 us
    pallas_call x1, Pallas kernels, per_device(): call(functools.partial(remote_kernel, capacity), 'remote', (all_rows, sha...  4.36 us
    ppermute x12, waiting for transfers between devices, passed(): return lax.ppermute(x, 'kx', route)  3.75 us
    pallas_call x1, Pallas kernels, per_device(): call(home_kernel, 'home', (all_rows,), [SMEM] + [VMEM] * 3, [VMEM], 6, mo...  3.67 us
    pallas_call x1, Pallas kernels, per_device(): call(early_kernel, 'early', (shape((most, samples, width), jnp.float32),)...  3.08 us
    pallas_call x1, Pallas kernels, per_device(): call(functools.partial(add_kernel, capacity), 'add', (all_rows,), [VMEM]...  1.8 us
    pallas_call x1, Pallas kernels, per_device(): call(index_kernel, 'index', (one_list, shape((2, 4 * SLOTS), jnp.int32),...  1.66 us
    pallas_call x1, Pallas kernels, per_device(): call(late_kernel, 'late', (shape((leaf_dev - most, samples, width), jnp.f...  1.51 us
  transfers between devices with their start and end apart: 12, of which 3 were waited for; matrix products, arithmetic and copies ran while one was open for 0% of the time, Pallas kernels for 23%

profile of v10, /device:TPU:15, one launch (start us, length us, event | category | flops | bytes accessed | tf_op | source)
XLA Modules:
  0.0 43.2 jit_solution(4212351799009741370)
XLA Ops:
  0.0 0.0 copy-start
  0.0 3.5 %collective-permute-start = (bf16[80,16,128]{2,1,0:T(8,128)(2,1)}, bf16[80,16,128]{2,1,0:T(8,128)(2,1)S(1)}, u32[]{:S(2)}, u32[]{:S(2)}) collective-permute-start(bf16[80,16,128]{2,1,0:T(8,128)(2,1)} %latent.1), channel_id=1, source_target_pairs={{0,4},{1,5},{2,6},{3,7},{4,8},{5,9},{6,10},{7,11},{8,12},{9,13},{1... | collective-permute-start | bytes 983048 | tf_op jit(solution)/shard_map/ppermute | solution.py:280
  3.5 1.7 %index.1 = (s32[1,128]{1,0:T(1,128)S(1)}, s32[2,128]{1,0:T(2,128)S(1)}, s32[3,80]{1,0:T(4,128)S(1)}, bf16[88,16,128]{2,1,0:T(8,128)(2,1)S(1)}) custom-call(s32[3,80]{1,0:T(4,128)} %bitcast.1, bf16[80,16,128]{2,1,0:T(8,128)(2,1)} %latent.1), custom_call_target="tpu_custom_call" | custom-call | bytes 2097152 | tf_op jit(solution)/shard_map/index/pallas_call | solution.py:285
  5.1 2.1 %collective-permute-start.3 = (s32[1,128]{1,0:T(1,128)S(1)}, s32[1,128]{1,0:T(1,128)S(1)}, u32[]{:S(2)}, u32[]{:S(2)}) collective-permute-start(s32[1,128]{1,0:T(1,128)S(1)} %get-tuple-element.19.asked.asked_row), channel_id=1, source_target_pairs={{4,0},{5,1},{6,2},{7,3},{8,4},{9,5},{10,6},{11,7},{12,8},{13,9},{1... | collective-permute-start | bytes 1544 | tf_op jit(solution)/shard_map/ppermute | solution.py:280
  7.2 0.3 collective-permute-start.2
  7.5 1.5 %collective-permute-start.1 = (s32[1,128]{1,0:T(1,128)S(1)}, s32[1,128]{1,0:T(1,128)S(1)}, u32[]{:S(2)}, u32[]{:S(2)}) collective-permute-start(s32[1,128]{1,0:T(1,128)S(1)} %get-tuple-element.19.asked.asked_row), channel_id=1, source_target_pairs={{0,3},{1,0},{2,1},{3,2},{4,7},{5,4},{6,5},{7,6},{8,11},{9,8},{10,9... | collective-permute-start | bytes 1544 | tf_op jit(solution)/shard_map/ppermute | solution.py:280
  9.0 0.0 copy-start.1
  9.0 3.1 %early.1.left = f32[32,16,128]{2,1,0:T(8,128)S(1)} custom-call(s32[3,80]{1,0:T(4,128)S(1)} %get-tuple-element.18.home, bf16[88,16,128]{2,1,0:T(8,128)(2,1)S(1)} %get-tuple-element.21.rows.latent, bf16[80,3,128,128]{3,2,1,0:T(8,128)(2,1)} %weights.7), custom_call_target="tpu_custom_call" | custom-call | bytes 3932160 | tf_op jit(solution)/shard_map/early/pallas_call | solution.py:297
  12.1 0.0 collective-permute-done.3.ask8
  12.1 0.0 collective-permute-done.2.ask2
  12.2 0.0 collective-permute-done.1.ask1
  12.2 0.0 collective-permute-done.before
  12.2 0.6 %serve.1 = (bf16[30,16,128]{2,1,0:T(8,128)(2,1)S(1)}, bf16[30,16,128]{2,1,0:T(8,128)(2,1)S(1)}, bf16[30,16,128]{2,1,0:T(8,128)(2,1)S(1)}) custom-call(s32[1,128]{1,0:T(1,128)S(1)} %collective-permute-done.1.ask1, s32[1,128]{1,0:T(1,128)S(1)} %collective-permute-done.2.ask2, s32[1,128]{1,0:T(1,128)S(1)} %collective-permute-done.3.ask8, ...), custom_call_target="tpu_custom_call" | custom-call | bytes 4194304 | tf_op jit(solution)/shard_map/serve/pallas_call | solution.py:302
  12.8 1.3 %collective-permute-start.4 = (bf16[30,16,128]{2,1,0:T(8,128)(2,1)S(1)}, bf16[30,16,128]{2,1,0:T(8,128)(2,1)S(1)}, u32[]{:S(2)}, u32[]{:S(2)}) collective-permute-start(bf16[30,16,128]{2,1,0:T(8,128)(2,1)S(1)} %get-tuple-element.22), channel_id=1, source_target_pairs={{0,2},{1,3},{2,0},{3,1},{4,6},{5,7},{6,4},{7,5},{8,10},{9,11},{10,... | collective-permute-start | bytes 368648 | tf_op jit(solution)/shard_map/ppermute | solution.py:280
  14.1 3.2 %collective-permute-start.5 = (bf16[30,16,128]{2,1,0:T(8,128)(2,1)S(1)}, bf16[30,16,128]{2,1,0:T(8,128)(2,1)S(1)}, u32[]{:S(2)}, u32[]{:S(2)}) collective-permute-start(bf16[30,16,128]{2,1,0:T(8,128)(2,1)S(1)} %get-tuple-element.23), channel_id=1, source_target_pairs={{4,8},{5,9},{6,10},{7,11},{8,12},{9,13},{10,14},{11,15},{20,24},{2... | collective-permute-start | bytes 368648 | tf_op jit(solution)/shard_map/ppermute | solution.py:280
  17.3 1.0 %collective-permute-start.6 = (bf16[30,16,128]{2,1,0:T(8,128)(2,1)S(1)}, bf16[30,16,128]{2,1,0:T(8,128)(2,1)S(1)}, u32[]{:S(2)}, u32[]{:S(2)}) collective-permute-start(bf16[30,16,128]{2,1,0:T(8,128)(2,1)S(1)} %get-tuple-element.24), channel_id=1, source_target_pairs={{0,1},{1,2},{2,3},{3,0},{4,5},{5,6},{6,7},{7,4},{8,9},{9,10},{10,1... | collective-permute-start | bytes 368648 | tf_op jit(solution)/shard_map/ppermute | solution.py:280
  18.4 0.0 copy-done
  18.4 1.5 %late.1.later = f32[48,16,128]{2,1,0:T(8,128)S(1)} custom-call(s32[3,80]{1,0:T(4,128)S(1)} %get-tuple-element.18.home, bf16[88,16,128]{2,1,0:T(8,128)(2,1)S(1)} %get-tuple-element.21.rows.latent, bf16[80,16,128]{2,1,0:T(8,128)(2,1)S(1)} %collective-permute-done.before, bf16[80,3,128,128]{3,2,1,0:T(8,128)(2,1)S(1)} %copy-done), custom_call_target="tpu_custom_call" | custom-call | bytes 3932160 | tf_op jit(solution)/shard_map/late/pallas_call | solution.py:309
  19.9 0.0 collective-permute-done.4.from2
  19.9 0.0 collective-permute-done.5.from8
  19.9 0.3 collective-permute-done.6.from1
  20.2 0.0 copy-done.1
  20.2 4.4 %remote.1 = (f32[80,16,128]{2,1,0:T(8,128)S(1)}, bf16[88,16,128]{2,1,0:T(8,128)(2,1)S(1)}, bf16[31,16,128]{2,1,0:T(8,128)(2,1)S(1)}, bf16[31,16,128]{2,1,0:T(8,1...) custom-call(s32[1,128]{1,0:T(1,128)S(1)} %get-tuple-element.19.asked.asked_row, ...), custom_call_target="tpu_custom_call" | custom-call | bytes 7864320 | tf_op jit(solution)/shard_map/remote/pallas_call | solution.py:313
  24.6 2.1 %collective-permute-start.8 = (bf16[31,16,128]{2,1,0:T(8,128)(2,1)S(1)}, bf16[31,16,128]{2,1,0:T(8,128)(2,1)S(1)}, u32[]{:S(2)}, u32[]{:S(2)}) collective-permute-start(bf16[31,16,128]{2,1,0:T(8,128)(2,1)S(1)} %get-tuple-element.28), channel_id=1, source_target_pairs={{0,3},{1,0},{2,1},{3,2},{4,7},{5,4},{6,5},{7,6},{8,11},{9,8},{10,9... | collective-permute-start | bytes 380936 | tf_op jit(solution)/shard_map/ppermute | solution.py:280
  26.7 1.3 %collective-permute-start.7 = (bf16[31,16,128]{2,1,0:T(8,128)(2,1)S(1)}, bf16[31,16,128]{2,1,0:T(8,128)(2,1)S(1)}, u32[]{:S(2)}, u32[]{:S(2)}) collective-permute-start(bf16[31,16,128]{2,1,0:T(8,128)(2,1)S(1)} %get-tuple-element.27), channel_id=1, source_target_pairs={{8,0},{9,1},{10,2},{11,3},{12,4},{13,5},{14,6},{15,7},{24,16},{25,... | collective-permute-start | bytes 380936 | tf_op jit(solution)/shard_map/ppermute | solution.py:280
  28.0 1.9 %collective-permute-start.9 = (bf16[31,16,128]{2,1,0:T(8,128)(2,1)S(1)}, bf16[31,16,128]{2,1,0:T(8,128)(2,1)S(1)}, u32[]{:S(2)}, u32[]{:S(2)}) collective-permute-start(bf16[31,16,128]{2,1,0:T(8,128)(2,1)S(1)} %get-tuple-element.29), channel_id=1, source_target_pairs={{4,0},{5,1},{6,2},{7,3},{8,4},{9,5},{10,6},{11,7},{12,8},{13,9},{1... | collective-permute-start | bytes 380936 | tf_op jit(solution)/shard_map/ppermute | solution.py:280
  29.9 2.4 %collective-permute-start.10 = (bf16[31,16,128]{2,1,0:T(8,128)(2,1)S(1)}, bf16[31,16,128]{2,1,0:T(8,128)(2,1)S(1)}, u32[]{:S(2)}, u32[]{:S(2)}) collective-permute-start(bf16[31,16,128]{2,1,0:T(8,128)(2,1)S(1)} %get-tuple-element.30), channel_id=1, source_target_pairs={{2,0},{3,1},{4,2},{5,3},{6,4},{7,5},{8,6},{9,7},{10,8},{11,9},{12,... | collective-permute-start | bytes 380936 | tf_op jit(solution)/shard_map/ppermute | solution.py:280
  32.3 0.0 collective-permute-done.8.ring
  32.3 1.9 %collective-permute-start.11 = (bf16[31,16,128]{2,1,0:T(8,128)(2,1)S(1)}, bf16[31,16,128]{2,1,0:T(8,128)(2,1)S(1)}, u32[]{:S(2)}, u32[]{:S(2)}) collective-permute-start(bf16[31,16,128]{2,1,0:T(8,128)(2,1)S(1)} %collective-permute-done.8.ring), channel_id=1, source_target_pairs={{7,3},{11,7},{15,11},{23,19},{27,23},{31,27}} | collective-permute-start | bytes 380936 | tf_op jit(solution)/shard_map/ppermute | solution.py:280
  34.3 3.7 %home.1.part = f32[80,16,128]{2,1,0:T(8,128)S(1)} custom-call(s32[3,80]{1,0:T(4,128)S(1)} %get-tuple-element.18.home, f32[80,16,128]{2,1,0:T(8,128)S(1)} %get-tuple-element.25.back, bf16[88,16,128]{2,1,0:T(8,128)(2,1)S(1)} %get-tuple-element.26.low, bf16[80,3,128,128]{3,2,1,0:T(8,128)(2,1)S(1)} %copy-done), custom_call_target="tpu_custom_call" | custom-call | bytes 7864320 | tf_op jit(solution)/shard_map/home/pallas_call | solution.py:325
  38.0 0.0 collective-permute-done.7.back8
  38.0 0.4 collective-permute-done.9.back4
  38.4 3.0 %collective-permute-done.10.back2 = bf16[31,16,128]{2,1,0:T(8,128)(2,1)S(1)} collective-permute-done((bf16[31,16,128]{2,1,0:T(8,128)(2,1)S(1)}, bf16[31,16,128]{2,1,0:T(8,128)(2,1)S(1)}, u32[]{:S(2)}, u32[]{:S(2)}) %collective-permute-start.10) | collective-permute-done | bytes 127008 | tf_op jit(solution)/shard_map/ppermute | solution.py:280
  41.4 0.0 collective-permute-done.11.relayed
  41.4 1.8 %add.1 = f32[80,16,128]{2,1,0:T(8,128)} custom-call(f32[80,16,128]{2,1,0:T(8,128)S(1)} %home.1.part, bf16[31,16,128]{2,1,0:T(8,128)(2,1)S(1)} %collective-permute-done.7.back8, bf16[31,16,128]{2,1,0:T(8,128)(2,1)S(1)} %collective-permute-done.8.ring, bf16[31,16,128]{2,1,0:T(8,128)(2,1)S(1)} %collective-permute-done.9.back4, ...), custom_call_target="tpu_custom_call" | custom-call | bytes 4194304 | tf_op jit(solution)/shard_map/add/pallas_call | solution.py:330
Async XLA Ops:
  0.0 18.4 %copy-start = (bf16[80,3,128,128]{3,2,1,0:T(8,128)(2,1)S(1)}, bf16[80,3,128,128]{3,2,1,0:T(8,128)(2,1)}, u32[]{:S(2)}) copy-start(bf16[80,3,128,128]{3,2,1,0:T(8,128)(2,1)} %weights.7) | copy-start | bytes 23592964
  0.0 12.2 %collective-permute-start = (bf16[80,16,128]{2,1,0:T(8,128)(2,1)}, bf16[80,16,128]{2,1,0:T(8,128)(2,1)S(1)}, u32[]{:S(2)}, u32[]{:S(2)}) collective-permute-start(bf16[80,16,128]{2,1,0:T(8,128)(2,1)} %latent.1), channel_id=1, source_target_pairs={{0,4},{1,5},{2,6},{3,7},{4,8},{5,9},{6,10},{7,11},{8,12},{9,13},{1... | collective-permute-start | bytes 983048 | tf_op jit(solution)/shard_map/ppermute | solution.py:280
  5.1 7.0 %collective-permute-start.3 = (s32[1,128]{1,0:T(1,128)S(1)}, s32[1,128]{1,0:T(1,128)S(1)}, u32[]{:S(2)}, u32[]{:S(2)}) collective-permute-start(s32[1,128]{1,0:T(1,128)S(1)} %get-tuple-element.19.asked.asked_row), channel_id=1, source_target_pairs={{4,0},{5,1},{6,2},{7,3},{8,4},{9,5},{10,6},{11,7},{12,8},{13,9},{1... | collective-permute-start | bytes 1544 | tf_op jit(solution)/shard_map/ppermute | solution.py:280
  7.2 4.9 %collective-permute-start.2 = (s32[1,128]{1,0:T(1,128)S(1)}, s32[1,128]{1,0:T(1,128)S(1)}, u32[]{:S(2)}, u32[]{:S(2)}) collective-permute-start(s32[1,128]{1,0:T(1,128)S(1)} %get-tuple-element.19.asked.asked_row), channel_id=1, source_target_pairs={{0,2},{1,3},{2,0},{3,1},{4,6},{5,7},{6,4},{7,5},{8,10},{9,11},{10,... | collective-permute-start | bytes 1544 | tf_op jit(solution)/shard_map/ppermute | solution.py:280
  7.5 4.6 %collective-permute-start.1 = (s32[1,128]{1,0:T(1,128)S(1)}, s32[1,128]{1,0:T(1,128)S(1)}, u32[]{:S(2)}, u32[]{:S(2)}) collective-permute-start(s32[1,128]{1,0:T(1,128)S(1)} %get-tuple-element.19.asked.asked_row), channel_id=1, source_target_pairs={{0,3},{1,0},{2,1},{3,2},{4,7},{5,4},{6,5},{7,6},{8,11},{9,8},{10,9... | collective-permute-start | bytes 1544 | tf_op jit(solution)/shard_map/ppermute | solution.py:280
  9.0 11.2 %copy-start.1 = (bf16[80,128,128]{2,1,0:T(8,128)(2,1)S(1)}, bf16[80,128,128]{2,1,0:T(8,128)(2,1)}, u32[]{:S(2)}) copy-start(bf16[80,128,128]{2,1,0:T(8,128)(2,1)} %factor.1) | copy-start | bytes 7864324
  12.8 7.1 %collective-permute-start.4 = (bf16[30,16,128]{2,1,0:T(8,128)(2,1)S(1)}, bf16[30,16,128]{2,1,0:T(8,128)(2,1)S(1)}, u32[]{:S(2)}, u32[]{:S(2)}) collective-permute-start(bf16[30,16,128]{2,1,0:T(8,128)(2,1)S(1)} %get-tuple-element.22), channel_id=1, source_target_pairs={{0,2},{1,3},{2,0},{3,1},{4,6},{5,7},{6,4},{7,5},{8,10},{9,11},{10,... | collective-permute-start | bytes 368648 | tf_op jit(solution)/shard_map/ppermute | solution.py:280
  14.1 5.8 %collective-permute-start.5 = (bf16[30,16,128]{2,1,0:T(8,128)(2,1)S(1)}, bf16[30,16,128]{2,1,0:T(8,128)(2,1)S(1)}, u32[]{:S(2)}, u32[]{:S(2)}) collective-permute-start(bf16[30,16,128]{2,1,0:T(8,128)(2,1)S(1)} %get-tuple-element.23), channel_id=1, source_target_pairs={{4,8},{5,9},{6,10},{7,11},{8,12},{9,13},{10,14},{11,15},{20,24},{2... | collective-permute-start | bytes 368648 | tf_op jit(solution)/shard_map/ppermute | solution.py:280
  17.3 2.9 %collective-permute-start.6 = (bf16[30,16,128]{2,1,0:T(8,128)(2,1)S(1)}, bf16[30,16,128]{2,1,0:T(8,128)(2,1)S(1)}, u32[]{:S(2)}, u32[]{:S(2)}) collective-permute-start(bf16[30,16,128]{2,1,0:T(8,128)(2,1)S(1)} %get-tuple-element.24), channel_id=1, source_target_pairs={{0,1},{1,2},{2,3},{3,0},{4,5},{5,6},{6,7},{7,4},{8,9},{9,10},{10,1... | collective-permute-start | bytes 368648 | tf_op jit(solution)/shard_map/ppermute | solution.py:280
  24.6 7.7 %collective-permute-start.8 = (bf16[31,16,128]{2,1,0:T(8,128)(2,1)S(1)}, bf16[31,16,128]{2,1,0:T(8,128)(2,1)S(1)}, u32[]{:S(2)}, u32[]{:S(2)}) collective-permute-start(bf16[31,16,128]{2,1,0:T(8,128)(2,1)S(1)} %get-tuple-element.28), channel_id=1, source_target_pairs={{0,3},{1,0},{2,1},{3,2},{4,7},{5,4},{6,5},{7,6},{8,11},{9,8},{10,9... | collective-permute-start | bytes 380936 | tf_op jit(solution)/shard_map/ppermute | solution.py:280
  26.7 11.3 %collective-permute-start.7 = (bf16[31,16,128]{2,1,0:T(8,128)(2,1)S(1)}, bf16[31,16,128]{2,1,0:T(8,128)(2,1)S(1)}, u32[]{:S(2)}, u32[]{:S(2)}) collective-permute-start(bf16[31,16,128]{2,1,0:T(8,128)(2,1)S(1)} %get-tuple-element.27), channel_id=1, source_target_pairs={{8,0},{9,1},{10,2},{11,3},{12,4},{13,5},{14,6},{15,7},{24,16},{25,... | collective-permute-start | bytes 380936 | tf_op jit(solution)/shard_map/ppermute | solution.py:280
  28.0 10.4 %collective-permute-start.9 = (bf16[31,16,128]{2,1,0:T(8,128)(2,1)S(1)}, bf16[31,16,128]{2,1,0:T(8,128)(2,1)S(1)}, u32[]{:S(2)}, u32[]{:S(2)}) collective-permute-start(bf16[31,16,128]{2,1,0:T(8,128)(2,1)S(1)} %get-tuple-element.29), channel_id=1, source_target_pairs={{4,0},{5,1},{6,2},{7,3},{8,4},{9,5},{10,6},{11,7},{12,8},{13,9},{1... | collective-permute-start | bytes 380936 | tf_op jit(solution)/shard_map/ppermute | solution.py:280
  29.9 11.5 %collective-permute-start.10 = (bf16[31,16,128]{2,1,0:T(8,128)(2,1)S(1)}, bf16[31,16,128]{2,1,0:T(8,128)(2,1)S(1)}, u32[]{:S(2)}, u32[]{:S(2)}) collective-permute-start(bf16[31,16,128]{2,1,0:T(8,128)(2,1)S(1)} %get-tuple-element.30), channel_id=1, source_target_pairs={{2,0},{3,1},{4,2},{5,3},{6,4},{7,5},{8,6},{9,7},{10,8},{11,9},{12,... | collective-permute-start | bytes 380936 | tf_op jit(solution)/shard_map/ppermute | solution.py:280
  32.3 9.0 %collective-permute-start.11 = (bf16[31,16,128]{2,1,0:T(8,128)(2,1)S(1)}, bf16[31,16,128]{2,1,0:T(8,128)(2,1)S(1)}, u32[]{:S(2)}, u32[]{:S(2)}) collective-permute-start(bf16[31,16,128]{2,1,0:T(8,128)(2,1)S(1)} %collective-permute-done.8.ring), channel_id=1, source_target_pairs={{7,3},{11,7},{15,11},{23,19},{27,23},{31,27}} | collective-permute-start | bytes 380936 | tf_op jit(solution)/shard_map/ppermute | solution.py:280

commit v11 on v10

--- a/solution.py
+++ b/solution.py
@@ -8,20 +8,14 @@
 from jax.sharding import PartitionSpec as P
 
 SLOTS = 32
-PART = 16
 LEAVES = 40
 MIB = 2**20
 BY_ROWS = (((1,), (1,)), ((), ()))
 VMEM, SMEM, HBM, ANY = pltpu.VMEM, pltpu.SMEM, pltpu.HBM, pl.ANY
 
 
-def index_kernel(
-    lists, latent, asked, slots, home, rows, row_sem
-):
+def index_kernel(lists, latent, weights, asked, slots, home):
     fan, leaf_dev = lists.shape
-    fetch = pltpu.make_async_copy(latent, rows.at[pl.ds(0, leaf_dev)], row_sem)
-    fetch.start()
-    rows[leaf_dev] = jnp.zeros(latent.shape[1:], latent.dtype)
     me = lax.axis_index("kx")
     behind = me * leaf_dev - lists[...]
     kind = (
@@ -71,7 +65,6 @@
     asked[...] = total[0:1].astype(jnp.int32)
     slots[0:1] = jnp.where(total[3:4] > 0.0, total[1:2], float(leaf_dev)).astype(jnp.int32)
     slots[1:2] = total[2:3].astype(jnp.int32)
-    fetch.wait()
 
 
 def beside(xs):
@@ -95,35 +88,25 @@
     return both[:samples, :wide], both[samples:, wide:]
 
 
-def local_means(home, rows, held, left, first, leaves):
-    fan, width = held.shape[1], held.shape[2]
-    for i in leaves:
-        mean = jnp.dot(
-            beside([rows[home[k, i]] for k in range(fan)]),
-            held[i].reshape(fan * width, width), preferred_element_type=jnp.float32,
-        )
-        left[i - first] = rows[i].astype(jnp.float32) - mean
-
-
-def early_kernel(home, rows, weights, left, held, sem):
-    parts = [pl.ds(at, PART) for at in range(0, left.shape[0], PART)]
-    fetches = [
-        pltpu.make_async_copy(weights.at[p], held.at[p], sem.at[n]) for n, p in enumerate(parts)
-    ]
-    for fetch in fetches:
-        fetch.start()
-    for n, fetch in enumerate(fetches):
-        fetch.wait()
-        local_means(home, rows, held, left, 0, range(n * PART, (n + 1) * PART))
-
-
-def late_kernel(home, rows, before, weights, left):
-    leaf_dev = weights.shape[0]
-    first = leaf_dev - left.shape[0]
-    local_means(home, rows, weights, left, first, range(first, leaf_dev))
-
-
-def serve_kernel(capacity, ask1, ask2, ask8, latent, before, left, out8, out2, out1):
+def local_kernel(home, latent, before, weights, left, rows):
+    leaf_dev, fan, width = latent.shape[0], weights.shape[1], weights.shape[2]
+    rows[pl.ds(0, leaf_dev)] = latent[...]
+    rows[leaf_dev] = jnp.zeros(latent.shape[1:], latent.dtype)
+
+    def some(c, carry):
+        for u in range(LEAVES):
+            i = c * LEAVES + u
+            mean = jnp.dot(
+                beside([rows[home[k, i]] for k in range(fan)]),
+                weights[i].reshape(fan * width, width), preferred_element_type=jnp.float32,
+            )
+            left[i] = latent[i].astype(jnp.float32) - mean
+        return carry
+
+    lax.fori_loop(0, leaf_dev // LEAVES, some, 0)
+
+
+def serve_kernel(capacity, ask1, ask2, ask8, latent, before, out8, out2, out1):
     me = lax.axis_index("kx")
     def pick(o, ask, rows, out):
         for r in range(capacity):
@@ -158,12 +141,11 @@
 
 
 def remote_kernel(
-    capacity, asked, slots, asked_row, left, later, before, from2, from8, from1,
+    capacity, asked, slots, asked_row, left, before, from2, from8, from1,
     weights, factor, back, low, out8, out4, out2, out1, resid,
 ):
-    leaf_dev, half = back.shape[0], left.shape[0]
-    resid[pl.ds(0, half)] = left[...]
-    resid[pl.ds(half, leaf_dev - half)] = later[...]
+    leaf_dev = back.shape[0]
+    resid[pl.ds(0, leaf_dev)] = left[...]
     resid[leaf_dev] = jnp.zeros(left.shape[1:], left.dtype)
     low[leaf_dev] = jnp.zeros(left.shape[1:], low.dtype)
 
@@ -281,41 +263,32 @@
 
     before = passed(latent, [(i, i + 4) for i in everyone if i + 4 < devices])
     weights, factor = placed(cond_weights, VMEM), placed(precision_factor, VMEM)
-    dma = pltpu.SemaphoreType.DMA
-    asked, slots, home, rows = call(
+    held_l = placed(latent, VMEM)
+    asked, slots, home = call(
         index_kernel, "index",
-        (
-            one_list, shape((2, 4 * SLOTS), jnp.int32), shape((fan, leaf_dev), jnp.int32),
-            shape((leaf_dev + 8, samples, width), jnp.bfloat16),
-        ),
-        [VMEM, HBM], [VMEM] * 4, 4, moved=2 * MIB, scratch=[dma],
-    )(placed(cond_lists.T, HBM), placed(latent, HBM))
+        (one_list, shape((2, 4 * SLOTS), jnp.int32), shape((fan, leaf_dev), jnp.int32)),
+        [VMEM, HBM, HBM], [VMEM] * 3, 4, moved=2 * MIB,
+    )(placed(cond_lists.T, HBM), placed(latent, HBM), placed(cond_weights, HBM))
     ask8 = passed(asked, [(i, i - 4) for i in everyone if i >= 4])
     ask2 = passed(asked, [(i, i ^ 2) for i in everyone])
     ask1 = passed(asked, [(i, i // 4 * 4 + (i + 3) % 4) for i in everyone])
-    most = 2 * leaf_dev // 5 // PART * PART
-    (left,) = call(
-        early_kernel, "early", (shape((most, samples, width), jnp.float32),),
-        [SMEM, VMEM, HBM], [VMEM], 6, moved=heavy // 2,
-        scratch=[VMEM((most,) + cond_weights.shape[1:], jnp.bfloat16), dma((most // PART,))],
-    )(home, rows, placed(cond_weights, HBM))
     serve8, serve2, serve1 = call(
         functools.partial(serve_kernel, capacity), "serve", (some_rows,) * 3,
-        [SMEM] * 3 + [VMEM] * 2 + [ANY], [VMEM] * 3, 4, moved=4 * MIB,
-    )(ask1, ask2, ask8, rows, before, left)
+        [SMEM] * 3 + [VMEM] * 2, [VMEM] * 3, 4, moved=4 * MIB,
+    )(ask1, ask2, ask8, held_l, before)
     from8 = passed(serve8, [(i, i + 4) for i in everyone if i >= 4 and i + 4 < devices])
     from2 = passed(serve2, [(i, i ^ 2) for i in everyone])
     from1 = passed(serve1, [(i, i // 4 * 4 + (i + 1) % 4) for i in everyone])
-    (later,) = call(
-        late_kernel, "late", (shape((leaf_dev - most, samples, width), jnp.float32),),
-        [SMEM, VMEM, ANY, VMEM], [VMEM], 4, moved=heavy // 2,
-    )(home, rows, before, weights)
+    (left,) = call(
+        local_kernel, "local", (all_rows,), [SMEM, VMEM, ANY, VMEM], [VMEM], 6, moved=heavy,
+        scratch=[VMEM((leaf_dev + 8, samples, width), jnp.bfloat16)],
+    )(home, held_l, before, weights)
     back, low, out8, out4, out2, out1 = call(
         functools.partial(remote_kernel, capacity), "remote",
         (all_rows, shape((leaf_dev + 8, samples, width), jnp.bfloat16)) + (sent,) * 4,
-        [SMEM] * 2 + [VMEM] * 9, [VMEM] * 6, 8, moved=heavy,
+        [SMEM] * 2 + [VMEM] * 8, [VMEM] * 6, 8, moved=heavy,
         scratch=[VMEM((leaf_dev + 8, samples, width), jnp.float32)],
-    )(asked, slots, asked, left, later, before, from2, from8, from1, weights, factor)
+    )(asked, slots, asked, left, before, from2, from8, from1, weights, factor)
     def back_by(x, reach):
         return passed(x, [(i, i - reach) for i in everyone if i >= reach])
 
@@ -329,7 +302,7 @@
     lists = (4, 4 * SLOTS)
     (gradient,) = call(
         functools.partial(add_kernel, capacity), "add", (all_rows,), [VMEM] * 6,
-        [VMEM], 6, moved=4 * MIB, scratch=[VMEM(lists, jnp.int32), SMEM(lists, jnp.int32), dma],
+        [VMEM], 6, moved=4 * MIB, scratch=[VMEM(lists, jnp.int32), SMEM(lists, jnp.int32), pltpu.SemaphoreType.DMA],
     )(part, back8, ring, back4, back2, relayed)
     return gradient
 

time: 43.5 us -> 43.5 us (level)
  Pallas kernels: 16.7 us -> 13.8 us
  waiting for transfers between devices: 3.75 us -> 6.06 us
  starting transfers between devices: 22.5 us -> 23.1 us
    pallas_call x2 -> x1, Pallas kernels: 4.6 us -> 2.19 us  [per_device(): call(local_kernel, 'local', (all_rows,), [SMEM, VMEM, ANY, VMEM], [VMEM],...]
    ppermute x12, waiting for transfers between devices: 3.75 us -> 6.06 us  [passed(): return lax.ppermute(x, 'kx', route)]
    ppermute x12, starting transfers between devices: 22.5 us -> 23.1 us  [passed(): return lax.ppermute(x, 'kx', route)]
    pallas_call x1, Pallas kernels: 1.66 us -> 1.16 us  [per_device(): call(index_kernel, 'index', (one_list, shape((2, 4 * SLOTS), jnp.int32),...]
  transfers between devices with their start and end apart: 12 -> 12, of which waited for: 3 -> 4; matrix products, arithmetic and copies ran while one was open for 0% -> 0% of each run, Pallas kernels for 23% -> 16%
where the time goes in v11:
time: 43.5 us; the launch traced here: 43.2 us
  starting transfers between devices  23.1 us (53%)
  Pallas kernels  13.8 us (32%)
  waiting for transfers between devices  6.06 us (14%)
    ppermute x12, starting transfers between devices, passed(): return lax.ppermute(x, 'kx', route)  23.1 us
    ppermute x12, waiting for transfers between devices, passed(): return lax.ppermute(x, 'kx', route)  6.06 us
    pallas_call x1, Pallas kernels, per_device(): call(functools.partial(remote_kernel, capacity), 'remote', (all_rows, sha...  4.37 us
    pallas_call x1, Pallas kernels, per_device(): call(home_kernel, 'home', (all_rows,), [SMEM] + [VMEM] * 3, [VMEM], 6, mo...  3.67 us
    pallas_call x1, Pallas kernels, per_device(): call(local_kernel, 'local', (all_rows,), [SMEM, VMEM, ANY, VMEM], [VMEM],...  2.19 us
    pallas_call x1, Pallas kernels, per_device(): call(functools.partial(add_kernel, capacity), 'add', (all_rows,), [VMEM]...  1.81 us
    pallas_call x1, Pallas kernels, per_device(): call(index_kernel, 'index', (one_list, shape((2, 4 * SLOTS), jnp.int32),...  1.16 us
  transfers between devices with their start and end apart: 12, of which 4 were waited for; matrix products, arithmetic and copies ran while one was open for 0% of the time, Pallas kernels for 16%

profile of v11, /device:TPU:15, one launch (start us, length us, event | category | flops | bytes accessed | tf_op | source)
XLA Modules:
  0.0 43.2 jit_solution(199715936029592131)
XLA Ops:
  0.0 0.0 copy-start.1
  0.0 0.0 copy-start
  0.0 3.5 %collective-permute-start = (bf16[80,16,128]{2,1,0:T(8,128)(2,1)}, bf16[80,16,128]{2,1,0:T(8,128)(2,1)S(1)}, u32[]{:S(2)}, u32[]{:S(2)}) collective-permute-start(bf16[80,16,128]{2,1,0:T(8,128)(2,1)} %latent.5), channel_id=1, source_target_pairs={{0,4},{1,5},{2,6},{3,7},{4,8},{5,9},{6,10},{7,11},{8,12},{9,13},{1... | collective-permute-start | bytes 983048 | tf_op jit(solution)/shard_map/ppermute | solution.py:262
  3.5 0.0 copy-start.2
  3.5 1.2 %index.1 = (s32[1,128]{1,0:T(1,128)S(1)}, s32[2,128]{1,0:T(2,128)S(1)}, s32[3,80]{1,0:T(4,128)S(1)}) custom-call(s32[3,80]{1,0:T(4,128)} %bitcast.1, bf16[80,16,128]{2,1,0:T(8,128)(2,1)} %latent.5, bf16[80,3,128,128]{3,2,1,0:T(8,128)(2,1)} %weights.7), custom_call_target="tpu_custom_call" | custom-call | bytes 2097152 | tf_op jit(solution)/shard_map/index/pallas_call | solution.py:267
  4.6 2.1 %collective-permute-start.3 = (s32[1,128]{1,0:T(1,128)S(1)}, s32[1,128]{1,0:T(1,128)S(1)}, u32[]{:S(2)}, u32[]{:S(2)}) collective-permute-start(s32[1,128]{1,0:T(1,128)S(1)} %get-tuple-element.18.asked.asked_row), channel_id=1, source_target_pairs={{4,0},{5,1},{6,2},{7,3},{8,4},{9,5},{10,6},{11,7},{12,8},{13,9},{1... | collective-permute-start | bytes 1544 | tf_op jit(solution)/shard_map/ppermute | solution.py:262
  6.8 0.3 collective-permute-start.2
  7.1 1.5 %collective-permute-start.1 = (s32[1,128]{1,0:T(1,128)S(1)}, s32[1,128]{1,0:T(1,128)S(1)}, u32[]{:S(2)}, u32[]{:S(2)}) collective-permute-start(s32[1,128]{1,0:T(1,128)S(1)} %get-tuple-element.18.asked.asked_row), channel_id=1, source_target_pairs={{0,3},{1,0},{2,1},{3,2},{4,7},{5,4},{6,5},{7,6},{8,11},{9,8},{10,9... | collective-permute-start | bytes 1544 | tf_op jit(solution)/shard_map/ppermute | solution.py:262
  8.6 0.7 %collective-permute-done.3.ask8 = s32[1,128]{1,0:T(1,128)S(1)} collective-permute-done((s32[1,128]{1,0:T(1,128)S(1)}, s32[1,128]{1,0:T(1,128)S(1)}, u32[]{:S(2)}, u32[]{:S(2)}) %collective-permute-start.3) | collective-permute-done | bytes 544 | tf_op jit(solution)/shard_map/ppermute | solution.py:262
  9.3 0.3 collective-permute-done.2.ask2
  9.5 1.7 %collective-permute-done.1.ask1 = s32[1,128]{1,0:T(1,128)S(1)} collective-permute-done((s32[1,128]{1,0:T(1,128)S(1)}, s32[1,128]{1,0:T(1,128)S(1)}, u32[]{:S(2)}, u32[]{:S(2)}) %collective-permute-start.1) | collective-permute-done | bytes 544 | tf_op jit(solution)/shard_map/ppermute | solution.py:262
  11.2 0.0 collective-permute-done.before
  11.3 0.0 copy-done.1
  11.3 0.6 %serve.1 = (bf16[30,16,128]{2,1,0:T(8,128)(2,1)S(1)}, bf16[30,16,128]{2,1,0:T(8,128)(2,1)S(1)}, bf16[30,16,128]{2,1,0:T(8,128)(2,1)S(1)}) custom-call(s32[1,128]{1,0:T(1,128)S(1)} %collective-permute-done.1.ask1, s32[1,128]{1,0:T(1,128)S(1)} %collective-permute-done.2.ask2, s32[1,128]{1,0:T(1,128)S(1)} %collective-permute-done.3.ask8, ...), custom_call_target="tpu_custom_call" | custom-call | bytes 4194304 | tf_op jit(solution)/shard_map/serve/pallas_call | solution.py:275
  11.9 0.4 collective-permute-start.4
  12.3 3.2 %collective-permute-start.5 = (bf16[30,16,128]{2,1,0:T(8,128)(2,1)S(1)}, bf16[30,16,128]{2,1,0:T(8,128)(2,1)S(1)}, u32[]{:S(2)}, u32[]{:S(2)}) collective-permute-start(bf16[30,16,128]{2,1,0:T(8,128)(2,1)S(1)} %get-tuple-element.21), channel_id=1, source_target_pairs={{4,8},{5,9},{6,10},{7,11},{8,12},{9,13},{10,14},{11,15},{20,24},{2... | collective-permute-start | bytes 368648 | tf_op jit(solution)/shard_map/ppermute | solution.py:262
  15.5 2.9 %collective-permute-start.6 = (bf16[30,16,128]{2,1,0:T(8,128)(2,1)S(1)}, bf16[30,16,128]{2,1,0:T(8,128)(2,1)S(1)}, u32[]{:S(2)}, u32[]{:S(2)}) collective-permute-start(bf16[30,16,128]{2,1,0:T(8,128)(2,1)S(1)} %get-tuple-element.22), channel_id=1, source_target_pairs={{0,1},{1,2},{2,3},{3,0},{4,5},{5,6},{6,7},{7,4},{8,9},{9,10},{10,1... | collective-permute-start | bytes 368648 | tf_op jit(solution)/shard_map/ppermute | solution.py:262
  18.4 0.0 copy-done
  18.4 2.2 %local.1.left = f32[80,16,128]{2,1,0:T(8,128)S(1)} custom-call(s32[3,80]{1,0:T(4,128)S(1)} %get-tuple-element.17.home, bf16[80,16,128]{2,1,0:T(8,128)(2,1)S(1)} %copy-done.1, bf16[80,16,128]{2,1,0:T(8,128)(2,1)S(1)} %collective-permute-done.before, bf16[80,3,128,128]{3,2,1,0:T(8,128)(2,1)S(1)} %copy-done), custom_call_target="tpu_custom_call" | custom-call | bytes 7864320 | tf_op jit(solution)/shard_map/local/pallas_call | solution.py:282
  20.6 0.0 collective-permute-done.4.from2
  20.6 0.0 collective-permute-done.5.from8
  20.6 0.0 collective-permute-done.6.from1
  20.6 0.0 copy-done.2
  20.6 4.4 %remote.1 = (f32[80,16,128]{2,1,0:T(8,128)S(1)}, bf16[88,16,128]{2,1,0:T(8,128)(2,1)S(1)}, bf16[31,16,128]{2,1,0:T(8,128)(2,1)S(1)}, bf16[31,16,128]{2,1,0:T(8,1...) custom-call(s32[1,128]{1,0:T(1,128)S(1)} %get-tuple-element.18.asked.asked_row, ...), custom_call_target="tpu_custom_call" | custom-call | bytes 7864320 | tf_op jit(solution)/shard_map/remote/pallas_call | solution.py:286
  25.0 1.0 %collective-permute-start.8 = (bf16[31,16,128]{2,1,0:T(8,128)(2,1)S(1)}, bf16[31,16,128]{2,1,0:T(8,128)(2,1)S(1)}, u32[]{:S(2)}, u32[]{:S(2)}) collective-permute-start(bf16[31,16,128]{2,1,0:T(8,128)(2,1)S(1)} %get-tuple-element.26), channel_id=1, source_target_pairs={{0,3},{1,0},{2,1},{3,2},{4,7},{5,4},{6,5},{7,6},{8,11},{9,8},{10,9... | collective-permute-start | bytes 380936 | tf_op jit(solution)/shard_map/ppermute | solution.py:262
  26.0 1.3 %collective-permute-start.7 = (bf16[31,16,128]{2,1,0:T(8,128)(2,1)S(1)}, bf16[31,16,128]{2,1,0:T(8,128)(2,1)S(1)}, u32[]{:S(2)}, u32[]{:S(2)}) collective-permute-start(bf16[31,16,128]{2,1,0:T(8,128)(2,1)S(1)} %get-tuple-element.25), channel_id=1, source_target_pairs={{8,0},{9,1},{10,2},{11,3},{12,4},{13,5},{14,6},{15,7},{24,16},{25,... | collective-permute-start | bytes 380936 | tf_op jit(solution)/shard_map/ppermute | solution.py:262
  27.3 1.9 %collective-permute-start.9 = (bf16[31,16,128]{2,1,0:T(8,128)(2,1)S(1)}, bf16[31,16,128]{2,1,0:T(8,128)(2,1)S(1)}, u32[]{:S(2)}, u32[]{:S(2)}) collective-permute-start(bf16[31,16,128]{2,1,0:T(8,128)(2,1)S(1)} %get-tuple-element.27), channel_id=1, source_target_pairs={{4,0},{5,1},{6,2},{7,3},{8,4},{9,5},{10,6},{11,7},{12,8},{13,9},{1... | collective-permute-start | bytes 380936 | tf_op jit(solution)/shard_map/ppermute | solution.py:262
  29.2 3.1 %collective-permute-start.10 = (bf16[31,16,128]{2,1,0:T(8,128)(2,1)S(1)}, bf16[31,16,128]{2,1,0:T(8,128)(2,1)S(1)}, u32[]{:S(2)}, u32[]{:S(2)}) collective-permute-start(bf16[31,16,128]{2,1,0:T(8,128)(2,1)S(1)} %get-tuple-element.28), channel_id=1, source_target_pairs={{2,0},{3,1},{4,2},{5,3},{6,4},{7,5},{8,6},{9,7},{10,8},{11,9},{12,... | collective-permute-start | bytes 380936 | tf_op jit(solution)/shard_map/ppermute | solution.py:262
  32.3 0.0 collective-permute-done.8.ring
  32.4 1.9 %collective-permute-start.11 = (bf16[31,16,128]{2,1,0:T(8,128)(2,1)S(1)}, bf16[31,16,128]{2,1,0:T(8,128)(2,1)S(1)}, u32[]{:S(2)}, u32[]{:S(2)}) collective-permute-start(bf16[31,16,128]{2,1,0:T(8,128)(2,1)S(1)} %collective-permute-done.8.ring), channel_id=1, source_target_pairs={{7,3},{11,7},{15,11},{23,19},{27,23},{31,27}} | collective-permute-start | bytes 380936 | tf_op jit(solution)/shard_map/ppermute | solution.py:262
  34.3 3.7 %home.1.part = f32[80,16,128]{2,1,0:T(8,128)S(1)} custom-call(s32[3,80]{1,0:T(4,128)S(1)} %get-tuple-element.17.home, f32[80,16,128]{2,1,0:T(8,128)S(1)} %get-tuple-element.23.back, bf16[88,16,128]{2,1,0:T(8,128)(2,1)S(1)} %get-tuple-element.24.low, bf16[80,3,128,128]{3,2,1,0:T(8,128)(2,1)S(1)} %copy-done), custom_call_target="tpu_custom_call" | custom-call | bytes 7864320 | tf_op jit(solution)/shard_map/home/pallas_call | solution.py:298
  38.0 0.0 collective-permute-done.7.back8
  38.0 0.0 collective-permute-done.9.back4
  38.0 3.4 %collective-permute-done.10.back2 = bf16[31,16,128]{2,1,0:T(8,128)(2,1)S(1)} collective-permute-done((bf16[31,16,128]{2,1,0:T(8,128)(2,1)S(1)}, bf16[31,16,128]{2,1,0:T(8,128)(2,1)S(1)}, u32[]{:S(2)}, u32[]{:S(2)}) %collective-permute-start.10) | collective-permute-done | bytes 127008 | tf_op jit(solution)/shard_map/ppermute | solution.py:262
  41.4 0.0 collective-permute-done.11.relayed
  41.4 1.8 %add.1 = f32[80,16,128]{2,1,0:T(8,128)} custom-call(f32[80,16,128]{2,1,0:T(8,128)S(1)} %home.1.part, bf16[31,16,128]{2,1,0:T(8,128)(2,1)S(1)} %collective-permute-done.7.back8, bf16[31,16,128]{2,1,0:T(8,128)(2,1)S(1)} %collective-permute-done.8.ring, bf16[31,16,128]{2,1,0:T(8,128)(2,1)S(1)} %collective-permute-done.9.back4, ...), custom_call_target="tpu_custom_call" | custom-call | bytes 4194304 | tf_op jit(solution)/shard_map/add/pallas_call | solution.py:303
Async XLA Ops:
  0.0 11.3 %copy-start.1 = (bf16[80,16,128]{2,1,0:T(8,128)(2,1)S(1)}, bf16[80,16,128]{2,1,0:T(8,128)(2,1)}, u32[]{:S(2)}) copy-start(bf16[80,16,128]{2,1,0:T(8,128)(2,1)} %latent.5) | copy-start | bytes 983044
  0.0 18.4 %copy-start = (bf16[80,3,128,128]{3,2,1,0:T(8,128)(2,1)S(1)}, bf16[80,3,128,128]{3,2,1,0:T(8,128)(2,1)}, u32[]{:S(2)}) copy-start(bf16[80,3,128,128]{3,2,1,0:T(8,128)(2,1)} %weights.7) | copy-start | bytes 23592964
  0.0 11.2 %collective-permute-start = (bf16[80,16,128]{2,1,0:T(8,128)(2,1)}, bf16[80,16,128]{2,1,0:T(8,128)(2,1)S(1)}, u32[]{:S(2)}, u32[]{:S(2)}) collective-permute-start(bf16[80,16,128]{2,1,0:T(8,128)(2,1)} %latent.5), channel_id=1, source_target_pairs={{0,4},{1,5},{2,6},{3,7},{4,8},{5,9},{6,10},{7,11},{8,12},{9,13},{1... | collective-permute-start | bytes 983048 | tf_op jit(solution)/shard_map/ppermute | solution.py:262
  3.5 17.1 %copy-start.2 = (bf16[80,128,128]{2,1,0:T(8,128)(2,1)S(1)}, bf16[80,128,128]{2,1,0:T(8,128)(2,1)}, u32[]{:S(2)}) copy-start(bf16[80,128,128]{2,1,0:T(8,128)(2,1)} %factor.1) | copy-start | bytes 7864324
  4.6 4.6 %collective-permute-start.3 = (s32[1,128]{1,0:T(1,128)S(1)}, s32[1,128]{1,0:T(1,128)S(1)}, u32[]{:S(2)}, u32[]{:S(2)}) collective-permute-start(s32[1,128]{1,0:T(1,128)S(1)} %get-tuple-element.18.asked.asked_row), channel_id=1, source_target_pairs={{4,0},{5,1},{6,2},{7,3},{8,4},{9,5},{10,6},{11,7},{12,8},{13,9},{1... | collective-permute-start | bytes 1544 | tf_op jit(solution)/shard_map/ppermute | solution.py:262
  6.8 2.8 %collective-permute-start.2 = (s32[1,128]{1,0:T(1,128)S(1)}, s32[1,128]{1,0:T(1,128)S(1)}, u32[]{:S(2)}, u32[]{:S(2)}) collective-permute-start(s32[1,128]{1,0:T(1,128)S(1)} %get-tuple-element.18.asked.asked_row), channel_id=1, source_target_pairs={{0,2},{1,3},{2,0},{3,1},{4,6},{5,7},{6,4},{7,5},{8,10},{9,11},{10,... | collective-permute-start | bytes 1544 | tf_op jit(solution)/shard_map/ppermute | solution.py:262
  7.1 4.2 %collective-permute-start.1 = (s32[1,128]{1,0:T(1,128)S(1)}, s32[1,128]{1,0:T(1,128)S(1)}, u32[]{:S(2)}, u32[]{:S(2)}) collective-permute-start(s32[1,128]{1,0:T(1,128)S(1)} %get-tuple-element.18.asked.asked_row), channel_id=1, source_target_pairs={{0,3},{1,0},{2,1},{3,2},{4,7},{5,4},{6,5},{7,6},{8,11},{9,8},{10,9... | collective-permute-start | bytes 1544 | tf_op jit(solution)/shard_map/ppermute | solution.py:262
  11.9 8.7 %collective-permute-start.4 = (bf16[30,16,128]{2,1,0:T(8,128)(2,1)S(1)}, bf16[30,16,128]{2,1,0:T(8,128)(2,1)S(1)}, u32[]{:S(2)}, u32[]{:S(2)}) collective-permute-start(bf16[30,16,128]{2,1,0:T(8,128)(2,1)S(1)} %get-tuple-element.20), channel_id=1, source_target_pairs={{0,2},{1,3},{2,0},{3,1},{4,6},{5,7},{6,4},{7,5},{8,10},{9,11},{10,... | collective-permute-start | bytes 368648 | tf_op jit(solution)/shard_map/ppermute | solution.py:262
  12.3 8.3 %collective-permute-start.5 = (bf16[30,16,128]{2,1,0:T(8,128)(2,1)S(1)}, bf16[30,16,128]{2,1,0:T(8,128)(2,1)S(1)}, u32[]{:S(2)}, u32[]{:S(2)}) collective-permute-start(bf16[30,16,128]{2,1,0:T(8,128)(2,1)S(1)} %get-tuple-element.21), channel_id=1, source_target_pairs={{4,8},{5,9},{6,10},{7,11},{8,12},{9,13},{10,14},{11,15},{20,24},{2... | collective-permute-start | bytes 368648 | tf_op jit(solution)/shard_map/ppermute | solution.py:262
  15.5 5.1 %collective-permute-start.6 = (bf16[30,16,128]{2,1,0:T(8,128)(2,1)S(1)}, bf16[30,16,128]{2,1,0:T(8,128)(2,1)S(1)}, u32[]{:S(2)}, u32[]{:S(2)}) collective-permute-start(bf16[30,16,128]{2,1,0:T(8,128)(2,1)S(1)} %get-tuple-element.22), channel_id=1, source_target_pairs={{0,1},{1,2},{2,3},{3,0},{4,5},{5,6},{6,7},{7,4},{8,9},{9,10},{10,1... | collective-permute-start | bytes 368648 | tf_op jit(solution)/shard_map/ppermute | solution.py:262
  25.0 7.4 %collective-permute-start.8 = (bf16[31,16,128]{2,1,0:T(8,128)(2,1)S(1)}, bf16[31,16,128]{2,1,0:T(8,128)(2,1)S(1)}, u32[]{:S(2)}, u32[]{:S(2)}) collective-permute-start(bf16[31,16,128]{2,1,0:T(8,128)(2,1)S(1)} %get-tuple-element.26), channel_id=1, source_target_pairs={{0,3},{1,0},{2,1},{3,2},{4,7},{5,4},{6,5},{7,6},{8,11},{9,8},{10,9... | collective-permute-start | bytes 380936 | tf_op jit(solution)/shard_map/ppermute | solution.py:262
  26.0 12.0 %collective-permute-start.7 = (bf16[31,16,128]{2,1,0:T(8,128)(2,1)S(1)}, bf16[31,16,128]{2,1,0:T(8,128)(2,1)S(1)}, u32[]{:S(2)}, u32[]{:S(2)}) collective-permute-start(bf16[31,16,128]{2,1,0:T(8,128)(2,1)S(1)} %get-tuple-element.25), channel_id=1, source_target_pairs={{8,0},{9,1},{10,2},{11,3},{12,4},{13,5},{14,6},{15,7},{24,16},{25,... | collective-permute-start | bytes 380936 | tf_op jit(solution)/shard_map/ppermute | solution.py:262
  27.3 10.7 %collective-permute-start.9 = (bf16[31,16,128]{2,1,0:T(8,128)(2,1)S(1)}, bf16[31,16,128]{2,1,0:T(8,128)(2,1)S(1)}, u32[]{:S(2)}, u32[]{:S(2)}) collective-permute-start(bf16[31,16,128]{2,1,0:T(8,128)(2,1)S(1)} %get-tuple-element.27), channel_id=1, source_target_pairs={{4,0},{5,1},{6,2},{7,3},{8,4},{9,5},{10,6},{11,7},{12,8},{13,9},{1... | collective-permute-start | bytes 380936 | tf_op jit(solution)/shard_map/ppermute | solution.py:262
  29.2 12.2 %collective-permute-start.10 = (bf16[31,16,128]{2,1,0:T(8,128)(2,1)S(1)}, bf16[31,16,128]{2,1,0:T(8,128)(2,1)S(1)}, u32[]{:S(2)}, u32[]{:S(2)}) collective-permute-start(bf16[31,16,128]{2,1,0:T(8,128)(2,1)S(1)} %get-tuple-element.28), channel_id=1, source_target_pairs={{2,0},{3,1},{4,2},{5,3},{6,4},{7,5},{8,6},{9,7},{10,8},{11,9},{12,... | collective-permute-start | bytes 380936 | tf_op jit(solution)/shard_map/ppermute | solution.py:262
  32.4 9.0 %collective-permute-start.11 = (bf16[31,16,128]{2,1,0:T(8,128)(2,1)S(1)}, bf16[31,16,128]{2,1,0:T(8,128)(2,1)S(1)}, u32[]{:S(2)}, u32[]{:S(2)}) collective-permute-start(bf16[31,16,128]{2,1,0:T(8,128)(2,1)S(1)} %collective-permute-done.8.ring), channel_id=1, source_target_pairs={{7,3},{11,7},{15,11},{23,19},{27,23},{31,27}} | collective-permute-start | bytes 380936 | tf_op jit(solution)/shard_map/ppermute | solution.py:262

commit v12 on v11

--- a/solution.py
+++ b/solution.py
@@ -8,7 +8,7 @@
 from jax.sharding import PartitionSpec as P
 
 SLOTS = 32
-LEAVES = 40
+LEAVES = 80
 MIB = 2**20
 BY_ROWS = (((1,), (1,)), ((), ()))
 VMEM, SMEM, HBM, ANY = pltpu.VMEM, pltpu.SMEM, pltpu.HBM, pl.ANY
@@ -206,7 +206,7 @@
     part[...] = acc[pl.ds(0, leaf_dev)]
 
 
-def add_kernel(capacity, part, back8, ring, back4, back2, relayed, out, listed, wanted, sem):
+def add_kernel(capacity, part, ring, back2, back8, back4, relayed, out, listed, wanted, sem):
     last = lax.bitwise_and(lax.axis_index("kx"), 3) == 3
 
     def back1(r):
@@ -303,7 +303,7 @@
     (gradient,) = call(
         functools.partial(add_kernel, capacity), "add", (all_rows,), [VMEM] * 6,
         [VMEM], 6, moved=4 * MIB, scratch=[VMEM(lists, jnp.int32), SMEM(lists, jnp.int32), pltpu.SemaphoreType.DMA],
-    )(part, back8, ring, back4, back2, relayed)
+    )(part, ring, back2, back8, back4, relayed)
     return gradient
 
 

time: 43.5 us -> 44.2 us (1.016)
  waiting for transfers between devices: 6.06 us -> 6.98 us
    ppermute x12, waiting for transfers between devices: 6.06 us -> 6.98 us  [passed(): return lax.ppermute(x, 'kx', route)]
  transfers between devices with their start and end apart: 12 -> 12, of which waited for: 4 -> 5; matrix products, arithmetic and copies ran while one was open for 0% -> 0% of each run, Pallas kernels for 16% -> 15%
where the time goes in v12:
time: 44.2 us; the launch traced here: 43.7 us
  starting transfers between devices  23.3 us (53%)
  Pallas kernels  13.4 us (30%)
  waiting for transfers between devices  6.98 us (16%)
    ppermute x12, starting transfers between devices, passed(): return lax.ppermute(x, 'kx', route)  23.3 us
    ppermute x12, waiting for transfers between devices, passed(): return lax.ppermute(x, 'kx', route)  6.98 us
    pallas_call x1, Pallas kernels, per_device(): call(functools.partial(remote_kernel, capacity), 'remote', (all_rows, sha...  4.19 us
    pallas_call x1, Pallas kernels, per_device(): call(home_kernel, 'home', (all_rows,), [SMEM] + [VMEM] * 3, [VMEM], 6, mo...  3.5 us
    pallas_call x1, Pallas kernels, per_device(): call(local_kernel, 'local', (all_rows,), [SMEM, VMEM, ANY, VMEM], [VMEM],...  2.06 us
    pallas_call x1, Pallas kernels, per_device(): call(functools.partial(add_kernel, capacity), 'add', (all_rows,), [VMEM]...  1.8 us
    pallas_call x1, Pallas kernels, per_device(): call(index_kernel, 'index', (one_list, shape((2, 4 * SLOTS), jnp.int32),...  1.16 us
  transfers between devices with their start and end apart: 12, of which 5 were waited for; matrix products, arithmetic and copies ran while one was open for 0% of the time, Pallas kernels for 15%

profile of v12, /device:TPU:15, one launch (start us, length us, event | category | flops | bytes accessed | tf_op | source)
XLA Modules:
  0.0 43.7 jit_solution(2799727995434301053)
XLA Ops:
  0.0 0.0 copy-start.1
  0.0 0.0 copy-start
  0.0 3.5 %collective-permute-start = (bf16[80,16,128]{2,1,0:T(8,128)(2,1)}, bf16[80,16,128]{2,1,0:T(8,128)(2,1)S(1)}, u32[]{:S(2)}, u32[]{:S(2)}) collective-permute-start(bf16[80,16,128]{2,1,0:T(8,128)(2,1)} %latent.5), channel_id=1, source_target_pairs={{0,4},{1,5},{2,6},{3,7},{4,8},{5,9},{6,10},{7,11},{8,12},{9,13},{1... | collective-permute-start | bytes 983048 | tf_op jit(solution)/shard_map/ppermute | solution.py:262
  3.5 0.0 copy-start.2
  3.5 1.2 %index.1 = (s32[1,128]{1,0:T(1,128)S(1)}, s32[2,128]{1,0:T(2,128)S(1)}, s32[3,80]{1,0:T(4,128)S(1)}) custom-call(s32[3,80]{1,0:T(4,128)} %bitcast.1, bf16[80,16,128]{2,1,0:T(8,128)(2,1)} %latent.5, bf16[80,3,128,128]{3,2,1,0:T(8,128)(2,1)} %weights.7), custom_call_target="tpu_custom_call" | custom-call | bytes 2097152 | tf_op jit(solution)/shard_map/index/pallas_call | solution.py:267
  4.6 2.1 %collective-permute-start.3 = (s32[1,128]{1,0:T(1,128)S(1)}, s32[1,128]{1,0:T(1,128)S(1)}, u32[]{:S(2)}, u32[]{:S(2)}) collective-permute-start(s32[1,128]{1,0:T(1,128)S(1)} %get-tuple-element.18.asked.asked_row), channel_id=1, source_target_pairs={{4,0},{5,1},{6,2},{7,3},{8,4},{9,5},{10,6},{11,7},{12,8},{13,9},{1... | collective-permute-start | bytes 1544 | tf_op jit(solution)/shard_map/ppermute | solution.py:262
  6.8 0.3 collective-permute-start.2
  7.1 1.5 %collective-permute-start.1 = (s32[1,128]{1,0:T(1,128)S(1)}, s32[1,128]{1,0:T(1,128)S(1)}, u32[]{:S(2)}, u32[]{:S(2)}) collective-permute-start(s32[1,128]{1,0:T(1,128)S(1)} %get-tuple-element.18.asked.asked_row), channel_id=1, source_target_pairs={{0,3},{1,0},{2,1},{3,2},{4,7},{5,4},{6,5},{7,6},{8,11},{9,8},{10,9... | collective-permute-start | bytes 1544 | tf_op jit(solution)/shard_map/ppermute | solution.py:262
  8.6 0.7 %collective-permute-done.3.ask8 = s32[1,128]{1,0:T(1,128)S(1)} collective-permute-done((s32[1,128]{1,0:T(1,128)S(1)}, s32[1,128]{1,0:T(1,128)S(1)}, u32[]{:S(2)}, u32[]{:S(2)}) %collective-permute-start.3) | collective-permute-done | bytes 544 | tf_op jit(solution)/shard_map/ppermute | solution.py:262
  9.3 0.3 collective-permute-done.2.ask2
  9.5 1.7 %collective-permute-done.1.ask1 = s32[1,128]{1,0:T(1,128)S(1)} collective-permute-done((s32[1,128]{1,0:T(1,128)S(1)}, s32[1,128]{1,0:T(1,128)S(1)}, u32[]{:S(2)}, u32[]{:S(2)}) %collective-permute-start.1) | collective-permute-done | bytes 544 | tf_op jit(solution)/shard_map/ppermute | solution.py:262
  11.2 0.0 collective-permute-done.before
  11.3 0.0 copy-done.1
  11.3 0.6 %serve.1 = (bf16[30,16,128]{2,1,0:T(8,128)(2,1)S(1)}, bf16[30,16,128]{2,1,0:T(8,128)(2,1)S(1)}, bf16[30,16,128]{2,1,0:T(8,128)(2,1)S(1)}) custom-call(s32[1,128]{1,0:T(1,128)S(1)} %collective-permute-done.1.ask1, s32[1,128]{1,0:T(1,128)S(1)} %collective-permute-done.2.ask2, s32[1,128]{1,0:T(1,128)S(1)} %collective-permute-done.3.ask8, ...), custom_call_target="tpu_custom_call" | custom-call | bytes 4194304 | tf_op jit(solution)/shard_map/serve/pallas_call | solution.py:275
  11.9 0.4 collective-permute-start.4
  12.3 3.2 %collective-permute-start.5 = (bf16[30,16,128]{2,1,0:T(8,128)(2,1)S(1)}, bf16[30,16,128]{2,1,0:T(8,128)(2,1)S(1)}, u32[]{:S(2)}, u32[]{:S(2)}) collective-permute-start(bf16[30,16,128]{2,1,0:T(8,128)(2,1)S(1)} %get-tuple-element.21), channel_id=1, source_target_pairs={{4,8},{5,9},{6,10},{7,11},{8,12},{9,13},{10,14},{11,15},{20,24},{2... | collective-permute-start | bytes 368648 | tf_op jit(solution)/shard_map/ppermute | solution.py:262
  15.5 2.9 %collective-permute-start.6 = (bf16[30,16,128]{2,1,0:T(8,128)(2,1)S(1)}, bf16[30,16,128]{2,1,0:T(8,128)(2,1)S(1)}, u32[]{:S(2)}, u32[]{:S(2)}) collective-permute-start(bf16[30,16,128]{2,1,0:T(8,128)(2,1)S(1)} %get-tuple-element.22), channel_id=1, source_target_pairs={{0,1},{1,2},{2,3},{3,0},{4,5},{5,6},{6,7},{7,4},{8,9},{9,10},{10,1... | collective-permute-start | bytes 368648 | tf_op jit(solution)/shard_map/ppermute | solution.py:262
  18.4 0.0 copy-done
  18.4 2.1 %local.1.left = f32[80,16,128]{2,1,0:T(8,128)S(1)} custom-call(s32[3,80]{1,0:T(4,128)S(1)} %get-tuple-element.17.home, bf16[80,16,128]{2,1,0:T(8,128)(2,1)S(1)} %copy-done.1, bf16[80,16,128]{2,1,0:T(8,128)(2,1)S(1)} %collective-permute-done.before, bf16[80,3,128,128]{3,2,1,0:T(8,128)(2,1)S(1)} %copy-done), custom_call_target="tpu_custom_call" | custom-call | bytes 7864320 | tf_op jit(solution)/shard_map/local/pallas_call | solution.py:282
  20.4 0.0 collective-permute-done.4.from2
  20.4 0.0 collective-permute-done.5.from8
  20.5 0.0 collective-permute-done.6.from1
  20.5 0.0 copy-done.2
  20.5 4.2 %remote.1 = (f32[80,16,128]{2,1,0:T(8,128)S(1)}, bf16[88,16,128]{2,1,0:T(8,128)(2,1)S(1)}, bf16[31,16,128]{2,1,0:T(8,128)(2,1)S(1)}, bf16[31,16,128]{2,1,0:T(8,1...) custom-call(s32[1,128]{1,0:T(1,128)S(1)} %get-tuple-element.18.asked.asked_row, ...), custom_call_target="tpu_custom_call" | custom-call | bytes 7864320 | tf_op jit(solution)/shard_map/remote/pallas_call | solution.py:286
  24.7 1.1 %collective-permute-start.7 = (bf16[31,16,128]{2,1,0:T(8,128)(2,1)S(1)}, bf16[31,16,128]{2,1,0:T(8,128)(2,1)S(1)}, u32[]{:S(2)}, u32[]{:S(2)}) collective-permute-start(bf16[31,16,128]{2,1,0:T(8,128)(2,1)S(1)} %get-tuple-element.25), channel_id=1, source_target_pairs={{0,3},{1,0},{2,1},{3,2},{4,7},{5,4},{6,5},{7,6},{8,11},{9,8},{10,9... | collective-permute-start | bytes 380936 | tf_op jit(solution)/shard_map/ppermute | solution.py:262
  25.8 3.1 %collective-permute-start.8 = (bf16[31,16,128]{2,1,0:T(8,128)(2,1)S(1)}, bf16[31,16,128]{2,1,0:T(8,128)(2,1)S(1)}, u32[]{:S(2)}, u32[]{:S(2)}) collective-permute-start(bf16[31,16,128]{2,1,0:T(8,128)(2,1)S(1)} %get-tuple-element.26), channel_id=1, source_target_pairs={{2,0},{3,1},{4,2},{5,3},{6,4},{7,5},{8,6},{9,7},{10,8},{11,9},{12,... | collective-permute-start | bytes 380936 | tf_op jit(solution)/shard_map/ppermute | solution.py:262
  28.9 1.3 %collective-permute-start.9 = (bf16[31,16,128]{2,1,0:T(8,128)(2,1)S(1)}, bf16[31,16,128]{2,1,0:T(8,128)(2,1)S(1)}, u32[]{:S(2)}, u32[]{:S(2)}) collective-permute-start(bf16[31,16,128]{2,1,0:T(8,128)(2,1)S(1)} %get-tuple-element.27), channel_id=1, source_target_pairs={{8,0},{9,1},{10,2},{11,3},{12,4},{13,5},{14,6},{15,7},{24,16},{25,... | collective-permute-start | bytes 380936 | tf_op jit(solution)/shard_map/ppermute | solution.py:262
  30.2 1.9 %collective-permute-start.10 = (bf16[31,16,128]{2,1,0:T(8,128)(2,1)S(1)}, bf16[31,16,128]{2,1,0:T(8,128)(2,1)S(1)}, u32[]{:S(2)}, u32[]{:S(2)}) collective-permute-start(bf16[31,16,128]{2,1,0:T(8,128)(2,1)S(1)} %get-tuple-element.28), channel_id=1, source_target_pairs={{4,0},{5,1},{6,2},{7,3},{8,4},{9,5},{10,6},{11,7},{12,8},{13,9},{1... | collective-permute-start | bytes 380936 | tf_op jit(solution)/shard_map/ppermute | solution.py:262
  32.2 0.0 collective-permute-done.7.ring
  32.2 1.9 %collective-permute-start.11 = (bf16[31,16,128]{2,1,0:T(8,128)(2,1)S(1)}, bf16[31,16,128]{2,1,0:T(8,128)(2,1)S(1)}, u32[]{:S(2)}, u32[]{:S(2)}) collective-permute-start(bf16[31,16,128]{2,1,0:T(8,128)(2,1)S(1)} %collective-permute-done.7.ring), channel_id=1, source_target_pairs={{7,3},{11,7},{15,11},{23,19},{27,23},{31,27}} | collective-permute-start | bytes 380936 | tf_op jit(solution)/shard_map/ppermute | solution.py:262
  34.1 3.5 %home.1.part = f32[80,16,128]{2,1,0:T(8,128)S(1)} custom-call(s32[3,80]{1,0:T(4,128)S(1)} %get-tuple-element.17.home, f32[80,16,128]{2,1,0:T(8,128)S(1)} %get-tuple-element.23.back, bf16[88,16,128]{2,1,0:T(8,128)(2,1)S(1)} %get-tuple-element.24.low, bf16[80,3,128,128]{3,2,1,0:T(8,128)(2,1)S(1)} %copy-done), custom_call_target="tpu_custom_call" | custom-call | bytes 7864320 | tf_op jit(solution)/shard_map/home/pallas_call | solution.py:298
  37.6 0.0 collective-permute-done.8.back2
  37.6 0.0 collective-permute-done.9.back8
  37.6 2.8 %collective-permute-done.10.back4 = bf16[31,16,128]{2,1,0:T(8,128)(2,1)S(1)} collective-permute-done((bf16[31,16,128]{2,1,0:T(8,128)(2,1)S(1)}, bf16[31,16,128]{2,1,0:T(8,128)(2,1)S(1)}, u32[]{:S(2)}, u32[]{:S(2)}) %collective-permute-start.10) | collective-permute-done | bytes 127008 | tf_op jit(solution)/shard_map/ppermute | solution.py:262
  40.5 1.5 %collective-permute-done.11.relayed = bf16[31,16,128]{2,1,0:T(8,128)(2,1)S(1)} collective-permute-done((bf16[31,16,128]{2,1,0:T(8,128)(2,1)S(1)}, bf16[31,16,128]{2,1,0:T(8,128)(2,1)S(1)}, u32[]{:S(2)}, u32[]{:S(2)}) %collective-permute-start.11) | collective-permute-done | bytes 127008 | tf_op jit(solution)/shard_map/ppermute | solution.py:262
  41.9 1.8 %add.1 = f32[80,16,128]{2,1,0:T(8,128)} custom-call(f32[80,16,128]{2,1,0:T(8,128)S(1)} %home.1.part, bf16[31,16,128]{2,1,0:T(8,128)(2,1)S(1)} %collective-permute-done.7.ring, bf16[31,16,128]{2,1,0:T(8,128)(2,1)S(1)} %collective-permute-done.8.back2, bf16[31,16,128]{2,1,0:T(8,128)(2,1)S(1)} %collective-permute-done.9.back8, ...), custom_call_target="tpu_custom_call" | custom-call | bytes 4194304 | tf_op jit(solution)/shard_map/add/pallas_call | solution.py:303
Async XLA Ops:
  0.0 11.3 %copy-start.1 = (bf16[80,16,128]{2,1,0:T(8,128)(2,1)S(1)}, bf16[80,16,128]{2,1,0:T(8,128)(2,1)}, u32[]{:S(2)}) copy-start(bf16[80,16,128]{2,1,0:T(8,128)(2,1)} %latent.5) | copy-start | bytes 983044
  0.0 18.4 %copy-start = (bf16[80,3,128,128]{3,2,1,0:T(8,128)(2,1)S(1)}, bf16[80,3,128,128]{3,2,1,0:T(8,128)(2,1)}, u32[]{:S(2)}) copy-start(bf16[80,3,128,128]{3,2,1,0:T(8,128)(2,1)} %weights.7) | copy-start | bytes 23592964
  0.0 11.2 %collective-permute-start = (bf16[80,16,128]{2,1,0:T(8,128)(2,1)}, bf16[80,16,128]{2,1,0:T(8,128)(2,1)S(1)}, u32[]{:S(2)}, u32[]{:S(2)}) collective-permute-start(bf16[80,16,128]{2,1,0:T(8,128)(2,1)} %latent.5), channel_id=1, source_target_pairs={{0,4},{1,5},{2,6},{3,7},{4,8},{5,9},{6,10},{7,11},{8,12},{9,13},{1... | collective-permute-start | bytes 983048 | tf_op jit(solution)/shard_map/ppermute | solution.py:262
  3.5 17.0 %copy-start.2 = (bf16[80,128,128]{2,1,0:T(8,128)(2,1)S(1)}, bf16[80,128,128]{2,1,0:T(8,128)(2,1)}, u32[]{:S(2)}) copy-start(bf16[80,128,128]{2,1,0:T(8,128)(2,1)} %factor.1) | copy-start | bytes 7864324
  4.6 4.6 %collective-permute-start.3 = (s32[1,128]{1,0:T(1,128)S(1)}, s32[1,128]{1,0:T(1,128)S(1)}, u32[]{:S(2)}, u32[]{:S(2)}) collective-permute-start(s32[1,128]{1,0:T(1,128)S(1)} %get-tuple-element.18.asked.asked_row), channel_id=1, source_target_pairs={{4,0},{5,1},{6,2},{7,3},{8,4},{9,5},{10,6},{11,7},{12,8},{13,9},{1... | collective-permute-start | bytes 1544 | tf_op jit(solution)/shard_map/ppermute | solution.py:262
  6.8 2.8 %collective-permute-start.2 = (s32[1,128]{1,0:T(1,128)S(1)}, s32[1,128]{1,0:T(1,128)S(1)}, u32[]{:S(2)}, u32[]{:S(2)}) collective-permute-start(s32[1,128]{1,0:T(1,128)S(1)} %get-tuple-element.18.asked.asked_row), channel_id=1, source_target_pairs={{0,2},{1,3},{2,0},{3,1},{4,6},{5,7},{6,4},{7,5},{8,10},{9,11},{10,... | collective-permute-start | bytes 1544 | tf_op jit(solution)/shard_map/ppermute | solution.py:262
  7.1 4.2 %collective-permute-start.1 = (s32[1,128]{1,0:T(1,128)S(1)}, s32[1,128]{1,0:T(1,128)S(1)}, u32[]{:S(2)}, u32[]{:S(2)}) collective-permute-start(s32[1,128]{1,0:T(1,128)S(1)} %get-tuple-element.18.asked.asked_row), channel_id=1, source_target_pairs={{0,3},{1,0},{2,1},{3,2},{4,7},{5,4},{6,5},{7,6},{8,11},{9,8},{10,9... | collective-permute-start | bytes 1544 | tf_op jit(solution)/shard_map/ppermute | solution.py:262
  11.9 8.5 %collective-permute-start.4 = (bf16[30,16,128]{2,1,0:T(8,128)(2,1)S(1)}, bf16[30,16,128]{2,1,0:T(8,128)(2,1)S(1)}, u32[]{:S(2)}, u32[]{:S(2)}) collective-permute-start(bf16[30,16,128]{2,1,0:T(8,128)(2,1)S(1)} %get-tuple-element.20), channel_id=1, source_target_pairs={{0,2},{1,3},{2,0},{3,1},{4,6},{5,7},{6,4},{7,5},{8,10},{9,11},{10,... | collective-permute-start | bytes 368648 | tf_op jit(solution)/shard_map/ppermute | solution.py:262
  12.3 8.1 %collective-permute-start.5 = (bf16[30,16,128]{2,1,0:T(8,128)(2,1)S(1)}, bf16[30,16,128]{2,1,0:T(8,128)(2,1)S(1)}, u32[]{:S(2)}, u32[]{:S(2)}) collective-permute-start(bf16[30,16,128]{2,1,0:T(8,128)(2,1)S(1)} %get-tuple-element.21), channel_id=1, source_target_pairs={{4,8},{5,9},{6,10},{7,11},{8,12},{9,13},{10,14},{11,15},{20,24},{2... | collective-permute-start | bytes 368648 | tf_op jit(solution)/shard_map/ppermute | solution.py:262
  15.5 5.0 %collective-permute-start.6 = (bf16[30,16,128]{2,1,0:T(8,128)(2,1)S(1)}, bf16[30,16,128]{2,1,0:T(8,128)(2,1)S(1)}, u32[]{:S(2)}, u32[]{:S(2)}) collective-permute-start(bf16[30,16,128]{2,1,0:T(8,128)(2,1)S(1)} %get-tuple-element.22), channel_id=1, source_target_pairs={{0,1},{1,2},{2,3},{3,0},{4,5},{5,6},{6,7},{7,4},{8,9},{9,10},{10,1... | collective-permute-start | bytes 368648 | tf_op jit(solution)/shard_map/ppermute | solution.py:262
  24.7 7.5 %collective-permute-start.7 = (bf16[31,16,128]{2,1,0:T(8,128)(2,1)S(1)}, bf16[31,16,128]{2,1,0:T(8,128)(2,1)S(1)}, u32[]{:S(2)}, u32[]{:S(2)}) collective-permute-start(bf16[31,16,128]{2,1,0:T(8,128)(2,1)S(1)} %get-tuple-element.25), channel_id=1, source_target_pairs={{0,3},{1,0},{2,1},{3,2},{4,7},{5,4},{6,5},{7,6},{8,11},{9,8},{10,9... | collective-permute-start | bytes 380936 | tf_op jit(solution)/shard_map/ppermute | solution.py:262
  25.8 11.8 %collective-permute-start.8 = (bf16[31,16,128]{2,1,0:T(8,128)(2,1)S(1)}, bf16[31,16,128]{2,1,0:T(8,128)(2,1)S(1)}, u32[]{:S(2)}, u32[]{:S(2)}) collective-permute-start(bf16[31,16,128]{2,1,0:T(8,128)(2,1)S(1)} %get-tuple-element.26), channel_id=1, source_target_pairs={{2,0},{3,1},{4,2},{5,3},{6,4},{7,5},{8,6},{9,7},{10,8},{11,9},{12,... | collective-permute-start | bytes 380936 | tf_op jit(solution)/shard_map/ppermute | solution.py:262
  28.9 8.7 %collective-permute-start.9 = (bf16[31,16,128]{2,1,0:T(8,128)(2,1)S(1)}, bf16[31,16,128]{2,1,0:T(8,128)(2,1)S(1)}, u32[]{:S(2)}, u32[]{:S(2)}) collective-permute-start(bf16[31,16,128]{2,1,0:T(8,128)(2,1)S(1)} %get-tuple-element.27), channel_id=1, source_target_pairs={{8,0},{9,1},{10,2},{11,3},{12,4},{13,5},{14,6},{15,7},{24,16},{25,... | collective-permute-start | bytes 380936 | tf_op jit(solution)/shard_map/ppermute | solution.py:262
  30.2 10.2 %collective-permute-start.10 = (bf16[31,16,128]{2,1,0:T(8,128)(2,1)S(1)}, bf16[31,16,128]{2,1,0:T(8,128)(2,1)S(1)}, u32[]{:S(2)}, u32[]{:S(2)}) collective-permute-start(bf16[31,16,128]{2,1,0:T(8,128)(2,1)S(1)} %get-tuple-element.28), channel_id=1, source_target_pairs={{4,0},{5,1},{6,2},{7,3},{8,4},{9,5},{10,6},{11,7},{12,8},{13,9},{1... | collective-permute-start | bytes 380936 | tf_op jit(solution)/shard_map/ppermute | solution.py:262
  32.2 9.8 %collective-permute-start.11 = (bf16[31,16,128]{2,1,0:T(8,128)(2,1)S(1)}, bf16[31,16,128]{2,1,0:T(8,128)(2,1)S(1)}, u32[]{:S(2)}, u32[]{:S(2)}) collective-permute-start(bf16[31,16,128]{2,1,0:T(8,128)(2,1)S(1)} %collective-permute-done.7.ring), channel_id=1, source_target_pairs={{7,3},{11,7},{15,11},{23,19},{27,23},{31,27}} | collective-permute-start | bytes 380936 | tf_op jit(solution)/shard_map/ppermute | solution.py:262

commit v13 on v11

--- a/solution.py
+++ b/solution.py
@@ -8,7 +8,7 @@
 from jax.sharding import PartitionSpec as P
 
 SLOTS = 32
-LEAVES = 40
+LEAVES = 80
 MIB = 2**20
 BY_ROWS = (((1,), (1,)), ((), ()))
 VMEM, SMEM, HBM, ANY = pltpu.VMEM, pltpu.SMEM, pltpu.HBM, pl.ANY
@@ -141,7 +141,7 @@
 
 
 def remote_kernel(
-    capacity, asked, slots, asked_row, left, before, from2, from8, from1,
+    capacity, asked, slots, asked_row, left, before, from2, from1, from8,
     weights, factor, back, low, out8, out4, out2, out1, resid,
 ):
     leaf_dev = back.shape[0]
@@ -288,7 +288,7 @@
         (all_rows, shape((leaf_dev + 8, samples, width), jnp.bfloat16)) + (sent,) * 4,
         [SMEM] * 2 + [VMEM] * 8, [VMEM] * 6, 8, moved=heavy,
         scratch=[VMEM((leaf_dev + 8, samples, width), jnp.float32)],
-    )(asked, slots, asked, left, before, from2, from8, from1, weights, factor)
+    )(asked, slots, asked, left, before, from2, from1, from8, weights, factor)
     def back_by(x, reach):
         return passed(x, [(i, i - reach) for i in everyone if i >= reach])
 

time: 43.5 us -> 43.1 us (level)
  waiting for transfers between devices: 6.06 us -> 7.3 us
  starting transfers between devices: 23.1 us -> 21.9 us
    ppermute x12, waiting for transfers between devices: 6.06 us -> 7.3 us  [passed(): return lax.ppermute(x, 'kx', route)]
    ppermute x12, starting transfers between devices: 23.1 us -> 21.9 us  [passed(): return lax.ppermute(x, 'kx', route)]
  transfers between devices with their start and end apart: 12 -> 12, of which waited for: 4 -> 5; matrix products, arithmetic and copies ran while one was open for 0% -> 0% of each run, Pallas kernels for 16% -> 16%
where the time goes in v13:
time: 43.1 us; the launch traced here: 42.7 us
  starting transfers between devices  21.9 us (51%)
  Pallas kernels  13.4 us (31%)
  waiting for transfers between devices  7.3 us (17%)
    ppermute x12, starting transfers between devices, passed(): return lax.ppermute(x, 'kx', route)  21.9 us
    ppermute x12, waiting for transfers between devices, passed(): return lax.ppermute(x, 'kx', route)  7.3 us
    pallas_call x1, Pallas kernels, per_device(): call(functools.partial(remote_kernel, capacity), 'remote', (all_rows, sha...  4.18 us
    pallas_call x1, Pallas kernels, per_device(): call(home_kernel, 'home', (all_rows,), [SMEM] + [VMEM] * 3, [VMEM], 6, mo...  3.5 us
    pallas_call x1, Pallas kernels, per_device(): call(local_kernel, 'local', (all_rows,), [SMEM, VMEM, ANY, VMEM], [VMEM],...  2.07 us
    pallas_call x1, Pallas kernels, per_device(): call(functools.partial(add_kernel, capacity), 'add', (all_rows,), [VMEM]...  1.81 us
    pallas_call x1, Pallas kernels, per_device(): call(index_kernel, 'index', (one_list, shape((2, 4 * SLOTS), jnp.int32),...  1.16 us
  transfers between devices with their start and end apart: 12, of which 5 were waited for; matrix products, arithmetic and copies ran while one was open for 0% of the time, Pallas kernels for 16%

profile of v13, /device:TPU:15, one launch (start us, length us, event | category | flops | bytes accessed | tf_op | source)
XLA Modules:
  0.0 42.7 jit_solution(3417210744969059052)
XLA Ops:
  0.0 0.0 copy-start.1
  0.0 0.0 copy-start
  0.0 3.5 %collective-permute-start = (bf16[80,16,128]{2,1,0:T(8,128)(2,1)}, bf16[80,16,128]{2,1,0:T(8,128)(2,1)S(1)}, u32[]{:S(2)}, u32[]{:S(2)}) collective-permute-start(bf16[80,16,128]{2,1,0:T(8,128)(2,1)} %latent.5), channel_id=1, source_target_pairs={{0,4},{1,5},{2,6},{3,7},{4,8},{5,9},{6,10},{7,11},{8,12},{9,13},{1... | collective-permute-start | bytes 983048 | tf_op jit(solution)/shard_map/ppermute | solution.py:262
  3.5 0.0 copy-start.2
  3.5 1.2 %index.1 = (s32[1,128]{1,0:T(1,128)S(1)}, s32[2,128]{1,0:T(2,128)S(1)}, s32[3,80]{1,0:T(4,128)S(1)}) custom-call(s32[3,80]{1,0:T(4,128)} %bitcast.1, bf16[80,16,128]{2,1,0:T(8,128)(2,1)} %latent.5, bf16[80,3,128,128]{3,2,1,0:T(8,128)(2,1)} %weights.7), custom_call_target="tpu_custom_call" | custom-call | bytes 2097152 | tf_op jit(solution)/shard_map/index/pallas_call | solution.py:267
  4.6 2.1 %collective-permute-start.3 = (s32[1,128]{1,0:T(1,128)S(1)}, s32[1,128]{1,0:T(1,128)S(1)}, u32[]{:S(2)}, u32[]{:S(2)}) collective-permute-start(s32[1,128]{1,0:T(1,128)S(1)} %get-tuple-element.18.asked.asked_row), channel_id=1, source_target_pairs={{4,0},{5,1},{6,2},{7,3},{8,4},{9,5},{10,6},{11,7},{12,8},{13,9},{1... | collective-permute-start | bytes 1544 | tf_op jit(solution)/shard_map/ppermute | solution.py:262
  6.8 0.3 collective-permute-start.2
  7.1 1.5 %collective-permute-start.1 = (s32[1,128]{1,0:T(1,128)S(1)}, s32[1,128]{1,0:T(1,128)S(1)}, u32[]{:S(2)}, u32[]{:S(2)}) collective-permute-start(s32[1,128]{1,0:T(1,128)S(1)} %get-tuple-element.18.asked.asked_row), channel_id=1, source_target_pairs={{0,3},{1,0},{2,1},{3,2},{4,7},{5,4},{6,5},{7,6},{8,11},{9,8},{10,9... | collective-permute-start | bytes 1544 | tf_op jit(solution)/shard_map/ppermute | solution.py:262
  8.6 0.7 %collective-permute-done.3.ask8 = s32[1,128]{1,0:T(1,128)S(1)} collective-permute-done((s32[1,128]{1,0:T(1,128)S(1)}, s32[1,128]{1,0:T(1,128)S(1)}, u32[]{:S(2)}, u32[]{:S(2)}) %collective-permute-start.3) | collective-permute-done | bytes 544 | tf_op jit(solution)/shard_map/ppermute | solution.py:262
  9.3 0.3 collective-permute-done.2.ask2
  9.5 1.7 %collective-permute-done.1.ask1 = s32[1,128]{1,0:T(1,128)S(1)} collective-permute-done((s32[1,128]{1,0:T(1,128)S(1)}, s32[1,128]{1,0:T(1,128)S(1)}, u32[]{:S(2)}, u32[]{:S(2)}) %collective-permute-start.1) | collective-permute-done | bytes 544 | tf_op jit(solution)/shard_map/ppermute | solution.py:262
  11.2 0.0 collective-permute-done.before
  11.3 0.0 copy-done.1
  11.3 0.6 %serve.1 = (bf16[30,16,128]{2,1,0:T(8,128)(2,1)S(1)}, bf16[30,16,128]{2,1,0:T(8,128)(2,1)S(1)}, bf16[30,16,128]{2,1,0:T(8,128)(2,1)S(1)}) custom-call(s32[1,128]{1,0:T(1,128)S(1)} %collective-permute-done.1.ask1, s32[1,128]{1,0:T(1,128)S(1)} %collective-permute-done.2.ask2, s32[1,128]{1,0:T(1,128)S(1)} %collective-permute-done.3.ask8, ...), custom_call_target="tpu_custom_call" | custom-call | bytes 4194304 | tf_op jit(solution)/shard_map/serve/pallas_call | solution.py:275
  11.9 0.4 collective-permute-start.4
  12.3 2.5 %collective-permute-start.5 = (bf16[30,16,128]{2,1,0:T(8,128)(2,1)S(1)}, bf16[30,16,128]{2,1,0:T(8,128)(2,1)S(1)}, u32[]{:S(2)}, u32[]{:S(2)}) collective-permute-start(bf16[30,16,128]{2,1,0:T(8,128)(2,1)S(1)} %get-tuple-element.21), channel_id=1, source_target_pairs={{0,1},{1,2},{2,3},{3,0},{4,5},{5,6},{6,7},{7,4},{8,9},{9,10},{10,1... | collective-permute-start | bytes 368648 | tf_op jit(solution)/shard_map/ppermute | solution.py:262
  14.8 3.2 %collective-permute-start.6 = (bf16[30,16,128]{2,1,0:T(8,128)(2,1)S(1)}, bf16[30,16,128]{2,1,0:T(8,128)(2,1)S(1)}, u32[]{:S(2)}, u32[]{:S(2)}) collective-permute-start(bf16[30,16,128]{2,1,0:T(8,128)(2,1)S(1)} %get-tuple-element.22), channel_id=1, source_target_pairs={{4,8},{5,9},{6,10},{7,11},{8,12},{9,13},{10,14},{11,15},{20,24},{2... | collective-permute-start | bytes 368648 | tf_op jit(solution)/shard_map/ppermute | solution.py:262
  18.0 0.0 copy-done
  18.1 2.1 %local.1.left = f32[80,16,128]{2,1,0:T(8,128)S(1)} custom-call(s32[3,80]{1,0:T(4,128)S(1)} %get-tuple-element.17.home, bf16[80,16,128]{2,1,0:T(8,128)(2,1)S(1)} %copy-done.1, bf16[80,16,128]{2,1,0:T(8,128)(2,1)S(1)} %collective-permute-done.before, bf16[80,3,128,128]{3,2,1,0:T(8,128)(2,1)S(1)} %copy-done), custom_call_target="tpu_custom_call" | custom-call | bytes 7864320 | tf_op jit(solution)/shard_map/local/pallas_call | solution.py:282
  20.1 0.0 collective-permute-done.4.from2
  20.1 0.0 collective-permute-done.5.from1
  20.1 0.4 collective-permute-done.6.from8
  20.5 0.0 copy-done.2
  20.5 4.2 %remote.1 = (f32[80,16,128]{2,1,0:T(8,128)S(1)}, bf16[88,16,128]{2,1,0:T(8,128)(2,1)S(1)}, bf16[31,16,128]{2,1,0:T(8,128)(2,1)S(1)}, bf16[31,16,128]{2,1,0:T(8,1...) custom-call(s32[1,128]{1,0:T(1,128)S(1)} %get-tuple-element.18.asked.asked_row, ...), custom_call_target="tpu_custom_call" | custom-call | bytes 7864320 | tf_op jit(solution)/shard_map/remote/pallas_call | solution.py:286
  24.7 0.1 collective-permute-start.8
  24.8 1.3 %collective-permute-start.7 = (bf16[31,16,128]{2,1,0:T(8,128)(2,1)S(1)}, bf16[31,16,128]{2,1,0:T(8,128)(2,1)S(1)}, u32[]{:S(2)}, u32[]{:S(2)}) collective-permute-start(bf16[31,16,128]{2,1,0:T(8,128)(2,1)S(1)} %get-tuple-element.25), channel_id=1, source_target_pairs={{8,0},{9,1},{10,2},{11,3},{12,4},{13,5},{14,6},{15,7},{24,16},{25,... | collective-permute-start | bytes 380936 | tf_op jit(solution)/shard_map/ppermute | solution.py:262
  26.1 1.9 %collective-permute-start.9 = (bf16[31,16,128]{2,1,0:T(8,128)(2,1)S(1)}, bf16[31,16,128]{2,1,0:T(8,128)(2,1)S(1)}, u32[]{:S(2)}, u32[]{:S(2)}) collective-permute-start(bf16[31,16,128]{2,1,0:T(8,128)(2,1)S(1)} %get-tuple-element.27), channel_id=1, source_target_pairs={{4,0},{5,1},{6,2},{7,3},{8,4},{9,5},{10,6},{11,7},{12,8},{13,9},{1... | collective-permute-start | bytes 380936 | tf_op jit(solution)/shard_map/ppermute | solution.py:262
  28.0 3.2 %collective-permute-start.10 = (bf16[31,16,128]{2,1,0:T(8,128)(2,1)S(1)}, bf16[31,16,128]{2,1,0:T(8,128)(2,1)S(1)}, u32[]{:S(2)}, u32[]{:S(2)}) collective-permute-start(bf16[31,16,128]{2,1,0:T(8,128)(2,1)S(1)} %get-tuple-element.28), channel_id=1, source_target_pairs={{2,0},{3,1},{4,2},{5,3},{6,4},{7,5},{8,6},{9,7},{10,8},{11,9},{12,... | collective-permute-start | bytes 380936 | tf_op jit(solution)/shard_map/ppermute | solution.py:262
  31.2 0.0 collective-permute-done.8.ring
  31.2 1.9 %collective-permute-start.11 = (bf16[31,16,128]{2,1,0:T(8,128)(2,1)S(1)}, bf16[31,16,128]{2,1,0:T(8,128)(2,1)S(1)}, u32[]{:S(2)}, u32[]{:S(2)}) collective-permute-start(bf16[31,16,128]{2,1,0:T(8,128)(2,1)S(1)} %collective-permute-done.8.ring), channel_id=1, source_target_pairs={{7,3},{11,7},{15,11},{23,19},{27,23},{31,27}} | collective-permute-start | bytes 380936 | tf_op jit(solution)/shard_map/ppermute | solution.py:262
  33.1 3.5 %home.1.part = f32[80,16,128]{2,1,0:T(8,128)S(1)} custom-call(s32[3,80]{1,0:T(4,128)S(1)} %get-tuple-element.17.home, f32[80,16,128]{2,1,0:T(8,128)S(1)} %get-tuple-element.23.back, bf16[88,16,128]{2,1,0:T(8,128)(2,1)S(1)} %get-tuple-element.24.low, bf16[80,3,128,128]{3,2,1,0:T(8,128)(2,1)S(1)} %copy-done), custom_call_target="tpu_custom_call" | custom-call | bytes 7864320 | tf_op jit(solution)/shard_map/home/pallas_call | solution.py:298
  36.6 0.0 collective-permute-done.7.back8
  36.6 0.0 collective-permute-done.9.back4
  36.6 4.3 %collective-permute-done.10.back2 = bf16[31,16,128]{2,1,0:T(8,128)(2,1)S(1)} collective-permute-done((bf16[31,16,128]{2,1,0:T(8,128)(2,1)S(1)}, bf16[31,16,128]{2,1,0:T(8,128)(2,1)S(1)}, u32[]{:S(2)}, u32[]{:S(2)}) %collective-permute-start.10) | collective-permute-done | bytes 127008 | tf_op jit(solution)/shard_map/ppermute | solution.py:262
  40.9 0.0 collective-permute-done.11.relayed
  40.9 1.8 %add.1 = f32[80,16,128]{2,1,0:T(8,128)} custom-call(f32[80,16,128]{2,1,0:T(8,128)S(1)} %home.1.part, bf16[31,16,128]{2,1,0:T(8,128)(2,1)S(1)} %collective-permute-done.7.back8, bf16[31,16,128]{2,1,0:T(8,128)(2,1)S(1)} %collective-permute-done.8.ring, bf16[31,16,128]{2,1,0:T(8,128)(2,1)S(1)} %collective-permute-done.9.back4, ...), custom_call_target="tpu_custom_call" | custom-call | bytes 4194304 | tf_op jit(solution)/shard_map/add/pallas_call | solution.py:303
Async XLA Ops:
  0.0 11.3 %copy-start.1 = (bf16[80,16,128]{2,1,0:T(8,128)(2,1)S(1)}, bf16[80,16,128]{2,1,0:T(8,128)(2,1)}, u32[]{:S(2)}) copy-start(bf16[80,16,128]{2,1,0:T(8,128)(2,1)} %latent.5) | copy-start | bytes 983044
  0.0 18.0 %copy-start = (bf16[80,3,128,128]{3,2,1,0:T(8,128)(2,1)S(1)}, bf16[80,3,128,128]{3,2,1,0:T(8,128)(2,1)}, u32[]{:S(2)}) copy-start(bf16[80,3,128,128]{3,2,1,0:T(8,128)(2,1)} %weights.7) | copy-start | bytes 23592964
  0.0 11.2 %collective-permute-start = (bf16[80,16,128]{2,1,0:T(8,128)(2,1)}, bf16[80,16,128]{2,1,0:T(8,128)(2,1)S(1)}, u32[]{:S(2)}, u32[]{:S(2)}) collective-permute-start(bf16[80,16,128]{2,1,0:T(8,128)(2,1)} %latent.5), channel_id=1, source_target_pairs={{0,4},{1,5},{2,6},{3,7},{4,8},{5,9},{6,10},{7,11},{8,12},{9,13},{1... | collective-permute-start | bytes 983048 | tf_op jit(solution)/shard_map/ppermute | solution.py:262
  3.5 17.0 %copy-start.2 = (bf16[80,128,128]{2,1,0:T(8,128)(2,1)S(1)}, bf16[80,128,128]{2,1,0:T(8,128)(2,1)}, u32[]{:S(2)}) copy-start(bf16[80,128,128]{2,1,0:T(8,128)(2,1)} %factor.1) | copy-start | bytes 7864324
  4.6 4.6 %collective-permute-start.3 = (s32[1,128]{1,0:T(1,128)S(1)}, s32[1,128]{1,0:T(1,128)S(1)}, u32[]{:S(2)}, u32[]{:S(2)}) collective-permute-start(s32[1,128]{1,0:T(1,128)S(1)} %get-tuple-element.18.asked.asked_row), channel_id=1, source_target_pairs={{4,0},{5,1},{6,2},{7,3},{8,4},{9,5},{10,6},{11,7},{12,8},{13,9},{1... | collective-permute-start | bytes 1544 | tf_op jit(solution)/shard_map/ppermute | solution.py:262
  6.8 2.8 %collective-permute-start.2 = (s32[1,128]{1,0:T(1,128)S(1)}, s32[1,128]{1,0:T(1,128)S(1)}, u32[]{:S(2)}, u32[]{:S(2)}) collective-permute-start(s32[1,128]{1,0:T(1,128)S(1)} %get-tuple-element.18.asked.asked_row), channel_id=1, source_target_pairs={{0,2},{1,3},{2,0},{3,1},{4,6},{5,7},{6,4},{7,5},{8,10},{9,11},{10,... | collective-permute-start | bytes 1544 | tf_op jit(solution)/shard_map/ppermute | solution.py:262
  7.1 4.2 %collective-permute-start.1 = (s32[1,128]{1,0:T(1,128)S(1)}, s32[1,128]{1,0:T(1,128)S(1)}, u32[]{:S(2)}, u32[]{:S(2)}) collective-permute-start(s32[1,128]{1,0:T(1,128)S(1)} %get-tuple-element.18.asked.asked_row), channel_id=1, source_target_pairs={{0,3},{1,0},{2,1},{3,2},{4,7},{5,4},{6,5},{7,6},{8,11},{9,8},{10,9... | collective-permute-start | bytes 1544 | tf_op jit(solution)/shard_map/ppermute | solution.py:262
  11.9 8.2 %collective-permute-start.4 = (bf16[30,16,128]{2,1,0:T(8,128)(2,1)S(1)}, bf16[30,16,128]{2,1,0:T(8,128)(2,1)S(1)}, u32[]{:S(2)}, u32[]{:S(2)}) collective-permute-start(bf16[30,16,128]{2,1,0:T(8,128)(2,1)S(1)} %get-tuple-element.20), channel_id=1, source_target_pairs={{0,2},{1,3},{2,0},{3,1},{4,6},{5,7},{6,4},{7,5},{8,10},{9,11},{10,... | collective-permute-start | bytes 368648 | tf_op jit(solution)/shard_map/ppermute | solution.py:262
  12.3 7.8 %collective-permute-start.5 = (bf16[30,16,128]{2,1,0:T(8,128)(2,1)S(1)}, bf16[30,16,128]{2,1,0:T(8,128)(2,1)S(1)}, u32[]{:S(2)}, u32[]{:S(2)}) collective-permute-start(bf16[30,16,128]{2,1,0:T(8,128)(2,1)S(1)} %get-tuple-element.21), channel_id=1, source_target_pairs={{0,1},{1,2},{2,3},{3,0},{4,5},{5,6},{6,7},{7,4},{8,9},{9,10},{10,1... | collective-permute-start | bytes 368648 | tf_op jit(solution)/shard_map/ppermute | solution.py:262
  14.8 5.7 %collective-permute-start.6 = (bf16[30,16,128]{2,1,0:T(8,128)(2,1)S(1)}, bf16[30,16,128]{2,1,0:T(8,128)(2,1)S(1)}, u32[]{:S(2)}, u32[]{:S(2)}) collective-permute-start(bf16[30,16,128]{2,1,0:T(8,128)(2,1)S(1)} %get-tuple-element.22), channel_id=1, source_target_pairs={{4,8},{5,9},{6,10},{7,11},{8,12},{9,13},{10,14},{11,15},{20,24},{2... | collective-permute-start | bytes 368648 | tf_op jit(solution)/shard_map/ppermute | solution.py:262
  24.7 6.5 %collective-permute-start.8 = (bf16[31,16,128]{2,1,0:T(8,128)(2,1)S(1)}, bf16[31,16,128]{2,1,0:T(8,128)(2,1)S(1)}, u32[]{:S(2)}, u32[]{:S(2)}) collective-permute-start(bf16[31,16,128]{2,1,0:T(8,128)(2,1)S(1)} %get-tuple-element.26), channel_id=1, source_target_pairs={{0,3},{1,0},{2,1},{3,2},{4,7},{5,4},{6,5},{7,6},{8,11},{9,8},{10,9... | collective-permute-start | bytes 380936 | tf_op jit(solution)/shard_map/ppermute | solution.py:262
  24.8 11.8 %collective-permute-start.7 = (bf16[31,16,128]{2,1,0:T(8,128)(2,1)S(1)}, bf16[31,16,128]{2,1,0:T(8,128)(2,1)S(1)}, u32[]{:S(2)}, u32[]{:S(2)}) collective-permute-start(bf16[31,16,128]{2,1,0:T(8,128)(2,1)S(1)} %get-tuple-element.25), channel_id=1, source_target_pairs={{8,0},{9,1},{10,2},{11,3},{12,4},{13,5},{14,6},{15,7},{24,16},{25,... | collective-permute-start | bytes 380936 | tf_op jit(solution)/shard_map/ppermute | solution.py:262
  26.1 10.6 %collective-permute-start.9 = (bf16[31,16,128]{2,1,0:T(8,128)(2,1)S(1)}, bf16[31,16,128]{2,1,0:T(8,128)(2,1)S(1)}, u32[]{:S(2)}, u32[]{:S(2)}) collective-permute-start(bf16[31,16,128]{2,1,0:T(8,128)(2,1)S(1)} %get-tuple-element.27), channel_id=1, source_target_pairs={{4,0},{5,1},{6,2},{7,3},{8,4},{9,5},{10,6},{11,7},{12,8},{13,9},{1... | collective-permute-start | bytes 380936 | tf_op jit(solution)/shard_map/ppermute | solution.py:262
  28.0 12.9 %collective-permute-start.10 = (bf16[31,16,128]{2,1,0:T(8,128)(2,1)S(1)}, bf16[31,16,128]{2,1,0:T(8,128)(2,1)S(1)}, u32[]{:S(2)}, u32[]{:S(2)}) collective-permute-start(bf16[31,16,128]{2,1,0:T(8,128)(2,1)S(1)} %get-tuple-element.28), channel_id=1, source_target_pairs={{2,0},{3,1},{4,2},{5,3},{6,4},{7,5},{8,6},{9,7},{10,8},{11,9},{12,... | collective-permute-start | bytes 380936 | tf_op jit(solution)/shard_map/ppermute | solution.py:262
  31.2 9.7 %collective-permute-start.11 = (bf16[31,16,128]{2,1,0:T(8,128)(2,1)S(1)}, bf16[31,16,128]{2,1,0:T(8,128)(2,1)S(1)}, u32[]{:S(2)}, u32[]{:S(2)}) collective-permute-start(bf16[31,16,128]{2,1,0:T(8,128)(2,1)S(1)} %collective-permute-done.8.ring), channel_id=1, source_target_pairs={{7,3},{11,7},{15,11},{23,19},{27,23},{31,27}} | collective-permute-start | bytes 380936 | tf_op jit(solution)/shard_map/ppermute | solution.py:262

commit v14 on v13

--- a/solution.py
+++ b/solution.py
@@ -206,24 +206,32 @@
     part[...] = acc[pl.ds(0, leaf_dev)]
 
 
-def add_kernel(capacity, part, back8, ring, back4, back2, relayed, out, listed, wanted, sem):
-    last = lax.bitwise_and(lax.axis_index("kx"), 3) == 3
-
-    def back1(r):
-        return jnp.where(last, relayed[r].astype(jnp.float32), ring[r].astype(jnp.float32))
-
-    returned = [(3, back8), (2, back4), (1, back2)]
-    returned = [(o, lambda r, x=x: x[r].astype(jnp.float32)) for o, x in returned] + [(0, back1)]
-    for o, row in returned:
-        listed[o : o + 1] = row(capacity)[0:1].astype(jnp.int32)
+def add_rows(capacity, returned, part, out, listed, wanted, sem):
+    for n, (_, row) in enumerate(returned):
+        listed[n : n + 1] = row(capacity)[0:1].astype(jnp.int32)
     fetch = pltpu.make_async_copy(listed, wanted, sem)
     fetch.start()
     out[...] = part[...]
     fetch.wait()
-    for o, row in returned:
+    for n, (o, row) in enumerate(returned):
         for r in range(capacity):
-            j = wanted[o, o * SLOTS + r]
+            j = wanted[n, o * SLOTS + r]
             out[j] = out[j] + row(r)
+
+
+def far_kernel(capacity, part, back8, back4, out, listed, wanted, sem):
+    returned = [(o, lambda r, x=x: x[r].astype(jnp.float32)) for o, x in ((3, back8), (2, back4))]
+    add_rows(capacity, returned, part, out, listed, wanted, sem)
+
+
+def add_kernel(capacity, part, ring, back2, relayed, out, listed, wanted, sem):
+    last = lax.bitwise_and(lax.axis_index("kx"), 3) == 3
+
+    def back1(r):
+        return jnp.where(last, relayed[r].astype(jnp.float32), ring[r].astype(jnp.float32))
+
+    returned = [(1, lambda r: back2[r].astype(jnp.float32)), (0, back1)]
+    add_rows(capacity, returned, part, out, listed, wanted, sem)
 
 
 def call(body, name, out_shape, ins, outs, limit, flops=0, moved=0, scratch=(), aliases={}):
@@ -299,11 +307,16 @@
         home_kernel, "home", (all_rows,), [SMEM] + [VMEM] * 3, [VMEM], 6, moved=heavy,
         scratch=[VMEM((leaf_dev + 8, samples, width), jnp.float32)],
     )(home, back, low, weights)
-    lists = (4, 4 * SLOTS)
+    lists = (2, 4 * SLOTS)
+    scratch = [VMEM(lists, jnp.int32), SMEM(lists, jnp.int32), pltpu.SemaphoreType.DMA]
+    (part,) = call(
+        functools.partial(far_kernel, capacity), "far", (all_rows,), [VMEM] * 3, [VMEM], 6,
+        moved=2 * MIB, scratch=scratch,
+    )(part, back8, back4)
     (gradient,) = call(
-        functools.partial(add_kernel, capacity), "add", (all_rows,), [VMEM] * 6,
-        [VMEM], 6, moved=4 * MIB, scratch=[VMEM(lists, jnp.int32), SMEM(lists, jnp.int32), pltpu.SemaphoreType.DMA],
-    )(part, back8, ring, back4, back2, relayed)
+        functools.partial(add_kernel, capacity), "add", (all_rows,), [VMEM] * 4, [VMEM], 6,
+        moved=2 * MIB, scratch=scratch,
+    )(part, ring, back2, relayed)
     return gradient
 
 

time: 43.1 us -> 42.9 us (level)
  waiting for transfers between devices: 7.3 us -> 6.55 us
  Pallas kernels: 13.4 us -> 13.9 us
    ppermute x12, waiting for transfers between devices: 7.3 us -> 6.55 us  [passed(): return lax.ppermute(x, 'kx', route)]
    pallas_call x0 -> x1, Pallas kernels: none -> 0.73 us  [per_device(): call(functools.partial(far_kernel, capacity), 'far', (all_rows,), [VMEM]...]
  transfers between devices with their start and end apart: 12 -> 12, of which waited for: 5 -> 5; matrix products, arithmetic and copies ran while one was open for 0% -> 0% of each run, Pallas kernels for 16% -> 18%
where the time goes in v14:
time: 42.9 us; the launch traced here: 42.5 us
  starting transfers between devices  21.9 us (51%)
  Pallas kernels  13.9 us (32%)
  waiting for transfers between devices  6.55 us (15%)
    ppermute x12, starting transfers between devices, passed(): return lax.ppermute(x, 'kx', route)  21.9 us
    ppermute x12, waiting for transfers between devices, passed(): return lax.ppermute(x, 'kx', route)  6.55 us
    pallas_call x1, Pallas kernels, per_device(): call(functools.partial(remote_kernel, capacity), 'remote', (all_rows, sha...  4.18 us
    pallas_call x1, Pallas kernels, per_device(): call(home_kernel, 'home', (all_rows,), [SMEM] + [VMEM] * 3, [VMEM], 6, mo...  3.5 us
    pallas_call x1, Pallas kernels, per_device(): call(local_kernel, 'local', (all_rows,), [SMEM, VMEM, ANY, VMEM], [VMEM],...  2.07 us
    pallas_call x1, Pallas kernels, per_device(): call(functools.partial(add_kernel, capacity), 'add', (all_rows,), [VMEM]...  1.65 us
    pallas_call x1, Pallas kernels, per_device(): call(index_kernel, 'index', (one_list, shape((2, 4 * SLOTS), jnp.int32),...  1.16 us
  transfers between devices with their start and end apart: 12, of which 5 were waited for; matrix products, arithmetic and copies ran while one was open for 0% of the time, Pallas kernels for 18%

profile of v14, /device:TPU:15, one launch (start us, length us, event | category | flops | bytes accessed | tf_op | source)
XLA Modules:
  0.0 42.5 jit_solution(15492741715195548016)
XLA Ops:
  0.0 0.0 copy-start.1
  0.0 0.0 copy-start
  0.0 3.5 %collective-permute-start = (bf16[80,16,128]{2,1,0:T(8,128)(2,1)}, bf16[80,16,128]{2,1,0:T(8,128)(2,1)S(1)}, u32[]{:S(2)}, u32[]{:S(2)}) collective-permute-start(bf16[80,16,128]{2,1,0:T(8,128)(2,1)} %latent.5), channel_id=1, source_target_pairs={{0,4},{1,5},{2,6},{3,7},{4,8},{5,9},{6,10},{7,11},{8,12},{9,13},{1... | collective-permute-start | bytes 983048 | tf_op jit(solution)/shard_map/ppermute | solution.py:270
  3.5 0.0 copy-start.2
  3.5 1.2 %index.1 = (s32[1,128]{1,0:T(1,128)S(1)}, s32[2,128]{1,0:T(2,128)S(1)}, s32[3,80]{1,0:T(4,128)S(1)}) custom-call(s32[3,80]{1,0:T(4,128)} %bitcast.1, bf16[80,16,128]{2,1,0:T(8,128)(2,1)} %latent.5, bf16[80,3,128,128]{3,2,1,0:T(8,128)(2,1)} %weights.7), custom_call_target="tpu_custom_call" | custom-call | bytes 2097152 | tf_op jit(solution)/shard_map/index/pallas_call | solution.py:275
  4.6 2.1 %collective-permute-start.3 = (s32[1,128]{1,0:T(1,128)S(1)}, s32[1,128]{1,0:T(1,128)S(1)}, u32[]{:S(2)}, u32[]{:S(2)}) collective-permute-start(s32[1,128]{1,0:T(1,128)S(1)} %get-tuple-element.18.asked.asked_row), channel_id=1, source_target_pairs={{4,0},{5,1},{6,2},{7,3},{8,4},{9,5},{10,6},{11,7},{12,8},{13,9},{1... | collective-permute-start | bytes 1544 | tf_op jit(solution)/shard_map/ppermute | solution.py:270
  6.8 0.3 collective-permute-start.2
  7.1 1.5 %collective-permute-start.1 = (s32[1,128]{1,0:T(1,128)S(1)}, s32[1,128]{1,0:T(1,128)S(1)}, u32[]{:S(2)}, u32[]{:S(2)}) collective-permute-start(s32[1,128]{1,0:T(1,128)S(1)} %get-tuple-element.18.asked.asked_row), channel_id=1, source_target_pairs={{0,3},{1,0},{2,1},{3,2},{4,7},{5,4},{6,5},{7,6},{8,11},{9,8},{10,9... | collective-permute-start | bytes 1544 | tf_op jit(solution)/shard_map/ppermute | solution.py:270
  8.6 0.7 %collective-permute-done.3.ask8 = s32[1,128]{1,0:T(1,128)S(1)} collective-permute-done((s32[1,128]{1,0:T(1,128)S(1)}, s32[1,128]{1,0:T(1,128)S(1)}, u32[]{:S(2)}, u32[]{:S(2)}) %collective-permute-start.3) | collective-permute-done | bytes 544 | tf_op jit(solution)/shard_map/ppermute | solution.py:270
  9.3 0.3 collective-permute-done.2.ask2
  9.5 1.7 %collective-permute-done.1.ask1 = s32[1,128]{1,0:T(1,128)S(1)} collective-permute-done((s32[1,128]{1,0:T(1,128)S(1)}, s32[1,128]{1,0:T(1,128)S(1)}, u32[]{:S(2)}, u32[]{:S(2)}) %collective-permute-start.1) | collective-permute-done | bytes 544 | tf_op jit(solution)/shard_map/ppermute | solution.py:270
  11.2 0.0 collective-permute-done.before
  11.3 0.0 copy-done.1
  11.3 0.6 %serve.1 = (bf16[30,16,128]{2,1,0:T(8,128)(2,1)S(1)}, bf16[30,16,128]{2,1,0:T(8,128)(2,1)S(1)}, bf16[30,16,128]{2,1,0:T(8,128)(2,1)S(1)}) custom-call(s32[1,128]{1,0:T(1,128)S(1)} %collective-permute-done.1.ask1, s32[1,128]{1,0:T(1,128)S(1)} %collective-permute-done.2.ask2, s32[1,128]{1,0:T(1,128)S(1)} %collective-permute-done.3.ask8, ...), custom_call_target="tpu_custom_call" | custom-call | bytes 4194304 | tf_op jit(solution)/shard_map/serve/pallas_call | solution.py:283
  11.9 0.4 collective-permute-start.4
  12.3 2.5 %collective-permute-start.5 = (bf16[30,16,128]{2,1,0:T(8,128)(2,1)S(1)}, bf16[30,16,128]{2,1,0:T(8,128)(2,1)S(1)}, u32[]{:S(2)}, u32[]{:S(2)}) collective-permute-start(bf16[30,16,128]{2,1,0:T(8,128)(2,1)S(1)} %get-tuple-element.21), channel_id=1, source_target_pairs={{0,1},{1,2},{2,3},{3,0},{4,5},{5,6},{6,7},{7,4},{8,9},{9,10},{10,1... | collective-permute-start | bytes 368648 | tf_op jit(solution)/shard_map/ppermute | solution.py:270
  14.8 3.2 %collective-permute-start.6 = (bf16[30,16,128]{2,1,0:T(8,128)(2,1)S(1)}, bf16[30,16,128]{2,1,0:T(8,128)(2,1)S(1)}, u32[]{:S(2)}, u32[]{:S(2)}) collective-permute-start(bf16[30,16,128]{2,1,0:T(8,128)(2,1)S(1)} %get-tuple-element.22), channel_id=1, source_target_pairs={{4,8},{5,9},{6,10},{7,11},{8,12},{9,13},{10,14},{11,15},{20,24},{2... | collective-permute-start | bytes 368648 | tf_op jit(solution)/shard_map/ppermute | solution.py:270
  18.0 0.0 copy-done
  18.1 2.1 %local.1.left = f32[80,16,128]{2,1,0:T(8,128)S(1)} custom-call(s32[3,80]{1,0:T(4,128)S(1)} %get-tuple-element.17.home, bf16[80,16,128]{2,1,0:T(8,128)(2,1)S(1)} %copy-done.1, bf16[80,16,128]{2,1,0:T(8,128)(2,1)S(1)} %collective-permute-done.before, bf16[80,3,128,128]{3,2,1,0:T(8,128)(2,1)S(1)} %copy-done), custom_call_target="tpu_custom_call" | custom-call | bytes 7864320 | tf_op jit(solution)/shard_map/local/pallas_call | solution.py:290
  20.1 0.0 collective-permute-done.4.from2
  20.1 0.0 collective-permute-done.5.from1
  20.1 0.4 collective-permute-done.6.from8
  20.5 0.0 copy-done.2
  20.5 4.2 %remote.1 = (f32[80,16,128]{2,1,0:T(8,128)S(1)}, bf16[88,16,128]{2,1,0:T(8,128)(2,1)S(1)}, bf16[31,16,128]{2,1,0:T(8,128)(2,1)S(1)}, bf16[31,16,128]{2,1,0:T(8,1...) custom-call(s32[1,128]{1,0:T(1,128)S(1)} %get-tuple-element.18.asked.asked_row, ...), custom_call_target="tpu_custom_call" | custom-call | bytes 7864320 | tf_op jit(solution)/shard_map/remote/pallas_call | solution.py:294
  24.7 0.1 collective-permute-start.9
  24.8 1.3 %collective-permute-start.7 = (bf16[31,16,128]{2,1,0:T(8,128)(2,1)S(1)}, bf16[31,16,128]{2,1,0:T(8,128)(2,1)S(1)}, u32[]{:S(2)}, u32[]{:S(2)}) collective-permute-start(bf16[31,16,128]{2,1,0:T(8,128)(2,1)S(1)} %get-tuple-element.25), channel_id=1, source_target_pairs={{8,0},{9,1},{10,2},{11,3},{12,4},{13,5},{14,6},{15,7},{24,16},{25,... | collective-permute-start | bytes 380936 | tf_op jit(solution)/shard_map/ppermute | solution.py:270
  26.1 1.9 %collective-permute-start.8 = (bf16[31,16,128]{2,1,0:T(8,128)(2,1)S(1)}, bf16[31,16,128]{2,1,0:T(8,128)(2,1)S(1)}, u32[]{:S(2)}, u32[]{:S(2)}) collective-permute-start(bf16[31,16,128]{2,1,0:T(8,128)(2,1)S(1)} %get-tuple-element.26), channel_id=1, source_target_pairs={{4,0},{5,1},{6,2},{7,3},{8,4},{9,5},{10,6},{11,7},{12,8},{13,9},{1... | collective-permute-start | bytes 380936 | tf_op jit(solution)/shard_map/ppermute | solution.py:270
  28.0 3.2 %collective-permute-start.10 = (bf16[31,16,128]{2,1,0:T(8,128)(2,1)S(1)}, bf16[31,16,128]{2,1,0:T(8,128)(2,1)S(1)}, u32[]{:S(2)}, u32[]{:S(2)}) collective-permute-start(bf16[31,16,128]{2,1,0:T(8,128)(2,1)S(1)} %get-tuple-element.28), channel_id=1, source_target_pairs={{2,0},{3,1},{4,2},{5,3},{6,4},{7,5},{8,6},{9,7},{10,8},{11,9},{12,... | collective-permute-start | bytes 380936 | tf_op jit(solution)/shard_map/ppermute | solution.py:270
  31.2 0.0 collective-permute-done.9.ring
  31.2 1.9 %collective-permute-start.11 = (bf16[31,16,128]{2,1,0:T(8,128)(2,1)S(1)}, bf16[31,16,128]{2,1,0:T(8,128)(2,1)S(1)}, u32[]{:S(2)}, u32[]{:S(2)}) collective-permute-start(bf16[31,16,128]{2,1,0:T(8,128)(2,1)S(1)} %collective-permute-done.9.ring), channel_id=1, source_target_pairs={{7,3},{11,7},{15,11},{23,19},{27,23},{31,27}} | collective-permute-start | bytes 380936 | tf_op jit(solution)/shard_map/ppermute | solution.py:270
  33.1 3.5 %home.1.part = f32[80,16,128]{2,1,0:T(8,128)S(1)} custom-call(s32[3,80]{1,0:T(4,128)S(1)} %get-tuple-element.17.home, f32[80,16,128]{2,1,0:T(8,128)S(1)} %get-tuple-element.23.back, bf16[88,16,128]{2,1,0:T(8,128)(2,1)S(1)} %get-tuple-element.24.low, bf16[80,3,128,128]{3,2,1,0:T(8,128)(2,1)S(1)} %copy-done), custom_call_target="tpu_custom_call" | custom-call | bytes 7864320 | tf_op jit(solution)/shard_map/home/pallas_call | solution.py:306
  36.6 0.0 collective-permute-done.7.back8
  36.6 0.0 collective-permute-done.8.back4
  36.6 0.7 %far.1.part = f32[80,16,128]{2,1,0:T(8,128)S(1)} custom-call(f32[80,16,128]{2,1,0:T(8,128)S(1)} %home.1.part, bf16[31,16,128]{2,1,0:T(8,128)(2,1)S(1)} %collective-permute-done.7.back8, bf16[31,16,128]{2,1,0:T(8,128)(2,1)S(1)} %collective-permute-done.8.back4), custom_call_target="tpu_custom_call" | custom-call | bytes 2097152 | tf_op jit(solution)/shard_map/far/pallas_call | solution.py:312
  37.4 3.5 %collective-permute-done.10.back2 = bf16[31,16,128]{2,1,0:T(8,128)(2,1)S(1)} collective-permute-done((bf16[31,16,128]{2,1,0:T(8,128)(2,1)S(1)}, bf16[31,16,128]{2,1,0:T(8,128)(2,1)S(1)}, u32[]{:S(2)}, u32[]{:S(2)}) %collective-permute-start.10) | collective-permute-done | bytes 127008 | tf_op jit(solution)/shard_map/ppermute | solution.py:270
  40.9 0.0 collective-permute-done.11.relayed
  40.9 1.6 %add.1 = f32[80,16,128]{2,1,0:T(8,128)} custom-call(f32[80,16,128]{2,1,0:T(8,128)S(1)} %far.1.part, bf16[31,16,128]{2,1,0:T(8,128)(2,1)S(1)} %collective-permute-done.9.ring, bf16[31,16,128]{2,1,0:T(8,128)(2,1)S(1)} %collective-permute-done.10.back2, bf16[31,16,128]{2,1,0:T(8,128)(2,1)S(1)} %collective-permute-done.11.relayed), custom_call_target="tpu_custom_call" | custom-call | bytes 2097152 | tf_op jit(solution)/shard_map/add/pallas_call | solution.py:316
Async XLA Ops:
  0.0 11.3 %copy-start.1 = (bf16[80,16,128]{2,1,0:T(8,128)(2,1)S(1)}, bf16[80,16,128]{2,1,0:T(8,128)(2,1)}, u32[]{:S(2)}) copy-start(bf16[80,16,128]{2,1,0:T(8,128)(2,1)} %latent.5) | copy-start | bytes 983044
  0.0 18.0 %copy-start = (bf16[80,3,128,128]{3,2,1,0:T(8,128)(2,1)S(1)}, bf16[80,3,128,128]{3,2,1,0:T(8,128)(2,1)}, u32[]{:S(2)}) copy-start(bf16[80,3,128,128]{3,2,1,0:T(8,128)(2,1)} %weights.7) | copy-start | bytes 23592964
  0.0 11.2 %collective-permute-start = (bf16[80,16,128]{2,1,0:T(8,128)(2,1)}, bf16[80,16,128]{2,1,0:T(8,128)(2,1)S(1)}, u32[]{:S(2)}, u32[]{:S(2)}) collective-permute-start(bf16[80,16,128]{2,1,0:T(8,128)(2,1)} %latent.5), channel_id=1, source_target_pairs={{0,4},{1,5},{2,6},{3,7},{4,8},{5,9},{6,10},{7,11},{8,12},{9,13},{1... | collective-permute-start | bytes 983048 | tf_op jit(solution)/shard_map/ppermute | solution.py:270
  3.5 17.0 %copy-start.2 = (bf16[80,128,128]{2,1,0:T(8,128)(2,1)S(1)}, bf16[80,128,128]{2,1,0:T(8,128)(2,1)}, u32[]{:S(2)}) copy-start(bf16[80,128,128]{2,1,0:T(8,128)(2,1)} %factor.1) | copy-start | bytes 7864324
  4.6 4.6 %collective-permute-start.3 = (s32[1,128]{1,0:T(1,128)S(1)}, s32[1,128]{1,0:T(1,128)S(1)}, u32[]{:S(2)}, u32[]{:S(2)}) collective-permute-start(s32[1,128]{1,0:T(1,128)S(1)} %get-tuple-element.18.asked.asked_row), channel_id=1, source_target_pairs={{4,0},{5,1},{6,2},{7,3},{8,4},{9,5},{10,6},{11,7},{12,8},{13,9},{1... | collective-permute-start | bytes 1544 | tf_op jit(solution)/shard_map/ppermute | solution.py:270
  6.8 2.8 %collective-permute-start.2 = (s32[1,128]{1,0:T(1,128)S(1)}, s32[1,128]{1,0:T(1,128)S(1)}, u32[]{:S(2)}, u32[]{:S(2)}) collective-permute-start(s32[1,128]{1,0:T(1,128)S(1)} %get-tuple-element.18.asked.asked_row), channel_id=1, source_target_pairs={{0,2},{1,3},{2,0},{3,1},{4,6},{5,7},{6,4},{7,5},{8,10},{9,11},{10,... | collective-permute-start | bytes 1544 | tf_op jit(solution)/shard_map/ppermute | solution.py:270
  7.1 4.2 %collective-permute-start.1 = (s32[1,128]{1,0:T(1,128)S(1)}, s32[1,128]{1,0:T(1,128)S(1)}, u32[]{:S(2)}, u32[]{:S(2)}) collective-permute-start(s32[1,128]{1,0:T(1,128)S(1)} %get-tuple-element.18.asked.asked_row), channel_id=1, source_target_pairs={{0,3},{1,0},{2,1},{3,2},{4,7},{5,4},{6,5},{7,6},{8,11},{9,8},{10,9... | collective-permute-start | bytes 1544 | tf_op jit(solution)/shard_map/ppermute | solution.py:270
  11.9 8.2 %collective-permute-start.4 = (bf16[30,16,128]{2,1,0:T(8,128)(2,1)S(1)}, bf16[30,16,128]{2,1,0:T(8,128)(2,1)S(1)}, u32[]{:S(2)}, u32[]{:S(2)}) collective-permute-start(bf16[30,16,128]{2,1,0:T(8,128)(2,1)S(1)} %get-tuple-element.20), channel_id=1, source_target_pairs={{0,2},{1,3},{2,0},{3,1},{4,6},{5,7},{6,4},{7,5},{8,10},{9,11},{10,... | collective-permute-start | bytes 368648 | tf_op jit(solution)/shard_map/ppermute | solution.py:270
  12.3 7.8 %collective-permute-start.5 = (bf16[30,16,128]{2,1,0:T(8,128)(2,1)S(1)}, bf16[30,16,128]{2,1,0:T(8,128)(2,1)S(1)}, u32[]{:S(2)}, u32[]{:S(2)}) collective-permute-start(bf16[30,16,128]{2,1,0:T(8,128)(2,1)S(1)} %get-tuple-element.21), channel_id=1, source_target_pairs={{0,1},{1,2},{2,3},{3,0},{4,5},{5,6},{6,7},{7,4},{8,9},{9,10},{10,1... | collective-permute-start | bytes 368648 | tf_op jit(solution)/shard_map/ppermute | solution.py:270
  14.8 5.7 %collective-permute-start.6 = (bf16[30,16,128]{2,1,0:T(8,128)(2,1)S(1)}, bf16[30,16,128]{2,1,0:T(8,128)(2,1)S(1)}, u32[]{:S(2)}, u32[]{:S(2)}) collective-permute-start(bf16[30,16,128]{2,1,0:T(8,128)(2,1)S(1)} %get-tuple-element.22), channel_id=1, source_target_pairs={{4,8},{5,9},{6,10},{7,11},{8,12},{9,13},{10,14},{11,15},{20,24},{2... | collective-permute-start | bytes 368648 | tf_op jit(solution)/shard_map/ppermute | solution.py:270
  24.7 6.5 %collective-permute-start.9 = (bf16[31,16,128]{2,1,0:T(8,128)(2,1)S(1)}, bf16[31,16,128]{2,1,0:T(8,128)(2,1)S(1)}, u32[]{:S(2)}, u32[]{:S(2)}) collective-permute-start(bf16[31,16,128]{2,1,0:T(8,128)(2,1)S(1)} %get-tuple-element.27), channel_id=1, source_target_pairs={{0,3},{1,0},{2,1},{3,2},{4,7},{5,4},{6,5},{7,6},{8,11},{9,8},{10,9... | collective-permute-start | bytes 380936 | tf_op jit(solution)/shard_map/ppermute | solution.py:270
  24.8 11.9 %collective-permute-start.7 = (bf16[31,16,128]{2,1,0:T(8,128)(2,1)S(1)}, bf16[31,16,128]{2,1,0:T(8,128)(2,1)S(1)}, u32[]{:S(2)}, u32[]{:S(2)}) collective-permute-start(bf16[31,16,128]{2,1,0:T(8,128)(2,1)S(1)} %get-tuple-element.25), channel_id=1, source_target_pairs={{8,0},{9,1},{10,2},{11,3},{12,4},{13,5},{14,6},{15,7},{24,16},{25,... | collective-permute-start | bytes 380936 | tf_op jit(solution)/shard_map/ppermute | solution.py:270
  26.1 10.6 %collective-permute-start.8 = (bf16[31,16,128]{2,1,0:T(8,128)(2,1)S(1)}, bf16[31,16,128]{2,1,0:T(8,128)(2,1)S(1)}, u32[]{:S(2)}, u32[]{:S(2)}) collective-permute-start(bf16[31,16,128]{2,1,0:T(8,128)(2,1)S(1)} %get-tuple-element.26), channel_id=1, source_target_pairs={{4,0},{5,1},{6,2},{7,3},{8,4},{9,5},{10,6},{11,7},{12,8},{13,9},{1... | collective-permute-start | bytes 380936 | tf_op jit(solution)/shard_map/ppermute | solution.py:270
  28.0 12.9 %collective-permute-start.10 = (bf16[31,16,128]{2,1,0:T(8,128)(2,1)S(1)}, bf16[31,16,128]{2,1,0:T(8,128)(2,1)S(1)}, u32[]{:S(2)}, u32[]{:S(2)}) collective-permute-start(bf16[31,16,128]{2,1,0:T(8,128)(2,1)S(1)} %get-tuple-element.28), channel_id=1, source_target_pairs={{2,0},{3,1},{4,2},{5,3},{6,4},{7,5},{8,6},{9,7},{10,8},{11,9},{12,... | collective-permute-start | bytes 380936 | tf_op jit(solution)/shard_map/ppermute | solution.py:270
  31.2 9.7 %collective-permute-start.11 = (bf16[31,16,128]{2,1,0:T(8,128)(2,1)S(1)}, bf16[31,16,128]{2,1,0:T(8,128)(2,1)S(1)}, u32[]{:S(2)}, u32[]{:S(2)}) collective-permute-start(bf16[31,16,128]{2,1,0:T(8,128)(2,1)S(1)} %collective-permute-done.9.ring), channel_id=1, source_target_pairs={{7,3},{11,7},{15,11},{23,19},{27,23},{31,27}} | collective-permute-start | bytes 380936 | tf_op jit(solution)/shard_map/ppermute | solution.py:270

commit v15 on v14

--- a/solution.py
+++ b/solution.py
@@ -219,18 +219,18 @@
             out[j] = out[j] + row(r)
 
 
-def far_kernel(capacity, part, back8, back4, out, listed, wanted, sem):
-    returned = [(o, lambda r, x=x: x[r].astype(jnp.float32)) for o, x in ((3, back8), (2, back4))]
+def far_kernel(capacity, part, back8, back2, out, listed, wanted, sem):
+    returned = [(o, lambda r, x=x: x[r].astype(jnp.float32)) for o, x in ((3, back8), (1, back2))]
     add_rows(capacity, returned, part, out, listed, wanted, sem)
 
 
-def add_kernel(capacity, part, ring, back2, relayed, out, listed, wanted, sem):
+def add_kernel(capacity, part, ring, back4, relayed, out, listed, wanted, sem):
     last = lax.bitwise_and(lax.axis_index("kx"), 3) == 3
 
     def back1(r):
         return jnp.where(last, relayed[r].astype(jnp.float32), ring[r].astype(jnp.float32))
 
-    returned = [(1, lambda r: back2[r].astype(jnp.float32)), (0, back1)]
+    returned = [(2, lambda r: back4[r].astype(jnp.float32)), (0, back1)]
     add_rows(capacity, returned, part, out, listed, wanted, sem)
 
 
@@ -312,11 +312,11 @@
     (part,) = call(
         functools.partial(far_kernel, capacity), "far", (all_rows,), [VMEM] * 3, [VMEM], 6,
         moved=2 * MIB, scratch=scratch,
-    )(part, back8, back4)
+    )(part, back8, back2)
     (gradient,) = call(
         functools.partial(add_kernel, capacity), "add", (all_rows,), [VMEM] * 4, [VMEM], 6,
         moved=2 * MIB, scratch=scratch,
-    )(part, ring, back2, relayed)
+    )(part, ring, back4, relayed)
     return gradient
 
 

time: 42.9 us -> 43 us (level)
  the two profiles are of different devices: /device:TPU:15 before, /device:TPU:8 now
where the time goes in v15:
time: 43 us; the launch traced here: 42.7 us
  starting transfers between devices  19.2 us (45%)
  Pallas kernels  13.9 us (32%)
  waiting for transfers between devices  9.4 us (22%)
    ppermute x12, starting transfers between devices, passed(): return lax.ppermute(x, 'kx', route)  19.2 us
    ppermute x12, waiting for transfers between devices, passed(): return lax.ppermute(x, 'kx', route)  9.4 us
    pallas_call x1, Pallas kernels, per_device(): call(functools.partial(remote_kernel, capacity), 'remote', (all_rows, sha...  4.18 us
    pallas_call x1, Pallas kernels, per_device(): call(home_kernel, 'home', (all_rows,), [SMEM] + [VMEM] * 3, [VMEM], 6, mo...  3.5 us
    pallas_call x1, Pallas kernels, per_device(): call(local_kernel, 'local', (all_rows,), [SMEM, VMEM, ANY, VMEM], [VMEM],...  2.07 us
    pallas_call x1, Pallas kernels, per_device(): call(functools.partial(add_kernel, capacity), 'add', (all_rows,), [VMEM]...  1.64 us
    pallas_call x1, Pallas kernels, per_device(): call(index_kernel, 'index', (one_list, shape((2, 4 * SLOTS), jnp.int32),...  1.16 us
  transfers between devices with their start and end apart: 12, of which 5 were waited for; matrix products, arithmetic and copies ran while one was open for 0% of the time, Pallas kernels for 17%

profile of v15, /device:TPU:8, one launch (start us, length us, event | category | flops | bytes accessed | tf_op | source)
XLA Modules:
  0.0 42.7 jit_solution(4226648979042869568)
XLA Ops:
  0.0 0.0 copy-start.1
  0.0 0.0 copy-start
  0.0 3.7 %collective-permute-start = (bf16[80,16,128]{2,1,0:T(8,128)(2,1)}, bf16[80,16,128]{2,1,0:T(8,128)(2,1)S(1)}, u32[]{:S(2)}, u32[]{:S(2)}) collective-permute-start(bf16[80,16,128]{2,1,0:T(8,128)(2,1)} %latent.5), channel_id=1, source_target_pairs={{0,4},{1,5},{2,6},{3,7},{4,8},{5,9},{6,10},{7,11},{8,12},{9,13},{1... | collective-permute-start | bytes 983048 | tf_op jit(solution)/shard_map/ppermute | solution.py:270
  3.7 0.0 copy-start.2
  3.8 1.2 %index.1 = (s32[1,128]{1,0:T(1,128)S(1)}, s32[2,128]{1,0:T(2,128)S(1)}, s32[3,80]{1,0:T(4,128)S(1)}) custom-call(s32[3,80]{1,0:T(4,128)} %bitcast.1, bf16[80,16,128]{2,1,0:T(8,128)(2,1)} %latent.5, bf16[80,3,128,128]{3,2,1,0:T(8,128)(2,1)} %weights.7), custom_call_target="tpu_custom_call" | custom-call | bytes 2097152 | tf_op jit(solution)/shard_map/index/pallas_call | solution.py:275
  4.9 2.4 %collective-permute-start.3 = (s32[1,128]{1,0:T(1,128)S(1)}, s32[1,128]{1,0:T(1,128)S(1)}, u32[]{:S(2)}, u32[]{:S(2)}) collective-permute-start(s32[1,128]{1,0:T(1,128)S(1)} %get-tuple-element.18.asked.asked_row), channel_id=1, source_target_pairs={{4,0},{5,1},{6,2},{7,3},{8,4},{9,5},{10,6},{11,7},{12,8},{13,9},{1... | collective-permute-start | bytes 1544 | tf_op jit(solution)/shard_map/ppermute | solution.py:270
  7.4 1.6 %collective-permute-start.2 = (s32[1,128]{1,0:T(1,128)S(1)}, s32[1,128]{1,0:T(1,128)S(1)}, u32[]{:S(2)}, u32[]{:S(2)}) collective-permute-start(s32[1,128]{1,0:T(1,128)S(1)} %get-tuple-element.18.asked.asked_row), channel_id=1, source_target_pairs={{0,2},{1,3},{2,0},{3,1},{4,6},{5,7},{6,4},{7,5},{8,10},{9,11},{10,... | collective-permute-start | bytes 1544 | tf_op jit(solution)/shard_map/ppermute | solution.py:270
  8.9 0.0 collective-permute-start.1
  8.9 1.5 %collective-permute-done.3.ask8 = s32[1,128]{1,0:T(1,128)S(1)} collective-permute-done((s32[1,128]{1,0:T(1,128)S(1)}, s32[1,128]{1,0:T(1,128)S(1)}, u32[]{:S(2)}, u32[]{:S(2)}) %collective-permute-start.3) | collective-permute-done | bytes 544 | tf_op jit(solution)/shard_map/ppermute | solution.py:270
  10.4 0.6 %collective-permute-done.2.ask2 = s32[1,128]{1,0:T(1,128)S(1)} collective-permute-done((s32[1,128]{1,0:T(1,128)S(1)}, s32[1,128]{1,0:T(1,128)S(1)}, u32[]{:S(2)}, u32[]{:S(2)}) %collective-permute-start.2) | collective-permute-done | bytes 544 | tf_op jit(solution)/shard_map/ppermute | solution.py:270
  11.0 0.0 collective-permute-done.1.ask1
  11.0 0.8 %collective-permute-done.before = bf16[80,16,128]{2,1,0:T(8,128)(2,1)S(1)} collective-permute-done((bf16[80,16,128]{2,1,0:T(8,128)(2,1)}, bf16[80,16,128]{2,1,0:T(8,128)(2,1)S(1)}, u32[]{:S(2)}, u32[]{:S(2)}) %collective-permute-start) | collective-permute-done | bytes 327712 | tf_op jit(solution)/shard_map/ppermute | solution.py:270
  11.8 0.0 copy-done.1
  11.8 0.6 %serve.1 = (bf16[30,16,128]{2,1,0:T(8,128)(2,1)S(1)}, bf16[30,16,128]{2,1,0:T(8,128)(2,1)S(1)}, bf16[30,16,128]{2,1,0:T(8,128)(2,1)S(1)}) custom-call(s32[1,128]{1,0:T(1,128)S(1)} %collective-permute-done.1.ask1, s32[1,128]{1,0:T(1,128)S(1)} %collective-permute-done.2.ask2, s32[1,128]{1,0:T(1,128)S(1)} %collective-permute-done.3.ask8, ...), custom_call_target="tpu_custom_call" | custom-call | bytes 4194304 | tf_op jit(solution)/shard_map/serve/pallas_call | solution.py:283
  12.5 1.6 %collective-permute-start.4 = (bf16[30,16,128]{2,1,0:T(8,128)(2,1)S(1)}, bf16[30,16,128]{2,1,0:T(8,128)(2,1)S(1)}, u32[]{:S(2)}, u32[]{:S(2)}) collective-permute-start(bf16[30,16,128]{2,1,0:T(8,128)(2,1)S(1)} %get-tuple-element.20), channel_id=1, source_target_pairs={{0,2},{1,3},{2,0},{3,1},{4,6},{5,7},{6,4},{7,5},{8,10},{9,11},{10,... | collective-permute-start | bytes 368648 | tf_op jit(solution)/shard_map/ppermute | solution.py:270
  14.1 0.0 collective-permute-start.5
  14.1 3.5 %collective-permute-start.6 = (bf16[30,16,128]{2,1,0:T(8,128)(2,1)S(1)}, bf16[30,16,128]{2,1,0:T(8,128)(2,1)S(1)}, u32[]{:S(2)}, u32[]{:S(2)}) collective-permute-start(bf16[30,16,128]{2,1,0:T(8,128)(2,1)S(1)} %get-tuple-element.22), channel_id=1, source_target_pairs={{4,8},{5,9},{6,10},{7,11},{8,12},{9,13},{10,14},{11,15},{20,24},{2... | collective-permute-start | bytes 368648 | tf_op jit(solution)/shard_map/ppermute | solution.py:270
  17.5 0.0 copy-done
  17.5 2.1 %local.1.left = f32[80,16,128]{2,1,0:T(8,128)S(1)} custom-call(s32[3,80]{1,0:T(4,128)S(1)} %get-tuple-element.17.home, bf16[80,16,128]{2,1,0:T(8,128)(2,1)S(1)} %copy-done.1, bf16[80,16,128]{2,1,0:T(8,128)(2,1)S(1)} %collective-permute-done.before, bf16[80,3,128,128]{3,2,1,0:T(8,128)(2,1)S(1)} %copy-done), custom_call_target="tpu_custom_call" | custom-call | bytes 7864320 | tf_op jit(solution)/shard_map/local/pallas_call | solution.py:290
  19.6 0.0 collective-permute-done.4.from2
  19.6 0.0 collective-permute-done.5.from1
  19.6 1.2 %collective-permute-done.6.from8 = bf16[30,16,128]{2,1,0:T(8,128)(2,1)S(1)} collective-permute-done((bf16[30,16,128]{2,1,0:T(8,128)(2,1)S(1)}, bf16[30,16,128]{2,1,0:T(8,128)(2,1)S(1)}, u32[]{:S(2)}, u32[]{:S(2)}) %collective-permute-start.6) | collective-permute-done | bytes 122912 | tf_op jit(solution)/shard_map/ppermute | solution.py:270
  20.9 0.0 copy-done.2
  20.9 4.2 %remote.1 = (f32[80,16,128]{2,1,0:T(8,128)S(1)}, bf16[88,16,128]{2,1,0:T(8,128)(2,1)S(1)}, bf16[31,16,128]{2,1,0:T(8,128)(2,1)S(1)}, bf16[31,16,128]{2,1,0:T(8,1...) custom-call(s32[1,128]{1,0:T(1,128)S(1)} %get-tuple-element.18.asked.asked_row, ...), custom_call_target="tpu_custom_call" | custom-call | bytes 7864320 | tf_op jit(solution)/shard_map/remote/pallas_call | solution.py:294
  25.1 0.6 %collective-permute-start.9 = (bf16[31,16,128]{2,1,0:T(8,128)(2,1)S(1)}, bf16[31,16,128]{2,1,0:T(8,128)(2,1)S(1)}, u32[]{:S(2)}, u32[]{:S(2)}) collective-permute-start(bf16[31,16,128]{2,1,0:T(8,128)(2,1)S(1)} %get-tuple-element.27), channel_id=1, source_target_pairs={{0,3},{1,0},{2,1},{3,2},{4,7},{5,4},{6,5},{7,6},{8,11},{9,8},{10,9... | collective-permute-start | bytes 380936 | tf_op jit(solution)/shard_map/ppermute | solution.py:270
  25.7 1.3 %collective-permute-start.7 = (bf16[31,16,128]{2,1,0:T(8,128)(2,1)S(1)}, bf16[31,16,128]{2,1,0:T(8,128)(2,1)S(1)}, u32[]{:S(2)}, u32[]{:S(2)}) collective-permute-start(bf16[31,16,128]{2,1,0:T(8,128)(2,1)S(1)} %get-tuple-element.25), channel_id=1, source_target_pairs={{8,0},{9,1},{10,2},{11,3},{12,4},{13,5},{14,6},{15,7},{24,16},{25,... | collective-permute-start | bytes 380936 | tf_op jit(solution)/shard_map/ppermute | solution.py:270
  27.0 1.9 %collective-permute-start.8 = (bf16[31,16,128]{2,1,0:T(8,128)(2,1)S(1)}, bf16[31,16,128]{2,1,0:T(8,128)(2,1)S(1)}, u32[]{:S(2)}, u32[]{:S(2)}) collective-permute-start(bf16[31,16,128]{2,1,0:T(8,128)(2,1)S(1)} %get-tuple-element.26), channel_id=1, source_target_pairs={{2,0},{3,1},{4,2},{5,3},{6,4},{7,5},{8,6},{9,7},{10,8},{11,9},{12,... | collective-permute-start | bytes 380936 | tf_op jit(solution)/shard_map/ppermute | solution.py:270
  28.9 1.9 %collective-permute-start.10 = (bf16[31,16,128]{2,1,0:T(8,128)(2,1)S(1)}, bf16[31,16,128]{2,1,0:T(8,128)(2,1)S(1)}, u32[]{:S(2)}, u32[]{:S(2)}) collective-permute-start(bf16[31,16,128]{2,1,0:T(8,128)(2,1)S(1)} %get-tuple-element.28), channel_id=1, source_target_pairs={{4,0},{5,1},{6,2},{7,3},{8,4},{9,5},{10,6},{11,7},{12,8},{13,9},{1... | collective-permute-start | bytes 380936 | tf_op jit(solution)/shard_map/ppermute | solution.py:270
  30.8 0.0 collective-permute-done.9.ring
  30.8 0.7 %collective-permute-start.11 = (bf16[31,16,128]{2,1,0:T(8,128)(2,1)S(1)}, bf16[31,16,128]{2,1,0:T(8,128)(2,1)S(1)}, u32[]{:S(2)}, u32[]{:S(2)}) collective-permute-start(bf16[31,16,128]{2,1,0:T(8,128)(2,1)S(1)} %collective-permute-done.9.ring), channel_id=1, source_target_pairs={{7,3},{11,7},{15,11},{23,19},{27,23},{31,27}} | collective-permute-start | bytes 380936 | tf_op jit(solution)/shard_map/ppermute | solution.py:270
  31.5 3.5 %home.1.part = f32[80,16,128]{2,1,0:T(8,128)S(1)} custom-call(s32[3,80]{1,0:T(4,128)S(1)} %get-tuple-element.17.home, f32[80,16,128]{2,1,0:T(8,128)S(1)} %get-tuple-element.23.back, bf16[88,16,128]{2,1,0:T(8,128)(2,1)S(1)} %get-tuple-element.24.low, bf16[80,3,128,128]{3,2,1,0:T(8,128)(2,1)S(1)} %copy-done), custom_call_target="tpu_custom_call" | custom-call | bytes 7864320 | tf_op jit(solution)/shard_map/home/pallas_call | solution.py:306
  35.0 0.0 collective-permute-done.7.back8
  35.0 0.0 collective-permute-done.8.back2
  35.0 0.7 %far.1.part = f32[80,16,128]{2,1,0:T(8,128)S(1)} custom-call(f32[80,16,128]{2,1,0:T(8,128)S(1)} %home.1.part, bf16[31,16,128]{2,1,0:T(8,128)(2,1)S(1)} %collective-permute-done.7.back8, bf16[31,16,128]{2,1,0:T(8,128)(2,1)S(1)} %collective-permute-done.8.back2), custom_call_target="tpu_custom_call" | custom-call | bytes 2097152 | tf_op jit(solution)/shard_map/far/pallas_call | solution.py:312
  35.8 5.3 %collective-permute-done.10.back4 = bf16[31,16,128]{2,1,0:T(8,128)(2,1)S(1)} collective-permute-done((bf16[31,16,128]{2,1,0:T(8,128)(2,1)S(1)}, bf16[31,16,128]{2,1,0:T(8,128)(2,1)S(1)}, u32[]{:S(2)}, u32[]{:S(2)}) %collective-permute-start.10) | collective-permute-done | bytes 127008 | tf_op jit(solution)/shard_map/ppermute | solution.py:270
  41.1 0.0 collective-permute-done.11.relayed
  41.1 1.6 %add.1 = f32[80,16,128]{2,1,0:T(8,128)} custom-call(f32[80,16,128]{2,1,0:T(8,128)S(1)} %far.1.part, bf16[31,16,128]{2,1,0:T(8,128)(2,1)S(1)} %collective-permute-done.9.ring, bf16[31,16,128]{2,1,0:T(8,128)(2,1)S(1)} %collective-permute-done.10.back4, bf16[31,16,128]{2,1,0:T(8,128)(2,1)S(1)} %collective-permute-done.11.relayed), custom_call_target="tpu_custom_call" | custom-call | bytes 2097152 | tf_op jit(solution)/shard_map/add/pallas_call | solution.py:316
Async XLA Ops:
  0.0 11.8 %copy-start.1 = (bf16[80,16,128]{2,1,0:T(8,128)(2,1)S(1)}, bf16[80,16,128]{2,1,0:T(8,128)(2,1)}, u32[]{:S(2)}) copy-start(bf16[80,16,128]{2,1,0:T(8,128)(2,1)} %latent.5) | copy-start | bytes 983044
  0.0 17.5 %copy-start = (bf16[80,3,128,128]{3,2,1,0:T(8,128)(2,1)S(1)}, bf16[80,3,128,128]{3,2,1,0:T(8,128)(2,1)}, u32[]{:S(2)}) copy-start(bf16[80,3,128,128]{3,2,1,0:T(8,128)(2,1)} %weights.7) | copy-start | bytes 23592964
  0.0 11.8 %collective-permute-start = (bf16[80,16,128]{2,1,0:T(8,128)(2,1)}, bf16[80,16,128]{2,1,0:T(8,128)(2,1)S(1)}, u32[]{:S(2)}, u32[]{:S(2)}) collective-permute-start(bf16[80,16,128]{2,1,0:T(8,128)(2,1)} %latent.5), channel_id=1, source_target_pairs={{0,4},{1,5},{2,6},{3,7},{4,8},{5,9},{6,10},{7,11},{8,12},{9,13},{1... | collective-permute-start | bytes 983048 | tf_op jit(solution)/shard_map/ppermute | solution.py:270
  3.7 17.1 %copy-start.2 = (bf16[80,128,128]{2,1,0:T(8,128)(2,1)S(1)}, bf16[80,128,128]{2,1,0:T(8,128)(2,1)}, u32[]{:S(2)}) copy-start(bf16[80,128,128]{2,1,0:T(8,128)(2,1)} %factor.1) | copy-start | bytes 7864324
  4.9 5.5 %collective-permute-start.3 = (s32[1,128]{1,0:T(1,128)S(1)}, s32[1,128]{1,0:T(1,128)S(1)}, u32[]{:S(2)}, u32[]{:S(2)}) collective-permute-start(s32[1,128]{1,0:T(1,128)S(1)} %get-tuple-element.18.asked.asked_row), channel_id=1, source_target_pairs={{4,0},{5,1},{6,2},{7,3},{8,4},{9,5},{10,6},{11,7},{12,8},{13,9},{1... | collective-permute-start | bytes 1544 | tf_op jit(solution)/shard_map/ppermute | solution.py:270
  7.4 3.6 %collective-permute-start.2 = (s32[1,128]{1,0:T(1,128)S(1)}, s32[1,128]{1,0:T(1,128)S(1)}, u32[]{:S(2)}, u32[]{:S(2)}) collective-permute-start(s32[1,128]{1,0:T(1,128)S(1)} %get-tuple-element.18.asked.asked_row), channel_id=1, source_target_pairs={{0,2},{1,3},{2,0},{3,1},{4,6},{5,7},{6,4},{7,5},{8,10},{9,11},{10,... | collective-permute-start | bytes 1544 | tf_op jit(solution)/shard_map/ppermute | solution.py:270
  8.9 2.0 %collective-permute-start.1 = (s32[1,128]{1,0:T(1,128)S(1)}, s32[1,128]{1,0:T(1,128)S(1)}, u32[]{:S(2)}, u32[]{:S(2)}) collective-permute-start(s32[1,128]{1,0:T(1,128)S(1)} %get-tuple-element.18.asked.asked_row), channel_id=1, source_target_pairs={{0,3},{1,0},{2,1},{3,2},{4,7},{5,4},{6,5},{7,6},{8,11},{9,8},{10,9... | collective-permute-start | bytes 1544 | tf_op jit(solution)/shard_map/ppermute | solution.py:270
  12.5 7.2 %collective-permute-start.4 = (bf16[30,16,128]{2,1,0:T(8,128)(2,1)S(1)}, bf16[30,16,128]{2,1,0:T(8,128)(2,1)S(1)}, u32[]{:S(2)}, u32[]{:S(2)}) collective-permute-start(bf16[30,16,128]{2,1,0:T(8,128)(2,1)S(1)} %get-tuple-element.20), channel_id=1, source_target_pairs={{0,2},{1,3},{2,0},{3,1},{4,6},{5,7},{6,4},{7,5},{8,10},{9,11},{10,... | collective-permute-start | bytes 368648 | tf_op jit(solution)/shard_map/ppermute | solution.py:270
  14.1 5.6 %collective-permute-start.5 = (bf16[30,16,128]{2,1,0:T(8,128)(2,1)S(1)}, bf16[30,16,128]{2,1,0:T(8,128)(2,1)S(1)}, u32[]{:S(2)}, u32[]{:S(2)}) collective-permute-start(bf16[30,16,128]{2,1,0:T(8,128)(2,1)S(1)} %get-tuple-element.21), channel_id=1, source_target_pairs={{0,1},{1,2},{2,3},{3,0},{4,5},{5,6},{6,7},{7,4},{8,9},{9,10},{10,1... | collective-permute-start | bytes 368648 | tf_op jit(solution)/shard_map/ppermute | solution.py:270
  14.1 6.8 %collective-permute-start.6 = (bf16[30,16,128]{2,1,0:T(8,128)(2,1)S(1)}, bf16[30,16,128]{2,1,0:T(8,128)(2,1)S(1)}, u32[]{:S(2)}, u32[]{:S(2)}) collective-permute-start(bf16[30,16,128]{2,1,0:T(8,128)(2,1)S(1)} %get-tuple-element.22), channel_id=1, source_target_pairs={{4,8},{5,9},{6,10},{7,11},{8,12},{9,13},{10,14},{11,15},{20,24},{2... | collective-permute-start | bytes 368648 | tf_op jit(solution)/shard_map/ppermute | solution.py:270
  25.1 5.8 %collective-permute-start.9 = (bf16[31,16,128]{2,1,0:T(8,128)(2,1)S(1)}, bf16[31,16,128]{2,1,0:T(8,128)(2,1)S(1)}, u32[]{:S(2)}, u32[]{:S(2)}) collective-permute-start(bf16[31,16,128]{2,1,0:T(8,128)(2,1)S(1)} %get-tuple-element.27), channel_id=1, source_target_pairs={{0,3},{1,0},{2,1},{3,2},{4,7},{5,4},{6,5},{7,6},{8,11},{9,8},{10,9... | collective-permute-start | bytes 380936 | tf_op jit(solution)/shard_map/ppermute | solution.py:270
  25.7 9.3 %collective-permute-start.7 = (bf16[31,16,128]{2,1,0:T(8,128)(2,1)S(1)}, bf16[31,16,128]{2,1,0:T(8,128)(2,1)S(1)}, u32[]{:S(2)}, u32[]{:S(2)}) collective-permute-start(bf16[31,16,128]{2,1,0:T(8,128)(2,1)S(1)} %get-tuple-element.25), channel_id=1, source_target_pairs={{8,0},{9,1},{10,2},{11,3},{12,4},{13,5},{14,6},{15,7},{24,16},{25,... | collective-permute-start | bytes 380936 | tf_op jit(solution)/shard_map/ppermute | solution.py:270
  27.0 8.1 %collective-permute-start.8 = (bf16[31,16,128]{2,1,0:T(8,128)(2,1)S(1)}, bf16[31,16,128]{2,1,0:T(8,128)(2,1)S(1)}, u32[]{:S(2)}, u32[]{:S(2)}) collective-permute-start(bf16[31,16,128]{2,1,0:T(8,128)(2,1)S(1)} %get-tuple-element.26), channel_id=1, source_target_pairs={{2,0},{3,1},{4,2},{5,3},{6,4},{7,5},{8,6},{9,7},{10,8},{11,9},{12,... | collective-permute-start | bytes 380936 | tf_op jit(solution)/shard_map/ppermute | solution.py:270
  28.9 12.2 %collective-permute-start.10 = (bf16[31,16,128]{2,1,0:T(8,128)(2,1)S(1)}, bf16[31,16,128]{2,1,0:T(8,128)(2,1)S(1)}, u32[]{:S(2)}, u32[]{:S(2)}) collective-permute-start(bf16[31,16,128]{2,1,0:T(8,128)(2,1)S(1)} %get-tuple-element.28), channel_id=1, source_target_pairs={{4,0},{5,1},{6,2},{7,3},{8,4},{9,5},{10,6},{11,7},{12,8},{13,9},{1... | collective-permute-start | bytes 380936 | tf_op jit(solution)/shard_map/ppermute | solution.py:270
  30.8 10.2 %collective-permute-start.11 = (bf16[31,16,128]{2,1,0:T(8,128)(2,1)S(1)}, bf16[31,16,128]{2,1,0:T(8,128)(2,1)S(1)}, u32[]{:S(2)}, u32[]{:S(2)}) collective-permute-start(bf16[31,16,128]{2,1,0:T(8,128)(2,1)S(1)} %collective-permute-done.9.ring), channel_id=1, source_target_pairs={{7,3},{11,7},{15,11},{23,19},{27,23},{31,27}} | collective-permute-start | bytes 380936 | tf_op jit(solution)/shard_map/ppermute | solution.py:270
